TPU v7x, 32 devices: a whole 2x2x4 slice. The times are simulated.
32 devices in a mesh: enc: 8 (over y, x, core), rep: 4 (over z).
Axes of the slice: x: 2, y: 2, z: 4, core: 2. Of those that a mesh axis runs over, the one named last changes fastest.
Arguments:
- pixels: bfloat16 [4096, 1280], P(('enc', 'rep')), may hold values from -6 to 6
- window_owner: int32 [256], P(('enc', 'rep')), may hold values from 0 to 7, as said below
- window_len: int32 [256], P(('enc', 'rep')), may hold values from 4 to 16, as said below
- slot_token: int32 [5120], P(('enc', 'rep')), may hold values from -1 to 31, as said below
- cotangent: bfloat16 [5120, 5120], P(('enc', 'rep')), may hold values from -6 to 6
- w_qkv: bfloat16 [1280, 1920], replicated
- w_out: bfloat16 [640, 1280], replicated, may hold values from -0.25 to 0.25
- gain: float32 [1280], replicated, may hold values from 0.1 to 1.9
Outputs:
- embeddings: bfloat16 [5120, 5120], P(('enc', 'rep'))
- grad_w_out: float32 [640, 1280], P('enc')
Inputs may be any that keep to these rules, and one draw needn't show every extreme that they name: `window_owner`: the 8 windows of one device name distinct owners, taken in the device's own rep group; in each rep group one owner is named by a window of every device. `window_len`: A multiple of 4. `slot_token`: on the device of enc index o and rep index r, the value 4 * s + m names merged token m of the window that the device of enc index s and rep index r sends to o. Each such value appears exactly once, for every m < window_len / 4 of that window and for no other m; -1 marks other tokens. The merged tokens of one window stand in consecutive rows in order, wrapping around at the end of the device's rows.
All inputs are finite; a program needn't handle non-finite values.
Results may differ from a plain program's by a relative error of at most 0.012.
The roundings to bfloat16 on the way count: a program that leaves them out, or rounds other values in their place, can miss the bound.
Values may be sent and summed in bfloat16 or wider, within the bound.
No kernel may reach another device: no remote copies, remote signals or barrier semaphores. Data moves between devices by JAX's collectives and lax.ppermute only.
A program may use at most 64 MiB of HBM per device.

v0:
```python
import math

import jax
import jax.numpy as jnp
from jax import lax
from jax.sharding import PartitionSpec as P

HD = 80
HEADS = 8
MERGE = 4


def normalize(inputs, gain):
    values = inputs.astype(jnp.float32)
    mean_square = jnp.mean(values * values, axis=-1, keepdims=True)
    return (values * lax.rsqrt(mean_square + 1e-06) * gain).astype(jnp.bfloat16)


def encode(windows, lengths, w_qkv, w_out, gain):
    number, window_size, feature_width = windows.shape
    inner_width = w_out.shape[0]
    flat_rows = windows.reshape(number * window_size, feature_width)
    normed = normalize(flat_rows, gain)
    projected = jnp.dot(normed, w_qkv, preferred_element_type=jnp.float32).astype(jnp.bfloat16)
    queries = projected[:, :inner_width].reshape(number, window_size, HEADS, HD)
    keys_all = projected[:, inner_width : 2 * inner_width].reshape(number, window_size, HEADS, HD)
    values_all = projected[:, 2 * inner_width :].reshape(number, window_size, HEADS, HD)
    scores = jnp.einsum(
        "nqhd,nkhd->nhqk", queries, keys_all, preferred_element_type=jnp.float32
    ) / math.sqrt(HD)
    live_keys = jnp.arange(window_size, dtype=jnp.int32)[None, :] < lengths[:, None]
    scores = jnp.where(live_keys[:, None, None, :], scores, -1e30)
    weights = jax.nn.softmax(scores, axis=-1).astype(jnp.bfloat16)
    attended = jnp.einsum(
        "nhqk,nkhd->nqhd", weights, values_all, preferred_element_type=jnp.float32
    )
    attended = attended.astype(jnp.bfloat16).reshape(number * window_size, inner_width)
    encoded = flat_rows.astype(jnp.float32) + jnp.dot(
        attended, w_out, preferred_element_type=jnp.float32
    )
    return (encoded.astype(jnp.bfloat16), attended)


def shards(pixels, window_owner, window_len, slot_token, cotangent, w_qkv, w_out, gain):
    group_size = lax.axis_size("enc")
    replica_count = lax.axis_size("rep")
    feature_width = pixels.shape[1]
    window_count = window_owner.shape[0]
    window_rows = pixels.shape[0] // window_count
    tokens_each = window_rows // MERGE
    merged_width = MERGE * feature_width
    owner_ids = jnp.arange(group_size, dtype=jnp.int32)
    route = (window_owner[None, :] == owner_ids[:, None]).astype(jnp.bfloat16)
    slot_ids = jnp.arange(group_size * tokens_each, dtype=jnp.int32)
    placing = (slot_token[:, None] == slot_ids[None, :]).astype(jnp.bfloat16)
    encoded, attended = encode(
        pixels.reshape(window_count, window_rows, feature_width), window_len, w_qkv, w_out, gain
    )
    outgoing = jnp.dot(
        route,
        encoded.reshape(window_count, window_rows * feature_width),
        preferred_element_type=jnp.float32,
    )
    outgoing = outgoing.astype(jnp.bfloat16).reshape(group_size, tokens_each, merged_width)
    arrived = lax.all_to_all(outgoing, "enc", split_axis=0, concat_axis=0, tiled=True)
    embeddings = jnp.dot(
        placing,
        arrived.reshape(group_size * tokens_each, merged_width),
        preferred_element_type=jnp.float32,
    ).astype(jnp.bfloat16)
    returning = lax.dot_general(
        placing, cotangent, (((0,), (0,)), ((), ())), preferred_element_type=jnp.float32
    )
    returning = returning.astype(jnp.bfloat16).reshape(group_size, tokens_each, merged_width)
    answered = lax.all_to_all(returning, "enc", split_axis=0, concat_axis=0, tiled=True)
    d_encoded = lax.dot_general(
        route,
        answered.reshape(group_size, tokens_each * merged_width),
        (((0,), (0,)), ((), ())),
        preferred_element_type=jnp.float32,
    )
    d_encoded = d_encoded.astype(jnp.bfloat16).reshape(window_count * window_rows, feature_width)
    reduced = lax.psum_scatter(
        lax.dot_general(
            attended, d_encoded, (((0,), (0,)), ((), ())), preferred_element_type=jnp.float32
        ),
        "enc",
        scatter_dimension=0,
        tiled=True,
    )
    summed = lax.psum(reduced, "rep")
    patch_total = window_count * window_rows * group_size * replica_count
    gradient = summed / math.sqrt(patch_total)
    return (embeddings, gradient)


def solution(mesh):
    return jax.shard_map(
        shards,
        mesh=mesh,
        in_specs=(
            P(("enc", "rep"), None),
            P(("enc", "rep")),
            P(("enc", "rep")),
            P(("enc", "rep")),
            P(("enc", "rep"), None),
            P(),
            P(),
            P(),
        ),
        out_specs=(P(("enc", "rep"), None), P("enc", None)),
        check_vma=False,
    )
```

profile of v0, /device:TPU:0, one launch (start us, length us, event | category | flops | bytes accessed | tf_op | source)
XLA Modules:
  0.0 123.2 jit_solution(14460333167618268343)
XLA Ops:
  7.2 0.0 copy-start
  7.2 0.0 copy-start.1
  7.2 0.0 copy-start.2
  7.2 1.4 %copy-done = bf16[160,5120]{1,0:T(8,128)(2,1)S(1)} copy-done((bf16[160,5120]{1,0:T(8,128)(2,1)S(1)}, bf16[160,5120]{1,0:T(8,128)(2,1)}, u32[]{:S(2)}) %copy-start) | copy-done | bytes 1638424
  8.6 1.1 convolution_convert_fusion.3
  9.7 0.9 reshape.71
  10.6 5.2 %all-to-all-start.1 = ((bf16[8,4,5120]{2,1,0:T(4,128)(2,1)}), bf16[8,4,5120]{2,1,0:T(4,128)(2,1)S(1)}, u32[]{:S(2)}, u32[]{:S(2)}) async-start(bf16[8,4,5120]{2,1,0:T(4,128)(2,1)} %reshape.71), calls=%async_computation.1 | async-start | bytes 655360 | tf_op jit(solution)/shard_map/all_to_all | solution.py:75
  15.8 0.0 reduce-scatter.2.cloned.1.call-start
  15.8 0.0 copy-done.1
  15.8 0.1 fusion.6
  16.0 0.0 copy-done.2
  16.0 3.3 %convolution_convert_fusion.4 = bf16[128,1920]{1,0:T(8,128)(2,1)S(1)} fusion(bf16[1280,1920]{1,0:T(8,128)(2,1)} %param.13, bf16[128,1280]{1,0:T(8,128)(2,1)S(1)} %copy-done.1, f32[1280]{0:T(1024)S(1)} %copy-done.2, f32[128]{0:T(128)S(1)} %add_rsqrt_fusion), kind=kOutput, calls=%fused_computation.7 | convolution fusion | flops 630046720 | bytes 5740032 | tf_op jit(solution)/shard_map/dot_general | solution.py:24
  19.4 0.0 copy-start.5
  19.4 0.3 reshape.65
  19.7 0.3 reshape.66
  20.0 0.0 copy-done.5
  20.0 0.1 iota_compare_fusion.3
  20.1 1.1 fusion.4
  21.2 0.4 fusion.26
  21.6 0.3 reshape.64
  21.8 0.0 copy-start.4
  21.8 1.6 %fusion.5 = bf16[8,16,8,80]{3,1,2,0:T(8,128)(2,1)S(1)} fusion(bf16[8,16,8,80]{3,2,1,0:T(8,128)(2,1)S(1)} %reshape.64, f32[8,8,16]{2,1,0:T(8,128)S(1)} %fusion.26, f32[8,8,16,16]{2,3,1,0:T(8,128)} %fusion.4), kind=kOutput, calls=%fused_computation.13 | convolution fusion | flops 2753551 | bytes 397312 | tf_op jit(solution)/shard_map/nhqk,nkhd->nqhd/dot_general | solution.py:34
  23.4 0.1 copy.18
  23.5 0.2 reshape.67
  23.7 0.0 all-to-all-done.1
  23.7 0.1 copy.21
  23.8 0.0 copy-done.4
  23.8 0.3 convolution_convert_fusion
  24.1 0.2 reshape.73
  24.3 2.3 %fusion.31 = f32[640,1280]{1,0:T(8,128)} fusion(bf16[128,640]{1,0:T(8,128)(2,1)S(1)} %reshape.67, bf16[128,1280]{1,0:T(8,128)(2,1)S(1)} %reshape.73), kind=kOutput, calls=%fused_computation.38 | convolution fusion | flops 209715200 | bytes 3768320 | tf_op jit(solution)/shard_map/dot_general | solution.py:84
  26.6 0.0 reduce-scatter.2.cloned.1.call-update
  26.6 1.9 %fusion.1 = bf16[128,1280]{1,0:T(8,128)(2,1)S(1)} fusion(bf16[128,640]{1,0:T(8,128)(2,1)S(1)} %reshape.67, bf16[640,1280]{1,0:T(8,128)(2,1)} %param.14, bf16[128,1280]{1,0:T(8,128)(2,1)S(1)} %copy-done.1), kind=kOutput, calls=%fused_computation.6 | convolution fusion | flops 210206720 | bytes 2457600 | tf_op jit(solution)/shard_map/dot_general | solution.py:38
  28.5 0.2 reshape.68
  28.7 0.0 copy-start.3
  28.7 0.2 convolution_convert_fusion.1
  28.9 1.0 copy.19
  29.9 4.2 %all-to-all-start = ((bf16[8,4,5120]{2,1,0:T(4,128)(2,1)}), bf16[8,4,5120]{2,1,0:T(4,128)(2,1)S(1)}, u32[]{:S(2)}, u32[]{:S(2)}) async-start(bf16[8,4,5120]{2,1,0:T(4,128)(2,1)} %copy.19), calls=%async_computation | async-start | bytes 655360 | tf_op jit(solution)/shard_map/all_to_all | solution.py:65
  34.1 0.0 all-reduce.2.cloned.1.call-start
  34.1 41.2 %reduce-scatter.2.cloned.1.call-done = f32[80,1280]{1,0:T(8,128)} async-done(((f32[640,1280]{1,0:T(8,128)}), f32[80,1280]{1,0:T(8,128)}) %reduce-scatter.2.cloned.1.call-update) | async-done | bytes 409616 | tf_op jit(solution)/shard_map/reduce_scatter | solution.py:83
  75.3 0.0 all-reduce.2.cloned.1.call-update
  75.3 0.0 all-to-all-done
  75.4 0.1 reshape.70
  75.4 0.0 copy-done.3
  75.4 1.8 %convolution_convert_fusion.2 = bf16[160,5120]{1,0:T(8,128)(2,1)} fusion(bf16[32,5120]{1,0:T(8,128)(2,1)S(1)} %reshape.70, s32[160]{0:T(256)S(1)} %copy-done.3), kind=kOutput, calls=%fused_computation.3 | convolution fusion | flops 53253120 | bytes 1966720 | tf_op jit(solution)/shard_map/dot_general | solution.py:66
  77.2 37.3 %all-reduce.2.cloned.1.call-done = f32[80,1280]{1,0:T(8,128)} async-done(((f32[80,1280]{1,0:T(8,128)}), f32[80,1280]{1,0:T(8,128)}) %all-reduce.2.cloned.1.call-update) | async-done | bytes 409616 | tf_op jit(solution)/shard_map/psum | solution.py:91
  114.6 1.8 %broadcast_multiply_fusion = f32[80,1280]{1,0:T(8,128)} fusion(f32[80,1280]{1,0:T(8,128)} %all-reduce.2.cloned.1.call-done), kind=kLoop, calls=%fused_computation.26 | loop fusion | flops 102400 | bytes 819200 | tf_op jit(solution)/shard_map/div | solution.py:93
  (2 shorter events, 0.1 us)
Async XLA Ops:
  7.2 1.4 %copy-start = (bf16[160,5120]{1,0:T(8,128)(2,1)S(1)}, bf16[160,5120]{1,0:T(8,128)(2,1)}, u32[]{:S(2)}) copy-start(bf16[160,5120]{1,0:T(8,128)(2,1)} %param.12) | copy-start | bytes 4915204
  7.2 8.7 %copy-start.1 = (bf16[128,1280]{1,0:T(8,128)(2,1)S(1)}, bf16[128,1280]{1,0:T(8,128)(2,1)}, u32[]{:S(2)}) copy-start(bf16[128,1280]{1,0:T(8,128)(2,1)} %param.8) | copy-start | bytes 983044
  7.2 8.8 %copy-start.2 = (f32[1280]{0:T(1024)S(1)}, f32[1280]{0:T(1024)}, u32[]{:S(2)}) copy-start(f32[1280]{0:T(1024)} %param.15) | copy-start | bytes 15364
  10.6 13.1 %all-to-all-start.1 = ((bf16[8,4,5120]{2,1,0:T(4,128)(2,1)}), bf16[8,4,5120]{2,1,0:T(4,128)(2,1)S(1)}, u32[]{:S(2)}, u32[]{:S(2)}) async-start(bf16[8,4,5120]{2,1,0:T(4,128)(2,1)} %reshape.71), calls=%async_computation.1 | async-start | bytes 655360 | tf_op jit(solution)/shard_map/all_to_all | solution.py:75
  15.8 59.5 %reduce-scatter.2.cloned.1.call-start = ((), (), s32[]{:S(2)}) async-start(), calls=%async_computation.3 | async-start | bytes 3686400 | tf_op jit(solution)/shard_map/reduce_scatter | solution.py:83
  19.4 0.7 copy-start.5
  21.8 2.0 %copy-start.4 = (s32[8]{0:T(128)S(1)}, s32[8]{0:T(128)}, u32[]{:S(2)}) copy-start(s32[8]{0:T(128)} %param.9) | copy-start | bytes 100
  28.7 46.8 %copy-start.3 = (s32[160]{0:T(256)S(1)}, s32[160]{0:T(256)}, u32[]{:S(2)}) copy-start(s32[160]{0:T(256)} %param.11) | copy-start | bytes 1924
  29.9 45.4 %all-to-all-start = ((bf16[8,4,5120]{2,1,0:T(4,128)(2,1)}), bf16[8,4,5120]{2,1,0:T(4,128)(2,1)S(1)}, u32[]{:S(2)}, u32[]{:S(2)}) async-start(bf16[8,4,5120]{2,1,0:T(4,128)(2,1)} %copy.19), calls=%async_computation | async-start | bytes 655360 | tf_op jit(solution)/shard_map/all_to_all | solution.py:65
  34.1 80.5 %all-reduce.2.cloned.1.call-start = ((), (), s32[]{:S(2)}) async-start(), calls=%async_computation.4 | async-start | bytes 819200 | tf_op jit(solution)/shard_map/psum | solution.py:91
Sparse Core Ops, SparseCore 0:
  26.7 48.5 reduce-scatter.1
  77.7 36.8 all-reduce.1
where the time goes:
time: 124 us; the launch traced here: 123 us
  waiting for transfers between devices  78.6 us (63%)
  between operations  14.2 us (11%)
  matrix products  14 us (11%)
  starting transfers between devices  9.41 us (8%)
  local copies, waits for them, and re-layouts  4.93 us (4%)
  other arithmetic  2.01 us (2%)
    reduce_scatter x1, waiting for transfers between devices, shards(): lax.psum_scatter(lax.dot_general(attended, d_encoded, (((0,), (0,)), ((),...  41.2 us
    psum x1, waiting for transfers between devices, shards(): summed = lax.psum(reduced, 'rep')  37.3 us
    all_to_all x1, starting transfers between devices, shards(): lax.all_to_all(returning, 'enc', split_axis=0, concat_axis=0, tiled=True)  5.18 us
    all_to_all x1, starting transfers between devices, shards(): lax.all_to_all(outgoing, 'enc', split_axis=0, concat_axis=0, tiled=True)  4.16 us
    dot_general x1, matrix products, encode(): jnp.dot(normed, w_qkv, preferred_element_type=jnp.float32)  3.35 us
  transfers between devices with their start and end apart: 4, of which 2 were waited for; matrix products, arithmetic and copies ran while one was open for 10% of the time, Pallas kernels for 0%

commit v1 on v0

--- a/solution.py
+++ b/solution.py
@@ -16,9 +16,9 @@
     return (values * lax.rsqrt(mean_square + 1e-06) * gain).astype(jnp.bfloat16)
 
 
-def encode(windows, lengths, w_qkv, w_out, gain):
+def attend(windows, lengths, w_qkv, gain):
     number, window_size, feature_width = windows.shape
-    inner_width = w_out.shape[0]
+    inner_width = w_qkv.shape[1] // 3
     flat_rows = windows.reshape(number * window_size, feature_width)
     normed = normalize(flat_rows, gain)
     projected = jnp.dot(normed, w_qkv, preferred_element_type=jnp.float32).astype(jnp.bfloat16)
@@ -34,14 +34,17 @@
     attended = jnp.einsum(
         "nhqk,nkhd->nqhd", weights, values_all, preferred_element_type=jnp.float32
     )
-    attended = attended.astype(jnp.bfloat16).reshape(number * window_size, inner_width)
+    return attended.astype(jnp.bfloat16).reshape(number * window_size, inner_width)
+
+
+def project(flat_rows, attended, w_out):
     encoded = flat_rows.astype(jnp.float32) + jnp.dot(
         attended, w_out, preferred_element_type=jnp.float32
     )
-    return (encoded.astype(jnp.bfloat16), attended)
-
-
-def shards(pixels, window_owner, window_len, slot_token, cotangent, w_qkv, w_out, gain):
+    return encoded.astype(jnp.bfloat16)
+
+
+def any_slice(pixels, window_owner, window_len, slot_token, cotangent, w_qkv, w_out, gain):
     group_size = lax.axis_size("enc")
     replica_count = lax.axis_size("rep")
     feature_width = pixels.shape[1]
@@ -53,9 +56,10 @@
     route = (window_owner[None, :] == owner_ids[:, None]).astype(jnp.bfloat16)
     slot_ids = jnp.arange(group_size * tokens_each, dtype=jnp.int32)
     placing = (slot_token[:, None] == slot_ids[None, :]).astype(jnp.bfloat16)
-    encoded, attended = encode(
-        pixels.reshape(window_count, window_rows, feature_width), window_len, w_qkv, w_out, gain
-    )
+    attended = attend(
+        pixels.reshape(window_count, window_rows, feature_width), window_len, w_qkv, gain
+    )
+    encoded = project(pixels, attended, w_out)
     outgoing = jnp.dot(
         route,
         encoded.reshape(window_count, window_rows * feature_width),
@@ -94,7 +98,92 @@
     return (embeddings, gradient)
 
 
+def swap(value, axis, bits):
+    size = lax.axis_size(axis)
+    return lax.ppermute(value, axis, [(i, i ^ bits) for i in range(size)])
+
+
+def xor_slice(pixels, window_owner, window_len, slot_token, cotangent, w_qkv, w_out, gain):
+    group = lax.axis_size("enc")
+    replicas = lax.axis_size("rep")
+    width = pixels.shape[1]
+    windows = window_owner.shape[0]
+    rows = pixels.shape[0]
+    window_rows = rows // windows
+    inner = w_out.shape[0]
+    head_columns = inner // group
+    row_ids = jnp.arange(rows, dtype=jnp.int32)
+    slot_of = row_ids // MERGE
+    me = lax.axis_index("enc")
+
+    held = jnp.zeros((rows, width), jnp.float32)
+    for j in range(MERGE):
+        pick = (slot_token[None, :] == slot_of[:, None]) & (row_ids[:, None] % MERGE == j)
+        held = held + jnp.dot(
+            pick.astype(jnp.bfloat16),
+            cotangent[:, j * width : (j + 1) * width],
+            preferred_element_type=jnp.float32,
+        )
+    held = held.astype(jnp.bfloat16)
+    blocks = {0: held}
+    for b in range(2, group, 2):
+        blocks[b] = swap(held, "enc", b)
+    for b in range(0, group, 2):
+        blocks[b + 1] = swap(blocks[b], "enc", 1)
+
+    owner_ids = jnp.arange(group, dtype=jnp.int32)
+    route = window_owner[None, :] == owner_ids[:, None]
+    lengths = jnp.sum(jnp.where(route, window_len[None, :], 0), axis=1)
+    by_row = jnp.repeat(jnp.repeat(route, window_rows, 0), window_rows, 1)
+    by_row = by_row & (row_ids[:, None] % window_rows == row_ids[None, :] % window_rows)
+    ordered = jnp.dot(
+        by_row.astype(jnp.bfloat16), pixels, preferred_element_type=jnp.float32
+    ).astype(jnp.bfloat16)
+    attended = attend(ordered.reshape(windows, window_rows, width), lengths, w_qkv, gain)
+    columns = attended.T.reshape(group, head_columns, rows)
+    gathered = lax.all_to_all(columns, "enc", split_axis=0, concat_axis=0, tiled=True)
+    encoded = project(ordered, attended, w_out)
+    arrived = lax.all_to_all(encoded, "enc", split_axis=0, concat_axis=0, tiled=True)
+
+    total = jnp.zeros((head_columns, width), jnp.float32)
+    relative = (row_ids[:, None] // window_rows) == ((row_ids[None, :] // window_rows) ^ me)
+    relative = relative & (row_ids[:, None] % window_rows == row_ids[None, :] % window_rows)
+    turned = jnp.dot(
+        gathered.reshape(group * head_columns, rows),
+        relative.astype(jnp.bfloat16),
+        preferred_element_type=jnp.float32,
+    ).astype(jnp.bfloat16)
+    stacked = jnp.stack([blocks[b].reshape(group, window_rows, width) for b in range(group)], 1)
+    total = jnp.einsum(
+        "scp,spf->cf",
+        turned.reshape(group, head_columns, rows),
+        stacked.reshape(group, rows, width),
+        preferred_element_type=jnp.float32,
+    )
+    total = total / math.sqrt(rows * group * replicas)
+    bit = 1
+    while bit < replicas:
+        part = total.astype(jnp.bfloat16)
+        total = part.astype(jnp.float32) + swap(part, "rep", bit).astype(jnp.float32)
+        bit *= 2
+
+    embeddings = []
+    for j in range(MERGE):
+        put = (slot_token[:, None] == slot_of[None, :]) & (row_ids[None, :] % MERGE == j)
+        embeddings.append(
+            jnp.dot(put.astype(jnp.bfloat16), arrived, preferred_element_type=jnp.float32)
+        )
+    return (jnp.concatenate(embeddings, 1).astype(jnp.bfloat16), total)
+
+
 def solution(mesh):
+    def shards(*args):
+        group = mesh.shape["enc"]
+        replicas = mesh.shape["rep"]
+        powers = group & (group - 1) == 0 and replicas & (replicas - 1) == 0
+        whole = powers and args[1].shape[0] == group
+        return (xor_slice if whole else any_slice)(*args)
+
     return jax.shard_map(
         shards,
         mesh=mesh,

time: 124 us -> 76.4 us (0.62)
  waiting for transfers between devices: 78.6 us -> 24.8 us
  between operations: 14.2 us -> 1.02 us
  local copies, waits for them, and re-layouts: 4.93 us -> 13.7 us
  starting transfers between devices: 9.41 us -> 17.2 us
  matrix products: 14 us -> 16 us
    reduce_scatter x1 -> x0, waiting for transfers between devices: 41.2 us -> none  [shards(): lax.psum_scatter(lax.dot_general(attended, d_encoded, (((0,), (0,)), ((),...]
    psum x1 -> x0, waiting for transfers between devices: 37.3 us -> none  [shards(): summed = lax.psum(reduced, 'rep')]
    ppermute x0 -> x9, waiting for transfers between devices: none -> 13.5 us  [swap(): return lax.ppermute(value, axis, [(i, i ^ bits) for i in range(size)])]
    all_to_all x2, waiting for transfers between devices: 0.01 us -> 11.2 us  [the longest x1 7.28 us: xor_slice(): lax.all_to_all(encoded, 'enc', split_axis=0, concat_axis=0, tiled=True)]
    ppermute x0 -> x9, starting transfers between devices: none -> 9.55 us  [swap(): return lax.ppermute(value, axis, [(i, i ^ bits) for i in range(size)])]
    unnamed x13 -> x31, local copies, waits for them, and re-layouts: 1.58 us -> 8.19 us
    another operation x0 -> x2, local copies, waits for them, and re-layouts: none -> 2.69 us  [xor_slice(): jnp.stack([blocks[b].reshape(group, window_rows, width) for b in range(gr...]
    div x1 -> x0, other arithmetic: 1.78 us -> none  [shards(): gradient = summed / math.sqrt(patch_total)]
  transfers between devices with their start and end apart: 4 -> 11, of which waited for: 2 -> 4; matrix products, arithmetic and copies ran while one was open for 10% -> 33% of each run, Pallas kernels for 0% -> 0%
where the time goes in v1:
time: 76.4 us; the launch traced here: 75.8 us
  waiting for transfers between devices  24.8 us (32%)
  starting transfers between devices  17.2 us (23%)
  matrix products  16 us (21%)
  local copies, waits for them, and re-layouts  13.7 us (18%)
  other arithmetic  3.15 us (4%)
  between operations  1.02 us (1%)
    ppermute x9, waiting for transfers between devices, swap(): return lax.ppermute(value, axis, [(i, i ^ bits) for i in range(size)])  13.5 us
    ppermute x9, starting transfers between devices, swap(): return lax.ppermute(value, axis, [(i, i ^ bits) for i in range(size)])  9.55 us
    unnamed x31, local copies, waits for them, and re-layouts  8.19 us
    all_to_all x1, waiting for transfers between devices, xor_slice(): lax.all_to_all(encoded, 'enc', split_axis=0, concat_axis=0, tiled=True)  7.28 us
    all_to_all x1, starting transfers between devices, xor_slice(): lax.all_to_all(columns, 'enc', split_axis=0, concat_axis=0, tiled=True)  4.17 us
    all_to_all x1, waiting for transfers between devices, xor_slice(): lax.all_to_all(columns, 'enc', split_axis=0, concat_axis=0, tiled=True)  3.95 us
    all_to_all x1, starting transfers between devices, xor_slice(): lax.all_to_all(encoded, 'enc', split_axis=0, concat_axis=0, tiled=True)  3.43 us
    dot_general x4, matrix products, xor_slice(): jnp.dot(pick.astype(jnp.bfloat16), cotangent[:, j * width:(j + 1) * width...  3.42 us
  transfers between devices with their start and end apart: 11, of which 4 were waited for; matrix products, arithmetic and copies ran while one was open for 33% of the time, Pallas kernels for 0%

profile of v1, /device:TPU:0, one launch (start us, length us, event | category | flops | bytes accessed | tf_op | source)
XLA Modules:
  0.0 75.8 jit_solution(1828373302334434798)
XLA Ops:
  0.6 0.0 copy-start
  0.6 0.0 copy-start.3
  0.7 0.0 copy-start.1
  0.8 1.5 %fusion.13 = f32[128,1280]{1,0:T(8,128)S(1)} fusion(bf16[160,5120]{1,0:T(8,128)(2,1)} %param.12, s32[160]{0:T(256)} %param.11, s32[128]{0:T(128)S(1)} %and_select_fusion.3, pred[128]{0:T(512)(128)(4,1)S(1)} %broadcast_compare_fusion.1), kind=kOutput, calls=%fused_computation.33 | convolution fusion | flops 52469760 | bytes 1066624 | tf_op jit(solution)/shard_map/dot_general | solution.py:122
  2.2 0.0 copy-start.11
  2.2 0.0 copy-start.2
  2.3 0.0 copy-start.4
  2.3 1.4 %convolution_add_fusion.3 = f32[128,1280]{1,0:T(8,128)S(1)} fusion(f32[128,1280]{1,0:T(8,128)S(1)} %fusion.13, bf16[160,5120]{1,0:T(8,128)(2,1)} %param.12, s32[160]{0:T(256)} %param.11, s32[128]{0:T(128)S(1)} %and_select_fusion.3, pred[128]{0:T(512)(128)(4,1)S(1)} %fusion.53), kind=kOutput, calls=%fused_computation.4 | convolution fusion | flops 52633600 | bytes 1721984 | tf_op jit(solution)/shard_map/dot_general | solution.py:122
  3.7 0.3 convolution_add_fusion.2
  4.0 0.3 fusion.1
  4.3 0.5 collective-permute-start
  4.8 2.6 %collective-permute-start.1 = (bf16[128,1280]{1,0:T(8,128)(2,1)S(1)}, bf16[128,1280]{1,0:T(8,128)(2,1)}, u32[]{:S(2)}, u32[]{:S(2)}) collective-permute-start(bf16[128,1280]{1,0:T(8,128)(2,1)S(1)} %fusion.1), channel_id=1, source_target_pairs={{0,8},{4,12},{8,0},{12,4},{16,24},{20,28},{24,16},{28,20},{1,9},{5... | collective-permute-start | bytes 983048 | tf_op jit(solution)/shard_map/ppermute | solution.py:103
  7.4 1.5 %collective-permute-start.3 = (bf16[128,1280]{1,0:T(8,128)(2,1)S(1)}, bf16[128,1280]{1,0:T(8,128)(2,1)}, u32[]{:S(2)}, u32[]{:S(2)}) collective-permute-start(bf16[128,1280]{1,0:T(8,128)(2,1)S(1)} %fusion.1), channel_id=1, source_target_pairs={{0,16},{4,20},{8,24},{12,28},{16,0},{20,4},{24,8},{28,12},{1,17},{... | collective-permute-start | bytes 983048 | tf_op jit(solution)/shard_map/ppermute | solution.py:103
  8.9 0.0 collective-permute-start.5
  8.9 0.1 iota_compare_fusion.1
  9.0 0.1 broadcast_in_dim.24
  9.1 0.1 reshape.248
  9.2 0.4 multiply_reduce_fusion
  9.7 3.3 %convolution_convert_fusion.4 = bf16[128,1920]{1,0:T(8,128)(2,1)S(1)} fusion(bf16[1280,1920]{1,0:T(8,128)(2,1)} %param.13, f32[128,1280]{1,0:T(8,128)S(1)} %get-tuple-element.6, f32[1280]{0:T(1024)S(1)} %copy-done.4, f32[128]{0:T(128)S(1)} %add_rsqrt_fusion), kind=kOutput, calls=%fused_computation.11 | convolution fusion | flops 629882880 | bytes 6067712 | tf_op jit(solution)/shard_map/dot_general | solution.py:24
  13.1 1.0 %reshape.251 = bf16[8,16,8,80]{3,2,1,0:T(8,128)(2,1)} reshape(bf16[128,640]{1,0:T(8,128)(2,1)S(1)} %get-tuple-element.2) | data formatting | bytes 327680 | tf_op jit(solution)/shard_map/reshape | solution.py:25
  14.0 0.3 reshape.252
  14.3 0.8 %select_reduce_fusion = s32[8]{0:T(128)S(1)} fusion(s32[8]{0:T(128)} %param.10, s32[8]{0:T(128)} %param.9), kind=kLoop, calls=%fused_computation.90 | loop fusion | flops 184 | bytes 96 | tf_op jit(solution)/shard_map/reduce_sum | solution.py:136
  15.1 0.1 iota_compare_fusion
  15.1 2.0 %fusion.8 = f32[8,8,16,16]{2,3,1,0:T(8,128)} fusion(bf16[8,16,8,80]{3,2,1,0:T(8,128)(2,1)S(1)} %reshape.252, bf16[8,16,8,80]{3,2,1,0:T(8,128)(2,1)} %reshape.251, pred[8,16]{1,0:T(8,128)(4,1)S(1)} %iota_compare_fusion), kind=kOutput, calls=%fused_computation.21 | convolution fusion | flops 2654208 | bytes 393344 | tf_op jit(solution)/shard_map/nqhd,nkhd->nhqk/dot_general | solution.py:28
  17.2 2.0 %fusion.59 = f32[8,8,16]{2,1,0:T(8,128)} fusion(bf16[8,16,8,80]{3,2,1,0:T(8,128)(2,1)S(1)} %reshape.252, bf16[8,16,8,80]{3,2,1,0:T(8,128)(2,1)} %reshape.251, pred[8,16]{1,0:T(8,128)(4,1)S(1)} %iota_compare_fusion), kind=kOutput, calls=%fused_computation.109 | convolution fusion | flops 2686991 | bytes 331904 | tf_op jit(solution)/shard_map/sub | solution.py:33
  19.1 0.3 reshape.250
  19.4 1.6 %fusion.9 = bf16[8,16,8,80]{3,1,2,0:T(8,128)(2,1)S(1)} fusion(bf16[8,16,8,80]{3,2,1,0:T(8,128)(2,1)S(1)} %reshape.250, f32[8,8,16]{2,1,0:T(8,128)} %fusion.59, f32[8,8,16,16]{2,3,1,0:T(8,128)} %fusion.8), kind=kOutput, calls=%fused_computation.23 | convolution fusion | flops 2753551 | bytes 397312 | tf_op jit(solution)/shard_map/nhqk,nkhd->nqhd/dot_general | solution.py:34
  21.0 0.1 copy.19
  21.0 0.2 reshape.253
  21.3 0.8 %copy.20 = bf16[640,128]{1,0:T(8,128)(2,1)} copy(bf16[640,128]{0,1:T(8,128)(2,1)S(1)} %bitcast.45) | data formatting | bytes 327680 | tf_op jit(solution)/shard_map/transpose | solution.py:143
  22.1 4.2 %all-to-all-start.1 = ((bf16[8,80,128]{2,1,0:T(8,128)(2,1)}), bf16[8,80,128]{2,1,0:T(8,128)(2,1)S(1)}, u32[]{:S(2)}, u32[]{:S(2)}) async-start(bf16[8,80,128]{2,1,0:T(8,128)(2,1)} %bitcast.5), calls=%async_computation.1 | async-start | bytes 327680 | tf_op jit(solution)/shard_map/all_to_all | solution.py:144
  26.3 1.2 %fusion.2 = bf16[128,1280]{1,0:T(8,128)(2,1)} fusion(f32[128,1280]{1,0:T(8,128)S(1)} %get-tuple-element.6, bf16[128,640]{1,0:T(8,128)(2,1)S(1)} %reshape.253, bf16[640,1280]{1,0:T(8,128)(2,1)S(1)} %copy-done), kind=kOutput, calls=%fused_computation.10 | convolution fusion | flops 210042880 | bytes 2785280 | tf_op jit(solution)/shard_map/dot_general | solution.py:41
  27.4 0.7 constant_dynamic-update-slice_fusion.7
  28.2 4.0 %all-to-all-done.1 = bf16[8,80,128]{2,1,0:T(8,128)(2,1)S(1)} async-done(((bf16[8,80,128]{2,1,0:T(8,128)(2,1)}), bf16[8,80,128]{2,1,0:T(8,128)(2,1)S(1)}, u32[]{:S(2)}, u32[]{:S(2)}) %all-to-all-start.1) | async-done | bytes 163872 | tf_op jit(solution)/shard_map/all_to_all | solution.py:144
  32.1 3.4 %all-to-all-start = ((bf16[8,16,1280]{2,1,0:T(8,128)(2,1)}), bf16[8,16,1280]{2,1,0:T(8,128)(2,1)S(1)}, u32[]{:S(2)}, u32[]{:S(2)}) async-start(bf16[8,16,1280]{2,1,0:T(8,128)(2,1)} %bitcast.2), calls=%async_computation | async-start | bytes 655360 | tf_op jit(solution)/shard_map/all_to_all | solution.py:146
  35.6 0.3 convolution_convert_fusion.7
  35.9 7.3 %all-to-all-done = bf16[8,16,1280]{2,1,0:T(8,128)(2,1)S(1)} async-done(((bf16[8,16,1280]{2,1,0:T(8,128)(2,1)}), bf16[8,16,1280]{2,1,0:T(8,128)(2,1)S(1)}, u32[]{:S(2)}, u32[]{:S(2)}) %all-to-all-start) | async-done | bytes 327712 | tf_op jit(solution)/shard_map/all_to_all | solution.py:146
  43.1 0.3 convolution_convert_fusion
  43.5 0.3 convolution_convert_fusion.1
  43.8 0.3 convolution_convert_fusion.2
  44.1 0.1 collective-permute-start.2
  44.2 0.0 collective-permute-done
  44.2 1.7 %constant_dynamic-update-slice_fusion.6 = bf16[8,8,16,1280]{3,2,0,1:T(8,128)(2,1)} fusion(bf16[8,8,16,1280]{3,2,0,1:T(8,128)(2,1)} %constant_dynamic-update-slice_fusion.7, bf16[8,1,16,1280]{3,2,0,1:T(8,128)(2,1)} %bitcast.9), kind=kLoop, calls=%fused_computation.88 | loop fusion | bytes 655360
  46.0 0.0 collective-permute-done.3
  46.0 0.5 collective-permute-start.4
  46.4 0.0 collective-permute-done.5
  46.4 0.1 collective-permute-start.6
  46.5 1.7 %constant_dynamic-update-slice_fusion.5 = bf16[8,8,16,1280]{3,2,0,1:T(8,128)(2,1)} fusion(bf16[8,8,16,1280]{3,2,0,1:T(8,128)(2,1)} %constant_dynamic-update-slice_fusion.6, bf16[8,1,16,1280]{3,2,0,1:T(8,128)(2,1)} %bitcast.10), kind=kLoop, calls=%fused_computation.87 | loop fusion | bytes 655360
  48.2 0.0 collective-permute-done.2
  48.2 0.8 %constant_dynamic-update-slice_fusion.4 = bf16[8,8,16,1280]{3,2,0,1:T(8,128)(2,1)} fusion(bf16[8,8,16,1280]{3,2,0,1:T(8,128)(2,1)} %constant_dynamic-update-slice_fusion.5, bf16[8,1,16,1280]{3,2,0,1:T(8,128)(2,1)S(1)} %bitcast.50), kind=kLoop, calls=%fused_computation.86 | loop fusion | bytes 655360
  49.0 1.7 %constant_dynamic-update-slice_fusion.3 = bf16[8,8,16,1280]{3,2,0,1:T(8,128)(2,1)} fusion(bf16[8,8,16,1280]{3,2,0,1:T(8,128)(2,1)} %constant_dynamic-update-slice_fusion.4, bf16[8,1,16,1280]{3,2,0,1:T(8,128)(2,1)} %bitcast.12), kind=kLoop, calls=%fused_computation.85 | loop fusion | bytes 655360
  50.7 0.7 constant_dynamic-update-slice_fusion.2
  51.5 0.7 constant_dynamic-update-slice_fusion.1
  52.2 0.7 constant_dynamic-update-slice_fusion
  52.9 2.0 %copy.21 = bf16[8,8,16,1280]{3,2,1,0:T(8,128)(2,1)S(1)} copy(bf16[8,8,16,1280]{3,2,0,1:T(8,128)(2,1)} %constant_dynamic-update-slice_fusion) | data formatting | bytes 5242880 | tf_op jit(solution)/shard_map/stack | solution.py:156
  54.9 0.6 fusion.5
  55.5 1.6 %collective-permute-start.7 = (bf16[80,1280]{1,0:T(8,128)(2,1)S(1)}, bf16[80,1280]{1,0:T(8,128)(2,1)S(1)}, u32[]{:S(2)}, u32[]{:S(2)}) collective-permute-start(bf16[80,1280]{1,0:T(8,128)(2,1)S(1)} %fusion.5), channel_id=1, source_target_pairs={{0,1},{1,0},{2,3},{3,2},{4,5},{5,4},{6,7},{7,6},{8,9},{9,8},{10,11... | collective-permute-start | bytes 614408 | tf_op jit(solution)/shard_map/ppermute | solution.py:103
  57.1 0.3 convolution_convert_fusion.3
  57.5 5.5 %collective-permute-done.7 = bf16[80,1280]{1,0:T(8,128)(2,1)S(1)} collective-permute-done((bf16[80,1280]{1,0:T(8,128)(2,1)S(1)}, bf16[80,1280]{1,0:T(8,128)(2,1)S(1)}, u32[]{:S(2)}, u32[]{:S(2)}) %collective-permute-start.7) | collective-permute-done | bytes 204832 | tf_op jit(solution)/shard_map/ppermute | solution.py:103
  63.0 0.1 add_convert_fusion
  63.0 2.7 %collective-permute-start.8 = (bf16[80,1280]{1,0:T(8,128)(2,1)S(1)}, bf16[80,1280]{1,0:T(8,128)(2,1)S(1)}, u32[]{:S(2)}, u32[]{:S(2)}) collective-permute-start(bf16[80,1280]{1,0:T(8,128)(2,1)S(1)} %add_convert_fusion), channel_id=1, source_target_pairs={{0,2},{1,3},{2,0},{3,1},{4,6},{5,7},{6,4},{7,5},{8,10},{9,11},{10,... | collective-permute-start | bytes 614408 | tf_op jit(solution)/shard_map/ppermute | solution.py:103
  65.7 1.3 %pad_maximum_fusion = bf16[160,5120]{1,0:T(8,128)(2,1)} fusion(bf16[160,1280]{1,0:T(8,128)(2,1)S(1)} %convolution_convert_fusion, bf16[160,1280]{1,0:T(8,128)(2,1)S(1)} %convolution_convert_fusion.1, bf16[160,1280]{1,0:T(8,128)(2,1)S(1)} %convolution_convert_fusion.2, bf16[160,1280]{1,0:T(8,128)(2,1)S(1)} %convolution_convert_fusion.3), kind=kLoop, calls=%fused_computation.17 | loop fusion | flops 6553600 | bytes 3276800 | tf_op jit(solution)/shard_map/concatenate | solution.py:176
  67.0 8.0 %collective-permute-done.8 = bf16[80,1280]{1,0:T(8,128)(2,1)S(1)} collective-permute-done((bf16[80,1280]{1,0:T(8,128)(2,1)S(1)}, bf16[80,1280]{1,0:T(8,128)(2,1)S(1)}, u32[]{:S(2)}, u32[]{:S(2)}) %collective-permute-start.8) | collective-permute-done | bytes 204832 | tf_op jit(solution)/shard_map/ppermute | solution.py:103
  75.0 0.8 %convert_add_fusion = f32[80,1280]{1,0:T(8,128)} fusion(bf16[80,1280]{1,0:T(8,128)(2,1)S(1)} %collective-permute-done.8, bf16[80,1280]{1,0:T(8,128)(2,1)S(1)} %add_convert_fusion), kind=kLoop, calls=%fused_computation.28 | loop fusion | flops 307200 | bytes 819200 | tf_op jit(solution)/shard_map/add | solution.py:167
  (31 shorter events, 0.2 us)
Async XLA Ops:
  0.6 25.6 %copy-start = (bf16[640,1280]{1,0:T(8,128)(2,1)S(1)}, bf16[640,1280]{1,0:T(8,128)(2,1)}, u32[]{:S(2)}) copy-start(bf16[640,1280]{1,0:T(8,128)(2,1)} %param.14) | copy-start | bytes 4915204
  0.6 3.0 %copy-start.3 = (s32[160]{0:T(256)S(1)}, s32[160]{0:T(256)}, u32[]{:S(2)}) copy-start(s32[160]{0:T(256)} %param.11) | copy-start | bytes 1924
  0.7 3.0 %copy-start.1 = (bf16[160,5120]{1,0:T(8,128)(2,1)S(1)}, bf16[160,5120]{1,0:T(8,128)(2,1)}, u32[]{:S(2)}) copy-start(bf16[160,5120]{1,0:T(8,128)(2,1)} %param.12) | copy-start | bytes 4915204
  0.7 3.6 %copy-start.5 = (pred[128]{0:T(512)(128)(4,1)}, pred[128]{0:T(512)(128)(4,1)S(1)}, u32[]{:S(2)}) copy-start(pred[128]{0:T(512)(128)(4,1)S(1)} %fusion.53) | copy-start | bytes 388
  0.7 3.5 %copy-start.7 = (pred[128]{0:T(512)(128)(4,1)}, pred[128]{0:T(512)(128)(4,1)S(1)}, u32[]{:S(2)}) copy-start(pred[128]{0:T(512)(128)(4,1)S(1)} %broadcast_compare_fusion) | copy-start | bytes 388
  0.7 3.5 %copy-start.9 = (pred[128]{0:T(512)(128)(4,1)}, pred[128]{0:T(512)(128)(4,1)S(1)}, u32[]{:S(2)}) copy-start(pred[128]{0:T(512)(128)(4,1)S(1)} %broadcast_compare_fusion.2) | copy-start | bytes 388
  2.2 6.7 %copy-start.11 = (s32[8]{0:T(128)S(1)}, s32[8]{0:T(128)}, u32[]{:S(2)}) copy-start(s32[8]{0:T(128)} %param.9) | copy-start | bytes 100
  2.2 7.0 %copy-start.2 = (bf16[128,1280]{1,0:T(8,128)(2,1)S(1)}, bf16[128,1280]{1,0:T(8,128)(2,1)}, u32[]{:S(2)}) copy-start(bf16[128,1280]{1,0:T(8,128)(2,1)} %param.8) | copy-start | bytes 983044
  2.3 7.4 %copy-start.4 = (f32[1280]{0:T(1024)S(1)}, f32[1280]{0:T(1024)}, u32[]{:S(2)}) copy-start(f32[1280]{0:T(1024)} %param.15) | copy-start | bytes 15364
  4.3 39.9 %collective-permute-start = (bf16[128,1280]{1,0:T(8,128)(2,1)S(1)}, bf16[128,1280]{1,0:T(8,128)(2,1)}, u32[]{:S(2)}, u32[]{:S(2)}) collective-permute-start(bf16[128,1280]{1,0:T(8,128)(2,1)S(1)} %fusion.1), channel_id=1, source_target_pairs={{0,4},{4,0},{8,12},{12,8},{16,20},{20,16},{24,28},{28,24},{1,5},{5... | collective-permute-start | bytes 983048 | tf_op jit(solution)/shard_map/ppermute | solution.py:103
  4.8 39.3 %collective-permute-start.1 = (bf16[128,1280]{1,0:T(8,128)(2,1)S(1)}, bf16[128,1280]{1,0:T(8,128)(2,1)}, u32[]{:S(2)}, u32[]{:S(2)}) collective-permute-start(bf16[128,1280]{1,0:T(8,128)(2,1)S(1)} %fusion.1), channel_id=1, source_target_pairs={{0,8},{4,12},{8,0},{12,4},{16,24},{20,28},{24,16},{28,20},{1,9},{5... | collective-permute-start | bytes 983048 | tf_op jit(solution)/shard_map/ppermute | solution.py:103
  7.4 38.6 %collective-permute-start.3 = (bf16[128,1280]{1,0:T(8,128)(2,1)S(1)}, bf16[128,1280]{1,0:T(8,128)(2,1)}, u32[]{:S(2)}, u32[]{:S(2)}) collective-permute-start(bf16[128,1280]{1,0:T(8,128)(2,1)S(1)} %fusion.1), channel_id=1, source_target_pairs={{0,16},{4,20},{8,24},{12,28},{16,0},{20,4},{24,8},{28,12},{1,17},{... | collective-permute-start | bytes 983048 | tf_op jit(solution)/shard_map/ppermute | solution.py:103
  8.9 37.6 %collective-permute-start.5 = (bf16[128,1280]{1,0:T(8,128)(2,1)S(1)}, bf16[128,1280]{1,0:T(8,128)(2,1)S(1)}, u32[]{:S(2)}, u32[]{:S(2)}) collective-permute-start(bf16[128,1280]{1,0:T(8,128)(2,1)S(1)} %fusion.1), channel_id=1, source_target_pairs={{0,24},{4,28},{8,16},{12,20},{16,8},{20,12},{24,0},{28,4},{1,25},{... | collective-permute-start | bytes 983048 | tf_op jit(solution)/shard_map/ppermute | solution.py:103
  21.2 21.9 %copy-start.10 = (pred[128]{0:T(512)(128)(4,1)S(1)}, pred[128]{0:T(512)(128)(4,1)}, u32[]{:S(2)}) copy-start(pred[128]{0:T(512)(128)(4,1)} %copy-done.9) | copy-start | bytes 388
  22.1 10.1 %all-to-all-start.1 = ((bf16[8,80,128]{2,1,0:T(8,128)(2,1)}), bf16[8,80,128]{2,1,0:T(8,128)(2,1)S(1)}, u32[]{:S(2)}, u32[]{:S(2)}) async-start(bf16[8,80,128]{2,1,0:T(8,128)(2,1)} %bitcast.5), calls=%async_computation.1 | async-start | bytes 327680 | tf_op jit(solution)/shard_map/all_to_all | solution.py:144
  26.2 17.2 %copy-start.8 = (pred[128]{0:T(512)(128)(4,1)S(1)}, pred[128]{0:T(512)(128)(4,1)}, u32[]{:S(2)}) copy-start(pred[128]{0:T(512)(128)(4,1)} %copy-done.7) | copy-start | bytes 388
  26.3 17.5 %copy-start.6 = (pred[128]{0:T(512)(128)(4,1)S(1)}, pred[128]{0:T(512)(128)(4,1)}, u32[]{:S(2)}) copy-start(pred[128]{0:T(512)(128)(4,1)} %copy-done.5) | copy-start | bytes 388
  32.1 11.0 %all-to-all-start = ((bf16[8,16,1280]{2,1,0:T(8,128)(2,1)}), bf16[8,16,1280]{2,1,0:T(8,128)(2,1)S(1)}, u32[]{:S(2)}, u32[]{:S(2)}) async-start(bf16[8,16,1280]{2,1,0:T(8,128)(2,1)} %bitcast.2), calls=%async_computation | async-start | bytes 655360 | tf_op jit(solution)/shard_map/all_to_all | solution.py:146
  44.1 4.1 %collective-permute-start.2 = (bf16[128,1280]{1,0:T(8,128)(2,1)}, bf16[128,1280]{1,0:T(8,128)(2,1)S(1)}, u32[]{:S(2)}, u32[]{:S(2)}) collective-permute-start(bf16[128,1280]{1,0:T(8,128)(2,1)} %collective-permute-done.1), channel_id=1, source_target_pairs={{0,4},{4,0},{8,12},{12,8},{16,20},{20,16},{24,28},{28,24},{1,5},{5... | collective-permute-start | bytes 983048 | tf_op jit(solution)/shard_map/ppermute | solution.py:103
  46.0 4.8 %collective-permute-start.4 = (bf16[128,1280]{1,0:T(8,128)(2,1)}, bf16[128,1280]{1,0:T(8,128)(2,1)S(1)}, u32[]{:S(2)}, u32[]{:S(2)}) collective-permute-start(bf16[128,1280]{1,0:T(8,128)(2,1)} %collective-permute-done.3), channel_id=1, source_target_pairs={{0,4},{4,0},{8,12},{12,8},{16,20},{20,16},{24,28},{28,24},{1,5},{5... | collective-permute-start | bytes 983048 | tf_op jit(solution)/shard_map/ppermute | solution.py:103
  46.4 5.7 %collective-permute-start.6 = (bf16[128,1280]{1,0:T(8,128)(2,1)S(1)}, bf16[128,1280]{1,0:T(8,128)(2,1)S(1)}, u32[]{:S(2)}, u32[]{:S(2)}) collective-permute-start(bf16[128,1280]{1,0:T(8,128)(2,1)S(1)} %collective-permute-done.5), channel_id=1, source_target_pairs={{0,4},{4,0},{8,12},{12,8},{16,20},{20,16},{24,28},{28,24},{1,5},{5... | collective-permute-start | bytes 983048 | tf_op jit(solution)/shard_map/ppermute | solution.py:103
  55.5 7.5 %collective-permute-start.7 = (bf16[80,1280]{1,0:T(8,128)(2,1)S(1)}, bf16[80,1280]{1,0:T(8,128)(2,1)S(1)}, u32[]{:S(2)}, u32[]{:S(2)}) collective-permute-start(bf16[80,1280]{1,0:T(8,128)(2,1)S(1)} %fusion.5), channel_id=1, source_target_pairs={{0,1},{1,0},{2,3},{3,2},{4,5},{5,4},{6,7},{7,6},{8,9},{9,8},{10,11... | collective-permute-start | bytes 614408 | tf_op jit(solution)/shard_map/ppermute | solution.py:103
  63.0 12.0 %collective-permute-start.8 = (bf16[80,1280]{1,0:T(8,128)(2,1)S(1)}, bf16[80,1280]{1,0:T(8,128)(2,1)S(1)}, u32[]{:S(2)}, u32[]{:S(2)}) collective-permute-start(bf16[80,1280]{1,0:T(8,128)(2,1)S(1)} %add_convert_fusion), channel_id=1, source_target_pairs={{0,2},{1,3},{2,0},{3,1},{4,6},{5,7},{6,4},{7,5},{8,10},{9,11},{10,... | collective-permute-start | bytes 614408 | tf_op jit(solution)/shard_map/ppermute | solution.py:103

commit v2 on v0

--- a/solution.py
+++ b/solution.py
@@ -1,8 +1,11 @@
+import functools
 import math
 
 import jax
 import jax.numpy as jnp
 from jax import lax
+from jax.experimental import pallas as pl
+from jax.experimental.pallas import tpu as pltpu
 from jax.sharding import PartitionSpec as P
 
 HD = 80
@@ -16,9 +19,9 @@
     return (values * lax.rsqrt(mean_square + 1e-06) * gain).astype(jnp.bfloat16)
 
 
-def encode(windows, lengths, w_qkv, w_out, gain):
+def attend(windows, lengths, w_qkv, gain):
     number, window_size, feature_width = windows.shape
-    inner_width = w_out.shape[0]
+    inner_width = w_qkv.shape[1] // 3
     flat_rows = windows.reshape(number * window_size, feature_width)
     normed = normalize(flat_rows, gain)
     projected = jnp.dot(normed, w_qkv, preferred_element_type=jnp.float32).astype(jnp.bfloat16)
@@ -34,14 +37,17 @@
     attended = jnp.einsum(
         "nhqk,nkhd->nqhd", weights, values_all, preferred_element_type=jnp.float32
     )
-    attended = attended.astype(jnp.bfloat16).reshape(number * window_size, inner_width)
+    return attended.astype(jnp.bfloat16).reshape(number * window_size, inner_width)
+
+
+def project(flat_rows, attended, w_out):
     encoded = flat_rows.astype(jnp.float32) + jnp.dot(
         attended, w_out, preferred_element_type=jnp.float32
     )
-    return (encoded.astype(jnp.bfloat16), attended)
-
-
-def shards(pixels, window_owner, window_len, slot_token, cotangent, w_qkv, w_out, gain):
+    return encoded.astype(jnp.bfloat16)
+
+
+def any_slice(pixels, window_owner, window_len, slot_token, cotangent, w_qkv, w_out, gain):
     group_size = lax.axis_size("enc")
     replica_count = lax.axis_size("rep")
     feature_width = pixels.shape[1]
@@ -53,9 +59,10 @@
     route = (window_owner[None, :] == owner_ids[:, None]).astype(jnp.bfloat16)
     slot_ids = jnp.arange(group_size * tokens_each, dtype=jnp.int32)
     placing = (slot_token[:, None] == slot_ids[None, :]).astype(jnp.bfloat16)
-    encoded, attended = encode(
-        pixels.reshape(window_count, window_rows, feature_width), window_len, w_qkv, w_out, gain
-    )
+    attended = attend(
+        pixels.reshape(window_count, window_rows, feature_width), window_len, w_qkv, gain
+    )
+    encoded = project(pixels, attended, w_out)
     outgoing = jnp.dot(
         route,
         encoded.reshape(window_count, window_rows * feature_width),
@@ -94,7 +101,314 @@
     return (embeddings, gradient)
 
 
+LANES = 128
+VMEM = pl.BlockSpec(memory_space=pltpu.VMEM)
+HBM = pl.BlockSpec(memory_space=pltpu.HBM)
+SMEM = pl.BlockSpec(memory_space=pltpu.SMEM)
+TRANSPOSED = (((0,), (0,)), ((), ()))
+ROWS_WITH_ROWS = (((1,), (1,)), ((), ()))
+
+
+def iota(shape, dim):
+    return lax.broadcasted_iota(jnp.int32, shape, dim)
+
+
+def cost(flops, moved):
+    return pl.CostEstimate(flops=flops, bytes_accessed=moved, transcendentals=0)
+
+
+def params(mib):
+    return pltpu.CompilerParams(vmem_limit_bytes=mib * 1024 * 1024)
+
+
+def pick_kernel(slots_ref, cotangent_hbm, held_ref, parts, sems):
+    rows, width = held_ref.shape
+    tokens = cotangent_hbm.shape[0]
+    copies = []
+    for j in range(MERGE):
+        columns = cotangent_hbm.at[:, pl.ds(j * width, width)]
+        copies.append(pltpu.make_async_copy(columns, parts.at[j], sems.at[j]))
+        copies[j].start()
+    row = iota((rows, tokens), 0)
+    holds = slots_ref[...] == row // MERGE
+    held = None
+    for j in range(MERGE):
+        pick = jnp.where(holds & (row % MERGE == j), 1.0, 0.0).astype(jnp.bfloat16)
+        copies[j].wait()
+        term = jnp.dot(pick, parts[j], preferred_element_type=jnp.float32)
+        held = term if held is None else held + term
+    held_ref[...] = held.astype(jnp.bfloat16)
+
+
+def pick_rows(slot_token, cotangent, rows, width):
+    tokens = cotangent.shape[0]
+    return pl.pallas_call(
+        pick_kernel,
+        out_shape=jax.ShapeDtypeStruct((rows, width), jnp.bfloat16),
+        in_specs=[VMEM, HBM],
+        out_specs=VMEM,
+        scratch_shapes=[
+            pltpu.VMEM((MERGE, tokens, width), jnp.bfloat16),
+            pltpu.SemaphoreType.DMA((MERGE,)),
+        ],
+        compiler_params=params(16),
+        cost_estimate=cost(2 * MERGE * rows * tokens * width, 2 * cotangent.size),
+        name="pick_rows",
+    )(slot_token.reshape(1, tokens), cotangent)
+
+
+def place_of(owner, group):
+    return owner % 2 * (group // 2) + owner // 2
+
+
+def attend_kernel(
+    owner_ref, len_ref, pixels_ref, gain_ref, w_hbm, sent_ref, attended_ref, ordered_ref,
+    weights, sems,
+):
+    rows, width = pixels_ref.shape
+    windows = owner_ref.shape[0]
+    window_rows = rows // windows
+    inner = attended_ref.shape[0]
+    copies = []
+    for part in range(3):
+        columns = w_hbm.at[:, pl.ds(part * inner, inner)]
+        copies.append(pltpu.make_async_copy(columns, weights.at[part], sems.at[part]))
+        copies[part].start()
+    key_row = iota((rows, rows), 0)
+    key_window = key_row // window_rows
+    live = jnp.zeros((rows, rows), jnp.int32)
+    for w in range(windows):
+        place = place_of(owner_ref[w], windows)
+        place_rows = pl.ds(pl.multiple_of(place * window_rows, window_rows), window_rows)
+        ordered_ref[place_rows, :] = pixels_ref[w * window_rows : (w + 1) * window_rows, :]
+        live = jnp.where(key_window == place, len_ref[w], live)
+    allowed = (key_window == iota((rows, rows), 1) // window_rows) & (
+        key_row % window_rows < live
+    )
+    values = ordered_ref[...].astype(jnp.float32)
+    mean_square = jnp.mean(values * values, axis=-1, keepdims=True)
+    normed = (values * lax.rsqrt(mean_square + 1e-06) * gain_ref[...]).astype(jnp.bfloat16)
+    projected = []
+    for part in range(3):
+        copies[part].wait()
+        projected.append(jnp.dot(normed, weights[part], preferred_element_type=jnp.float32))
+    queries = projected[0].astype(jnp.bfloat16)
+    keys_all = projected[1].astype(jnp.bfloat16)
+    values_across = projected[2].T.astype(jnp.bfloat16)
+    scale = 1.0 / math.sqrt(HD)
+    first_half = iota((HD, rows), 1) < rows // 2
+    for pair in range(inner // HD // 2):
+        across = []
+        for head in (2 * pair, 2 * pair + 1):
+            first = head * HD
+            low = first // LANES * LANES
+            high = -(-(first + HD) // LANES) * LANES
+            lane = iota((rows, high - low), 1) + low
+            own = (lane >= first) & (lane < first + HD)
+            keys = jnp.where(own, keys_all[:, low:high], jnp.zeros((), jnp.bfloat16))
+            scores = lax.dot_general(
+                keys, queries[:, low:high], ROWS_WITH_ROWS, preferred_element_type=jnp.float32
+            )
+            scores = jnp.where(allowed, scores * scale, -1e30)
+            raised = jnp.exp(scores - jnp.max(scores, axis=0, keepdims=True))
+            weight = (raised / jnp.sum(raised, axis=0, keepdims=True)).astype(jnp.bfloat16)
+            mixed = jnp.dot(
+                values_across[first : first + HD, :], weight, preferred_element_type=jnp.float32
+            )
+            attended_ref[first : first + HD, :] = mixed.astype(jnp.bfloat16)
+            across.append(mixed)
+        one, two = across
+        first = 2 * pair * HD
+        sent_ref[first : first + HD, :] = jnp.where(
+            first_half, one, pltpu.roll(two, rows // 2, 1)
+        ).astype(jnp.bfloat16)
+        sent_ref[first + HD : first + 2 * HD, :] = jnp.where(
+            first_half, pltpu.roll(one, rows // 2, 1), two
+        ).astype(jnp.bfloat16)
+
+
+def attend_ordered(window_owner, window_len, pixels, gain, w_qkv):
+    rows, width = pixels.shape
+    inner = w_qkv.shape[1] // 3
+    return pl.pallas_call(
+        attend_kernel,
+        out_shape=(
+            jax.ShapeDtypeStruct((inner, rows), jnp.bfloat16),
+            jax.ShapeDtypeStruct((inner, rows), jnp.bfloat16),
+            jax.ShapeDtypeStruct((rows, width), jnp.bfloat16),
+        ),
+        in_specs=[SMEM, SMEM, VMEM, VMEM, HBM],
+        out_specs=(VMEM, VMEM, VMEM),
+        scratch_shapes=[
+            pltpu.VMEM((3, width, inner), jnp.bfloat16),
+            pltpu.SemaphoreType.DMA((3,)),
+        ],
+        compiler_params=params(60),
+        cost_estimate=cost(2 * rows * width * 3 * inner, 2 * w_qkv.size),
+        name="attend",
+    )(window_owner, window_len, pixels, gain.reshape(1, width), w_qkv)
+
+
+def project_kernel(group, attended_ref, ordered_ref, w_ref, encoded_ref):
+    window_rows = ordered_ref.shape[0] // group
+    added = lax.dot_general(
+        attended_ref[...], w_ref[...], TRANSPOSED, preferred_element_type=jnp.float32
+    )
+    encoded = (ordered_ref[...].astype(jnp.float32) + added).astype(jnp.bfloat16)
+    for owner in range(group):
+        place = place_of(owner, group) * window_rows
+        encoded_ref[owner * window_rows : (owner + 1) * window_rows, :] = encoded[
+            place : place + window_rows
+        ]
+
+
+def project_ordered(attended, ordered, w_out, group):
+    return pl.pallas_call(
+        functools.partial(project_kernel, group),
+        out_shape=jax.ShapeDtypeStruct(ordered.shape, jnp.bfloat16),
+        in_specs=[VMEM] * 3,
+        out_specs=VMEM,
+        compiler_params=params(16),
+        cost_estimate=cost(2 * ordered.size * w_out.shape[0], 2 * w_out.size),
+        name="project",
+    )(attended, ordered, w_out)
+
+
+def gradient_kernel(scale, me_ref, gathered_ref, *refs):
+    kept_ref, given_ref = refs[-2:]
+    blocks = refs[:-2]
+    pairs = len(blocks)
+    group = 2 * pairs
+    rows = gathered_ref.shape[1]
+    half = rows // 2
+    window_rows = half // pairs
+    head = gathered_ref.shape[0] // group
+    mine = me_ref[0] // 2
+    source = iota((rows, rows), 0)
+    target = iota((rows, rows), 1)
+    same = (source // window_rows % pairs == (target // window_rows % pairs) ^ mine) & (
+        source % window_rows == target % window_rows
+    )
+    straight = jnp.where(same & (source // half == target // half), 1.0, 0.0)
+    crossed = jnp.where(same & (source // half != target // half), 1.0, 0.0)
+    gathered = gathered_ref[...]
+    straight = jnp.dot(
+        gathered, straight.astype(jnp.bfloat16), preferred_element_type=jnp.float32
+    ).astype(jnp.bfloat16)
+    crossed = jnp.dot(
+        gathered, crossed.astype(jnp.bfloat16), preferred_element_type=jnp.float32
+    ).astype(jnp.bfloat16)
+    left = iota((head, rows), 1) < half
+    one, two = [], []
+    for s in range(0, group, 2):
+        here = slice(s * head, (s + 1) * head)
+        there = slice((s + 1) * head, (s + 2) * head)
+        one.append(jnp.where(left, straight[here], crossed[there]))
+        two.append(jnp.where(left, crossed[here], straight[there]))
+    columns = jnp.concatenate([jnp.concatenate(one, 1), jnp.concatenate(two, 1)], 0)
+    against = jnp.concatenate(
+        [
+            block[s * window_rows : (s + 1) * window_rows, :]
+            for s in range(group)
+            for block in blocks
+        ],
+        0,
+    )
+    total = jnp.dot(columns, against, preferred_element_type=jnp.float32) * scale
+    first = me_ref[0] % 2 == 0
+    kept_ref[...] = jnp.where(first, total[:head], total[head:])
+    given_ref[...] = jnp.where(first, total[head:], total[:head]).astype(jnp.bfloat16)
+
+
+def gradient_rows(me, gathered, blocks, scale):
+    group = 2 * len(blocks)
+    head = gathered.shape[0] // group
+    rows, width = blocks[0].shape
+    return pl.pallas_call(
+        functools.partial(gradient_kernel, scale),
+        out_shape=(
+            jax.ShapeDtypeStruct((head, width), jnp.float32),
+            jax.ShapeDtypeStruct((head, width), jnp.bfloat16),
+        ),
+        in_specs=[SMEM] + [VMEM] * (1 + len(blocks)),
+        out_specs=(VMEM, VMEM),
+        compiler_params=params(24),
+        cost_estimate=cost(2 * head * rows * group * width, group * rows * width),
+        name="gradient_rows",
+    )(me.reshape(1), gathered, *blocks)
+
+
+def place_kernel(slots_ref, arrived_ref, embeddings_ref):
+    rows, width = arrived_ref.shape
+    tokens = embeddings_ref.shape[0]
+    row = iota((tokens, rows), 1)
+    holds = slots_ref[...] == row // MERGE
+    for j in range(MERGE):
+        put = jnp.where(holds & (row % MERGE == j), 1.0, 0.0).astype(jnp.bfloat16)
+        part = jnp.dot(put, arrived_ref[...], preferred_element_type=jnp.float32)
+        embeddings_ref[:, j * width : (j + 1) * width] = part.astype(jnp.bfloat16)
+
+
+def place_rows(slot_token, arrived):
+    rows, width = arrived.shape
+    tokens = slot_token.shape[0]
+    return pl.pallas_call(
+        place_kernel,
+        out_shape=jax.ShapeDtypeStruct((tokens, MERGE * width), jnp.bfloat16),
+        in_specs=[VMEM, VMEM],
+        out_specs=VMEM,
+        compiler_params=params(16),
+        cost_estimate=cost(2 * MERGE * rows * tokens * width, 2 * MERGE * tokens * width),
+        name="place_rows",
+    )(slot_token.reshape(tokens, 1), arrived)
+
+
+def after(value, other):
+    return lax.optimization_barrier((value, other))[0]
+
+
+def swap(value, axis, bits):
+    size = lax.axis_size(axis)
+    return lax.ppermute(value, axis, [(i, i ^ bits) for i in range(size)])
+
+
+def xor_slice(pixels, window_owner, window_len, slot_token, cotangent, w_qkv, w_out, gain):
+    group = lax.axis_size("enc")
+    replicas = lax.axis_size("rep")
+    rows, width = pixels.shape
+    inner = w_out.shape[0]
+    me = lax.axis_index("enc")
+
+    held = pick_rows(slot_token, cotangent, rows, width)
+    blocks = [held] + [swap(held, "enc", b) for b in range(2, group, 2)]
+    sent, attended, ordered = attend_ordered(window_owner, window_len, pixels, gain, w_qkv)
+    gathered = lax.all_to_all(
+        sent.reshape(group, inner // group, rows), "enc", split_axis=0, concat_axis=0, tiled=True
+    )
+    encoded = project_ordered(attended, ordered, w_out, group)
+    scale = 1.0 / math.sqrt(rows * group * replicas)
+    kept, given = gradient_rows(me, gathered.reshape(inner, rows), blocks, scale)
+    part = (kept + swap(given, "enc", 1).astype(jnp.float32)).astype(jnp.bfloat16)
+    arrived = lax.all_to_all(
+        after(encoded, part), "enc", split_axis=0, concat_axis=0, tiled=True
+    )
+    bit = 1
+    while bit < replicas:
+        total = part.astype(jnp.float32) + swap(part, "rep", bit).astype(jnp.float32)
+        part = total.astype(jnp.bfloat16)
+        bit *= 2
+    embeddings = place_rows(slot_token, arrived)
+    return (embeddings, total)
+
+
 def solution(mesh):
+    def shards(*args):
+        group = mesh.shape["enc"]
+        replicas = mesh.shape["rep"]
+        powers = group & (group - 1) == 0 and replicas & (replicas - 1) == 0
+        whole = powers and args[1].shape[0] == group
+        return (xor_slice if whole else any_slice)(*args)
+
     return jax.shard_map(
         shards,
         mesh=mesh,

time: 124 us -> 47.5 us (0.38)
  waiting for transfers between devices: 78.6 us -> 15.5 us
  matrix products: 14 us -> 0 us
  between operations: 14.2 us -> 0.74 us
  Pallas kernels: 0 us -> 10.5 us
  starting transfers between devices: 9.41 us -> 16.7 us
  local copies, waits for them, and re-layouts: 4.93 us -> 2.83 us
    reduce_scatter x1 -> x0, waiting for transfers between devices: 41.2 us -> none  [shards(): lax.psum_scatter(lax.dot_general(attended, d_encoded, (((0,), (0,)), ((),...]
    psum x1 -> x0, waiting for transfers between devices: 37.3 us -> none  [shards(): summed = lax.psum(reduced, 'rep')]
    dot_general x9 -> x0, matrix products: 13.6 us -> none  [the longest x1 3.35 us: encode(): jnp.dot(normed, w_qkv, preferred_element_type=jnp.float32)]
    pallas_call x0 -> x5, Pallas kernels: none -> 10.5 us  [the longest x1 6.04 us: attend_ordered(): pl.pallas_call(attend_kernel, out_shape=(jax.ShapeDtypeStruct((inner, row...]
    all_to_all x2, waiting for transfers between devices: 0.01 us -> 9.71 us  [the longest x1 5.88 us: xor_slice(): lax.all_to_all(sent.reshape(group, inner // group, rows), 'enc', split_ax...]
    ppermute x0 -> x6, starting transfers between devices: none -> 8.97 us  [swap(): return lax.ppermute(value, axis, [(i, i ^ bits) for i in range(size)])]
    ppermute x0 -> x6, waiting for transfers between devices: none -> 5.79 us  [swap(): return lax.ppermute(value, axis, [(i, i ^ bits) for i in range(size)])]
    reshape x9 -> x2, local copies, waits for them, and re-layouts: 3.23 us -> 0.7 us  [the longest x1 0.59 us: attend_ordered(): gain.reshape(1, width)]
  transfers between devices with their start and end apart: 4 -> 8, of which waited for: 2 -> 5; matrix products, arithmetic and copies ran while one was open for 10% -> 2% of each run, Pallas kernels for 0% -> 19%
where the time goes in v2:
time: 47.5 us; the launch traced here: 47.1 us
  starting transfers between devices  16.7 us (35%)
  waiting for transfers between devices  15.5 us (33%)
  Pallas kernels  10.5 us (22%)
  local copies, waits for them, and re-layouts  2.83 us (6%)
  other arithmetic  0.89 us (2%)
  between operations  0.74 us (2%)
    ppermute x6, starting transfers between devices, swap(): return lax.ppermute(value, axis, [(i, i ^ bits) for i in range(size)])  8.97 us
    pallas_call x1, Pallas kernels, attend_ordered(): pl.pallas_call(attend_kernel, out_shape=(jax.ShapeDtypeStruct((inner, row...  6.04 us
    all_to_all x1, waiting for transfers between devices, xor_slice(): lax.all_to_all(sent.reshape(group, inner // group, rows), 'enc', split_ax...  5.88 us
    ppermute x6, waiting for transfers between devices, swap(): return lax.ppermute(value, axis, [(i, i ^ bits) for i in range(size)])  5.79 us
    all_to_all x1, starting transfers between devices, xor_slice(): lax.all_to_all(sent.reshape(group, inner // group, rows), 'enc', split_ax...  4.26 us
    all_to_all x1, waiting for transfers between devices, xor_slice(): lax.all_to_all(after(encoded, part), 'enc', split_axis=0, concat_axis=0,...  3.83 us
    all_to_all x1, starting transfers between devices, xor_slice(): lax.all_to_all(after(encoded, part), 'enc', split_axis=0, concat_axis=0,...  3.43 us
    unnamed x14, local copies, waits for them, and re-layouts  2.13 us
  transfers between devices with their start and end apart: 8, of which 5 were waited for; matrix products, arithmetic and copies ran while one was open for 2% of the time, Pallas kernels for 19%

profile of v2, /device:TPU:0, one launch (start us, length us, event | category | flops | bytes accessed | tf_op | source)
XLA Modules:
  0.0 47.1 jit_solution(7649857443262337206)
XLA Ops:
  0.6 0.0 copy-start
  0.6 1.4 %copy-done = bf16[160,5120]{1,0:T(8,128)(2,1)S(1)} copy-done((bf16[160,5120]{1,0:T(8,128)(2,1)S(1)}, bf16[160,5120]{1,0:T(8,128)(2,1)}, u32[]{:S(2)}) %copy-start) | copy-done | bytes 1638424
  2.1 0.0 copy-start.4
  2.1 0.7 %copy-done.4 = s32[160]{0:T(256)S(1)} copy-done((s32[160]{0:T(256)S(1)}, s32[160]{0:T(256)}, u32[]{:S(2)}) %copy-start.4) | copy-done | bytes 664
  2.7 0.0 copy-start.6
  2.7 0.9 %pick_rows.1.refs_0_ = bf16[128,1280]{1,0:T(8,128)(2,1)S(1)} custom-call(s32[1,160]{1,0:T(1,128)S(1)} %bitcast.9, bf16[160,5120]{1,0:T(8,128)(2,1)S(1)} %copy-done), custom_call_target="tpu_custom_call" | custom-call | flops 209715200 | bytes 1638400 | tf_op jit(solution)/shard_map/pick_rows/pallas_call | solution.py:145
  3.6 4.0 %collective-permute-start.2 = (bf16[128,1280]{1,0:T(8,128)(2,1)S(1)}, bf16[128,1280]{1,0:T(8,128)(2,1)S(1)}, u32[]{:S(2)}, u32[]{:S(2)}) collective-permute-start(bf16[128,1280]{1,0:T(8,128)(2,1)S(1)} %pick_rows.1.refs_0_), channel_id=1, source_target_pairs={{0,24},{4,28},{8,16},{12,20},{16,8},{20,12},{24,0},{28,4},{1,25},{... | collective-permute-start | bytes 983048 | tf_op jit(solution)/shard_map/ppermute | solution.py:372
  7.6 0.5 %collective-permute-start.1 = (bf16[128,1280]{1,0:T(8,128)(2,1)S(1)}, bf16[128,1280]{1,0:T(8,128)(2,1)S(1)}, u32[]{:S(2)}, u32[]{:S(2)}) collective-permute-start(bf16[128,1280]{1,0:T(8,128)(2,1)S(1)} %pick_rows.1.refs_0_), channel_id=1, source_target_pairs={{0,16},{4,20},{8,24},{12,28},{16,0},{20,4},{24,8},{28,12},{1,17},{... | collective-permute-start | bytes 983048 | tf_op jit(solution)/shard_map/ppermute | solution.py:372
  8.1 0.1 collective-permute-start
  8.2 0.0 copy-done.6
  8.2 0.6 %reshape.25.gain_ref = f32[1,1280]{1,0:T(1,128)} reshape(f32[1280]{0:T(1024)S(1)} %copy-done.6) | data formatting | bytes 10240 | tf_op jit(solution)/shard_map/reshape | solution.py:249
  8.8 6.0 %attend.1 = (bf16[640,128]{1,0:T(8,128)(2,1)}, bf16[640,128]{1,0:T(8,128)(2,1)}, bf16[128,1280]{1,0:T(8,128)(2,1)}) custom-call(s32[8]{0:T(128)} %owner_ref.1, s32[8]{0:T(128)} %len_ref.1, bf16[128,1280]{1,0:T(8,128)(2,1)} %pixels_ref.1, f32[1,1280]{1,0:T(1,128)} %reshape.25.gain_ref, bf16[1280,1920]{1,0:T(8,128)(2,1)} %w_hbm.1), custom_call_target="tpu_custom_call" | custom-call | flops 629145600 | bytes 4915200 | tf_op jit(solution)/shard_map/attend/pallas_call | solution.py:233
  14.9 0.0 copy-start.1
  14.9 0.0 copy-start.2
  14.9 4.3 %all-to-all-start = ((bf16[8,80,128]{2,1,0:T(8,128)(2,1)}), bf16[8,80,128]{2,1,0:T(8,128)(2,1)S(1)}, u32[]{:S(2)}, u32[]{:S(2)}) async-start(bf16[8,80,128]{2,1,0:T(8,128)(2,1)} %bitcast.11), calls=%async_computation | async-start | bytes 327680 | tf_op jit(solution)/shard_map/all_to_all | solution.py:385
  19.2 5.9 %all-to-all-done = bf16[8,80,128]{2,1,0:T(8,128)(2,1)S(1)} async-done(((bf16[8,80,128]{2,1,0:T(8,128)(2,1)}), bf16[8,80,128]{2,1,0:T(8,128)(2,1)S(1)}, u32[]{:S(2)}, u32[]{:S(2)}) %all-to-all-start) | async-done | bytes 163872 | tf_op jit(solution)/shard_map/all_to_all | solution.py:385
  25.0 0.0 copy-start.3
  25.0 0.0 collective-permute-done.2.refs_3_
  25.0 0.0 collective-permute-done.1.refs_2_
  25.0 0.0 collective-permute-done.refs_1_
  25.1 0.6 %gradient_rows.1 = (f32[80,1280]{1,0:T(8,128)S(1)}, bf16[80,1280]{1,0:T(8,128)(2,1)S(1)}) custom-call(s32[1]{0:T(128)} %bitcast.1.me_ref, bf16[640,128]{1,0:T(8,128)(2,1)S(1)} %bitcast.8, bf16[128,1280]{1,0:T(8,128)(2,1)S(1)} %pick_rows.1.refs_0_, bf16[128,1280]{1,0:T(8,128)(2,1)S(1)} %collective-permute-done.refs_1_, ...), custom_call_target="tpu_custom_call" | custom-call | flops 209715200 | bytes 1310720 | tf_op jit(solution)/shard_map/gradient_rows/pallas_call | solution.py:327
  25.7 0.1 collective-permute-start.3
  25.8 1.4 %collective-permute-done.3 = bf16[80,1280]{1,0:T(8,128)(2,1)S(1)} collective-permute-done((bf16[80,1280]{1,0:T(8,128)(2,1)S(1)}, bf16[80,1280]{1,0:T(8,128)(2,1)S(1)}, u32[]{:S(2)}, u32[]{:S(2)}) %collective-permute-start.3) | collective-permute-done | bytes 204832 | tf_op jit(solution)/shard_map/ppermute | solution.py:372
  27.3 1.6 %collective-permute-start.4 = (bf16[80,1280]{1,0:T(8,128)(2,1)S(1)}, bf16[80,1280]{1,0:T(8,128)(2,1)S(1)}, u32[]{:S(2)}, u32[]{:S(2)}) collective-permute-start(bf16[80,1280]{1,0:T(8,128)(2,1)S(1)} %add_convert_fusion.1), channel_id=1, source_target_pairs={{0,1},{1,0},{2,3},{3,2},{4,5},{5,4},{6,7},{7,6},{8,9},{9,8},{10,11... | collective-permute-start | bytes 614408 | tf_op jit(solution)/shard_map/ppermute | solution.py:372
  28.9 0.0 copy-done.1
  28.9 0.0 copy-done.2
  28.9 0.0 copy-done.3
  28.9 0.0 copy-start.5
  28.9 1.2 %project.1 = bf16[128,1280]{1,0:T(8,128)(2,1)} custom-call(bf16[640,128]{1,0:T(8,128)(2,1)S(1)} %copy-done.3, bf16[128,1280]{1,0:T(8,128)(2,1)S(1)} %copy-done.2, bf16[640,1280]{1,0:T(8,128)(2,1)S(1)} %copy-done.1), custom_call_target="tpu_custom_call" | custom-call | flops 209715200 | bytes 1638400 | tf_op jit(solution)/shard_map/project/pallas_call | solution.py:266
  30.1 3.4 %all-to-all-start.1 = ((bf16[8,16,1280]{2,1,0:T(8,128)(2,1)}), bf16[8,16,1280]{2,1,0:T(8,128)(2,1)S(1)}, u32[]{:S(2)}, u32[]{:S(2)}) async-start(bf16[8,16,1280]{2,1,0:T(8,128)(2,1)} %bitcast.5), calls=%async_computation.1 | async-start | bytes 655360 | tf_op jit(solution)/shard_map/all_to_all | solution.py:392
  33.5 0.9 %collective-permute-done.4 = bf16[80,1280]{1,0:T(8,128)(2,1)S(1)} collective-permute-done((bf16[80,1280]{1,0:T(8,128)(2,1)S(1)}, bf16[80,1280]{1,0:T(8,128)(2,1)S(1)}, u32[]{:S(2)}, u32[]{:S(2)}) %collective-permute-start.4) | collective-permute-done | bytes 204832 | tf_op jit(solution)/shard_map/ppermute | solution.py:372
  34.5 0.1 add_convert_fusion
  34.5 2.7 %collective-permute-start.5 = (bf16[80,1280]{1,0:T(8,128)(2,1)S(1)}, bf16[80,1280]{1,0:T(8,128)(2,1)S(1)}, u32[]{:S(2)}, u32[]{:S(2)}) collective-permute-start(bf16[80,1280]{1,0:T(8,128)(2,1)S(1)} %add_convert_fusion), channel_id=1, source_target_pairs={{0,2},{1,3},{2,0},{3,1},{4,6},{5,7},{6,4},{7,5},{8,10},{9,11},{10,... | collective-permute-start | bytes 614408 | tf_op jit(solution)/shard_map/ppermute | solution.py:372
  37.2 0.0 copy-done.5
  37.2 0.1 copy.10.slots_ref
  37.3 3.8 %all-to-all-done.1 = bf16[8,16,1280]{2,1,0:T(8,128)(2,1)S(1)} async-done(((bf16[8,16,1280]{2,1,0:T(8,128)(2,1)}), bf16[8,16,1280]{2,1,0:T(8,128)(2,1)S(1)}, u32[]{:S(2)}, u32[]{:S(2)}) %all-to-all-start.1) | async-done | bytes 327712 | tf_op jit(solution)/shard_map/all_to_all | solution.py:392
  41.1 1.8 %place_rows.1 = bf16[160,5120]{1,0:T(8,128)(2,1)} custom-call(s32[160,1]{1,0:T(8,128)S(1)} %copy.10.slots_ref, bf16[128,1280]{1,0:T(8,128)(2,1)S(1)} %bitcast.7), custom_call_target="tpu_custom_call" | custom-call | flops 209715200 | bytes 1638400 | tf_op jit(solution)/shard_map/place_rows/pallas_call | solution.py:355
  42.9 3.4 %collective-permute-done.5 = bf16[80,1280]{1,0:T(8,128)(2,1)S(1)} collective-permute-done((bf16[80,1280]{1,0:T(8,128)(2,1)S(1)}, bf16[80,1280]{1,0:T(8,128)(2,1)S(1)}, u32[]{:S(2)}, u32[]{:S(2)}) %collective-permute-start.5) | collective-permute-done | bytes 204832 | tf_op jit(solution)/shard_map/ppermute | solution.py:372
  46.3 0.8 %convert_add_fusion = f32[80,1280]{1,0:T(8,128)} fusion(bf16[80,1280]{1,0:T(8,128)(2,1)S(1)} %collective-permute-done.5, bf16[80,1280]{1,0:T(8,128)(2,1)S(1)} %add_convert_fusion), kind=kLoop, calls=%fused_computation | loop fusion | flops 307200 | bytes 819200 | tf_op jit(solution)/shard_map/add | solution.py:397
  (1 shorter events, 0.0 us)
Async XLA Ops:
  0.6 1.4 %copy-start = (bf16[160,5120]{1,0:T(8,128)(2,1)S(1)}, bf16[160,5120]{1,0:T(8,128)(2,1)}, u32[]{:S(2)}) copy-start(bf16[160,5120]{1,0:T(8,128)(2,1)} %cotangent_hbm.1) | copy-start | bytes 4915204
  2.1 0.7 %copy-start.4 = (s32[160]{0:T(256)S(1)}, s32[160]{0:T(256)}, u32[]{:S(2)}) copy-start(s32[160]{0:T(256)} %param.11) | copy-start | bytes 1924
  2.7 5.5 %copy-start.6 = (f32[1280]{0:T(1024)S(1)}, f32[1280]{0:T(1024)}, u32[]{:S(2)}) copy-start(f32[1280]{0:T(1024)} %param.15) | copy-start | bytes 15364
  3.6 21.4 %collective-permute-start.2 = (bf16[128,1280]{1,0:T(8,128)(2,1)S(1)}, bf16[128,1280]{1,0:T(8,128)(2,1)S(1)}, u32[]{:S(2)}, u32[]{:S(2)}) collective-permute-start(bf16[128,1280]{1,0:T(8,128)(2,1)S(1)} %pick_rows.1.refs_0_), channel_id=1, source_target_pairs={{0,24},{4,28},{8,16},{12,20},{16,8},{20,12},{24,0},{28,4},{1,25},{... | collective-permute-start | bytes 983048 | tf_op jit(solution)/shard_map/ppermute | solution.py:372
  7.6 17.5 %collective-permute-start.1 = (bf16[128,1280]{1,0:T(8,128)(2,1)S(1)}, bf16[128,1280]{1,0:T(8,128)(2,1)S(1)}, u32[]{:S(2)}, u32[]{:S(2)}) collective-permute-start(bf16[128,1280]{1,0:T(8,128)(2,1)S(1)} %pick_rows.1.refs_0_), channel_id=1, source_target_pairs={{0,16},{4,20},{8,24},{12,28},{16,0},{20,4},{24,8},{28,12},{1,17},{... | collective-permute-start | bytes 983048 | tf_op jit(solution)/shard_map/ppermute | solution.py:372
  8.1 17.0 %collective-permute-start = (bf16[128,1280]{1,0:T(8,128)(2,1)S(1)}, bf16[128,1280]{1,0:T(8,128)(2,1)S(1)}, u32[]{:S(2)}, u32[]{:S(2)}) collective-permute-start(bf16[128,1280]{1,0:T(8,128)(2,1)S(1)} %pick_rows.1.refs_0_), channel_id=1, source_target_pairs={{0,8},{4,12},{8,0},{12,4},{16,24},{20,28},{24,16},{28,20},{1,9},{5... | collective-permute-start | bytes 983048 | tf_op jit(solution)/shard_map/ppermute | solution.py:372
  14.9 14.0 %copy-start.1 = (bf16[640,1280]{1,0:T(8,128)(2,1)S(1)}, bf16[640,1280]{1,0:T(8,128)(2,1)}, u32[]{:S(2)}) copy-start(bf16[640,1280]{1,0:T(8,128)(2,1)} %w_ref.1) | copy-start | bytes 4915204
  14.9 14.0 %copy-start.2 = (bf16[128,1280]{1,0:T(8,128)(2,1)S(1)}, bf16[128,1280]{1,0:T(8,128)(2,1)}, u32[]{:S(2)}) copy-start(bf16[128,1280]{1,0:T(8,128)(2,1)} %get-tuple-element.9.ordered_ref) | copy-start | bytes 983044
  14.9 10.1 %all-to-all-start = ((bf16[8,80,128]{2,1,0:T(8,128)(2,1)}), bf16[8,80,128]{2,1,0:T(8,128)(2,1)S(1)}, u32[]{:S(2)}, u32[]{:S(2)}) async-start(bf16[8,80,128]{2,1,0:T(8,128)(2,1)} %bitcast.11), calls=%async_computation | async-start | bytes 327680 | tf_op jit(solution)/shard_map/all_to_all | solution.py:385
  25.0 3.9 %copy-start.3 = (bf16[640,128]{1,0:T(8,128)(2,1)S(1)}, bf16[640,128]{1,0:T(8,128)(2,1)}, u32[]{:S(2)}) copy-start(bf16[640,128]{1,0:T(8,128)(2,1)} %get-tuple-element.8.attended_ref) | copy-start | bytes 491524
  25.7 1.5 %collective-permute-start.3 = (bf16[80,1280]{1,0:T(8,128)(2,1)S(1)}, bf16[80,1280]{1,0:T(8,128)(2,1)S(1)}, u32[]{:S(2)}, u32[]{:S(2)}) collective-permute-start(bf16[80,1280]{1,0:T(8,128)(2,1)S(1)} %get-tuple-element.12), channel_id=1, source_target_pairs={{0,4},{4,0},{8,12},{12,8},{16,20},{20,16},{24,28},{28,24},{1,5},{5... | collective-permute-start | bytes 614408 | tf_op jit(solution)/shard_map/ppermute | solution.py:372
  27.3 7.2 %collective-permute-start.4 = (bf16[80,1280]{1,0:T(8,128)(2,1)S(1)}, bf16[80,1280]{1,0:T(8,128)(2,1)S(1)}, u32[]{:S(2)}, u32[]{:S(2)}) collective-permute-start(bf16[80,1280]{1,0:T(8,128)(2,1)S(1)} %add_convert_fusion.1), channel_id=1, source_target_pairs={{0,1},{1,0},{2,3},{3,2},{4,5},{5,4},{6,7},{7,6},{8,9},{9,8},{10,11... | collective-permute-start | bytes 614408 | tf_op jit(solution)/shard_map/ppermute | solution.py:372
  28.9 8.3 %copy-start.5 = (s32[160]{0:T(256)S(1)}, s32[160]{0:T(256)}, u32[]{:S(2)}) copy-start(s32[160]{0:T(256)} %param.11) | copy-start | bytes 1924
  30.1 11.0 %all-to-all-start.1 = ((bf16[8,16,1280]{2,1,0:T(8,128)(2,1)}), bf16[8,16,1280]{2,1,0:T(8,128)(2,1)S(1)}, u32[]{:S(2)}, u32[]{:S(2)}) async-start(bf16[8,16,1280]{2,1,0:T(8,128)(2,1)} %bitcast.5), calls=%async_computation.1 | async-start | bytes 655360 | tf_op jit(solution)/shard_map/all_to_all | solution.py:392
  34.5 11.8 %collective-permute-start.5 = (bf16[80,1280]{1,0:T(8,128)(2,1)S(1)}, bf16[80,1280]{1,0:T(8,128)(2,1)S(1)}, u32[]{:S(2)}, u32[]{:S(2)}) collective-permute-start(bf16[80,1280]{1,0:T(8,128)(2,1)S(1)} %add_convert_fusion), channel_id=1, source_target_pairs={{0,2},{1,3},{2,0},{3,1},{4,6},{5,7},{6,4},{7,5},{8,10},{9,11},{10,... | collective-permute-start | bytes 614408 | tf_op jit(solution)/shard_map/ppermute | solution.py:372

commit v3 on v0

--- a/solution.py
+++ b/solution.py
@@ -1,8 +1,11 @@
+import functools
 import math
 
 import jax
 import jax.numpy as jnp
 from jax import lax
+from jax.experimental import pallas as pl
+from jax.experimental.pallas import tpu as pltpu
 from jax.sharding import PartitionSpec as P
 
 HD = 80
@@ -16,9 +19,9 @@
     return (values * lax.rsqrt(mean_square + 1e-06) * gain).astype(jnp.bfloat16)
 
 
-def encode(windows, lengths, w_qkv, w_out, gain):
+def attend(windows, lengths, w_qkv, gain):
     number, window_size, feature_width = windows.shape
-    inner_width = w_out.shape[0]
+    inner_width = w_qkv.shape[1] // 3
     flat_rows = windows.reshape(number * window_size, feature_width)
     normed = normalize(flat_rows, gain)
     projected = jnp.dot(normed, w_qkv, preferred_element_type=jnp.float32).astype(jnp.bfloat16)
@@ -34,14 +37,17 @@
     attended = jnp.einsum(
         "nhqk,nkhd->nqhd", weights, values_all, preferred_element_type=jnp.float32
     )
-    attended = attended.astype(jnp.bfloat16).reshape(number * window_size, inner_width)
+    return attended.astype(jnp.bfloat16).reshape(number * window_size, inner_width)
+
+
+def project(flat_rows, attended, w_out):
     encoded = flat_rows.astype(jnp.float32) + jnp.dot(
         attended, w_out, preferred_element_type=jnp.float32
     )
-    return (encoded.astype(jnp.bfloat16), attended)
-
-
-def shards(pixels, window_owner, window_len, slot_token, cotangent, w_qkv, w_out, gain):
+    return encoded.astype(jnp.bfloat16)
+
+
+def any_slice(pixels, window_owner, window_len, slot_token, cotangent, w_qkv, w_out, gain):
     group_size = lax.axis_size("enc")
     replica_count = lax.axis_size("rep")
     feature_width = pixels.shape[1]
@@ -53,9 +59,10 @@
     route = (window_owner[None, :] == owner_ids[:, None]).astype(jnp.bfloat16)
     slot_ids = jnp.arange(group_size * tokens_each, dtype=jnp.int32)
     placing = (slot_token[:, None] == slot_ids[None, :]).astype(jnp.bfloat16)
-    encoded, attended = encode(
-        pixels.reshape(window_count, window_rows, feature_width), window_len, w_qkv, w_out, gain
-    )
+    attended = attend(
+        pixels.reshape(window_count, window_rows, feature_width), window_len, w_qkv, gain
+    )
+    encoded = project(pixels, attended, w_out)
     outgoing = jnp.dot(
         route,
         encoded.reshape(window_count, window_rows * feature_width),
@@ -94,7 +101,352 @@
     return (embeddings, gradient)
 
 
+LANES = 128
+SUBLANES = 16
+PAIR_BITS = 2
+VMEM = pl.BlockSpec(memory_space=pltpu.VMEM)
+HBM = pl.BlockSpec(memory_space=pltpu.HBM)
+SMEM = pl.BlockSpec(memory_space=pltpu.SMEM)
+TRANSPOSED = (((0,), (0,)), ((), ()))
+ROWS_WITH_ROWS = (((1,), (1,)), ((), ()))
+
+
+def turn(relative, core):
+    other = relative % 2 * 2 + relative // 2
+    if isinstance(core, int):
+        return other if core else relative
+    return jnp.where(core == 1, other, relative)
+
+
+def iota(shape, dim):
+    return lax.broadcasted_iota(jnp.int32, shape, dim)
+
+
+def cost(flops, moved):
+    return pl.CostEstimate(flops=flops, bytes_accessed=moved, transcendentals=0)
+
+
+def params(mib):
+    return pltpu.CompilerParams(vmem_limit_bytes=mib * 1024 * 1024)
+
+
+def in_hbm(value):
+    return pltpu.with_memory_space_constraint(value, pltpu.HBM)
+
+
+def place(index, size):
+    return pl.ds(pl.multiple_of(index * size, size), size)
+
+
+def slot_of_row(row, me, window_rows):
+    pair = turn(row // (2 * window_rows), me % 2) ^ (me // 2)
+    source = pair * 2 + row // window_rows % 2
+    return source * (window_rows // MERGE) + row % window_rows // MERGE
+
+
+def pick_kernel(
+    me_ref, owner_ref, len_ref, slots_ref, pixels_hbm, cotangent_hbm,
+    held_ref, kept_ref, given_ref, parts, pixels_buf, windows_buf, sems,
+):
+    rows, width = held_ref.shape
+    tokens = cotangent_hbm.shape[0]
+    windows = owner_ref.shape[0]
+    window_rows = rows // windows
+    me = me_ref[0]
+    copies = [pltpu.make_async_copy(pixels_hbm, pixels_buf, sems.at[MERGE])]
+    copies[0].start()
+    for j in range(MERGE):
+        columns = cotangent_hbm.at[:, pl.ds(j * width, width)]
+        copies.append(pltpu.make_async_copy(columns, parts.at[j], sems.at[j]))
+        copies[1 + j].start()
+    row = iota((rows, tokens), 0)
+    holds = slots_ref[...] == slot_of_row(row, me, window_rows)
+    picks = [
+        jnp.where(holds & (row % MERGE == j), 1.0, 0.0).astype(jnp.bfloat16) for j in range(MERGE)
+    ]
+    copies[0].wait()
+    which = iota((SUBLANES, width), 0)
+    lengths = [jnp.zeros((SUBLANES, width), jnp.int32)] * 2
+    for w in range(windows):
+        owner = owner_ref[w]
+        across = (owner + me) % 2
+        relative = turn((owner // 2) ^ (me // 2), owner % 2)
+        windows_buf[across, place(relative, window_rows), :] = pixels_buf[
+            w * window_rows : (w + 1) * window_rows, :
+        ]
+        for side in range(2):
+            here = jnp.where(across == side, relative, -1)
+            lengths[side] = jnp.where(which == here, len_ref[w], lengths[side])
+    for side, ref in enumerate((kept_ref, given_ref)):
+        ref[: rows // 2, :] = windows_buf[side]
+        ref[rows // 2 :, :] = lengths[side].astype(jnp.float32).astype(jnp.bfloat16)
+    held = None
+    for j in range(MERGE):
+        copies[1 + j].wait()
+        term = jnp.dot(picks[j], parts[j], preferred_element_type=jnp.float32)
+        held = term if held is None else held + term
+    held_ref[...] = held.astype(jnp.bfloat16)
+
+
+def pick_rows(me, window_owner, window_len, slot_token, pixels, cotangent):
+    rows, width = pixels.shape
+    tokens = cotangent.shape[0]
+    half = jax.ShapeDtypeStruct((rows // 2 + SUBLANES, width), jnp.bfloat16)
+    return pl.pallas_call(
+        pick_kernel,
+        out_shape=(jax.ShapeDtypeStruct((rows, width), jnp.bfloat16), half, half),
+        in_specs=[SMEM, SMEM, SMEM, VMEM, HBM, HBM],
+        out_specs=(VMEM, VMEM, VMEM),
+        scratch_shapes=[
+            pltpu.VMEM((MERGE, tokens, width), jnp.bfloat16),
+            pltpu.VMEM((rows, width), jnp.bfloat16),
+            pltpu.VMEM((2, rows // 2, width), jnp.bfloat16),
+            pltpu.SemaphoreType.DMA((MERGE + 1,)),
+        ],
+        compiler_params=params(16),
+        cost_estimate=cost(2 * MERGE * rows * tokens * width, 2 * cotangent.size),
+        name="pick_rows",
+    )(
+        me,
+        in_hbm(window_owner),
+        in_hbm(window_len),
+        in_hbm(slot_token.reshape(1, tokens)),
+        in_hbm(pixels),
+        in_hbm(cotangent),
+    )
+
+
+def attend_kernel(
+    me_ref, kept_ref, given_ref, gain_ref, w_hbm, *refs
+):
+    attended_ref, ordered_ref = refs[:2]
+    sent_refs = refs[2:-3]
+    sent, weights, sems = refs[-3:]
+    rows, width = ordered_ref.shape
+    pairs = len(sent_refs)
+    window_rows = rows // (2 * pairs)
+    inner = attended_ref.shape[0]
+    me = me_ref[0]
+    core = me % 2
+    copies = []
+    for part in range(3):
+        columns = w_hbm.at[:, pl.ds(part * inner, inner)]
+        copies.append(pltpu.make_async_copy(columns, weights.at[part], sems.at[part]))
+        copies[part].start()
+    key_row = iota((rows, rows), 0)
+    key_window = key_row // window_rows
+    live = jnp.zeros((rows, rows), jnp.float32)
+    for ref, side in ((kept_ref, core), (given_ref, 1 - core)):
+        lengths = ref[rows // 2 :, :rows].astype(jnp.float32)
+        for b in range(pairs):
+            window = 2 * b + side
+            ordered_ref[place(window, window_rows), :] = ref[
+                b * window_rows : (b + 1) * window_rows, :
+            ]
+            live = jnp.where(key_window == window, lengths[b : b + 1], live)
+    allowed = (key_window == iota((rows, rows), 1) // window_rows) & (
+        (key_row % window_rows).astype(jnp.float32) < live
+    )
+    values = ordered_ref[...].astype(jnp.float32)
+    mean_square = jnp.mean(values * values, axis=-1, keepdims=True)
+    normed = (values * lax.rsqrt(mean_square + 1e-06) * gain_ref[...][None, :]).astype(jnp.bfloat16)
+    projected = []
+    for part in range(3):
+        copies[part].wait()
+        projected.append(jnp.dot(normed, weights[part], preferred_element_type=jnp.float32))
+    queries = projected[0].astype(jnp.bfloat16)
+    keys_all = projected[1].astype(jnp.bfloat16)
+    values_across = projected[2].T.astype(jnp.bfloat16)
+    scale = 1.0 / math.sqrt(HD)
+    for head in range(inner // HD):
+        first = head * HD
+        low = first // LANES * LANES
+        high = -(-(first + HD) // LANES) * LANES
+        lane = iota((rows, high - low), 1) + low
+        own = (lane >= first) & (lane < first + HD)
+        keys = jnp.where(own, keys_all[:, low:high], jnp.zeros((), jnp.bfloat16))
+        scores = lax.dot_general(
+            keys, queries[:, low:high], ROWS_WITH_ROWS, preferred_element_type=jnp.float32
+        )
+        scores = jnp.where(allowed, scores * scale, -1e30)
+        raised = jnp.exp(scores - jnp.max(scores, axis=0, keepdims=True))
+        weight = (raised / jnp.sum(raised, axis=0, keepdims=True)).astype(jnp.bfloat16)
+        mixed = jnp.dot(
+            values_across[first : first + HD, :], weight, preferred_element_type=jnp.float32
+        ).astype(jnp.bfloat16)
+        attended_ref[first : first + HD, :] = mixed
+        relative = turn((head // 2) ^ (me // 2), core)
+        sent[relative, head % 2 * HD : (head % 2 + 1) * HD, :] = mixed
+    for b in range(pairs):
+        sent_refs[b][...] = sent[b]
+
+
+def attend_ordered(me, kept, given, gain, w_qkv, pairs):
+    width = kept.shape[1]
+    rows = 2 * (kept.shape[0] - SUBLANES)
+    inner = w_qkv.shape[1] // 3
+    heads = inner // pairs
+    return pl.pallas_call(
+        attend_kernel,
+        out_shape=(
+            jax.ShapeDtypeStruct((inner, rows), jnp.bfloat16),
+            jax.ShapeDtypeStruct((rows, width), jnp.bfloat16),
+        )
+        + (jax.ShapeDtypeStruct((heads, rows), jnp.bfloat16),) * pairs,
+        in_specs=[SMEM, VMEM, VMEM, VMEM, HBM],
+        out_specs=(VMEM,) * (2 + pairs),
+        scratch_shapes=[
+            pltpu.VMEM((pairs, heads, rows), jnp.bfloat16),
+            pltpu.VMEM((3, width, inner), jnp.bfloat16),
+            pltpu.SemaphoreType.DMA((3,)),
+        ],
+        compiler_params=params(24),
+        cost_estimate=cost(2 * rows * width * 3 * inner, 2 * w_qkv.size),
+        name="attend",
+    )(me, kept, given, in_hbm(gain), in_hbm(w_qkv))
+
+
+def project_kernel(attended_ref, ordered_ref, w_ref, *encoded_refs):
+    added = lax.dot_general(
+        attended_ref[...], w_ref[...], TRANSPOSED, preferred_element_type=jnp.float32
+    )
+    encoded = (ordered_ref[...].astype(jnp.float32) + added).astype(jnp.bfloat16)
+    size = ordered_ref.shape[0] // len(encoded_refs)
+    for b, ref in enumerate(encoded_refs):
+        ref[...] = encoded[b * size : (b + 1) * size]
+
+
+def project_ordered(attended, ordered, w_out, pairs):
+    rows, width = ordered.shape
+    return pl.pallas_call(
+        project_kernel,
+        out_shape=(jax.ShapeDtypeStruct((rows // pairs, width), jnp.bfloat16),) * pairs,
+        in_specs=[VMEM] * 3,
+        out_specs=(VMEM,) * pairs,
+        compiler_params=params(16),
+        cost_estimate=cost(2 * ordered.size * w_out.shape[0], 2 * w_out.size),
+        name="project",
+    )(attended, ordered, w_out)
+
+
+def gradient_kernel(scale, pairs, me_ref, *refs):
+    columns, blocks = refs[:pairs], refs[pairs : 2 * pairs]
+    kept_ref, given_ref = refs[2 * pairs :]
+    size = blocks[0].shape[0] // pairs
+    head = kept_ref.shape[0]
+    left = jnp.concatenate([ref[...] for ref in columns], 1)
+    right = jnp.concatenate(
+        [
+            blocks[b ^ r][r * size : (r + 1) * size, :]
+            for b in range(pairs)
+            for r in range(pairs)
+        ],
+        0,
+    )
+    total = jnp.dot(left, right, preferred_element_type=jnp.float32) * scale
+    first = me_ref[0] % 2 == 0
+    kept_ref[...] = jnp.where(first, total[:head], total[head:])
+    given_ref[...] = jnp.where(first, total[head:], total[:head]).astype(jnp.bfloat16)
+
+
+def gradient_rows(me, columns, blocks, scale):
+    pairs = len(blocks)
+    heads, rows = columns[0].shape
+    width = blocks[0].shape[1]
+    return pl.pallas_call(
+        functools.partial(gradient_kernel, scale, pairs),
+        out_shape=(
+            jax.ShapeDtypeStruct((heads // 2, width), jnp.float32),
+            jax.ShapeDtypeStruct((heads // 2, width), jnp.bfloat16),
+        ),
+        in_specs=[SMEM] + [VMEM] * (2 * pairs),
+        out_specs=(VMEM, VMEM),
+        compiler_params=params(24),
+        cost_estimate=cost(2 * heads * rows * pairs * width, 2 * pairs * rows * width),
+        name="gradient_rows",
+    )(me, *columns, *blocks)
+
+
+def place_kernel(me_ref, slots_ref, *refs):
+    embeddings_ref = refs[-1]
+    arrived = jnp.concatenate([ref[...] for ref in refs[:-1]], 0)
+    rows, width = arrived.shape
+    tokens = embeddings_ref.shape[0]
+    row = iota((rows, tokens), 0)
+    window_rows = rows // (2 * (len(refs) - 1))
+    holds = slots_ref[...] == slot_of_row(row, me_ref[0], window_rows)
+    for j in range(MERGE):
+        put = jnp.where(holds & (row % MERGE == j), 1.0, 0.0).astype(jnp.bfloat16)
+        part = lax.dot_general(put, arrived, TRANSPOSED, preferred_element_type=jnp.float32)
+        embeddings_ref[:, j * width : (j + 1) * width] = part.astype(jnp.bfloat16)
+
+
+def place_rows(me, slot_token, arrived):
+    size, width = arrived[0].shape
+    rows = size * len(arrived)
+    tokens = slot_token.shape[0]
+    return pl.pallas_call(
+        place_kernel,
+        out_shape=jax.ShapeDtypeStruct((tokens, MERGE * width), jnp.bfloat16),
+        in_specs=[SMEM, VMEM] + [VMEM] * len(arrived),
+        out_specs=VMEM,
+        compiler_params=params(16),
+        cost_estimate=cost(2 * MERGE * rows * tokens * width, 2 * MERGE * tokens * width),
+        name="place_rows",
+    )(me, slot_token.reshape(1, tokens), *arrived)
+
+
+def after(value, other):
+    return lax.optimization_barrier((value, other))[0]
+
+
+def swap(value, axis, bits):
+    size = lax.axis_size(axis)
+    return lax.ppermute(value, axis, [(i, i ^ bits) for i in range(size)])
+
+
+def chip_swap(value, relative):
+    size = lax.axis_size("enc")
+    return lax.ppermute(value, "enc", [(i, i ^ 2 * turn(relative, i % 2)) for i in range(size)])
+
+
+def xor_slice(pixels, window_owner, window_len, slot_token, cotangent, w_qkv, w_out, gain):
+    group = lax.axis_size("enc")
+    replicas = lax.axis_size("rep")
+    pairs = group // 2
+    rows = pixels.shape[0]
+    me = lax.axis_index("enc").astype(jnp.int32).reshape(1)
+
+    held, kept, given = pick_rows(me, window_owner, window_len, slot_token, pixels, cotangent)
+    given = swap(given, "enc", 1)
+    blocks = [held, chip_swap(held, 1), chip_swap(held, 2)]
+    attended, ordered, *sent = attend_ordered(me, kept, given, gain, w_qkv, pairs)
+    blocks.append(chip_swap(after(blocks[1], attended), 2))
+    columns = [sent[0]] + [chip_swap(sent[b], b) for b in range(1, pairs)]
+    encoded = project_ordered(attended, ordered, w_out, pairs)
+    scale = 1.0 / math.sqrt(rows * group * replicas)
+    mine, other = gradient_rows(me, columns, blocks, scale)
+    part = (mine + swap(other, "enc", 1).astype(jnp.float32)).astype(jnp.bfloat16)
+    arrived = [encoded[0]]
+    for b in range(1, pairs):
+        arrived.append(chip_swap(after(encoded[b], part), b))
+    bit = 1
+    while bit < replicas:
+        total = part.astype(jnp.float32) + swap(part, "rep", bit).astype(jnp.float32)
+        part = total.astype(jnp.bfloat16)
+        bit *= 2
+    embeddings = place_rows(me, slot_token, arrived)
+    return (embeddings, total)
+
+
 def solution(mesh):
+    def shards(*args):
+        group = mesh.shape["enc"]
+        replicas = mesh.shape["rep"]
+        square = group == 2 << PAIR_BITS and replicas & (replicas - 1) == 0
+        whole = square and args[1].shape[0] == group
+        return (xor_slice if whole else any_slice)(*args)
+
     return jax.shard_map(
         shards,
         mesh=mesh,

time: 124 us -> 47.2 us (0.38)
  waiting for transfers between devices: 78.6 us -> 17.2 us
  matrix products: 14 us -> 0 us
  between operations: 14.2 us -> 0.7 us
  Pallas kernels: 0 us -> 10.3 us
  starting transfers between devices: 9.41 us -> 18 us
  local copies, waits for them, and re-layouts: 4.93 us -> 0.01 us
    reduce_scatter x1 -> x0, waiting for transfers between devices: 41.2 us -> none  [shards(): lax.psum_scatter(lax.dot_general(attended, d_encoded, (((0,), (0,)), ((),...]
    psum x1 -> x0, waiting for transfers between devices: 37.3 us -> none  [shards(): summed = lax.psum(reduced, 'rep')]
    ppermute x0 -> x13, starting transfers between devices: none -> 18 us  [the longest x9 13.6 us: chip_swap(): lax.ppermute(value, 'enc', [(i, i ^ 2 * turn(relative, i % 2)) for i in r...]
    ppermute x0 -> x13, waiting for transfers between devices: none -> 17.2 us  [the longest x9 10.2 us: chip_swap(): lax.ppermute(value, 'enc', [(i, i ^ 2 * turn(relative, i % 2)) for i in r...]
    dot_general x9 -> x0, matrix products: 13.6 us -> none  [the longest x1 3.35 us: encode(): jnp.dot(normed, w_qkv, preferred_element_type=jnp.float32)]
    pallas_call x0 -> x5, Pallas kernels: none -> 10.3 us  [the longest x1 5 us: attend_ordered(): pl.pallas_call(attend_kernel, out_shape=(jax.ShapeDtypeStruct((inner, row...]
    all_to_all x2 -> x0, starting transfers between devices: 9.34 us -> none  [the longest x1 5.18 us: shards(): lax.all_to_all(returning, 'enc', split_axis=0, concat_axis=0, tiled=True)]
    reshape x9 -> x0, local copies, waits for them, and re-layouts: 3.23 us -> none  [the longest x1 0.98 us: shards(): outgoing.astype(jnp.bfloat16).reshape(group_size, tokens_each, merged_width)]
  transfers between devices with their start and end apart: 4 -> 13, of which waited for: 2 -> 9; matrix products, arithmetic and copies ran while one was open for 10% -> 0% of each run, Pallas kernels for 0% -> 15%
where the time goes in v3:
time: 47.2 us; the launch traced here: 47.1 us
  starting transfers between devices  18 us (38%)
  waiting for transfers between devices  17.2 us (36%)
  Pallas kernels  10.3 us (22%)
  other arithmetic  0.88 us (2%)
  between operations  0.7 us (1%)
    ppermute x9, starting transfers between devices, chip_swap(): lax.ppermute(value, 'enc', [(i, i ^ 2 * turn(relative, i % 2)) for i in r...  13.6 us
    ppermute x9, waiting for transfers between devices, chip_swap(): lax.ppermute(value, 'enc', [(i, i ^ 2 * turn(relative, i % 2)) for i in r...  10.2 us
    ppermute x4, waiting for transfers between devices, swap(): return lax.ppermute(value, axis, [(i, i ^ bits) for i in range(size)])  6.98 us
    pallas_call x1, Pallas kernels, attend_ordered(): pl.pallas_call(attend_kernel, out_shape=(jax.ShapeDtypeStruct((inner, row...  5 us
    ppermute x4, starting transfers between devices, swap(): return lax.ppermute(value, axis, [(i, i ^ bits) for i in range(size)])  4.4 us
    pallas_call x1, Pallas kernels, pick_rows(): pl.pallas_call(pick_kernel, out_shape=(jax.ShapeDtypeStruct((rows, width)...  2.6 us
    pallas_call x1, Pallas kernels, place_rows(): pl.pallas_call(place_kernel, out_shape=jax.ShapeDtypeStruct((tokens, MERG...  1.82 us
  transfers between devices with their start and end apart: 13, of which 9 were waited for; matrix products, arithmetic and copies ran while one was open for 0% of the time, Pallas kernels for 15%

profile of v3, /device:TPU:0, one launch (start us, length us, event | category | flops | bytes accessed | tf_op | source)
XLA Modules:
  0.0 47.1 jit_solution(8566469973531328295)
XLA Ops:
  0.6 2.6 %pick_rows.1 = (bf16[128,1280]{1,0:T(8,128)(2,1)S(1)}, bf16[80,1280]{1,0:T(8,128)(2,1)S(1)}, bf16[80,1280]{1,0:T(8,128)(2,1)S(1)}) custom-call(s32[1]{0:T(128)} %bitcast.me_ref, s32[8]{0:T(128)} %owner_ref.1, s32[8]{0:T(128)} %len_ref.1, s32[1,160]{1,0:T(1,128)} %bitcast.2, bf16[128,1280]{1,0:T(8,128)(2,1)} %pixels_hbm.1, bf16[160,5120]{1,0:T(8,128)(2,1)} %cotangent_hbm.1), custom_call_target="tpu_custom_call" | custom-call | flops 209715200 | bytes 1638400 | tf_op jit(solution)/shard_map/pick_rows/pallas_call | solution.py:195
  3.2 3.0 %collective-permute-start.4 = (bf16[128,1280]{1,0:T(8,128)(2,1)S(1)}, bf16[128,1280]{1,0:T(8,128)(2,1)S(1)}, u32[]{:S(2)}, u32[]{:S(2)}) collective-permute-start(bf16[128,1280]{1,0:T(8,128)(2,1)S(1)} %get-tuple-element.31.refs_4_), channel_id=1, source_target_pairs={{0,8},{4,20},{8,0},{12,28},{16,24},{20,4},{24,16},{28,12},{1,9},{5... | collective-permute-start | bytes 983048 | tf_op jit(solution)/shard_map/ppermute | solution.py:410
  6.2 0.0 collective-permute-start
  6.3 1.5 %collective-permute-start.5 = (bf16[128,1280]{1,0:T(8,128)(2,1)S(1)}, bf16[128,1280]{1,0:T(8,128)(2,1)S(1)}, u32[]{:S(2)}, u32[]{:S(2)}) collective-permute-start(bf16[128,1280]{1,0:T(8,128)(2,1)S(1)} %get-tuple-element.31.refs_4_), channel_id=1, source_target_pairs={{0,16},{4,12},{8,24},{12,4},{16,0},{20,28},{24,8},{28,20},{1,17},{... | collective-permute-start | bytes 983048 | tf_op jit(solution)/shard_map/ppermute | solution.py:410
  7.8 0.0 collective-permute-done.given_ref
  7.8 5.0 %attend.1 = (bf16[640,128]{1,0:T(8,128)(2,1)S(1)}, bf16[128,1280]{1,0:T(8,128)(2,1)S(1)}, bf16[160,128]{1,0:T(8,128)(2,1)S(1)}, bf16[160,128]{1,0:T(8,128)(2,1)S...) custom-call(s32[1]{0:T(128)} %bitcast.me_ref, bf16[80,1280]{1,0:T(8,128)(2,1)S(1)} %get-tuple-element.21.kept_ref, ...), custom_call_target="tpu_custom_call" | custom-call | flops 629145600 | bytes 4915200 | tf_op jit(solution)/shard_map/attend/pallas_call | solution.py:289
  12.8 0.0 copy-start
  12.8 1.4 %collective-permute-done.4.refs_5_ = bf16[128,1280]{1,0:T(8,128)(2,1)S(1)} collective-permute-done((bf16[128,1280]{1,0:T(8,128)(2,1)S(1)}, bf16[128,1280]{1,0:T(8,128)(2,1)S(1)}, u32[]{:S(2)}, u32[]{:S(2)}) %collective-permute-start.4) | collective-permute-done | bytes 327712 | tf_op jit(solution)/shard_map/ppermute | solution.py:410
  14.2 1.6 %collective-permute-start.6 = (bf16[128,1280]{1,0:T(8,128)(2,1)S(1)}, bf16[128,1280]{1,0:T(8,128)(2,1)S(1)}, u32[]{:S(2)}, u32[]{:S(2)}) collective-permute-start(bf16[128,1280]{1,0:T(8,128)(2,1)S(1)} %collective-permute-done.4.refs_5_), channel_id=1, source_target_pairs={{0,16},{4,12},{8,24},{12,4},{16,0},{20,28},{24,8},{28,20},{1,17},{... | collective-permute-start | bytes 983048 | tf_op jit(solution)/shard_map/ppermute | solution.py:410
  15.8 2.4 %collective-permute-start.1 = (bf16[160,128]{1,0:T(8,128)(2,1)S(1)}, bf16[160,128]{1,0:T(8,128)(2,1)S(1)}, u32[]{:S(2)}, u32[]{:S(2)}) collective-permute-start(bf16[160,128]{1,0:T(8,128)(2,1)S(1)} %get-tuple-element.28), channel_id=1, source_target_pairs={{0,8},{4,20},{8,0},{12,28},{16,24},{20,4},{24,16},{28,12},{1,9},{5... | collective-permute-start | bytes 122888 | tf_op jit(solution)/shard_map/ppermute | solution.py:410
  18.3 0.5 collective-permute-start.2
  18.7 1.0 %collective-permute-start.3 = (bf16[160,128]{1,0:T(8,128)(2,1)S(1)}, bf16[160,128]{1,0:T(8,128)(2,1)S(1)}, u32[]{:S(2)}, u32[]{:S(2)}) collective-permute-start(bf16[160,128]{1,0:T(8,128)(2,1)S(1)} %get-tuple-element.30), channel_id=1, source_target_pairs={{0,24},{4,28},{8,16},{12,20},{16,8},{20,12},{24,0},{28,4},{1,25},{... | collective-permute-start | bytes 122888 | tf_op jit(solution)/shard_map/ppermute | solution.py:410
  19.7 0.6 %collective-permute-done.1.refs_1_ = bf16[160,128]{1,0:T(8,128)(2,1)S(1)} collective-permute-done((bf16[160,128]{1,0:T(8,128)(2,1)S(1)}, bf16[160,128]{1,0:T(8,128)(2,1)S(1)}, u32[]{:S(2)}, u32[]{:S(2)}) %collective-permute-start.1) | collective-permute-done | bytes 40992 | tf_op jit(solution)/shard_map/ppermute | solution.py:410
  20.4 1.9 %collective-permute-done.2.refs_2_ = bf16[160,128]{1,0:T(8,128)(2,1)S(1)} collective-permute-done((bf16[160,128]{1,0:T(8,128)(2,1)S(1)}, bf16[160,128]{1,0:T(8,128)(2,1)S(1)}, u32[]{:S(2)}, u32[]{:S(2)}) %collective-permute-start.2) | collective-permute-done | bytes 40992 | tf_op jit(solution)/shard_map/ppermute | solution.py:410
  22.3 1.4 %collective-permute-done.3.refs_3_ = bf16[160,128]{1,0:T(8,128)(2,1)S(1)} collective-permute-done((bf16[160,128]{1,0:T(8,128)(2,1)S(1)}, bf16[160,128]{1,0:T(8,128)(2,1)S(1)}, u32[]{:S(2)}, u32[]{:S(2)}) %collective-permute-start.3) | collective-permute-done | bytes 40992 | tf_op jit(solution)/shard_map/ppermute | solution.py:410
  23.6 0.0 collective-permute-done.5.refs_6_
  23.6 0.0 collective-permute-done.6.refs_7_
  23.6 0.4 gradient_rows.1
  24.1 0.1 collective-permute-start.7
  24.1 1.4 %collective-permute-done.7 = bf16[80,1280]{1,0:T(8,128)(2,1)S(1)} collective-permute-done((bf16[80,1280]{1,0:T(8,128)(2,1)S(1)}, bf16[80,1280]{1,0:T(8,128)(2,1)S(1)}, u32[]{:S(2)}, u32[]{:S(2)}) %collective-permute-start.7) | collective-permute-done | bytes 204832 | tf_op jit(solution)/shard_map/ppermute | solution.py:405
  25.6 0.0 copy-start.1
  25.6 1.6 %collective-permute-start.11 = (bf16[80,1280]{1,0:T(8,128)(2,1)S(1)}, bf16[80,1280]{1,0:T(8,128)(2,1)S(1)}, u32[]{:S(2)}, u32[]{:S(2)}) collective-permute-start(bf16[80,1280]{1,0:T(8,128)(2,1)S(1)} %add_convert_fusion.1), channel_id=1, source_target_pairs={{0,1},{1,0},{2,3},{3,2},{4,5},{5,4},{6,7},{7,6},{8,9},{9,8},{10,11... | collective-permute-start | bytes 614408 | tf_op jit(solution)/shard_map/ppermute | solution.py:405
  27.3 5.5 %collective-permute-done.11 = bf16[80,1280]{1,0:T(8,128)(2,1)S(1)} collective-permute-done((bf16[80,1280]{1,0:T(8,128)(2,1)S(1)}, bf16[80,1280]{1,0:T(8,128)(2,1)S(1)}, u32[]{:S(2)}, u32[]{:S(2)}) %collective-permute-start.11) | collective-permute-done | bytes 204832 | tf_op jit(solution)/shard_map/ppermute | solution.py:405
  32.8 0.1 add_convert_fusion
  32.9 2.7 %collective-permute-start.12 = (bf16[80,1280]{1,0:T(8,128)(2,1)S(1)}, bf16[80,1280]{1,0:T(8,128)(2,1)S(1)}, u32[]{:S(2)}, u32[]{:S(2)}) collective-permute-start(bf16[80,1280]{1,0:T(8,128)(2,1)S(1)} %add_convert_fusion), channel_id=1, source_target_pairs={{0,2},{1,3},{2,0},{3,1},{4,6},{5,7},{6,4},{7,5},{8,10},{9,11},{10,... | collective-permute-start | bytes 614408 | tf_op jit(solution)/shard_map/ppermute | solution.py:405
  35.5 0.0 copy-done
  35.5 0.5 project.1
  36.0 1.5 %collective-permute-start.8 = (bf16[32,1280]{1,0:T(8,128)(2,1)S(1)}, bf16[32,1280]{1,0:T(8,128)(2,1)S(1)}, u32[]{:S(2)}, u32[]{:S(2)}) collective-permute-start(bf16[32,1280]{1,0:T(8,128)(2,1)S(1)} %get-tuple-element.35), channel_id=1, source_target_pairs={{0,8},{4,20},{8,0},{12,28},{16,24},{20,4},{24,16},{28,12},{1,9},{5... | collective-permute-start | bytes 245768 | tf_op jit(solution)/shard_map/ppermute | solution.py:410
  37.5 1.5 %collective-permute-start.9 = (bf16[32,1280]{1,0:T(8,128)(2,1)S(1)}, bf16[32,1280]{1,0:T(8,128)(2,1)S(1)}, u32[]{:S(2)}, u32[]{:S(2)}) collective-permute-start(bf16[32,1280]{1,0:T(8,128)(2,1)S(1)} %get-tuple-element.37), channel_id=1, source_target_pairs={{0,16},{4,12},{8,24},{12,4},{16,0},{20,28},{24,8},{28,20},{1,17},{... | collective-permute-start | bytes 245768 | tf_op jit(solution)/shard_map/ppermute | solution.py:410
  39.1 0.5 %collective-permute-start.10 = (bf16[32,1280]{1,0:T(8,128)(2,1)S(1)}, bf16[32,1280]{1,0:T(8,128)(2,1)S(1)}, u32[]{:S(2)}, u32[]{:S(2)}) collective-permute-start(bf16[32,1280]{1,0:T(8,128)(2,1)S(1)} %get-tuple-element.39), channel_id=1, source_target_pairs={{0,24},{4,28},{8,16},{12,20},{16,8},{20,12},{24,0},{28,4},{1,25},{... | collective-permute-start | bytes 245768 | tf_op jit(solution)/shard_map/ppermute | solution.py:410
  39.6 1.8 %collective-permute-done.8.refs_1_ = bf16[32,1280]{1,0:T(8,128)(2,1)S(1)} collective-permute-done((bf16[32,1280]{1,0:T(8,128)(2,1)S(1)}, bf16[32,1280]{1,0:T(8,128)(2,1)S(1)}, u32[]{:S(2)}, u32[]{:S(2)}) %collective-permute-start.8) | collective-permute-done | bytes 81952 | tf_op jit(solution)/shard_map/ppermute | solution.py:410
  41.3 1.5 %collective-permute-done.9.refs_2_ = bf16[32,1280]{1,0:T(8,128)(2,1)S(1)} collective-permute-done((bf16[32,1280]{1,0:T(8,128)(2,1)S(1)}, bf16[32,1280]{1,0:T(8,128)(2,1)S(1)}, u32[]{:S(2)}, u32[]{:S(2)}) %collective-permute-start.9) | collective-permute-done | bytes 81952 | tf_op jit(solution)/shard_map/ppermute | solution.py:410
  42.8 1.6 %collective-permute-done.10.refs_3_ = bf16[32,1280]{1,0:T(8,128)(2,1)S(1)} collective-permute-done((bf16[32,1280]{1,0:T(8,128)(2,1)S(1)}, bf16[32,1280]{1,0:T(8,128)(2,1)S(1)}, u32[]{:S(2)}, u32[]{:S(2)}) %collective-permute-start.10) | collective-permute-done | bytes 81952 | tf_op jit(solution)/shard_map/ppermute | solution.py:410
  44.4 0.0 copy-done.1
  44.4 1.8 %place_rows.1 = bf16[160,5120]{1,0:T(8,128)(2,1)} custom-call(s32[1]{0:T(128)} %bitcast.me_ref, s32[1,160]{1,0:T(1,128)S(1)} %bitcast.3, bf16[32,1280]{1,0:T(8,128)(2,1)S(1)} %get-tuple-element.25.refs_0_, bf16[32,1280]{1,0:T(8,128)(2,1)S(1)} %collective-permute-done.8.refs_1_, bf16[32,1280]{1,0:T(8,128)(2,1)S(1)} %collective-permute-done.9.refs_2_, ...), custom_call_target="tpu_custom_call" | custom-call | flops 209715200 | bytes 1638400 | tf_op jit(solution)/shard_map/place_rows/pallas_call | solution.py:388
  46.2 0.0 collective-permute-done.12
  46.3 0.8 %convert_add_fusion = f32[80,1280]{1,0:T(8,128)} fusion(bf16[80,1280]{1,0:T(8,128)(2,1)S(1)} %collective-permute-done.12, bf16[80,1280]{1,0:T(8,128)(2,1)S(1)} %add_convert_fusion), kind=kLoop, calls=%fused_computation | loop fusion | flops 307200 | bytes 819200 | tf_op jit(solution)/shard_map/add | solution.py:435
  (1 shorter events, 0.0 us)
Async XLA Ops:
  3.2 11.0 %collective-permute-start.4 = (bf16[128,1280]{1,0:T(8,128)(2,1)S(1)}, bf16[128,1280]{1,0:T(8,128)(2,1)S(1)}, u32[]{:S(2)}, u32[]{:S(2)}) collective-permute-start(bf16[128,1280]{1,0:T(8,128)(2,1)S(1)} %get-tuple-element.31.refs_4_), channel_id=1, source_target_pairs={{0,8},{4,20},{8,0},{12,28},{16,24},{20,4},{24,16},{28,12},{1,9},{5... | collective-permute-start | bytes 983048 | tf_op jit(solution)/shard_map/ppermute | solution.py:410
  6.2 1.5 %collective-permute-start = (bf16[80,1280]{1,0:T(8,128)(2,1)S(1)}, bf16[80,1280]{1,0:T(8,128)(2,1)S(1)}, u32[]{:S(2)}, u32[]{:S(2)}) collective-permute-start(bf16[80,1280]{1,0:T(8,128)(2,1)S(1)} %get-tuple-element.22), channel_id=1, source_target_pairs={{0,4},{4,0},{8,12},{12,8},{16,20},{20,16},{24,28},{28,24},{1,5},{5... | collective-permute-start | bytes 614408 | tf_op jit(solution)/shard_map/ppermute | solution.py:405
  6.3 17.4 %collective-permute-start.5 = (bf16[128,1280]{1,0:T(8,128)(2,1)S(1)}, bf16[128,1280]{1,0:T(8,128)(2,1)S(1)}, u32[]{:S(2)}, u32[]{:S(2)}) collective-permute-start(bf16[128,1280]{1,0:T(8,128)(2,1)S(1)} %get-tuple-element.31.refs_4_), channel_id=1, source_target_pairs={{0,16},{4,12},{8,24},{12,4},{16,0},{20,28},{24,8},{28,20},{1,17},{... | collective-permute-start | bytes 983048 | tf_op jit(solution)/shard_map/ppermute | solution.py:410
  12.8 22.8 %copy-start = (bf16[640,1280]{1,0:T(8,128)(2,1)S(1)}, bf16[640,1280]{1,0:T(8,128)(2,1)}, u32[]{:S(2)}) copy-start(bf16[640,1280]{1,0:T(8,128)(2,1)} %w_ref.1) | copy-start | bytes 4915204
  14.2 9.4 %collective-permute-start.6 = (bf16[128,1280]{1,0:T(8,128)(2,1)S(1)}, bf16[128,1280]{1,0:T(8,128)(2,1)S(1)}, u32[]{:S(2)}, u32[]{:S(2)}) collective-permute-start(bf16[128,1280]{1,0:T(8,128)(2,1)S(1)} %collective-permute-done.4.refs_5_), channel_id=1, source_target_pairs={{0,16},{4,12},{8,24},{12,4},{16,0},{20,28},{24,8},{28,20},{1,17},{... | collective-permute-start | bytes 983048 | tf_op jit(solution)/shard_map/ppermute | solution.py:410
  15.8 4.5 %collective-permute-start.1 = (bf16[160,128]{1,0:T(8,128)(2,1)S(1)}, bf16[160,128]{1,0:T(8,128)(2,1)S(1)}, u32[]{:S(2)}, u32[]{:S(2)}) collective-permute-start(bf16[160,128]{1,0:T(8,128)(2,1)S(1)} %get-tuple-element.28), channel_id=1, source_target_pairs={{0,8},{4,20},{8,0},{12,28},{16,24},{20,4},{24,16},{28,12},{1,9},{5... | collective-permute-start | bytes 122888 | tf_op jit(solution)/shard_map/ppermute | solution.py:410
  18.3 4.0 %collective-permute-start.2 = (bf16[160,128]{1,0:T(8,128)(2,1)S(1)}, bf16[160,128]{1,0:T(8,128)(2,1)S(1)}, u32[]{:S(2)}, u32[]{:S(2)}) collective-permute-start(bf16[160,128]{1,0:T(8,128)(2,1)S(1)} %get-tuple-element.29), channel_id=1, source_target_pairs={{0,16},{4,12},{8,24},{12,4},{16,0},{20,28},{24,8},{28,20},{1,17},{... | collective-permute-start | bytes 122888 | tf_op jit(solution)/shard_map/ppermute | solution.py:410
  18.7 4.9 %collective-permute-start.3 = (bf16[160,128]{1,0:T(8,128)(2,1)S(1)}, bf16[160,128]{1,0:T(8,128)(2,1)S(1)}, u32[]{:S(2)}, u32[]{:S(2)}) collective-permute-start(bf16[160,128]{1,0:T(8,128)(2,1)S(1)} %get-tuple-element.30), channel_id=1, source_target_pairs={{0,24},{4,28},{8,16},{12,20},{16,8},{20,12},{24,0},{28,4},{1,25},{... | collective-permute-start | bytes 122888 | tf_op jit(solution)/shard_map/ppermute | solution.py:410
  24.1 1.5 %collective-permute-start.7 = (bf16[80,1280]{1,0:T(8,128)(2,1)S(1)}, bf16[80,1280]{1,0:T(8,128)(2,1)S(1)}, u32[]{:S(2)}, u32[]{:S(2)}) collective-permute-start(bf16[80,1280]{1,0:T(8,128)(2,1)S(1)} %get-tuple-element.34), channel_id=1, source_target_pairs={{0,4},{4,0},{8,12},{12,8},{16,20},{20,16},{24,28},{28,24},{1,5},{5... | collective-permute-start | bytes 614408 | tf_op jit(solution)/shard_map/ppermute | solution.py:405
  25.6 18.8 %copy-start.1 = (s32[160]{0:T(256)S(1)}, s32[160]{0:T(256)}, u32[]{:S(2)}) copy-start(s32[160]{0:T(256)} %param.11) | copy-start | bytes 1924
  25.6 7.2 %collective-permute-start.11 = (bf16[80,1280]{1,0:T(8,128)(2,1)S(1)}, bf16[80,1280]{1,0:T(8,128)(2,1)S(1)}, u32[]{:S(2)}, u32[]{:S(2)}) collective-permute-start(bf16[80,1280]{1,0:T(8,128)(2,1)S(1)} %add_convert_fusion.1), channel_id=1, source_target_pairs={{0,1},{1,0},{2,3},{3,2},{4,5},{5,4},{6,7},{7,6},{8,9},{9,8},{10,11... | collective-permute-start | bytes 614408 | tf_op jit(solution)/shard_map/ppermute | solution.py:405
  32.9 13.4 %collective-permute-start.12 = (bf16[80,1280]{1,0:T(8,128)(2,1)S(1)}, bf16[80,1280]{1,0:T(8,128)(2,1)S(1)}, u32[]{:S(2)}, u32[]{:S(2)}) collective-permute-start(bf16[80,1280]{1,0:T(8,128)(2,1)S(1)} %add_convert_fusion), channel_id=1, source_target_pairs={{0,2},{1,3},{2,0},{3,1},{4,6},{5,7},{6,4},{7,5},{8,10},{9,11},{10,... | collective-permute-start | bytes 614408 | tf_op jit(solution)/shard_map/ppermute | solution.py:405
  36.0 5.3 %collective-permute-start.8 = (bf16[32,1280]{1,0:T(8,128)(2,1)S(1)}, bf16[32,1280]{1,0:T(8,128)(2,1)S(1)}, u32[]{:S(2)}, u32[]{:S(2)}) collective-permute-start(bf16[32,1280]{1,0:T(8,128)(2,1)S(1)} %get-tuple-element.35), channel_id=1, source_target_pairs={{0,8},{4,20},{8,0},{12,28},{16,24},{20,4},{24,16},{28,12},{1,9},{5... | collective-permute-start | bytes 245768 | tf_op jit(solution)/shard_map/ppermute | solution.py:410
  37.5 5.3 %collective-permute-start.9 = (bf16[32,1280]{1,0:T(8,128)(2,1)S(1)}, bf16[32,1280]{1,0:T(8,128)(2,1)S(1)}, u32[]{:S(2)}, u32[]{:S(2)}) collective-permute-start(bf16[32,1280]{1,0:T(8,128)(2,1)S(1)} %get-tuple-element.37), channel_id=1, source_target_pairs={{0,16},{4,12},{8,24},{12,4},{16,0},{20,28},{24,8},{28,20},{1,17},{... | collective-permute-start | bytes 245768 | tf_op jit(solution)/shard_map/ppermute | solution.py:410
  39.1 5.3 %collective-permute-start.10 = (bf16[32,1280]{1,0:T(8,128)(2,1)S(1)}, bf16[32,1280]{1,0:T(8,128)(2,1)S(1)}, u32[]{:S(2)}, u32[]{:S(2)}) collective-permute-start(bf16[32,1280]{1,0:T(8,128)(2,1)S(1)} %get-tuple-element.39), channel_id=1, source_target_pairs={{0,24},{4,28},{8,16},{12,20},{16,8},{20,12},{24,0},{28,4},{1,25},{... | collective-permute-start | bytes 245768 | tf_op jit(solution)/shard_map/ppermute | solution.py:410

commit v4 on v3

--- a/solution.py
+++ b/solution.py
@@ -134,6 +134,10 @@
     return pltpu.with_memory_space_constraint(value, pltpu.HBM)
 
 
+def in_vmem(value):
+    return pltpu.with_memory_space_constraint(value, pltpu.VMEM)
+
+
 def place(index, size):
     return pl.ds(pl.multiple_of(index * size, size), size)
 
@@ -145,26 +149,43 @@
 
 
 def pick_kernel(
-    me_ref, owner_ref, len_ref, slots_ref, pixels_hbm, cotangent_hbm,
-    held_ref, kept_ref, given_ref, parts, pixels_buf, windows_buf, sems,
+    owner_hbm, len_hbm, slots_hbm, pixels_hbm, cotangent_hbm, held_ref, kept_ref, given_ref,
+    owner_ref, len_ref, slots_ref, pixels_buf, parts, windows_buf, sems,
 ):
     rows, width = held_ref.shape
     tokens = cotangent_hbm.shape[0]
     windows = owner_ref.shape[0]
     window_rows = rows // windows
-    me = me_ref[0]
-    copies = [pltpu.make_async_copy(pixels_hbm, pixels_buf, sems.at[MERGE])]
-    copies[0].start()
+    me = lax.axis_index("enc")
+    pairs_of_refs = [
+        (slots_hbm, slots_ref),
+        (owner_hbm, owner_ref),
+        (len_hbm, len_ref),
+    ]
     for j in range(MERGE):
-        columns = cotangent_hbm.at[:, pl.ds(j * width, width)]
-        copies.append(pltpu.make_async_copy(columns, parts.at[j], sems.at[j]))
-        copies[1 + j].start()
+        pairs_of_refs.append((cotangent_hbm.at[:, pl.ds(j * width, width)], parts.at[j]))
+    pairs_of_refs.append((pixels_hbm, pixels_buf))
+    copies = [
+        pltpu.make_async_copy(source, target, sems.at[i])
+        for i, (source, target) in enumerate(pairs_of_refs)
+    ]
+    for copy in copies:
+        copy.start()
     row = iota((rows, tokens), 0)
+    copies[0].wait()
     holds = slots_ref[...] == slot_of_row(row, me, window_rows)
     picks = [
         jnp.where(holds & (row % MERGE == j), 1.0, 0.0).astype(jnp.bfloat16) for j in range(MERGE)
     ]
-    copies[0].wait()
+    held = None
+    for j in range(MERGE):
+        copies[3 + j].wait()
+        term = jnp.dot(picks[j], parts[j], preferred_element_type=jnp.float32)
+        held = term if held is None else held + term
+    held_ref[...] = held.astype(jnp.bfloat16)
+    copies[1].wait()
+    copies[2].wait()
+    copies[3 + MERGE].wait()
     which = iota((SUBLANES, width), 0)
     lengths = [jnp.zeros((SUBLANES, width), jnp.int32)] * 2
     for w in range(windows):
@@ -180,34 +201,30 @@
     for side, ref in enumerate((kept_ref, given_ref)):
         ref[: rows // 2, :] = windows_buf[side]
         ref[rows // 2 :, :] = lengths[side].astype(jnp.float32).astype(jnp.bfloat16)
-    held = None
-    for j in range(MERGE):
-        copies[1 + j].wait()
-        term = jnp.dot(picks[j], parts[j], preferred_element_type=jnp.float32)
-        held = term if held is None else held + term
-    held_ref[...] = held.astype(jnp.bfloat16)
-
-
-def pick_rows(me, window_owner, window_len, slot_token, pixels, cotangent):
+
+
+def pick_rows(window_owner, window_len, slot_token, pixels, cotangent):
     rows, width = pixels.shape
     tokens = cotangent.shape[0]
     half = jax.ShapeDtypeStruct((rows // 2 + SUBLANES, width), jnp.bfloat16)
     return pl.pallas_call(
         pick_kernel,
         out_shape=(jax.ShapeDtypeStruct((rows, width), jnp.bfloat16), half, half),
-        in_specs=[SMEM, SMEM, SMEM, VMEM, HBM, HBM],
+        in_specs=[HBM] * 5,
         out_specs=(VMEM, VMEM, VMEM),
         scratch_shapes=[
+            pltpu.SMEM(window_owner.shape, jnp.int32),
+            pltpu.SMEM(window_len.shape, jnp.int32),
+            pltpu.VMEM((1, tokens), jnp.int32),
+            pltpu.VMEM((rows, width), jnp.bfloat16),
             pltpu.VMEM((MERGE, tokens, width), jnp.bfloat16),
-            pltpu.VMEM((rows, width), jnp.bfloat16),
             pltpu.VMEM((2, rows // 2, width), jnp.bfloat16),
-            pltpu.SemaphoreType.DMA((MERGE + 1,)),
+            pltpu.SemaphoreType.DMA((MERGE + 4,)),
         ],
         compiler_params=params(16),
-        cost_estimate=cost(2 * MERGE * rows * tokens * width, 2 * cotangent.size),
+        cost_estimate=cost(200 * MERGE * rows * tokens * width, 2 * cotangent.size),
         name="pick_rows",
     )(
-        me,
         in_hbm(window_owner),
         in_hbm(window_len),
         in_hbm(slot_token.reshape(1, tokens)),
@@ -217,22 +234,17 @@
 
 
 def attend_kernel(
-    me_ref, kept_ref, given_ref, gain_ref, w_hbm, *refs
+    kept_ref, given_ref, gain_ref, w_ref, *refs
 ):
     attended_ref, ordered_ref = refs[:2]
-    sent_refs = refs[2:-3]
-    sent, weights, sems = refs[-3:]
+    sent_refs = refs[2:-1]
+    sent = refs[-1]
     rows, width = ordered_ref.shape
     pairs = len(sent_refs)
     window_rows = rows // (2 * pairs)
     inner = attended_ref.shape[0]
-    me = me_ref[0]
+    me = lax.axis_index("enc")
     core = me % 2
-    copies = []
-    for part in range(3):
-        columns = w_hbm.at[:, pl.ds(part * inner, inner)]
-        copies.append(pltpu.make_async_copy(columns, weights.at[part], sems.at[part]))
-        copies[part].start()
     key_row = iota((rows, rows), 0)
     key_window = key_row // window_rows
     live = jnp.zeros((rows, rows), jnp.float32)
@@ -252,8 +264,8 @@
     normed = (values * lax.rsqrt(mean_square + 1e-06) * gain_ref[...][None, :]).astype(jnp.bfloat16)
     projected = []
     for part in range(3):
-        copies[part].wait()
-        projected.append(jnp.dot(normed, weights[part], preferred_element_type=jnp.float32))
+        columns = w_ref[:, part * inner : (part + 1) * inner]
+        projected.append(jnp.dot(normed, columns, preferred_element_type=jnp.float32))
     queries = projected[0].astype(jnp.bfloat16)
     keys_all = projected[1].astype(jnp.bfloat16)
     values_across = projected[2].T.astype(jnp.bfloat16)
@@ -281,7 +293,7 @@
         sent_refs[b][...] = sent[b]
 
 
-def attend_ordered(me, kept, given, gain, w_qkv, pairs):
+def attend_ordered(kept, given, gain, w_qkv, pairs):
     width = kept.shape[1]
     rows = 2 * (kept.shape[0] - SUBLANES)
     inner = w_qkv.shape[1] // 3
@@ -293,17 +305,15 @@
             jax.ShapeDtypeStruct((rows, width), jnp.bfloat16),
         )
         + (jax.ShapeDtypeStruct((heads, rows), jnp.bfloat16),) * pairs,
-        in_specs=[SMEM, VMEM, VMEM, VMEM, HBM],
+        in_specs=[VMEM] * 4,
         out_specs=(VMEM,) * (2 + pairs),
         scratch_shapes=[
             pltpu.VMEM((pairs, heads, rows), jnp.bfloat16),
-            pltpu.VMEM((3, width, inner), jnp.bfloat16),
-            pltpu.SemaphoreType.DMA((3,)),
         ],
         compiler_params=params(24),
         cost_estimate=cost(2 * rows * width * 3 * inner, 2 * w_qkv.size),
         name="attend",
-    )(me, kept, given, in_hbm(gain), in_hbm(w_qkv))
+    )(kept, given, in_hbm(gain), in_vmem(w_qkv))
 
 
 def project_kernel(attended_ref, ordered_ref, w_ref, *encoded_refs):
@@ -329,7 +339,7 @@
     )(attended, ordered, w_out)
 
 
-def gradient_kernel(scale, pairs, me_ref, *refs):
+def gradient_kernel(scale, pairs, *refs):
     columns, blocks = refs[:pairs], refs[pairs : 2 * pairs]
     kept_ref, given_ref = refs[2 * pairs :]
     size = blocks[0].shape[0] // pairs
@@ -344,12 +354,12 @@
         0,
     )
     total = jnp.dot(left, right, preferred_element_type=jnp.float32) * scale
-    first = me_ref[0] % 2 == 0
+    first = lax.axis_index("enc") % 2 == 0
     kept_ref[...] = jnp.where(first, total[:head], total[head:])
     given_ref[...] = jnp.where(first, total[head:], total[:head]).astype(jnp.bfloat16)
 
 
-def gradient_rows(me, columns, blocks, scale):
+def gradient_rows(columns, blocks, scale):
     pairs = len(blocks)
     heads, rows = columns[0].shape
     width = blocks[0].shape[1]
@@ -359,41 +369,69 @@
             jax.ShapeDtypeStruct((heads // 2, width), jnp.float32),
             jax.ShapeDtypeStruct((heads // 2, width), jnp.bfloat16),
         ),
-        in_specs=[SMEM] + [VMEM] * (2 * pairs),
+        in_specs=[VMEM] * (2 * pairs),
         out_specs=(VMEM, VMEM),
         compiler_params=params(24),
         cost_estimate=cost(2 * heads * rows * pairs * width, 2 * pairs * rows * width),
         name="gradient_rows",
-    )(me, *columns, *blocks)
-
-
-def place_kernel(me_ref, slots_ref, *refs):
+    )(*columns, *blocks)
+
+
+def place_kernel(slots_ref, *refs):
     embeddings_ref = refs[-1]
     arrived = jnp.concatenate([ref[...] for ref in refs[:-1]], 0)
     rows, width = arrived.shape
     tokens = embeddings_ref.shape[0]
     row = iota((rows, tokens), 0)
     window_rows = rows // (2 * (len(refs) - 1))
-    holds = slots_ref[...] == slot_of_row(row, me_ref[0], window_rows)
+    holds = slots_ref[...] == slot_of_row(row, lax.axis_index("enc"), window_rows)
     for j in range(MERGE):
         put = jnp.where(holds & (row % MERGE == j), 1.0, 0.0).astype(jnp.bfloat16)
         part = lax.dot_general(put, arrived, TRANSPOSED, preferred_element_type=jnp.float32)
         embeddings_ref[:, j * width : (j + 1) * width] = part.astype(jnp.bfloat16)
 
 
-def place_rows(me, slot_token, arrived):
+def place_rows(slot_token, arrived):
     size, width = arrived[0].shape
     rows = size * len(arrived)
     tokens = slot_token.shape[0]
     return pl.pallas_call(
         place_kernel,
         out_shape=jax.ShapeDtypeStruct((tokens, MERGE * width), jnp.bfloat16),
-        in_specs=[SMEM, VMEM] + [VMEM] * len(arrived),
+        in_specs=[VMEM] * (1 + len(arrived)),
         out_specs=VMEM,
         compiler_params=params(16),
         cost_estimate=cost(2 * MERGE * rows * tokens * width, 2 * MERGE * tokens * width),
         name="place_rows",
-    )(me, slot_token.reshape(1, tokens), *arrived)
+    )(slot_token.reshape(1, tokens), *arrived)
+
+
+def add_kernel(split, *refs):
+    ins = len(refs) - (2 if split else 1)
+    sums = [
+        refs[i][...].astype(jnp.float32) + refs[i + 1][...].astype(jnp.float32)
+        for i in range(0, ins, 2)
+    ]
+    outs = refs[ins:]
+    whole = sums[0] if len(sums) == 1 else jnp.concatenate(sums, 1)
+    width = outs[0].shape[1]
+    for i, ref in enumerate(outs):
+        ref[...] = whole[:, i * width : (i + 1) * width].astype(ref.dtype)
+
+
+def add_halves(terms, kind, split):
+    rows = terms[0][0].shape[0]
+    width = sum(pair[0].shape[1] for pair in terms)
+    count = 2 if split else 1
+    return pl.pallas_call(
+        functools.partial(add_kernel, split),
+        out_shape=(jax.ShapeDtypeStruct((rows, width // count), kind),) * count,
+        in_specs=[VMEM] * (2 * len(terms)),
+        out_specs=(VMEM,) * count,
+        compiler_params=params(8),
+        cost_estimate=cost(rows * width, 8 * rows * width),
+        name="add_halves",
+    )(*[value for pair in terms for value in pair])
 
 
 def after(value, other):
@@ -415,27 +453,30 @@
     replicas = lax.axis_size("rep")
     pairs = group // 2
     rows = pixels.shape[0]
-    me = lax.axis_index("enc").astype(jnp.int32).reshape(1)
-
-    held, kept, given = pick_rows(me, window_owner, window_len, slot_token, pixels, cotangent)
+
+    held, kept, given = pick_rows(window_owner, window_len, slot_token, pixels, cotangent)
     given = swap(given, "enc", 1)
-    blocks = [held, chip_swap(held, 1), chip_swap(held, 2)]
-    attended, ordered, *sent = attend_ordered(me, kept, given, gain, w_qkv, pairs)
-    blocks.append(chip_swap(after(blocks[1], attended), 2))
+    blocks = [held] + [chip_swap(held, b) for b in range(1, pairs)]
+    attended, ordered, *sent = attend_ordered(kept, given, gain, w_qkv, pairs)
     columns = [sent[0]] + [chip_swap(sent[b], b) for b in range(1, pairs)]
     encoded = project_ordered(attended, ordered, w_out, pairs)
     scale = 1.0 / math.sqrt(rows * group * replicas)
-    mine, other = gradient_rows(me, columns, blocks, scale)
-    part = (mine + swap(other, "enc", 1).astype(jnp.float32)).astype(jnp.bfloat16)
+    mine, other = gradient_rows(columns, blocks, scale)
+    halves = add_halves([(mine, swap(other, "enc", 1))], jnp.bfloat16, split=True)
     arrived = [encoded[0]]
     for b in range(1, pairs):
-        arrived.append(chip_swap(after(encoded[b], part), b))
-    bit = 1
-    while bit < replicas:
-        total = part.astype(jnp.float32) + swap(part, "rep", bit).astype(jnp.float32)
-        part = total.astype(jnp.bfloat16)
-        bit *= 2
-    embeddings = place_rows(me, slot_token, arrived)
+        arrived.append(chip_swap(after(encoded[b], halves[0]), b))
+    bits = [1 << i for i in range(replicas.bit_length() - 1)]
+    for first, last in zip(bits, bits[::-1]):
+        done = first == bits[-1]
+        if done:
+            halves = [after(half, arrived) for half in halves]
+        swapped = [swap(halves[0], "rep", first), swap(halves[1], "rep", last)]
+        halves = add_halves(
+            list(zip(halves, swapped)), jnp.float32 if done else jnp.bfloat16, split=not done
+        )
+    total = halves[0]
+    embeddings = place_rows(slot_token, arrived)
     return (embeddings, total)
 
 
@@ -443,7 +484,7 @@
     def shards(*args):
         group = mesh.shape["enc"]
         replicas = mesh.shape["rep"]
-        square = group == 2 << PAIR_BITS and replicas & (replicas - 1) == 0
+        square = group == 2 << PAIR_BITS and replicas & (replicas - 1) == 0 and replicas > 1
         whole = square and args[1].shape[0] == group
         return (xor_slice if whole else any_slice)(*args)
 

time: 47.2 us -> 49.8 us (1.055)
  waiting for transfers between devices: 17.2 us -> 22 us
  Pallas kernels: 10.3 us -> 8.83 us
  other arithmetic: 0.88 us -> 0.01 us
    ppermute x9, waiting for transfers between devices: 10.2 us -> 16.9 us  [chip_swap(): lax.ppermute(value, 'enc', [(i, i ^ 2 * turn(relative, i % 2)) for i in r...]
    pallas_call x1, Pallas kernels: 5 us -> 3.04 us  [attend_ordered(): pl.pallas_call(attend_kernel, out_shape=(jax.ShapeDtypeStruct((inner, row...]
    ppermute x4 -> x6, waiting for transfers between devices: 6.98 us -> 5.08 us  [swap(): return lax.ppermute(value, axis, [(i, i ^ bits) for i in range(size)])]
    ppermute x4 -> x6, starting transfers between devices: 4.4 us -> 5.46 us  [swap(): return lax.ppermute(value, axis, [(i, i ^ bits) for i in range(size)])]
    ppermute x9, starting transfers between devices: 13.6 us -> 12.6 us  [chip_swap(): lax.ppermute(value, 'enc', [(i, i ^ 2 * turn(relative, i % 2)) for i in r...]
    pallas_call x0 -> x3, Pallas kernels: none -> 0.9 us  [add_halves(): pl.pallas_call(functools.partial(add_kernel, split), out_shape=(jax.Shape...]
    add x1 -> x0, other arithmetic: 0.8 us -> none  [xor_slice(): part.astype(jnp.float32) + swap(part, 'rep', bit).astype(jnp.float32)]
  transfers between devices with their start and end apart: 13 -> 15, of which waited for: 9 -> 9; matrix products, arithmetic and copies ran while one was open for 0% -> 0% of each run, Pallas kernels for 15% -> 11%
where the time goes in v4:
time: 49.8 us; the launch traced here: 49.7 us
  waiting for transfers between devices  22 us (44%)
  starting transfers between devices  18.1 us (36%)
  Pallas kernels  8.83 us (18%)
  between operations  0.74 us (1%)
    ppermute x9, waiting for transfers between devices, chip_swap(): lax.ppermute(value, 'enc', [(i, i ^ 2 * turn(relative, i % 2)) for i in r...  16.9 us
    ppermute x9, starting transfers between devices, chip_swap(): lax.ppermute(value, 'enc', [(i, i ^ 2 * turn(relative, i % 2)) for i in r...  12.6 us
    ppermute x6, starting transfers between devices, swap(): return lax.ppermute(value, axis, [(i, i ^ bits) for i in range(size)])  5.46 us
    ppermute x6, waiting for transfers between devices, swap(): return lax.ppermute(value, axis, [(i, i ^ bits) for i in range(size)])  5.08 us
    pallas_call x1, Pallas kernels, attend_ordered(): pl.pallas_call(attend_kernel, out_shape=(jax.ShapeDtypeStruct((inner, row...  3.04 us
    pallas_call x1, Pallas kernels, pick_rows(): pl.pallas_call(pick_kernel, out_shape=(jax.ShapeDtypeStruct((rows, width)...  2.2 us
    pallas_call x1, Pallas kernels, place_rows(): pl.pallas_call(place_kernel, out_shape=jax.ShapeDtypeStruct((tokens, MERG...  1.83 us
  transfers between devices with their start and end apart: 15, of which 9 were waited for; matrix products, arithmetic and copies ran while one was open for 0% of the time, Pallas kernels for 11%

profile of v4, /device:TPU:0, one launch (start us, length us, event | category | flops | bytes accessed | tf_op | source)
XLA Modules:
  0.0 49.7 jit_solution(15844829498959421980)
XLA Ops:
  0.6 0.0 slice-start
  0.6 0.0 slice-start.1
  0.7 2.2 %pick_rows.1 = (bf16[128,1280]{1,0:T(8,128)(2,1)S(1)}, bf16[80,1280]{1,0:T(8,128)(2,1)S(1)}, bf16[80,1280]{1,0:T(8,128)(2,1)S(1)}) custom-call(s32[8]{0:T(128)} %owner_hbm.1, s32[8]{0:T(128)} %len_hbm.1, s32[1,160]{1,0:T(1,128)} %bitcast.3, bf16[128,1280]{1,0:T(8,128)(2,1)} %pixels_hbm.1, bf16[160,5120]{1,0:T(8,128)(2,1)} %cotangent_hbm.1), custom_call_target="tpu_custom_call" | custom-call | flops 20971520000 | bytes 1638400 | tf_op jit(solution)/shard_map/pick_rows/pallas_call | solution.py:210
  2.9 0.5 %collective-permute-start = (bf16[80,1280]{1,0:T(8,128)(2,1)S(1)}, bf16[80,1280]{1,0:T(8,128)(2,1)S(1)}, u32[]{:S(2)}, u32[]{:S(2)}) collective-permute-start(bf16[80,1280]{1,0:T(8,128)(2,1)S(1)} %get-tuple-element.27), channel_id=1, source_target_pairs={{0,4},{4,0},{8,12},{12,8},{16,20},{20,16},{24,28},{28,24},{1,5},{5... | collective-permute-start | bytes 614408 | tf_op jit(solution)/shard_map/ppermute | solution.py:443
  3.4 3.5 %collective-permute-start.6 = (bf16[128,1280]{1,0:T(8,128)(2,1)S(1)}, bf16[128,1280]{1,0:T(8,128)(2,1)S(1)}, u32[]{:S(2)}, u32[]{:S(2)}) collective-permute-start(bf16[128,1280]{1,0:T(8,128)(2,1)S(1)} %get-tuple-element.36.refs_4_), channel_id=1, source_target_pairs={{0,24},{4,28},{8,16},{12,20},{16,8},{20,12},{24,0},{28,4},{1,25},{... | collective-permute-start | bytes 983048 | tf_op jit(solution)/shard_map/ppermute | solution.py:448
  6.9 0.5 %collective-permute-start.5 = (bf16[128,1280]{1,0:T(8,128)(2,1)S(1)}, bf16[128,1280]{1,0:T(8,128)(2,1)S(1)}, u32[]{:S(2)}, u32[]{:S(2)}) collective-permute-start(bf16[128,1280]{1,0:T(8,128)(2,1)S(1)} %get-tuple-element.36.refs_4_), channel_id=1, source_target_pairs={{0,16},{4,12},{8,24},{12,4},{16,0},{20,28},{24,8},{28,20},{1,17},{... | collective-permute-start | bytes 983048 | tf_op jit(solution)/shard_map/ppermute | solution.py:448
  7.4 0.1 collective-permute-start.4
  7.5 0.0 collective-permute-done.given_ref
  7.5 0.0 slice-done
  7.5 0.0 slice-done.1
  7.6 3.0 %attend.1 = (bf16[640,128]{1,0:T(8,128)(2,1)S(1)}, bf16[128,1280]{1,0:T(8,128)(2,1)S(1)}, bf16[160,128]{1,0:T(8,128)(2,1)S(1)}, bf16[160,128]{1,0:T(8,128)(2,1)S...) custom-call(bf16[80,1280]{1,0:T(8,128)(2,1)S(1)} %get-tuple-element.26.kept_ref, ...), custom_call_target="tpu_custom_call" | custom-call | flops 629145600 | bytes 4915200 | tf_op jit(solution)/shard_map/attend/pallas_call | solution.py:301
  10.6 0.0 copy-start
  10.6 1.9 %collective-permute-start.1 = (bf16[160,128]{1,0:T(8,128)(2,1)S(1)}, bf16[160,128]{1,0:T(8,128)(2,1)S(1)}, u32[]{:S(2)}, u32[]{:S(2)}) collective-permute-start(bf16[160,128]{1,0:T(8,128)(2,1)S(1)} %get-tuple-element.33), channel_id=1, source_target_pairs={{0,8},{4,20},{8,0},{12,28},{16,24},{20,4},{24,16},{28,12},{1,9},{5... | collective-permute-start | bytes 122888 | tf_op jit(solution)/shard_map/ppermute | solution.py:448
  12.6 1.5 %collective-permute-start.2 = (bf16[160,128]{1,0:T(8,128)(2,1)S(1)}, bf16[160,128]{1,0:T(8,128)(2,1)S(1)}, u32[]{:S(2)}, u32[]{:S(2)}) collective-permute-start(bf16[160,128]{1,0:T(8,128)(2,1)S(1)} %get-tuple-element.34), channel_id=1, source_target_pairs={{0,16},{4,12},{8,24},{12,4},{16,0},{20,28},{24,8},{28,20},{1,17},{... | collective-permute-start | bytes 122888 | tf_op jit(solution)/shard_map/ppermute | solution.py:448
  14.1 9.3 %collective-permute-done.1.refs_1_ = bf16[160,128]{1,0:T(8,128)(2,1)S(1)} collective-permute-done((bf16[160,128]{1,0:T(8,128)(2,1)S(1)}, bf16[160,128]{1,0:T(8,128)(2,1)S(1)}, u32[]{:S(2)}, u32[]{:S(2)}) %collective-permute-start.1) | collective-permute-done | bytes 40992 | tf_op jit(solution)/shard_map/ppermute | solution.py:448
  23.4 1.4 %collective-permute-start.3 = (bf16[160,128]{1,0:T(8,128)(2,1)S(1)}, bf16[160,128]{1,0:T(8,128)(2,1)S(1)}, u32[]{:S(2)}, u32[]{:S(2)}) collective-permute-start(bf16[160,128]{1,0:T(8,128)(2,1)S(1)} %get-tuple-element.35), channel_id=1, source_target_pairs={{0,24},{4,28},{8,16},{12,20},{16,8},{20,12},{24,0},{28,4},{1,25},{... | collective-permute-start | bytes 122888 | tf_op jit(solution)/shard_map/ppermute | solution.py:448
  24.8 0.0 collective-permute-done.2.refs_2_
  24.8 3.5 %collective-permute-done.3.refs_3_ = bf16[160,128]{1,0:T(8,128)(2,1)S(1)} collective-permute-done((bf16[160,128]{1,0:T(8,128)(2,1)S(1)}, bf16[160,128]{1,0:T(8,128)(2,1)S(1)}, u32[]{:S(2)}, u32[]{:S(2)}) %collective-permute-start.3) | collective-permute-done | bytes 40992 | tf_op jit(solution)/shard_map/ppermute | solution.py:448
  28.3 0.0 collective-permute-done.6.refs_7_
  28.3 0.0 collective-permute-done.5.refs_6_
  28.3 0.0 collective-permute-done.4.refs_5_
  28.3 0.4 gradient_rows.1
  28.7 0.0 copy-start.1
  28.7 0.1 collective-permute-start.7
  28.8 1.4 %collective-permute-done.7.refs_1_ = bf16[80,1280]{1,0:T(8,128)(2,1)S(1)} collective-permute-done((bf16[80,1280]{1,0:T(8,128)(2,1)S(1)}, bf16[80,1280]{1,0:T(8,128)(2,1)S(1)}, u32[]{:S(2)}, u32[]{:S(2)}) %collective-permute-start.7) | collective-permute-done | bytes 204832 | tf_op jit(solution)/shard_map/ppermute | solution.py:443
  30.3 2.7 %collective-permute-start.12 = (bf16[80,640]{1,0:T(8,128)(2,1)S(1)}, bf16[80,640]{1,0:T(8,128)(2,1)S(1)}, u32[]{:S(2)}, u32[]{:S(2)}) collective-permute-start(bf16[80,640]{1,0:T(8,128)(2,1)S(1)} %get-tuple-element.45.refs_2_), channel_id=1, source_target_pairs={{0,2},{1,3},{2,0},{3,1},{4,6},{5,7},{6,4},{7,5},{8,10},{9,11},{10,... | collective-permute-start | bytes 307208 | tf_op jit(solution)/shard_map/ppermute | solution.py:443
  33.0 1.6 %collective-permute-start.11 = (bf16[80,640]{1,0:T(8,128)(2,1)S(1)}, bf16[80,640]{1,0:T(8,128)(2,1)S(1)}, u32[]{:S(2)}, u32[]{:S(2)}) collective-permute-start(bf16[80,640]{1,0:T(8,128)(2,1)S(1)} %get-tuple-element.39.refs_0_), channel_id=1, source_target_pairs={{0,1},{1,0},{2,3},{3,2},{4,5},{5,4},{6,7},{7,6},{8,9},{9,8},{10,11... | collective-permute-start | bytes 307208 | tf_op jit(solution)/shard_map/ppermute | solution.py:443
  34.5 0.0 copy-done
  34.5 0.5 project.1
  35.0 1.5 %collective-permute-start.8 = (bf16[32,1280]{1,0:T(8,128)(2,1)S(1)}, bf16[32,1280]{1,0:T(8,128)(2,1)S(1)}, u32[]{:S(2)}, u32[]{:S(2)}) collective-permute-start(bf16[32,1280]{1,0:T(8,128)(2,1)S(1)} %get-tuple-element.40), channel_id=1, source_target_pairs={{0,8},{4,20},{8,0},{12,28},{16,24},{20,4},{24,16},{28,12},{1,9},{5... | collective-permute-start | bytes 245768 | tf_op jit(solution)/shard_map/ppermute | solution.py:448
  36.6 1.0 %collective-permute-start.9 = (bf16[32,1280]{1,0:T(8,128)(2,1)S(1)}, bf16[32,1280]{1,0:T(8,128)(2,1)S(1)}, u32[]{:S(2)}, u32[]{:S(2)}) collective-permute-start(bf16[32,1280]{1,0:T(8,128)(2,1)S(1)} %get-tuple-element.42), channel_id=1, source_target_pairs={{0,16},{4,12},{8,24},{12,4},{16,0},{20,28},{24,8},{28,20},{1,17},{... | collective-permute-start | bytes 245768 | tf_op jit(solution)/shard_map/ppermute | solution.py:448
  37.5 1.0 %collective-permute-start.10 = (bf16[32,1280]{1,0:T(8,128)(2,1)S(1)}, bf16[32,1280]{1,0:T(8,128)(2,1)S(1)}, u32[]{:S(2)}, u32[]{:S(2)}) collective-permute-start(bf16[32,1280]{1,0:T(8,128)(2,1)S(1)} %get-tuple-element.44), channel_id=1, source_target_pairs={{0,24},{4,28},{8,16},{12,20},{16,8},{20,12},{24,0},{28,4},{1,25},{... | collective-permute-start | bytes 245768 | tf_op jit(solution)/shard_map/ppermute | solution.py:448
  38.6 0.0 collective-permute-done.12.refs_3_
  38.6 0.1 collective-permute-done.11.refs_1_
  38.7 0.1 add_halves.4
  38.8 0.9 %collective-permute-done.8.refs_1_ = bf16[32,1280]{1,0:T(8,128)(2,1)S(1)} collective-permute-done((bf16[32,1280]{1,0:T(8,128)(2,1)S(1)}, bf16[32,1280]{1,0:T(8,128)(2,1)S(1)}, u32[]{:S(2)}, u32[]{:S(2)}) %collective-permute-start.8) | collective-permute-done | bytes 81952 | tf_op jit(solution)/shard_map/ppermute | solution.py:448
  39.7 2.2 %collective-permute-done.9.refs_2_ = bf16[32,1280]{1,0:T(8,128)(2,1)S(1)} collective-permute-done((bf16[32,1280]{1,0:T(8,128)(2,1)S(1)}, bf16[32,1280]{1,0:T(8,128)(2,1)S(1)}, u32[]{:S(2)}, u32[]{:S(2)}) %collective-permute-start.9) | collective-permute-done | bytes 81952 | tf_op jit(solution)/shard_map/ppermute | solution.py:448
  41.8 1.0 %collective-permute-done.10.refs_3_ = bf16[32,1280]{1,0:T(8,128)(2,1)S(1)} collective-permute-done((bf16[32,1280]{1,0:T(8,128)(2,1)S(1)}, bf16[32,1280]{1,0:T(8,128)(2,1)S(1)}, u32[]{:S(2)}, u32[]{:S(2)}) %collective-permute-start.10) | collective-permute-done | bytes 81952 | tf_op jit(solution)/shard_map/ppermute | solution.py:448
  42.9 0.4 collective-permute-start.14
  43.3 0.2 collective-permute-start.13
  43.5 0.0 copy-done.1
  43.5 1.8 %place_rows.1 = bf16[160,5120]{1,0:T(8,128)(2,1)} custom-call(s32[1,160]{1,0:T(1,128)S(1)} %bitcast.4, bf16[32,1280]{1,0:T(8,128)(2,1)S(1)} %get-tuple-element.30.refs_0_, bf16[32,1280]{1,0:T(8,128)(2,1)S(1)} %collective-permute-done.8.refs_1_, bf16[32,1280]{1,0:T(8,128)(2,1)S(1)} %collective-permute-done.9.refs_2_, ...), custom_call_target="tpu_custom_call" | custom-call | flops 209715200 | bytes 1638400 | tf_op jit(solution)/shard_map/place_rows/pallas_call | solution.py:398
  45.4 2.2 %collective-permute-done.14.refs_3_ = bf16[80,640]{1,0:T(8,128)(2,1)S(1)} collective-permute-done((bf16[80,640]{1,0:T(8,128)(2,1)S(1)}, bf16[80,640]{1,0:T(8,128)(2,1)S(1)}, u32[]{:S(2)}, u32[]{:S(2)}) %collective-permute-start.14) | collective-permute-done | bytes 102432 | tf_op jit(solution)/shard_map/ppermute | solution.py:443
  47.5 1.3 %collective-permute-done.13.refs_1_ = bf16[80,640]{1,0:T(8,128)(2,1)S(1)} collective-permute-done((bf16[80,640]{1,0:T(8,128)(2,1)S(1)}, bf16[80,640]{1,0:T(8,128)(2,1)S(1)}, u32[]{:S(2)}, u32[]{:S(2)}) %collective-permute-start.13) | collective-permute-done | bytes 102432 | tf_op jit(solution)/shard_map/ppermute | solution.py:443
  48.9 0.8 %add_halves.5 = f32[80,1280]{1,0:T(8,128)} custom-call(bf16[80,640]{1,0:T(8,128)(2,1)S(1)} %get-tuple-element.47.refs_0_, bf16[80,640]{1,0:T(8,128)(2,1)S(1)} %collective-permute-done.13.refs_1_, bf16[80,640]{1,0:T(8,128)(2,1)S(1)} %get-tuple-element.49.refs_2_, bf16[80,640]{1,0:T(8,128)(2,1)S(1)} %collective-permute-done.14.refs_3_), custom_call_target="tpu_custom_call" | custom-call | flops 102400 | bytes 819200 | tf_op jit(solution)/shard_map/add_halves/pallas_call | solution.py:426
  (2 shorter events, 0.0 us)
Async XLA Ops:
  0.6 6.9 %slice-start = ((s8[4915200]{0:T(1024)(128)(4,1)}), s8[4194304]{0:T(1024)(128)(4,1)S(1)}, s32[]{:S(2)}) async-start(s8[4915200]{0:T(1024)(128)(4,1)} %bitcast.1), calls=%async_computation | async-start | bytes 8388608
  0.6 6.9 %slice-start.1 = ((s8[4915200]{0:T(1024)(128)(4,1)}), s8[720896]{0:T(1024)(128)(4,1)S(1)}, s32[]{:S(2)}) async-start(s8[4915200]{0:T(1024)(128)(4,1)} %bitcast.1), calls=%async_computation.1 | async-start | bytes 1441792
  2.9 4.7 %collective-permute-start = (bf16[80,1280]{1,0:T(8,128)(2,1)S(1)}, bf16[80,1280]{1,0:T(8,128)(2,1)S(1)}, u32[]{:S(2)}, u32[]{:S(2)}) collective-permute-start(bf16[80,1280]{1,0:T(8,128)(2,1)S(1)} %get-tuple-element.27), channel_id=1, source_target_pairs={{0,4},{4,0},{8,12},{12,8},{16,20},{20,16},{24,28},{28,24},{1,5},{5... | collective-permute-start | bytes 614408 | tf_op jit(solution)/shard_map/ppermute | solution.py:443
  3.4 24.9 %collective-permute-start.6 = (bf16[128,1280]{1,0:T(8,128)(2,1)S(1)}, bf16[128,1280]{1,0:T(8,128)(2,1)S(1)}, u32[]{:S(2)}, u32[]{:S(2)}) collective-permute-start(bf16[128,1280]{1,0:T(8,128)(2,1)S(1)} %get-tuple-element.36.refs_4_), channel_id=1, source_target_pairs={{0,24},{4,28},{8,16},{12,20},{16,8},{20,12},{24,0},{28,4},{1,25},{... | collective-permute-start | bytes 983048 | tf_op jit(solution)/shard_map/ppermute | solution.py:448
  6.9 21.4 %collective-permute-start.5 = (bf16[128,1280]{1,0:T(8,128)(2,1)S(1)}, bf16[128,1280]{1,0:T(8,128)(2,1)S(1)}, u32[]{:S(2)}, u32[]{:S(2)}) collective-permute-start(bf16[128,1280]{1,0:T(8,128)(2,1)S(1)} %get-tuple-element.36.refs_4_), channel_id=1, source_target_pairs={{0,16},{4,12},{8,24},{12,4},{16,0},{20,28},{24,8},{28,20},{1,17},{... | collective-permute-start | bytes 983048 | tf_op jit(solution)/shard_map/ppermute | solution.py:448
  7.4 20.9 %collective-permute-start.4 = (bf16[128,1280]{1,0:T(8,128)(2,1)S(1)}, bf16[128,1280]{1,0:T(8,128)(2,1)S(1)}, u32[]{:S(2)}, u32[]{:S(2)}) collective-permute-start(bf16[128,1280]{1,0:T(8,128)(2,1)S(1)} %get-tuple-element.36.refs_4_), channel_id=1, source_target_pairs={{0,8},{4,20},{8,0},{12,28},{16,24},{20,4},{24,16},{28,12},{1,9},{5... | collective-permute-start | bytes 983048 | tf_op jit(solution)/shard_map/ppermute | solution.py:448
  10.6 23.9 %copy-start = (bf16[640,1280]{1,0:T(8,128)(2,1)S(1)}, bf16[640,1280]{1,0:T(8,128)(2,1)}, u32[]{:S(2)}) copy-start(bf16[640,1280]{1,0:T(8,128)(2,1)} %w_ref.3) | copy-start | bytes 4915204
  10.6 12.8 %collective-permute-start.1 = (bf16[160,128]{1,0:T(8,128)(2,1)S(1)}, bf16[160,128]{1,0:T(8,128)(2,1)S(1)}, u32[]{:S(2)}, u32[]{:S(2)}) collective-permute-start(bf16[160,128]{1,0:T(8,128)(2,1)S(1)} %get-tuple-element.33), channel_id=1, source_target_pairs={{0,8},{4,20},{8,0},{12,28},{16,24},{20,4},{24,16},{28,12},{1,9},{5... | collective-permute-start | bytes 122888 | tf_op jit(solution)/shard_map/ppermute | solution.py:448
  12.6 12.3 %collective-permute-start.2 = (bf16[160,128]{1,0:T(8,128)(2,1)S(1)}, bf16[160,128]{1,0:T(8,128)(2,1)S(1)}, u32[]{:S(2)}, u32[]{:S(2)}) collective-permute-start(bf16[160,128]{1,0:T(8,128)(2,1)S(1)} %get-tuple-element.34), channel_id=1, source_target_pairs={{0,16},{4,12},{8,24},{12,4},{16,0},{20,28},{24,8},{28,20},{1,17},{... | collective-permute-start | bytes 122888 | tf_op jit(solution)/shard_map/ppermute | solution.py:448
  23.4 4.9 %collective-permute-start.3 = (bf16[160,128]{1,0:T(8,128)(2,1)S(1)}, bf16[160,128]{1,0:T(8,128)(2,1)S(1)}, u32[]{:S(2)}, u32[]{:S(2)}) collective-permute-start(bf16[160,128]{1,0:T(8,128)(2,1)S(1)} %get-tuple-element.35), channel_id=1, source_target_pairs={{0,24},{4,28},{8,16},{12,20},{16,8},{20,12},{24,0},{28,4},{1,25},{... | collective-permute-start | bytes 122888 | tf_op jit(solution)/shard_map/ppermute | solution.py:448
  28.7 14.8 %copy-start.1 = (s32[160]{0:T(256)S(1)}, s32[160]{0:T(256)}, u32[]{:S(2)}) copy-start(s32[160]{0:T(256)} %param.11) | copy-start | bytes 1924
  28.7 1.5 %collective-permute-start.7 = (bf16[80,1280]{1,0:T(8,128)(2,1)S(1)}, bf16[80,1280]{1,0:T(8,128)(2,1)S(1)}, u32[]{:S(2)}, u32[]{:S(2)}) collective-permute-start(bf16[80,1280]{1,0:T(8,128)(2,1)S(1)} %get-tuple-element.38), channel_id=1, source_target_pairs={{0,4},{4,0},{8,12},{12,8},{16,20},{20,16},{24,28},{28,24},{1,5},{5... | collective-permute-start | bytes 614408 | tf_op jit(solution)/shard_map/ppermute | solution.py:443
  30.3 8.3 %collective-permute-start.12 = (bf16[80,640]{1,0:T(8,128)(2,1)S(1)}, bf16[80,640]{1,0:T(8,128)(2,1)S(1)}, u32[]{:S(2)}, u32[]{:S(2)}) collective-permute-start(bf16[80,640]{1,0:T(8,128)(2,1)S(1)} %get-tuple-element.45.refs_2_), channel_id=1, source_target_pairs={{0,2},{1,3},{2,0},{3,1},{4,6},{5,7},{6,4},{7,5},{8,10},{9,11},{10,... | collective-permute-start | bytes 307208 | tf_op jit(solution)/shard_map/ppermute | solution.py:443
  33.0 5.7 %collective-permute-start.11 = (bf16[80,640]{1,0:T(8,128)(2,1)S(1)}, bf16[80,640]{1,0:T(8,128)(2,1)S(1)}, u32[]{:S(2)}, u32[]{:S(2)}) collective-permute-start(bf16[80,640]{1,0:T(8,128)(2,1)S(1)} %get-tuple-element.39.refs_0_), channel_id=1, source_target_pairs={{0,1},{1,0},{2,3},{3,2},{4,5},{5,4},{6,7},{7,6},{8,9},{9,8},{10,11... | collective-permute-start | bytes 307208 | tf_op jit(solution)/shard_map/ppermute | solution.py:443
  35.0 4.7 %collective-permute-start.8 = (bf16[32,1280]{1,0:T(8,128)(2,1)S(1)}, bf16[32,1280]{1,0:T(8,128)(2,1)S(1)}, u32[]{:S(2)}, u32[]{:S(2)}) collective-permute-start(bf16[32,1280]{1,0:T(8,128)(2,1)S(1)} %get-tuple-element.40), channel_id=1, source_target_pairs={{0,8},{4,20},{8,0},{12,28},{16,24},{20,4},{24,16},{28,12},{1,9},{5... | collective-permute-start | bytes 245768 | tf_op jit(solution)/shard_map/ppermute | solution.py:448
  36.6 5.3 %collective-permute-start.9 = (bf16[32,1280]{1,0:T(8,128)(2,1)S(1)}, bf16[32,1280]{1,0:T(8,128)(2,1)S(1)}, u32[]{:S(2)}, u32[]{:S(2)}) collective-permute-start(bf16[32,1280]{1,0:T(8,128)(2,1)S(1)} %get-tuple-element.42), channel_id=1, source_target_pairs={{0,16},{4,12},{8,24},{12,4},{16,0},{20,28},{24,8},{28,20},{1,17},{... | collective-permute-start | bytes 245768 | tf_op jit(solution)/shard_map/ppermute | solution.py:448
  37.5 5.3 %collective-permute-start.10 = (bf16[32,1280]{1,0:T(8,128)(2,1)S(1)}, bf16[32,1280]{1,0:T(8,128)(2,1)S(1)}, u32[]{:S(2)}, u32[]{:S(2)}) collective-permute-start(bf16[32,1280]{1,0:T(8,128)(2,1)S(1)} %get-tuple-element.44), channel_id=1, source_target_pairs={{0,24},{4,28},{8,16},{12,20},{16,8},{20,12},{24,0},{28,4},{1,25},{... | collective-permute-start | bytes 245768 | tf_op jit(solution)/shard_map/ppermute | solution.py:448
  42.9 4.7 %collective-permute-start.14 = (bf16[80,640]{1,0:T(8,128)(2,1)S(1)}, bf16[80,640]{1,0:T(8,128)(2,1)S(1)}, u32[]{:S(2)}, u32[]{:S(2)}) collective-permute-start(bf16[80,640]{1,0:T(8,128)(2,1)S(1)} %get-tuple-element.49.refs_2_), channel_id=1, source_target_pairs={{0,1},{1,0},{2,3},{3,2},{4,5},{5,4},{6,7},{7,6},{8,9},{9,8},{10,11... | collective-permute-start | bytes 307208 | tf_op jit(solution)/shard_map/ppermute | solution.py:443
  43.3 5.6 %collective-permute-start.13 = (bf16[80,640]{1,0:T(8,128)(2,1)S(1)}, bf16[80,640]{1,0:T(8,128)(2,1)S(1)}, u32[]{:S(2)}, u32[]{:S(2)}) collective-permute-start(bf16[80,640]{1,0:T(8,128)(2,1)S(1)} %get-tuple-element.47.refs_0_), channel_id=1, source_target_pairs={{0,2},{1,3},{2,0},{3,1},{4,6},{5,7},{6,4},{7,5},{8,10},{9,11},{10,... | collective-permute-start | bytes 307208 | tf_op jit(solution)/shard_map/ppermute | solution.py:443

commit v5 on v4

--- a/solution.py
+++ b/solution.py
@@ -104,6 +104,8 @@
 LANES = 128
 SUBLANES = 16
 PAIR_BITS = 2
+NEAR = 100
+PLACE = 200
 VMEM = pl.BlockSpec(memory_space=pltpu.VMEM)
 HBM = pl.BlockSpec(memory_space=pltpu.HBM)
 SMEM = pl.BlockSpec(memory_space=pltpu.SMEM)
@@ -339,42 +341,64 @@
     )(attended, ordered, w_out)
 
 
-def gradient_kernel(scale, pairs, *refs):
-    columns, blocks = refs[:pairs], refs[pairs : 2 * pairs]
-    kept_ref, given_ref = refs[2 * pairs :]
-    size = blocks[0].shape[0] // pairs
+def products(columns, blocks, offsets):
+    pairs = len(columns)
+    size = columns[0].shape[1] // pairs
+    left, right = [], []
+    for b in range(pairs):
+        for offset in offsets:
+            r = b ^ offset
+            left.append(columns[b][:, r * size : (r + 1) * size])
+            right.append(blocks[offsets.index(offset)][r * size : (r + 1) * size, :])
+    return jnp.dot(
+        jnp.concatenate(left, 1), jnp.concatenate(right, 0), preferred_element_type=jnp.float32
+    )
+
+
+def near_kernel(pairs, *refs):
+    columns, blocks = refs[:pairs], refs[pairs:-1]
+    refs[-1][...] = products(columns, blocks, list(range(pairs - 1)))
+
+
+def far_kernel(scale, pairs, *refs):
+    columns, block, near_ref = refs[:pairs], refs[pairs], refs[pairs + 1]
+    kept_ref, given_ref = refs[pairs + 2 :]
     head = kept_ref.shape[0]
-    left = jnp.concatenate([ref[...] for ref in columns], 1)
-    right = jnp.concatenate(
-        [
-            blocks[b ^ r][r * size : (r + 1) * size, :]
-            for b in range(pairs)
-            for r in range(pairs)
-        ],
-        0,
-    )
-    total = jnp.dot(left, right, preferred_element_type=jnp.float32) * scale
+    total = (near_ref[...] + products(columns, [block], [pairs - 1])) * scale
     first = lax.axis_index("enc") % 2 == 0
     kept_ref[...] = jnp.where(first, total[:head], total[head:])
     given_ref[...] = jnp.where(first, total[head:], total[:head]).astype(jnp.bfloat16)
 
 
-def gradient_rows(columns, blocks, scale):
-    pairs = len(blocks)
+def near_rows(columns, blocks):
     heads, rows = columns[0].shape
     width = blocks[0].shape[1]
     return pl.pallas_call(
-        functools.partial(gradient_kernel, scale, pairs),
+        functools.partial(near_kernel, len(columns)),
+        out_shape=jax.ShapeDtypeStruct((heads, width), jnp.float32),
+        in_specs=[VMEM] * (len(columns) + len(blocks)),
+        out_specs=VMEM,
+        compiler_params=params(24),
+        cost_estimate=cost(NEAR * heads * rows * len(blocks) * width, 2 * len(blocks) * rows * width),
+        name="near_rows",
+    )(*columns, *blocks)
+
+
+def far_rows(columns, block, near, scale):
+    heads, rows = columns[0].shape
+    width = block.shape[1]
+    return pl.pallas_call(
+        functools.partial(far_kernel, scale, len(columns)),
         out_shape=(
             jax.ShapeDtypeStruct((heads // 2, width), jnp.float32),
             jax.ShapeDtypeStruct((heads // 2, width), jnp.bfloat16),
         ),
-        in_specs=[VMEM] * (2 * pairs),
+        in_specs=[VMEM] * (len(columns) + 2),
         out_specs=(VMEM, VMEM),
         compiler_params=params(24),
-        cost_estimate=cost(2 * heads * rows * pairs * width, 2 * pairs * rows * width),
-        name="gradient_rows",
-    )(*columns, *blocks)
+        cost_estimate=cost(2 * heads * rows * width, 2 * rows * width),
+        name="far_rows",
+    )(*columns, block, near)
 
 
 def place_kernel(slots_ref, *refs):
@@ -401,7 +425,7 @@
         in_specs=[VMEM] * (1 + len(arrived)),
         out_specs=VMEM,
         compiler_params=params(16),
-        cost_estimate=cost(2 * MERGE * rows * tokens * width, 2 * MERGE * tokens * width),
+        cost_estimate=cost(PLACE * MERGE * rows * tokens * width, 2 * MERGE * tokens * width),
         name="place_rows",
     )(slot_token.reshape(1, tokens), *arrived)
 
@@ -456,12 +480,14 @@
 
     held, kept, given = pick_rows(window_owner, window_len, slot_token, pixels, cotangent)
     given = swap(given, "enc", 1)
-    blocks = [held] + [chip_swap(held, b) for b in range(1, pairs)]
+    blocks = [held, chip_swap(held, 1), chip_swap(held, 2)]
     attended, ordered, *sent = attend_ordered(kept, given, gain, w_qkv, pairs)
     columns = [sent[0]] + [chip_swap(sent[b], b) for b in range(1, pairs)]
     encoded = project_ordered(attended, ordered, w_out, pairs)
+    blocks.append(chip_swap(after(blocks[1], encoded), 2))
     scale = 1.0 / math.sqrt(rows * group * replicas)
-    mine, other = gradient_rows(columns, blocks, scale)
+    near = near_rows(columns, blocks[:-1])
+    mine, other = far_rows(columns, blocks[-1], near, scale)
     halves = add_halves([(mine, swap(other, "enc", 1))], jnp.bfloat16, split=True)
     arrived = [encoded[0]]
     for b in range(1, pairs):
@@ -469,8 +495,6 @@
     bits = [1 << i for i in range(replicas.bit_length() - 1)]
     for first, last in zip(bits, bits[::-1]):
         done = first == bits[-1]
-        if done:
-            halves = [after(half, arrived) for half in halves]
         swapped = [swap(halves[0], "rep", first), swap(halves[1], "rep", last)]
         halves = add_halves(
             list(zip(halves, swapped)), jnp.float32 if done else jnp.bfloat16, split=not done

time: 49.8 us -> 42.3 us (0.85)
  waiting for transfers between devices: 22 us -> 11.8 us
  starting transfers between devices: 18.1 us -> 20.2 us
    ppermute x9, waiting for transfers between devices: 16.9 us -> 6.14 us  [chip_swap(): lax.ppermute(value, 'enc', [(i, i ^ 2 * turn(relative, i % 2)) for i in r...]
    ppermute x6, starting transfers between devices: 5.46 us -> 8.1 us  [swap(): return lax.ppermute(value, axis, [(i, i ^ bits) for i in range(size)])]
    ppermute x6, waiting for transfers between devices: 5.08 us -> 5.63 us  [swap(): return lax.ppermute(value, axis, [(i, i ^ bits) for i in range(size)])]
  transfers between devices with their start and end apart: 15 -> 15, of which waited for: 9 -> 9; matrix products, arithmetic and copies ran while one was open for 0% -> 0% of each run, Pallas kernels for 11% -> 14%
where the time goes in v5:
time: 42.3 us; the launch traced here: 42.1 us
  starting transfers between devices  20.2 us (48%)
  waiting for transfers between devices  11.8 us (28%)
  Pallas kernels  9.29 us (22%)
  between operations  0.75 us (2%)
    ppermute x9, starting transfers between devices, chip_swap(): lax.ppermute(value, 'enc', [(i, i ^ 2 * turn(relative, i % 2)) for i in r...  12.1 us
    ppermute x6, starting transfers between devices, swap(): return lax.ppermute(value, axis, [(i, i ^ bits) for i in range(size)])  8.1 us
    ppermute x9, waiting for transfers between devices, chip_swap(): lax.ppermute(value, 'enc', [(i, i ^ 2 * turn(relative, i % 2)) for i in r...  6.14 us
    ppermute x6, waiting for transfers between devices, swap(): return lax.ppermute(value, axis, [(i, i ^ bits) for i in range(size)])  5.63 us
    pallas_call x1, Pallas kernels, attend_ordered(): pl.pallas_call(attend_kernel, out_shape=(jax.ShapeDtypeStruct((inner, row...  3.15 us
    pallas_call x1, Pallas kernels, pick_rows(): pl.pallas_call(pick_kernel, out_shape=(jax.ShapeDtypeStruct((rows, width)...  2.2 us
    pallas_call x1, Pallas kernels, place_rows(): pl.pallas_call(place_kernel, out_shape=jax.ShapeDtypeStruct((tokens, MERG...  1.83 us
    pallas_call x3, Pallas kernels, add_halves(): pl.pallas_call(functools.partial(add_kernel, split), out_shape=(jax.Shape...  0.89 us
  transfers between devices with their start and end apart: 15, of which 9 were waited for; matrix products, arithmetic and copies ran while one was open for 0% of the time, Pallas kernels for 14%

profile of v5, /device:TPU:0, one launch (start us, length us, event | category | flops | bytes accessed | tf_op | source)
XLA Modules:
  0.0 42.1 jit_solution(2290419521643197019)
XLA Ops:
  0.6 0.0 slice-start
  0.6 0.0 slice-start.1
  0.7 2.2 %pick_rows.1 = (bf16[128,1280]{1,0:T(8,128)(2,1)S(1)}, bf16[80,1280]{1,0:T(8,128)(2,1)S(1)}, bf16[80,1280]{1,0:T(8,128)(2,1)S(1)}) custom-call(s32[8]{0:T(128)} %owner_hbm.1, s32[8]{0:T(128)} %len_hbm.1, s32[1,160]{1,0:T(1,128)} %bitcast.3, bf16[128,1280]{1,0:T(8,128)(2,1)} %pixels_hbm.1, bf16[160,5120]{1,0:T(8,128)(2,1)} %cotangent_hbm.1), custom_call_target="tpu_custom_call" | custom-call | flops 20971520000 | bytes 1638400 | tf_op jit(solution)/shard_map/pick_rows/pallas_call | solution.py:212
  2.9 3.0 %collective-permute-start.4 = (bf16[128,1280]{1,0:T(8,128)(2,1)S(1)}, bf16[128,1280]{1,0:T(8,128)(2,1)S(1)}, u32[]{:S(2)}, u32[]{:S(2)}) collective-permute-start(bf16[128,1280]{1,0:T(8,128)(2,1)S(1)} %get-tuple-element.35.refs_4_), channel_id=1, source_target_pairs={{0,8},{4,20},{8,0},{12,28},{16,24},{20,4},{24,16},{28,12},{1,9},{5... | collective-permute-start | bytes 983048 | tf_op jit(solution)/shard_map/ppermute | solution.py:472
  5.9 1.5 %collective-permute-start.6 = (bf16[128,1280]{1,0:T(8,128)(2,1)S(1)}, bf16[128,1280]{1,0:T(8,128)(2,1)S(1)}, u32[]{:S(2)}, u32[]{:S(2)}) collective-permute-start(bf16[128,1280]{1,0:T(8,128)(2,1)S(1)} %get-tuple-element.35.refs_4_), channel_id=1, source_target_pairs={{0,16},{4,12},{8,24},{12,4},{16,0},{20,28},{24,8},{28,20},{1,17},{... | collective-permute-start | bytes 983048 | tf_op jit(solution)/shard_map/ppermute | solution.py:472
  7.4 0.0 collective-permute-start
  7.4 1.5 %collective-permute-done.given_ref = bf16[80,1280]{1,0:T(8,128)(2,1)S(1)} collective-permute-done((bf16[80,1280]{1,0:T(8,128)(2,1)S(1)}, bf16[80,1280]{1,0:T(8,128)(2,1)S(1)}, u32[]{:S(2)}, u32[]{:S(2)}) %collective-permute-start) | collective-permute-done | bytes 204832 | tf_op jit(solution)/shard_map/ppermute | solution.py:467
  8.8 0.0 slice-done
  8.8 0.0 slice-done.1
  8.8 0.0 copy-start
  8.8 3.2 %attend.1 = (bf16[640,128]{1,0:T(8,128)(2,1)S(1)}, bf16[128,1280]{1,0:T(8,128)(2,1)S(1)}, bf16[160,128]{1,0:T(8,128)(2,1)S(1)}, bf16[160,128]{1,0:T(8,128)(2,1)S...) custom-call(bf16[80,1280]{1,0:T(8,128)(2,1)S(1)} %get-tuple-element.25.kept_ref, ...), custom_call_target="tpu_custom_call" | custom-call | flops 629145600 | bytes 4915200 | tf_op jit(solution)/shard_map/attend/pallas_call | solution.py:303
  12.0 0.6 %collective-permute-start.1 = (bf16[160,128]{1,0:T(8,128)(2,1)S(1)}, bf16[160,128]{1,0:T(8,128)(2,1)S(1)}, u32[]{:S(2)}, u32[]{:S(2)}) collective-permute-start(bf16[160,128]{1,0:T(8,128)(2,1)S(1)} %get-tuple-element.32), channel_id=1, source_target_pairs={{0,8},{4,20},{8,0},{12,28},{16,24},{20,4},{24,16},{28,12},{1,9},{5... | collective-permute-start | bytes 122888 | tf_op jit(solution)/shard_map/ppermute | solution.py:472
  12.6 0.1 collective-permute-start.2
  12.7 2.9 %collective-permute-start.3 = (bf16[160,128]{1,0:T(8,128)(2,1)S(1)}, bf16[160,128]{1,0:T(8,128)(2,1)S(1)}, u32[]{:S(2)}, u32[]{:S(2)}) collective-permute-start(bf16[160,128]{1,0:T(8,128)(2,1)S(1)} %get-tuple-element.34), channel_id=1, source_target_pairs={{0,24},{4,28},{8,16},{12,20},{16,8},{20,12},{24,0},{28,4},{1,25},{... | collective-permute-start | bytes 122888 | tf_op jit(solution)/shard_map/ppermute | solution.py:472
  15.6 0.0 copy-done
  15.6 0.5 %project.1 = (bf16[32,1280]{1,0:T(8,128)(2,1)S(1)}, bf16[32,1280]{1,0:T(8,128)(2,1)S(1)}, bf16[32,1280]{1,0:T(8,128)(2,1)S(1)}, bf16[32,1280]{1,0:T(8,128)(2,1)S(1)}) custom-call(bf16[640,128]{1,0:T(8,128)(2,1)S(1)} %get-tuple-element.27.attended_ref, bf16[128,1280]{1,0:T(8,128)(2,1)S(1)} %get-tuple-element.28.ordered_ref, bf16[640,1280]{1,0:T(8,128)(2,1)S(1)} %copy-done), custom_call_target="tpu_custom_call" | custom-call | flops 209715200 | bytes 1638400 | tf_op jit(solution)/shard_map/project/pallas_call | solution.py:333
  16.0 0.0 collective-permute-done.4.refs_5_
  16.1 0.6 %collective-permute-start.5 = (bf16[128,1280]{1,0:T(8,128)(2,1)S(1)}, bf16[128,1280]{1,0:T(8,128)(2,1)S(1)}, u32[]{:S(2)}, u32[]{:S(2)}) collective-permute-start(bf16[128,1280]{1,0:T(8,128)(2,1)S(1)} %collective-permute-done.4.refs_5_), channel_id=1, source_target_pairs={{0,16},{4,12},{8,24},{12,4},{16,0},{20,28},{24,8},{28,20},{1,17},{... | collective-permute-start | bytes 983048 | tf_op jit(solution)/shard_map/ppermute | solution.py:472
  16.6 0.0 collective-permute-done.1.refs_1_
  16.6 0.4 %collective-permute-done.2.refs_2_ = bf16[160,128]{1,0:T(8,128)(2,1)S(1)} collective-permute-done((bf16[160,128]{1,0:T(8,128)(2,1)S(1)}, bf16[160,128]{1,0:T(8,128)(2,1)S(1)}, u32[]{:S(2)}, u32[]{:S(2)}) %collective-permute-start.2) | collective-permute-done | bytes 40992 | tf_op jit(solution)/shard_map/ppermute | solution.py:472
  17.1 0.5 %collective-permute-done.3.refs_3_ = bf16[160,128]{1,0:T(8,128)(2,1)S(1)} collective-permute-done((bf16[160,128]{1,0:T(8,128)(2,1)S(1)}, bf16[160,128]{1,0:T(8,128)(2,1)S(1)}, u32[]{:S(2)}, u32[]{:S(2)}) %collective-permute-start.3) | collective-permute-done | bytes 40992 | tf_op jit(solution)/shard_map/ppermute | solution.py:472
  17.6 0.0 collective-permute-done.6.refs_6_
  17.6 0.4 %near_rows.1.refs_5_ = f32[160,1280]{1,0:T(8,128)S(1)} custom-call(bf16[160,128]{1,0:T(8,128)(2,1)S(1)} %get-tuple-element.31.refs_0_, bf16[160,128]{1,0:T(8,128)(2,1)S(1)} %collective-permute-done.1.refs_1_, bf16[160,128]{1,0:T(8,128)(2,1)S(1)} %collective-permute-done.2.refs_2_, bf16[160,128]{1,0:T(8,128)(2,1)S(1)} %collective-permute-done.3.refs_3_, ...), custom_call_target="tpu_custom_call" | custom-call | flops 7864320000 | bytes 983040 | tf_op jit(solution)/shard_map/near_rows/pallas_call | solution.py:376
  18.0 0.0 copy-start.1
  18.0 5.2 %collective-permute-done.5.refs_4_ = bf16[128,1280]{1,0:T(8,128)(2,1)S(1)} collective-permute-done((bf16[128,1280]{1,0:T(8,128)(2,1)S(1)}, bf16[128,1280]{1,0:T(8,128)(2,1)S(1)}, u32[]{:S(2)}, u32[]{:S(2)}) %collective-permute-start.5) | collective-permute-done | bytes 327712 | tf_op jit(solution)/shard_map/ppermute | solution.py:472
  23.2 0.3 far_rows.1
  23.5 0.1 collective-permute-start.7
  23.6 1.4 %collective-permute-done.7.refs_1_ = bf16[80,1280]{1,0:T(8,128)(2,1)S(1)} collective-permute-done((bf16[80,1280]{1,0:T(8,128)(2,1)S(1)}, bf16[80,1280]{1,0:T(8,128)(2,1)S(1)}, u32[]{:S(2)}, u32[]{:S(2)}) %collective-permute-start.7) | collective-permute-done | bytes 204832 | tf_op jit(solution)/shard_map/ppermute | solution.py:467
  25.1 2.7 %collective-permute-start.12 = (bf16[80,640]{1,0:T(8,128)(2,1)S(1)}, bf16[80,640]{1,0:T(8,128)(2,1)S(1)}, u32[]{:S(2)}, u32[]{:S(2)}) collective-permute-start(bf16[80,640]{1,0:T(8,128)(2,1)S(1)} %get-tuple-element.45.refs_2_), channel_id=1, source_target_pairs={{0,2},{1,3},{2,0},{3,1},{4,6},{5,7},{6,4},{7,5},{8,10},{9,11},{10,... | collective-permute-start | bytes 307208 | tf_op jit(solution)/shard_map/ppermute | solution.py:467
  27.8 1.6 %collective-permute-start.11 = (bf16[80,640]{1,0:T(8,128)(2,1)S(1)}, bf16[80,640]{1,0:T(8,128)(2,1)S(1)}, u32[]{:S(2)}, u32[]{:S(2)}) collective-permute-start(bf16[80,640]{1,0:T(8,128)(2,1)S(1)} %get-tuple-element.41.refs_0_), channel_id=1, source_target_pairs={{0,1},{1,0},{2,3},{3,2},{4,5},{5,4},{6,7},{7,6},{8,9},{9,8},{10,11... | collective-permute-start | bytes 307208 | tf_op jit(solution)/shard_map/ppermute | solution.py:467
  29.3 0.5 %collective-permute-start.8 = (bf16[32,1280]{1,0:T(8,128)(2,1)S(1)}, bf16[32,1280]{1,0:T(8,128)(2,1)S(1)}, u32[]{:S(2)}, u32[]{:S(2)}) collective-permute-start(bf16[32,1280]{1,0:T(8,128)(2,1)S(1)} %get-tuple-element.42), channel_id=1, source_target_pairs={{0,8},{4,20},{8,0},{12,28},{16,24},{20,4},{24,16},{28,12},{1,9},{5... | collective-permute-start | bytes 245768 | tf_op jit(solution)/shard_map/ppermute | solution.py:472
  29.9 0.8 %collective-permute-start.9 = (bf16[32,1280]{1,0:T(8,128)(2,1)S(1)}, bf16[32,1280]{1,0:T(8,128)(2,1)S(1)}, u32[]{:S(2)}, u32[]{:S(2)}) collective-permute-start(bf16[32,1280]{1,0:T(8,128)(2,1)S(1)} %get-tuple-element.43), channel_id=1, source_target_pairs={{0,16},{4,12},{8,24},{12,4},{16,0},{20,28},{24,8},{28,20},{1,17},{... | collective-permute-start | bytes 245768 | tf_op jit(solution)/shard_map/ppermute | solution.py:472
  30.7 2.1 %collective-permute-start.10 = (bf16[32,1280]{1,0:T(8,128)(2,1)S(1)}, bf16[32,1280]{1,0:T(8,128)(2,1)S(1)}, u32[]{:S(2)}, u32[]{:S(2)}) collective-permute-start(bf16[32,1280]{1,0:T(8,128)(2,1)S(1)} %get-tuple-element.44), channel_id=1, source_target_pairs={{0,24},{4,28},{8,16},{12,20},{16,8},{20,12},{24,0},{28,4},{1,25},{... | collective-permute-start | bytes 245768 | tf_op jit(solution)/shard_map/ppermute | solution.py:472
  32.8 0.5 %collective-permute-done.12.refs_3_ = bf16[80,640]{1,0:T(8,128)(2,1)S(1)} collective-permute-done((bf16[80,640]{1,0:T(8,128)(2,1)S(1)}, bf16[80,640]{1,0:T(8,128)(2,1)S(1)}, u32[]{:S(2)}, u32[]{:S(2)}) %collective-permute-start.12) | collective-permute-done | bytes 102432 | tf_op jit(solution)/shard_map/ppermute | solution.py:467
  33.3 0.2 collective-permute-done.11.refs_1_
  33.5 0.1 add_halves.4
  33.6 1.3 %collective-permute-start.13 = (bf16[80,640]{1,0:T(8,128)(2,1)S(1)}, bf16[80,640]{1,0:T(8,128)(2,1)S(1)}, u32[]{:S(2)}, u32[]{:S(2)}) collective-permute-start(bf16[80,640]{1,0:T(8,128)(2,1)S(1)} %get-tuple-element.46.refs_0_), channel_id=1, source_target_pairs={{0,2},{1,3},{2,0},{3,1},{4,6},{5,7},{6,4},{7,5},{8,10},{9,11},{10,... | collective-permute-start | bytes 307208 | tf_op jit(solution)/shard_map/ppermute | solution.py:467
  34.9 2.5 %collective-permute-start.14 = (bf16[80,640]{1,0:T(8,128)(2,1)S(1)}, bf16[80,640]{1,0:T(8,128)(2,1)S(1)}, u32[]{:S(2)}, u32[]{:S(2)}) collective-permute-start(bf16[80,640]{1,0:T(8,128)(2,1)S(1)} %get-tuple-element.47.refs_2_), channel_id=1, source_target_pairs={{0,1},{1,0},{2,3},{3,2},{4,5},{5,4},{6,7},{7,6},{8,9},{9,8},{10,11... | collective-permute-start | bytes 307208 | tf_op jit(solution)/shard_map/ppermute | solution.py:467
  37.4 0.0 collective-permute-done.8.refs_1_
  37.4 0.0 collective-permute-done.9.refs_2_
  37.4 0.0 collective-permute-done.10.refs_3_
  37.4 0.0 copy-done.1
  37.4 1.8 %place_rows.1 = bf16[160,5120]{1,0:T(8,128)(2,1)} custom-call(s32[1,160]{1,0:T(1,128)S(1)} %bitcast.4, bf16[32,1280]{1,0:T(8,128)(2,1)S(1)} %get-tuple-element.29.refs_0_, bf16[32,1280]{1,0:T(8,128)(2,1)S(1)} %collective-permute-done.8.refs_1_, bf16[32,1280]{1,0:T(8,128)(2,1)S(1)} %collective-permute-done.9.refs_2_, ...), custom_call_target="tpu_custom_call" | custom-call | flops 20971520000 | bytes 1638400 | tf_op jit(solution)/shard_map/place_rows/pallas_call | solution.py:422
  39.2 1.6 %collective-permute-done.13.refs_1_ = bf16[80,640]{1,0:T(8,128)(2,1)S(1)} collective-permute-done((bf16[80,640]{1,0:T(8,128)(2,1)S(1)}, bf16[80,640]{1,0:T(8,128)(2,1)S(1)}, u32[]{:S(2)}, u32[]{:S(2)}) %collective-permute-start.13) | collective-permute-done | bytes 102432 | tf_op jit(solution)/shard_map/ppermute | solution.py:467
  40.8 0.4 %collective-permute-done.14.refs_3_ = bf16[80,640]{1,0:T(8,128)(2,1)S(1)} collective-permute-done((bf16[80,640]{1,0:T(8,128)(2,1)S(1)}, bf16[80,640]{1,0:T(8,128)(2,1)S(1)}, u32[]{:S(2)}, u32[]{:S(2)}) %collective-permute-start.14) | collective-permute-done | bytes 102432 | tf_op jit(solution)/shard_map/ppermute | solution.py:467
  41.3 0.8 %add_halves.5 = f32[80,1280]{1,0:T(8,128)} custom-call(bf16[80,640]{1,0:T(8,128)(2,1)S(1)} %get-tuple-element.46.refs_0_, bf16[80,640]{1,0:T(8,128)(2,1)S(1)} %collective-permute-done.13.refs_1_, bf16[80,640]{1,0:T(8,128)(2,1)S(1)} %get-tuple-element.47.refs_2_, bf16[80,640]{1,0:T(8,128)(2,1)S(1)} %collective-permute-done.14.refs_3_), custom_call_target="tpu_custom_call" | custom-call | flops 102400 | bytes 819200 | tf_op jit(solution)/shard_map/add_halves/pallas_call | solution.py:450
  (2 shorter events, 0.0 us)
Async XLA Ops:
  0.6 8.2 %slice-start = ((s8[4915200]{0:T(1024)(128)(4,1)}), s8[4194304]{0:T(1024)(128)(4,1)S(1)}, s32[]{:S(2)}) async-start(s8[4915200]{0:T(1024)(128)(4,1)} %bitcast.1), calls=%async_computation | async-start | bytes 8388608
  0.6 8.2 %slice-start.1 = ((s8[4915200]{0:T(1024)(128)(4,1)}), s8[720896]{0:T(1024)(128)(4,1)S(1)}, s32[]{:S(2)}) async-start(s8[4915200]{0:T(1024)(128)(4,1)} %bitcast.1), calls=%async_computation.1 | async-start | bytes 1441792
  2.9 13.2 %collective-permute-start.4 = (bf16[128,1280]{1,0:T(8,128)(2,1)S(1)}, bf16[128,1280]{1,0:T(8,128)(2,1)S(1)}, u32[]{:S(2)}, u32[]{:S(2)}) collective-permute-start(bf16[128,1280]{1,0:T(8,128)(2,1)S(1)} %get-tuple-element.35.refs_4_), channel_id=1, source_target_pairs={{0,8},{4,20},{8,0},{12,28},{16,24},{20,4},{24,16},{28,12},{1,9},{5... | collective-permute-start | bytes 983048 | tf_op jit(solution)/shard_map/ppermute | solution.py:472
  5.9 11.7 %collective-permute-start.6 = (bf16[128,1280]{1,0:T(8,128)(2,1)S(1)}, bf16[128,1280]{1,0:T(8,128)(2,1)S(1)}, u32[]{:S(2)}, u32[]{:S(2)}) collective-permute-start(bf16[128,1280]{1,0:T(8,128)(2,1)S(1)} %get-tuple-element.35.refs_4_), channel_id=1, source_target_pairs={{0,16},{4,12},{8,24},{12,4},{16,0},{20,28},{24,8},{28,20},{1,17},{... | collective-permute-start | bytes 983048 | tf_op jit(solution)/shard_map/ppermute | solution.py:472
  7.4 1.5 %collective-permute-start = (bf16[80,1280]{1,0:T(8,128)(2,1)S(1)}, bf16[80,1280]{1,0:T(8,128)(2,1)S(1)}, u32[]{:S(2)}, u32[]{:S(2)}) collective-permute-start(bf16[80,1280]{1,0:T(8,128)(2,1)S(1)} %get-tuple-element.26), channel_id=1, source_target_pairs={{0,4},{4,0},{8,12},{12,8},{16,20},{20,16},{24,28},{28,24},{1,5},{5... | collective-permute-start | bytes 614408 | tf_op jit(solution)/shard_map/ppermute | solution.py:467
  8.8 6.7 %copy-start = (bf16[640,1280]{1,0:T(8,128)(2,1)S(1)}, bf16[640,1280]{1,0:T(8,128)(2,1)}, u32[]{:S(2)}) copy-start(bf16[640,1280]{1,0:T(8,128)(2,1)} %w_ref.3) | copy-start | bytes 4915204
  12.0 4.6 %collective-permute-start.1 = (bf16[160,128]{1,0:T(8,128)(2,1)S(1)}, bf16[160,128]{1,0:T(8,128)(2,1)S(1)}, u32[]{:S(2)}, u32[]{:S(2)}) collective-permute-start(bf16[160,128]{1,0:T(8,128)(2,1)S(1)} %get-tuple-element.32), channel_id=1, source_target_pairs={{0,8},{4,20},{8,0},{12,28},{16,24},{20,4},{24,16},{28,12},{1,9},{5... | collective-permute-start | bytes 122888 | tf_op jit(solution)/shard_map/ppermute | solution.py:472
  12.6 4.4 %collective-permute-start.2 = (bf16[160,128]{1,0:T(8,128)(2,1)S(1)}, bf16[160,128]{1,0:T(8,128)(2,1)S(1)}, u32[]{:S(2)}, u32[]{:S(2)}) collective-permute-start(bf16[160,128]{1,0:T(8,128)(2,1)S(1)} %get-tuple-element.33), channel_id=1, source_target_pairs={{0,16},{4,12},{8,24},{12,4},{16,0},{20,28},{24,8},{28,20},{1,17},{... | collective-permute-start | bytes 122888 | tf_op jit(solution)/shard_map/ppermute | solution.py:472
  12.7 4.9 %collective-permute-start.3 = (bf16[160,128]{1,0:T(8,128)(2,1)S(1)}, bf16[160,128]{1,0:T(8,128)(2,1)S(1)}, u32[]{:S(2)}, u32[]{:S(2)}) collective-permute-start(bf16[160,128]{1,0:T(8,128)(2,1)S(1)} %get-tuple-element.34), channel_id=1, source_target_pairs={{0,24},{4,28},{8,16},{12,20},{16,8},{20,12},{24,0},{28,4},{1,25},{... | collective-permute-start | bytes 122888 | tf_op jit(solution)/shard_map/ppermute | solution.py:472
  16.1 7.1 %collective-permute-start.5 = (bf16[128,1280]{1,0:T(8,128)(2,1)S(1)}, bf16[128,1280]{1,0:T(8,128)(2,1)S(1)}, u32[]{:S(2)}, u32[]{:S(2)}) collective-permute-start(bf16[128,1280]{1,0:T(8,128)(2,1)S(1)} %collective-permute-done.4.refs_5_), channel_id=1, source_target_pairs={{0,16},{4,12},{8,24},{12,4},{16,0},{20,28},{24,8},{28,20},{1,17},{... | collective-permute-start | bytes 983048 | tf_op jit(solution)/shard_map/ppermute | solution.py:472
  18.0 19.4 %copy-start.1 = (s32[160]{0:T(256)S(1)}, s32[160]{0:T(256)}, u32[]{:S(2)}) copy-start(s32[160]{0:T(256)} %param.11) | copy-start | bytes 1924
  23.5 1.5 %collective-permute-start.7 = (bf16[80,1280]{1,0:T(8,128)(2,1)S(1)}, bf16[80,1280]{1,0:T(8,128)(2,1)S(1)}, u32[]{:S(2)}, u32[]{:S(2)}) collective-permute-start(bf16[80,1280]{1,0:T(8,128)(2,1)S(1)} %get-tuple-element.40), channel_id=1, source_target_pairs={{0,4},{4,0},{8,12},{12,8},{16,20},{20,16},{24,28},{28,24},{1,5},{5... | collective-permute-start | bytes 614408 | tf_op jit(solution)/shard_map/ppermute | solution.py:467
  25.1 8.2 %collective-permute-start.12 = (bf16[80,640]{1,0:T(8,128)(2,1)S(1)}, bf16[80,640]{1,0:T(8,128)(2,1)S(1)}, u32[]{:S(2)}, u32[]{:S(2)}) collective-permute-start(bf16[80,640]{1,0:T(8,128)(2,1)S(1)} %get-tuple-element.45.refs_2_), channel_id=1, source_target_pairs={{0,2},{1,3},{2,0},{3,1},{4,6},{5,7},{6,4},{7,5},{8,10},{9,11},{10,... | collective-permute-start | bytes 307208 | tf_op jit(solution)/shard_map/ppermute | solution.py:467
  27.8 5.8 %collective-permute-start.11 = (bf16[80,640]{1,0:T(8,128)(2,1)S(1)}, bf16[80,640]{1,0:T(8,128)(2,1)S(1)}, u32[]{:S(2)}, u32[]{:S(2)}) collective-permute-start(bf16[80,640]{1,0:T(8,128)(2,1)S(1)} %get-tuple-element.41.refs_0_), channel_id=1, source_target_pairs={{0,1},{1,0},{2,3},{3,2},{4,5},{5,4},{6,7},{7,6},{8,9},{9,8},{10,11... | collective-permute-start | bytes 307208 | tf_op jit(solution)/shard_map/ppermute | solution.py:467
  29.3 8.0 %collective-permute-start.8 = (bf16[32,1280]{1,0:T(8,128)(2,1)S(1)}, bf16[32,1280]{1,0:T(8,128)(2,1)S(1)}, u32[]{:S(2)}, u32[]{:S(2)}) collective-permute-start(bf16[32,1280]{1,0:T(8,128)(2,1)S(1)} %get-tuple-element.42), channel_id=1, source_target_pairs={{0,8},{4,20},{8,0},{12,28},{16,24},{20,4},{24,16},{28,12},{1,9},{5... | collective-permute-start | bytes 245768 | tf_op jit(solution)/shard_map/ppermute | solution.py:472
  29.9 7.5 %collective-permute-start.9 = (bf16[32,1280]{1,0:T(8,128)(2,1)S(1)}, bf16[32,1280]{1,0:T(8,128)(2,1)S(1)}, u32[]{:S(2)}, u32[]{:S(2)}) collective-permute-start(bf16[32,1280]{1,0:T(8,128)(2,1)S(1)} %get-tuple-element.43), channel_id=1, source_target_pairs={{0,16},{4,12},{8,24},{12,4},{16,0},{20,28},{24,8},{28,20},{1,17},{... | collective-permute-start | bytes 245768 | tf_op jit(solution)/shard_map/ppermute | solution.py:472
  30.7 6.7 %collective-permute-start.10 = (bf16[32,1280]{1,0:T(8,128)(2,1)S(1)}, bf16[32,1280]{1,0:T(8,128)(2,1)S(1)}, u32[]{:S(2)}, u32[]{:S(2)}) collective-permute-start(bf16[32,1280]{1,0:T(8,128)(2,1)S(1)} %get-tuple-element.44), channel_id=1, source_target_pairs={{0,24},{4,28},{8,16},{12,20},{16,8},{20,12},{24,0},{28,4},{1,25},{... | collective-permute-start | bytes 245768 | tf_op jit(solution)/shard_map/ppermute | solution.py:472
  33.6 7.3 %collective-permute-start.13 = (bf16[80,640]{1,0:T(8,128)(2,1)S(1)}, bf16[80,640]{1,0:T(8,128)(2,1)S(1)}, u32[]{:S(2)}, u32[]{:S(2)}) collective-permute-start(bf16[80,640]{1,0:T(8,128)(2,1)S(1)} %get-tuple-element.46.refs_0_), channel_id=1, source_target_pairs={{0,2},{1,3},{2,0},{3,1},{4,6},{5,7},{6,4},{7,5},{8,10},{9,11},{10,... | collective-permute-start | bytes 307208 | tf_op jit(solution)/shard_map/ppermute | solution.py:467
  34.9 6.3 %collective-permute-start.14 = (bf16[80,640]{1,0:T(8,128)(2,1)S(1)}, bf16[80,640]{1,0:T(8,128)(2,1)S(1)}, u32[]{:S(2)}, u32[]{:S(2)}) collective-permute-start(bf16[80,640]{1,0:T(8,128)(2,1)S(1)} %get-tuple-element.47.refs_2_), channel_id=1, source_target_pairs={{0,1},{1,0},{2,3},{3,2},{4,5},{5,4},{6,7},{7,6},{8,9},{9,8},{10,11... | collective-permute-start | bytes 307208 | tf_op jit(solution)/shard_map/ppermute | solution.py:467

commit v6 on v5

--- a/solution.py
+++ b/solution.py
@@ -480,11 +480,11 @@
 
     held, kept, given = pick_rows(window_owner, window_len, slot_token, pixels, cotangent)
     given = swap(given, "enc", 1)
-    blocks = [held, chip_swap(held, 1), chip_swap(held, 2)]
+    blocks = [held, chip_swap(held, 1), chip_swap(after(held, given), 2)]
     attended, ordered, *sent = attend_ordered(kept, given, gain, w_qkv, pairs)
     columns = [sent[0]] + [chip_swap(sent[b], b) for b in range(1, pairs)]
     encoded = project_ordered(attended, ordered, w_out, pairs)
-    blocks.append(chip_swap(after(blocks[1], encoded), 2))
+    blocks.append(chip_swap(after(blocks[1], attended), 2))
     scale = 1.0 / math.sqrt(rows * group * replicas)
     near = near_rows(columns, blocks[:-1])
     mine, other = far_rows(columns, blocks[-1], near, scale)

time: 42.3 us -> 40.5 us (0.957)
  waiting for transfers between devices: 11.8 us -> 8.31 us
  starting transfers between devices: 20.2 us -> 22.1 us
    ppermute x6, waiting for transfers between devices: 5.63 us -> 2.53 us  [swap(): return lax.ppermute(value, axis, [(i, i ^ bits) for i in range(size)])]
    ppermute x9, starting transfers between devices: 12.1 us -> 13.2 us  [chip_swap(): lax.ppermute(value, 'enc', [(i, i ^ 2 * turn(relative, i % 2)) for i in r...]
    ppermute x6, starting transfers between devices: 8.1 us -> 8.89 us  [swap(): return lax.ppermute(value, axis, [(i, i ^ bits) for i in range(size)])]
  transfers between devices with their start and end apart: 15 -> 15, of which waited for: 9 -> 7; matrix products, arithmetic and copies ran while one was open for 0% -> 0% of each run, Pallas kernels for 14% -> 14%
where the time goes in v6:
time: 40.5 us; the launch traced here: 40.3 us
  starting transfers between devices  22.1 us (55%)
  Pallas kernels  9.18 us (23%)
  waiting for transfers between devices  8.31 us (21%)
  between operations  0.73 us (2%)
    ppermute x9, starting transfers between devices, chip_swap(): lax.ppermute(value, 'enc', [(i, i ^ 2 * turn(relative, i % 2)) for i in r...  13.2 us
    ppermute x6, starting transfers between devices, swap(): return lax.ppermute(value, axis, [(i, i ^ bits) for i in range(size)])  8.89 us
    ppermute x9, waiting for transfers between devices, chip_swap(): lax.ppermute(value, 'enc', [(i, i ^ 2 * turn(relative, i % 2)) for i in r...  5.78 us
    pallas_call x1, Pallas kernels, attend_ordered(): pl.pallas_call(attend_kernel, out_shape=(jax.ShapeDtypeStruct((inner, row...  3.03 us
    ppermute x6, waiting for transfers between devices, swap(): return lax.ppermute(value, axis, [(i, i ^ bits) for i in range(size)])  2.53 us
    pallas_call x1, Pallas kernels, pick_rows(): pl.pallas_call(pick_kernel, out_shape=(jax.ShapeDtypeStruct((rows, width)...  2.2 us
    pallas_call x1, Pallas kernels, place_rows(): pl.pallas_call(place_kernel, out_shape=jax.ShapeDtypeStruct((tokens, MERG...  1.82 us
    pallas_call x3, Pallas kernels, add_halves(): pl.pallas_call(functools.partial(add_kernel, split), out_shape=(jax.Shape...  0.9 us
  transfers between devices with their start and end apart: 15, of which 7 were waited for; matrix products, arithmetic and copies ran while one was open for 0% of the time, Pallas kernels for 14%

profile of v6, /device:TPU:0, one launch (start us, length us, event | category | flops | bytes accessed | tf_op | source)
XLA Modules:
  0.0 40.3 jit_solution(14096850839747711627)
XLA Ops:
  0.6 0.0 slice-start
  0.6 0.0 slice-start.1
  0.7 2.2 %pick_rows.1 = (bf16[128,1280]{1,0:T(8,128)(2,1)S(1)}, bf16[80,1280]{1,0:T(8,128)(2,1)S(1)}, bf16[80,1280]{1,0:T(8,128)(2,1)S(1)}) custom-call(s32[8]{0:T(128)} %owner_hbm.1, s32[8]{0:T(128)} %len_hbm.1, s32[1,160]{1,0:T(1,128)} %bitcast.3, bf16[128,1280]{1,0:T(8,128)(2,1)} %pixels_hbm.1, bf16[160,5120]{1,0:T(8,128)(2,1)} %cotangent_hbm.1), custom_call_target="tpu_custom_call" | custom-call | flops 20971520000 | bytes 1638400 | tf_op jit(solution)/shard_map/pick_rows/pallas_call | solution.py:212
  2.9 0.5 %collective-permute-start = (bf16[80,1280]{1,0:T(8,128)(2,1)S(1)}, bf16[80,1280]{1,0:T(8,128)(2,1)S(1)}, u32[]{:S(2)}, u32[]{:S(2)}) collective-permute-start(bf16[80,1280]{1,0:T(8,128)(2,1)S(1)} %get-tuple-element.27), channel_id=1, source_target_pairs={{0,4},{4,0},{8,12},{12,8},{16,20},{20,16},{24,28},{28,24},{1,5},{5... | collective-permute-start | bytes 614408 | tf_op jit(solution)/shard_map/ppermute | solution.py:467
  3.4 2.6 %collective-permute-start.4 = (bf16[128,1280]{1,0:T(8,128)(2,1)S(1)}, bf16[128,1280]{1,0:T(8,128)(2,1)S(1)}, u32[]{:S(2)}, u32[]{:S(2)}) collective-permute-start(bf16[128,1280]{1,0:T(8,128)(2,1)S(1)} %get-tuple-element.38.refs_4_), channel_id=1, source_target_pairs={{0,8},{4,20},{8,0},{12,28},{16,24},{20,4},{24,16},{28,12},{1,9},{5... | collective-permute-start | bytes 983048 | tf_op jit(solution)/shard_map/ppermute | solution.py:472
  5.9 0.0 collective-permute-done.given_ref
  5.9 1.5 %collective-permute-start.6 = (bf16[128,1280]{1,0:T(8,128)(2,1)S(1)}, bf16[128,1280]{1,0:T(8,128)(2,1)S(1)}, u32[]{:S(2)}, u32[]{:S(2)}) collective-permute-start(bf16[128,1280]{1,0:T(8,128)(2,1)S(1)} %get-tuple-element.38.refs_4_), channel_id=1, source_target_pairs={{0,16},{4,12},{8,24},{12,4},{16,0},{20,28},{24,8},{28,20},{1,17},{... | collective-permute-start | bytes 983048 | tf_op jit(solution)/shard_map/ppermute | solution.py:472
  7.5 0.0 slice-done
  7.5 0.0 slice-done.1
  7.5 3.0 %attend.1 = (bf16[640,128]{1,0:T(8,128)(2,1)S(1)}, bf16[128,1280]{1,0:T(8,128)(2,1)S(1)}, bf16[160,128]{1,0:T(8,128)(2,1)S(1)}, bf16[160,128]{1,0:T(8,128)(2,1)S...) custom-call(bf16[80,1280]{1,0:T(8,128)(2,1)S(1)} %get-tuple-element.26.kept_ref, ...), custom_call_target="tpu_custom_call" | custom-call | flops 629145600 | bytes 4915200 | tf_op jit(solution)/shard_map/attend/pallas_call | solution.py:303
  10.5 1.4 %collective-permute-start.1 = (bf16[160,128]{1,0:T(8,128)(2,1)S(1)}, bf16[160,128]{1,0:T(8,128)(2,1)S(1)}, u32[]{:S(2)}, u32[]{:S(2)}) collective-permute-start(bf16[160,128]{1,0:T(8,128)(2,1)S(1)} %get-tuple-element.33), channel_id=1, source_target_pairs={{0,8},{4,20},{8,0},{12,28},{16,24},{20,4},{24,16},{28,12},{1,9},{5... | collective-permute-start | bytes 122888 | tf_op jit(solution)/shard_map/ppermute | solution.py:472
  12.0 0.5 %collective-permute-start.2 = (bf16[160,128]{1,0:T(8,128)(2,1)S(1)}, bf16[160,128]{1,0:T(8,128)(2,1)S(1)}, u32[]{:S(2)}, u32[]{:S(2)}) collective-permute-start(bf16[160,128]{1,0:T(8,128)(2,1)S(1)} %get-tuple-element.34), channel_id=1, source_target_pairs={{0,16},{4,12},{8,24},{12,4},{16,0},{20,28},{24,8},{28,20},{1,17},{... | collective-permute-start | bytes 122888 | tf_op jit(solution)/shard_map/ppermute | solution.py:472
  12.5 1.6 %collective-permute-start.3 = (bf16[160,128]{1,0:T(8,128)(2,1)S(1)}, bf16[160,128]{1,0:T(8,128)(2,1)S(1)}, u32[]{:S(2)}, u32[]{:S(2)}) collective-permute-start(bf16[160,128]{1,0:T(8,128)(2,1)S(1)} %get-tuple-element.35), channel_id=1, source_target_pairs={{0,24},{4,28},{8,16},{12,20},{16,8},{20,12},{24,0},{28,4},{1,25},{... | collective-permute-start | bytes 122888 | tf_op jit(solution)/shard_map/ppermute | solution.py:472
  14.1 0.0 collective-permute-done.4.refs_5_
  14.1 2.0 %collective-permute-start.5 = (bf16[128,1280]{1,0:T(8,128)(2,1)S(1)}, bf16[128,1280]{1,0:T(8,128)(2,1)S(1)}, u32[]{:S(2)}, u32[]{:S(2)}) collective-permute-start(bf16[128,1280]{1,0:T(8,128)(2,1)S(1)} %collective-permute-done.4.refs_5_), channel_id=1, source_target_pairs={{0,16},{4,12},{8,24},{12,4},{16,0},{20,28},{24,8},{28,20},{1,17},{... | collective-permute-start | bytes 983048 | tf_op jit(solution)/shard_map/ppermute | solution.py:472
  16.1 0.0 collective-permute-done.1.refs_1_
  16.1 0.0 collective-permute-done.2.refs_2_
  16.1 1.8 %collective-permute-done.3.refs_3_ = bf16[160,128]{1,0:T(8,128)(2,1)S(1)} collective-permute-done((bf16[160,128]{1,0:T(8,128)(2,1)S(1)}, bf16[160,128]{1,0:T(8,128)(2,1)S(1)}, u32[]{:S(2)}, u32[]{:S(2)}) %collective-permute-start.3) | collective-permute-done | bytes 40992 | tf_op jit(solution)/shard_map/ppermute | solution.py:472
  17.9 0.0 collective-permute-done.6.refs_6_
  17.9 0.4 %near_rows.1.refs_5_ = f32[160,1280]{1,0:T(8,128)S(1)} custom-call(bf16[160,128]{1,0:T(8,128)(2,1)S(1)} %get-tuple-element.32.refs_0_, bf16[160,128]{1,0:T(8,128)(2,1)S(1)} %collective-permute-done.1.refs_1_, bf16[160,128]{1,0:T(8,128)(2,1)S(1)} %collective-permute-done.2.refs_2_, bf16[160,128]{1,0:T(8,128)(2,1)S(1)} %collective-permute-done.3.refs_3_, ...), custom_call_target="tpu_custom_call" | custom-call | flops 7864320000 | bytes 983040 | tf_op jit(solution)/shard_map/near_rows/pallas_call | solution.py:376
  18.3 0.0 copy-start
  18.3 3.0 %collective-permute-done.5.refs_4_ = bf16[128,1280]{1,0:T(8,128)(2,1)S(1)} collective-permute-done((bf16[128,1280]{1,0:T(8,128)(2,1)S(1)}, bf16[128,1280]{1,0:T(8,128)(2,1)S(1)}, u32[]{:S(2)}, u32[]{:S(2)}) %collective-permute-start.5) | collective-permute-done | bytes 327712 | tf_op jit(solution)/shard_map/ppermute | solution.py:472
  21.3 0.3 far_rows.1
  21.6 0.0 copy-start.1
  21.6 0.1 collective-permute-start.7
  21.7 1.4 %collective-permute-done.7.refs_1_ = bf16[80,1280]{1,0:T(8,128)(2,1)S(1)} collective-permute-done((bf16[80,1280]{1,0:T(8,128)(2,1)S(1)}, bf16[80,1280]{1,0:T(8,128)(2,1)S(1)}, u32[]{:S(2)}, u32[]{:S(2)}) %collective-permute-start.7) | collective-permute-done | bytes 204832 | tf_op jit(solution)/shard_map/ppermute | solution.py:467
  23.2 2.8 %collective-permute-start.12 = (bf16[80,640]{1,0:T(8,128)(2,1)S(1)}, bf16[80,640]{1,0:T(8,128)(2,1)S(1)}, u32[]{:S(2)}, u32[]{:S(2)}) collective-permute-start(bf16[80,640]{1,0:T(8,128)(2,1)S(1)} %get-tuple-element.47.refs_2_), channel_id=1, source_target_pairs={{0,2},{1,3},{2,0},{3,1},{4,6},{5,7},{6,4},{7,5},{8,10},{9,11},{10,... | collective-permute-start | bytes 307208 | tf_op jit(solution)/shard_map/ppermute | solution.py:467
  26.0 1.6 %collective-permute-start.11 = (bf16[80,640]{1,0:T(8,128)(2,1)S(1)}, bf16[80,640]{1,0:T(8,128)(2,1)S(1)}, u32[]{:S(2)}, u32[]{:S(2)}) collective-permute-start(bf16[80,640]{1,0:T(8,128)(2,1)S(1)} %get-tuple-element.41.refs_0_), channel_id=1, source_target_pairs={{0,1},{1,0},{2,3},{3,2},{4,5},{5,4},{6,7},{7,6},{8,9},{9,8},{10,11... | collective-permute-start | bytes 307208 | tf_op jit(solution)/shard_map/ppermute | solution.py:467
  27.6 0.0 copy-done
  27.6 0.5 %project.1 = (bf16[32,1280]{1,0:T(8,128)(2,1)S(1)}, bf16[32,1280]{1,0:T(8,128)(2,1)S(1)}, bf16[32,1280]{1,0:T(8,128)(2,1)S(1)}, bf16[32,1280]{1,0:T(8,128)(2,1)S(1)}) custom-call(bf16[640,128]{1,0:T(8,128)(2,1)S(1)} %get-tuple-element.28.attended_ref, bf16[128,1280]{1,0:T(8,128)(2,1)S(1)} %get-tuple-element.29.ordered_ref, bf16[640,1280]{1,0:T(8,128)(2,1)S(1)} %copy-done), custom_call_target="tpu_custom_call" | custom-call | flops 209715200 | bytes 1638400 | tf_op jit(solution)/shard_map/project/pallas_call | solution.py:333
  28.1 1.6 %collective-permute-start.8 = (bf16[32,1280]{1,0:T(8,128)(2,1)S(1)}, bf16[32,1280]{1,0:T(8,128)(2,1)S(1)}, u32[]{:S(2)}, u32[]{:S(2)}) collective-permute-start(bf16[32,1280]{1,0:T(8,128)(2,1)S(1)} %get-tuple-element.42), channel_id=1, source_target_pairs={{0,8},{4,20},{8,0},{12,28},{16,24},{20,4},{24,16},{28,12},{1,9},{5... | collective-permute-start | bytes 245768 | tf_op jit(solution)/shard_map/ppermute | solution.py:472
  29.7 1.7 %collective-permute-start.9 = (bf16[32,1280]{1,0:T(8,128)(2,1)S(1)}, bf16[32,1280]{1,0:T(8,128)(2,1)S(1)}, u32[]{:S(2)}, u32[]{:S(2)}) collective-permute-start(bf16[32,1280]{1,0:T(8,128)(2,1)S(1)} %get-tuple-element.44), channel_id=1, source_target_pairs={{0,16},{4,12},{8,24},{12,4},{16,0},{20,28},{24,8},{28,20},{1,17},{... | collective-permute-start | bytes 245768 | tf_op jit(solution)/shard_map/ppermute | solution.py:472
  31.3 0.3 collective-permute-start.10
  31.6 0.0 collective-permute-done.12.refs_3_
  31.6 0.1 collective-permute-done.11.refs_1_
  31.7 0.1 add_halves.4
  31.8 1.5 %collective-permute-start.13 = (bf16[80,640]{1,0:T(8,128)(2,1)S(1)}, bf16[80,640]{1,0:T(8,128)(2,1)S(1)}, u32[]{:S(2)}, u32[]{:S(2)}) collective-permute-start(bf16[80,640]{1,0:T(8,128)(2,1)S(1)} %get-tuple-element.48.refs_0_), channel_id=1, source_target_pairs={{0,2},{1,3},{2,0},{3,1},{4,6},{5,7},{6,4},{7,5},{8,10},{9,11},{10,... | collective-permute-start | bytes 307208 | tf_op jit(solution)/shard_map/ppermute | solution.py:467
  33.2 2.4 %collective-permute-start.14 = (bf16[80,640]{1,0:T(8,128)(2,1)S(1)}, bf16[80,640]{1,0:T(8,128)(2,1)S(1)}, u32[]{:S(2)}, u32[]{:S(2)}) collective-permute-start(bf16[80,640]{1,0:T(8,128)(2,1)S(1)} %get-tuple-element.49.refs_2_), channel_id=1, source_target_pairs={{0,1},{1,0},{2,3},{3,2},{4,5},{5,4},{6,7},{7,6},{8,9},{9,8},{10,11... | collective-permute-start | bytes 307208 | tf_op jit(solution)/shard_map/ppermute | solution.py:467
  35.6 0.0 collective-permute-done.8.refs_1_
  35.6 0.0 collective-permute-done.9.refs_2_
  35.6 1.0 %collective-permute-done.10.refs_3_ = bf16[32,1280]{1,0:T(8,128)(2,1)S(1)} collective-permute-done((bf16[32,1280]{1,0:T(8,128)(2,1)S(1)}, bf16[32,1280]{1,0:T(8,128)(2,1)S(1)}, u32[]{:S(2)}, u32[]{:S(2)}) %collective-permute-start.10) | collective-permute-done | bytes 81952 | tf_op jit(solution)/shard_map/ppermute | solution.py:472
  36.7 0.0 copy-done.1
  36.7 1.8 %place_rows.1 = bf16[160,5120]{1,0:T(8,128)(2,1)} custom-call(s32[1,160]{1,0:T(1,128)S(1)} %bitcast.4, bf16[32,1280]{1,0:T(8,128)(2,1)S(1)} %get-tuple-element.30.refs_0_, bf16[32,1280]{1,0:T(8,128)(2,1)S(1)} %collective-permute-done.8.refs_1_, bf16[32,1280]{1,0:T(8,128)(2,1)S(1)} %collective-permute-done.9.refs_2_, ...), custom_call_target="tpu_custom_call" | custom-call | flops 20971520000 | bytes 1638400 | tf_op jit(solution)/shard_map/place_rows/pallas_call | solution.py:422
  38.5 0.6 %collective-permute-done.13.refs_1_ = bf16[80,640]{1,0:T(8,128)(2,1)S(1)} collective-permute-done((bf16[80,640]{1,0:T(8,128)(2,1)S(1)}, bf16[80,640]{1,0:T(8,128)(2,1)S(1)}, u32[]{:S(2)}, u32[]{:S(2)}) %collective-permute-start.13) | collective-permute-done | bytes 102432 | tf_op jit(solution)/shard_map/ppermute | solution.py:467
  39.1 0.4 %collective-permute-done.14.refs_3_ = bf16[80,640]{1,0:T(8,128)(2,1)S(1)} collective-permute-done((bf16[80,640]{1,0:T(8,128)(2,1)S(1)}, bf16[80,640]{1,0:T(8,128)(2,1)S(1)}, u32[]{:S(2)}, u32[]{:S(2)}) %collective-permute-start.14) | collective-permute-done | bytes 102432 | tf_op jit(solution)/shard_map/ppermute | solution.py:467
  39.5 0.8 %add_halves.5 = f32[80,1280]{1,0:T(8,128)} custom-call(bf16[80,640]{1,0:T(8,128)(2,1)S(1)} %get-tuple-element.48.refs_0_, bf16[80,640]{1,0:T(8,128)(2,1)S(1)} %collective-permute-done.13.refs_1_, bf16[80,640]{1,0:T(8,128)(2,1)S(1)} %get-tuple-element.49.refs_2_, bf16[80,640]{1,0:T(8,128)(2,1)S(1)} %collective-permute-done.14.refs_3_), custom_call_target="tpu_custom_call" | custom-call | flops 102400 | bytes 819200 | tf_op jit(solution)/shard_map/add_halves/pallas_call | solution.py:450
  (2 shorter events, 0.0 us)
Async XLA Ops:
  0.6 6.8 %slice-start = ((s8[4915200]{0:T(1024)(128)(4,1)}), s8[4194304]{0:T(1024)(128)(4,1)S(1)}, s32[]{:S(2)}) async-start(s8[4915200]{0:T(1024)(128)(4,1)} %bitcast.1), calls=%async_computation | async-start | bytes 8388608
  0.6 6.8 %slice-start.1 = ((s8[4915200]{0:T(1024)(128)(4,1)}), s8[720896]{0:T(1024)(128)(4,1)S(1)}, s32[]{:S(2)}) async-start(s8[4915200]{0:T(1024)(128)(4,1)} %bitcast.1), calls=%async_computation.1 | async-start | bytes 1441792
  2.9 3.1 %collective-permute-start = (bf16[80,1280]{1,0:T(8,128)(2,1)S(1)}, bf16[80,1280]{1,0:T(8,128)(2,1)S(1)}, u32[]{:S(2)}, u32[]{:S(2)}) collective-permute-start(bf16[80,1280]{1,0:T(8,128)(2,1)S(1)} %get-tuple-element.27), channel_id=1, source_target_pairs={{0,4},{4,0},{8,12},{12,8},{16,20},{20,16},{24,28},{28,24},{1,5},{5... | collective-permute-start | bytes 614408 | tf_op jit(solution)/shard_map/ppermute | solution.py:467
  3.4 10.7 %collective-permute-start.4 = (bf16[128,1280]{1,0:T(8,128)(2,1)S(1)}, bf16[128,1280]{1,0:T(8,128)(2,1)S(1)}, u32[]{:S(2)}, u32[]{:S(2)}) collective-permute-start(bf16[128,1280]{1,0:T(8,128)(2,1)S(1)} %get-tuple-element.38.refs_4_), channel_id=1, source_target_pairs={{0,8},{4,20},{8,0},{12,28},{16,24},{20,4},{24,16},{28,12},{1,9},{5... | collective-permute-start | bytes 983048 | tf_op jit(solution)/shard_map/ppermute | solution.py:472
  5.9 11.9 %collective-permute-start.6 = (bf16[128,1280]{1,0:T(8,128)(2,1)S(1)}, bf16[128,1280]{1,0:T(8,128)(2,1)S(1)}, u32[]{:S(2)}, u32[]{:S(2)}) collective-permute-start(bf16[128,1280]{1,0:T(8,128)(2,1)S(1)} %get-tuple-element.38.refs_4_), channel_id=1, source_target_pairs={{0,16},{4,12},{8,24},{12,4},{16,0},{20,28},{24,8},{28,20},{1,17},{... | collective-permute-start | bytes 983048 | tf_op jit(solution)/shard_map/ppermute | solution.py:472
  10.5 5.6 %collective-permute-start.1 = (bf16[160,128]{1,0:T(8,128)(2,1)S(1)}, bf16[160,128]{1,0:T(8,128)(2,1)S(1)}, u32[]{:S(2)}, u32[]{:S(2)}) collective-permute-start(bf16[160,128]{1,0:T(8,128)(2,1)S(1)} %get-tuple-element.33), channel_id=1, source_target_pairs={{0,8},{4,20},{8,0},{12,28},{16,24},{20,4},{24,16},{28,12},{1,9},{5... | collective-permute-start | bytes 122888 | tf_op jit(solution)/shard_map/ppermute | solution.py:472
  12.0 4.1 %collective-permute-start.2 = (bf16[160,128]{1,0:T(8,128)(2,1)S(1)}, bf16[160,128]{1,0:T(8,128)(2,1)S(1)}, u32[]{:S(2)}, u32[]{:S(2)}) collective-permute-start(bf16[160,128]{1,0:T(8,128)(2,1)S(1)} %get-tuple-element.34), channel_id=1, source_target_pairs={{0,16},{4,12},{8,24},{12,4},{16,0},{20,28},{24,8},{28,20},{1,17},{... | collective-permute-start | bytes 122888 | tf_op jit(solution)/shard_map/ppermute | solution.py:472
  12.5 5.4 %collective-permute-start.3 = (bf16[160,128]{1,0:T(8,128)(2,1)S(1)}, bf16[160,128]{1,0:T(8,128)(2,1)S(1)}, u32[]{:S(2)}, u32[]{:S(2)}) collective-permute-start(bf16[160,128]{1,0:T(8,128)(2,1)S(1)} %get-tuple-element.35), channel_id=1, source_target_pairs={{0,24},{4,28},{8,16},{12,20},{16,8},{20,12},{24,0},{28,4},{1,25},{... | collective-permute-start | bytes 122888 | tf_op jit(solution)/shard_map/ppermute | solution.py:472
  14.1 7.2 %collective-permute-start.5 = (bf16[128,1280]{1,0:T(8,128)(2,1)S(1)}, bf16[128,1280]{1,0:T(8,128)(2,1)S(1)}, u32[]{:S(2)}, u32[]{:S(2)}) collective-permute-start(bf16[128,1280]{1,0:T(8,128)(2,1)S(1)} %collective-permute-done.4.refs_5_), channel_id=1, source_target_pairs={{0,16},{4,12},{8,24},{12,4},{16,0},{20,28},{24,8},{28,20},{1,17},{... | collective-permute-start | bytes 983048 | tf_op jit(solution)/shard_map/ppermute | solution.py:472
  18.3 9.3 %copy-start = (bf16[640,1280]{1,0:T(8,128)(2,1)S(1)}, bf16[640,1280]{1,0:T(8,128)(2,1)}, u32[]{:S(2)}) copy-start(bf16[640,1280]{1,0:T(8,128)(2,1)} %w_ref.3) | copy-start | bytes 4915204
  21.6 15.1 %copy-start.1 = (s32[160]{0:T(256)S(1)}, s32[160]{0:T(256)}, u32[]{:S(2)}) copy-start(s32[160]{0:T(256)} %param.11) | copy-start | bytes 1924
  21.6 1.5 %collective-permute-start.7 = (bf16[80,1280]{1,0:T(8,128)(2,1)S(1)}, bf16[80,1280]{1,0:T(8,128)(2,1)S(1)}, u32[]{:S(2)}, u32[]{:S(2)}) collective-permute-start(bf16[80,1280]{1,0:T(8,128)(2,1)S(1)} %get-tuple-element.40), channel_id=1, source_target_pairs={{0,4},{4,0},{8,12},{12,8},{16,20},{20,16},{24,28},{28,24},{1,5},{5... | collective-permute-start | bytes 614408 | tf_op jit(solution)/shard_map/ppermute | solution.py:467
  23.2 8.5 %collective-permute-start.12 = (bf16[80,640]{1,0:T(8,128)(2,1)S(1)}, bf16[80,640]{1,0:T(8,128)(2,1)S(1)}, u32[]{:S(2)}, u32[]{:S(2)}) collective-permute-start(bf16[80,640]{1,0:T(8,128)(2,1)S(1)} %get-tuple-element.47.refs_2_), channel_id=1, source_target_pairs={{0,2},{1,3},{2,0},{3,1},{4,6},{5,7},{6,4},{7,5},{8,10},{9,11},{10,... | collective-permute-start | bytes 307208 | tf_op jit(solution)/shard_map/ppermute | solution.py:467
  26.0 5.7 %collective-permute-start.11 = (bf16[80,640]{1,0:T(8,128)(2,1)S(1)}, bf16[80,640]{1,0:T(8,128)(2,1)S(1)}, u32[]{:S(2)}, u32[]{:S(2)}) collective-permute-start(bf16[80,640]{1,0:T(8,128)(2,1)S(1)} %get-tuple-element.41.refs_0_), channel_id=1, source_target_pairs={{0,1},{1,0},{2,3},{3,2},{4,5},{5,4},{6,7},{7,6},{8,9},{9,8},{10,11... | collective-permute-start | bytes 307208 | tf_op jit(solution)/shard_map/ppermute | solution.py:467
  28.1 7.6 %collective-permute-start.8 = (bf16[32,1280]{1,0:T(8,128)(2,1)S(1)}, bf16[32,1280]{1,0:T(8,128)(2,1)S(1)}, u32[]{:S(2)}, u32[]{:S(2)}) collective-permute-start(bf16[32,1280]{1,0:T(8,128)(2,1)S(1)} %get-tuple-element.42), channel_id=1, source_target_pairs={{0,8},{4,20},{8,0},{12,28},{16,24},{20,4},{24,16},{28,12},{1,9},{5... | collective-permute-start | bytes 245768 | tf_op jit(solution)/shard_map/ppermute | solution.py:472
  29.7 6.0 %collective-permute-start.9 = (bf16[32,1280]{1,0:T(8,128)(2,1)S(1)}, bf16[32,1280]{1,0:T(8,128)(2,1)S(1)}, u32[]{:S(2)}, u32[]{:S(2)}) collective-permute-start(bf16[32,1280]{1,0:T(8,128)(2,1)S(1)} %get-tuple-element.44), channel_id=1, source_target_pairs={{0,16},{4,12},{8,24},{12,4},{16,0},{20,28},{24,8},{28,20},{1,17},{... | collective-permute-start | bytes 245768 | tf_op jit(solution)/shard_map/ppermute | solution.py:472
  31.3 5.3 %collective-permute-start.10 = (bf16[32,1280]{1,0:T(8,128)(2,1)S(1)}, bf16[32,1280]{1,0:T(8,128)(2,1)S(1)}, u32[]{:S(2)}, u32[]{:S(2)}) collective-permute-start(bf16[32,1280]{1,0:T(8,128)(2,1)S(1)} %get-tuple-element.46), channel_id=1, source_target_pairs={{0,24},{4,28},{8,16},{12,20},{16,8},{20,12},{24,0},{28,4},{1,25},{... | collective-permute-start | bytes 245768 | tf_op jit(solution)/shard_map/ppermute | solution.py:472
  31.8 7.4 %collective-permute-start.13 = (bf16[80,640]{1,0:T(8,128)(2,1)S(1)}, bf16[80,640]{1,0:T(8,128)(2,1)S(1)}, u32[]{:S(2)}, u32[]{:S(2)}) collective-permute-start(bf16[80,640]{1,0:T(8,128)(2,1)S(1)} %get-tuple-element.48.refs_0_), channel_id=1, source_target_pairs={{0,2},{1,3},{2,0},{3,1},{4,6},{5,7},{6,4},{7,5},{8,10},{9,11},{10,... | collective-permute-start | bytes 307208 | tf_op jit(solution)/shard_map/ppermute | solution.py:467
  33.2 6.3 %collective-permute-start.14 = (bf16[80,640]{1,0:T(8,128)(2,1)S(1)}, bf16[80,640]{1,0:T(8,128)(2,1)S(1)}, u32[]{:S(2)}, u32[]{:S(2)}) collective-permute-start(bf16[80,640]{1,0:T(8,128)(2,1)S(1)} %get-tuple-element.49.refs_2_), channel_id=1, source_target_pairs={{0,1},{1,0},{2,3},{3,2},{4,5},{5,4},{6,7},{7,6},{8,9},{9,8},{10,11... | collective-permute-start | bytes 307208 | tf_op jit(solution)/shard_map/ppermute | solution.py:467

commit v7 on v6

--- a/solution.py
+++ b/solution.py
@@ -104,7 +104,7 @@
 LANES = 128
 SUBLANES = 16
 PAIR_BITS = 2
-NEAR = 100
+NEAR = 40
 PLACE = 200
 VMEM = pl.BlockSpec(memory_space=pltpu.VMEM)
 HBM = pl.BlockSpec(memory_space=pltpu.HBM)
@@ -160,34 +160,21 @@
     window_rows = rows // windows
     me = lax.axis_index("enc")
     pairs_of_refs = [
-        (slots_hbm, slots_ref),
         (owner_hbm, owner_ref),
         (len_hbm, len_ref),
+        (slots_hbm, slots_ref),
+        (pixels_hbm, pixels_buf),
     ]
     for j in range(MERGE):
         pairs_of_refs.append((cotangent_hbm.at[:, pl.ds(j * width, width)], parts.at[j]))
-    pairs_of_refs.append((pixels_hbm, pixels_buf))
     copies = [
         pltpu.make_async_copy(source, target, sems.at[i])
         for i, (source, target) in enumerate(pairs_of_refs)
     ]
     for copy in copies:
         copy.start()
-    row = iota((rows, tokens), 0)
-    copies[0].wait()
-    holds = slots_ref[...] == slot_of_row(row, me, window_rows)
-    picks = [
-        jnp.where(holds & (row % MERGE == j), 1.0, 0.0).astype(jnp.bfloat16) for j in range(MERGE)
-    ]
-    held = None
-    for j in range(MERGE):
-        copies[3 + j].wait()
-        term = jnp.dot(picks[j], parts[j], preferred_element_type=jnp.float32)
-        held = term if held is None else held + term
-    held_ref[...] = held.astype(jnp.bfloat16)
-    copies[1].wait()
-    copies[2].wait()
-    copies[3 + MERGE].wait()
+    for i in (0, 1, 3):
+        copies[i].wait()
     which = iota((SUBLANES, width), 0)
     lengths = [jnp.zeros((SUBLANES, width), jnp.int32)] * 2
     for w in range(windows):
@@ -203,7 +190,18 @@
     for side, ref in enumerate((kept_ref, given_ref)):
         ref[: rows // 2, :] = windows_buf[side]
         ref[rows // 2 :, :] = lengths[side].astype(jnp.float32).astype(jnp.bfloat16)
-
+    row = iota((rows, tokens), 0)
+    copies[2].wait()
+    holds = slots_ref[...] == slot_of_row(row, me, window_rows)
+    picks = [
+        jnp.where(holds & (row % MERGE == j), 1.0, 0.0).astype(jnp.bfloat16) for j in range(MERGE)
+    ]
+    held = None
+    for j in range(MERGE):
+        copies[4 + j].wait()
+        term = jnp.dot(picks[j], parts[j], preferred_element_type=jnp.float32)
+        held = term if held is None else held + term
+    held_ref[...] = held.astype(jnp.bfloat16)
 
 def pick_rows(window_owner, window_len, slot_token, pixels, cotangent):
     rows, width = pixels.shape
@@ -341,30 +339,31 @@
     )(attended, ordered, w_out)
 
 
-def products(columns, blocks, offsets):
-    pairs = len(columns)
-    size = columns[0].shape[1] // pairs
+def products(columns, blocks, places):
     left, right = [], []
-    for b in range(pairs):
-        for offset in offsets:
-            r = b ^ offset
-            left.append(columns[b][:, r * size : (r + 1) * size])
-            right.append(blocks[offsets.index(offset)][r * size : (r + 1) * size, :])
+    for b, o in places:
+        size = columns[b].shape[1] // (1 << PAIR_BITS)
+        r = b ^ o
+        left.append(columns[b][:, r * size : (r + 1) * size])
+        right.append(blocks[o][r * size : (r + 1) * size, :])
     return jnp.dot(
         jnp.concatenate(left, 1), jnp.concatenate(right, 0), preferred_element_type=jnp.float32
     )
 
 
 def near_kernel(pairs, *refs):
-    columns, blocks = refs[:pairs], refs[pairs:-1]
-    refs[-1][...] = products(columns, blocks, list(range(pairs - 1)))
+    columns, blocks = refs[: pairs - 1], refs[pairs - 1 : -1]
+    near = range(pairs - 1)
+    refs[-1][...] = products(columns, blocks, [(b, o) for b in near for o in near])
 
 
 def far_kernel(scale, pairs, *refs):
-    columns, block, near_ref = refs[:pairs], refs[pairs], refs[pairs + 1]
-    kept_ref, given_ref = refs[pairs + 2 :]
+    columns, blocks, near_ref = refs[:pairs], refs[pairs : 2 * pairs], refs[2 * pairs]
+    kept_ref, given_ref = refs[2 * pairs + 1 :]
     head = kept_ref.shape[0]
-    total = (near_ref[...] + products(columns, [block], [pairs - 1])) * scale
+    last = pairs - 1
+    places = [(last, o) for o in range(pairs)] + [(b, last) for b in range(last)]
+    total = (near_ref[...] + products(columns, blocks, places)) * scale
     first = lax.axis_index("enc") % 2 == 0
     kept_ref[...] = jnp.where(first, total[:head], total[head:])
     given_ref[...] = jnp.where(first, total[head:], total[:head]).astype(jnp.bfloat16)
@@ -374,7 +373,7 @@
     heads, rows = columns[0].shape
     width = blocks[0].shape[1]
     return pl.pallas_call(
-        functools.partial(near_kernel, len(columns)),
+        functools.partial(near_kernel, len(columns) + 1),
         out_shape=jax.ShapeDtypeStruct((heads, width), jnp.float32),
         in_specs=[VMEM] * (len(columns) + len(blocks)),
         out_specs=VMEM,
@@ -384,21 +383,21 @@
     )(*columns, *blocks)
 
 
-def far_rows(columns, block, near, scale):
+def far_rows(columns, blocks, near, scale):
     heads, rows = columns[0].shape
-    width = block.shape[1]
+    width = near.shape[1]
     return pl.pallas_call(
         functools.partial(far_kernel, scale, len(columns)),
         out_shape=(
             jax.ShapeDtypeStruct((heads // 2, width), jnp.float32),
             jax.ShapeDtypeStruct((heads // 2, width), jnp.bfloat16),
         ),
-        in_specs=[VMEM] * (len(columns) + 2),
+        in_specs=[VMEM] * (2 * len(columns) + 1),
         out_specs=(VMEM, VMEM),
         compiler_params=params(24),
         cost_estimate=cost(2 * heads * rows * width, 2 * rows * width),
         name="far_rows",
-    )(*columns, block, near)
+    )(*columns, *blocks, near)
 
 
 def place_kernel(slots_ref, *refs):
@@ -480,14 +479,14 @@
 
     held, kept, given = pick_rows(window_owner, window_len, slot_token, pixels, cotangent)
     given = swap(given, "enc", 1)
-    blocks = [held, chip_swap(held, 1), chip_swap(after(held, given), 2)]
     attended, ordered, *sent = attend_ordered(kept, given, gain, w_qkv, pairs)
+    blocks = [held, chip_swap(held, 1), chip_swap(after(held, attended), 2)]
+    blocks.append(chip_swap(after(blocks[1], attended), 2))
     columns = [sent[0]] + [chip_swap(sent[b], b) for b in range(1, pairs)]
     encoded = project_ordered(attended, ordered, w_out, pairs)
-    blocks.append(chip_swap(after(blocks[1], attended), 2))
     scale = 1.0 / math.sqrt(rows * group * replicas)
-    near = near_rows(columns, blocks[:-1])
-    mine, other = far_rows(columns, blocks[-1], near, scale)
+    near = near_rows(columns[:-1], blocks[:-1])
+    mine, other = far_rows(columns, blocks, near, scale)
     halves = add_halves([(mine, swap(other, "enc", 1))], jnp.bfloat16, split=True)
     arrived = [encoded[0]]
     for b in range(1, pairs):

time: 40.5 us -> 40.1 us (level)
  starting transfers between devices: 22.1 us -> 20.6 us
  waiting for transfers between devices: 8.31 us -> 9.47 us
    ppermute x9, starting transfers between devices: 13.2 us -> 11.7 us  [chip_swap(): lax.ppermute(value, 'enc', [(i, i ^ 2 * turn(relative, i % 2)) for i in r...]
    ppermute x9, waiting for transfers between devices: 5.78 us -> 6.59 us  [chip_swap(): lax.ppermute(value, 'enc', [(i, i ^ 2 * turn(relative, i % 2)) for i in r...]
  transfers between devices with their start and end apart: 15 -> 15, of which waited for: 7 -> 9; matrix products, arithmetic and copies ran while one was open for 0% -> 0% of each run, Pallas kernels for 14% -> 15%
where the time goes in v7:
time: 40.1 us; the launch traced here: 39.9 us
  starting transfers between devices  20.6 us (51%)
  waiting for transfers between devices  9.47 us (24%)
  Pallas kernels  9.13 us (23%)
  between operations  0.73 us (2%)
    ppermute x9, starting transfers between devices, chip_swap(): lax.ppermute(value, 'enc', [(i, i ^ 2 * turn(relative, i % 2)) for i in r...  11.7 us
    ppermute x6, starting transfers between devices, swap(): return lax.ppermute(value, axis, [(i, i ^ bits) for i in range(size)])  8.89 us
    ppermute x9, waiting for transfers between devices, chip_swap(): lax.ppermute(value, 'enc', [(i, i ^ 2 * turn(relative, i % 2)) for i in r...  6.59 us
    pallas_call x1, Pallas kernels, attend_ordered(): pl.pallas_call(attend_kernel, out_shape=(jax.ShapeDtypeStruct((inner, row...  3.04 us
    ppermute x6, waiting for transfers between devices, swap(): return lax.ppermute(value, axis, [(i, i ^ bits) for i in range(size)])  2.88 us
    pallas_call x1, Pallas kernels, pick_rows(): pl.pallas_call(pick_kernel, out_shape=(jax.ShapeDtypeStruct((rows, width)...  2.14 us
    pallas_call x1, Pallas kernels, place_rows(): pl.pallas_call(place_kernel, out_shape=jax.ShapeDtypeStruct((tokens, MERG...  1.83 us
    pallas_call x3, Pallas kernels, add_halves(): pl.pallas_call(functools.partial(add_kernel, split), out_shape=(jax.Shape...  0.9 us
  transfers between devices with their start and end apart: 15, of which 9 were waited for; matrix products, arithmetic and copies ran while one was open for 0% of the time, Pallas kernels for 15%

profile of v7, /device:TPU:0, one launch (start us, length us, event | category | flops | bytes accessed | tf_op | source)
XLA Modules:
  0.0 39.9 jit_solution(10472030742283019930)
XLA Ops:
  0.6 0.0 slice-start
  0.6 0.0 slice-start.1
  0.7 2.1 %pick_rows.1 = (bf16[128,1280]{1,0:T(8,128)(2,1)S(1)}, bf16[80,1280]{1,0:T(8,128)(2,1)S(1)}, bf16[80,1280]{1,0:T(8,128)(2,1)S(1)}) custom-call(s32[8]{0:T(128)} %owner_hbm.1, s32[8]{0:T(128)} %len_hbm.1, s32[1,160]{1,0:T(1,128)} %bitcast.3, bf16[128,1280]{1,0:T(8,128)(2,1)} %pixels_hbm.1, bf16[160,5120]{1,0:T(8,128)(2,1)} %cotangent_hbm.1), custom_call_target="tpu_custom_call" | custom-call | flops 20971520000 | bytes 1638400 | tf_op jit(solution)/shard_map/pick_rows/pallas_call | solution.py:210
  2.8 0.5 %collective-permute-start = (bf16[80,1280]{1,0:T(8,128)(2,1)S(1)}, bf16[80,1280]{1,0:T(8,128)(2,1)S(1)}, u32[]{:S(2)}, u32[]{:S(2)}) collective-permute-start(bf16[80,1280]{1,0:T(8,128)(2,1)S(1)} %get-tuple-element.27), channel_id=1, source_target_pairs={{0,4},{4,0},{8,12},{12,8},{16,20},{20,16},{24,28},{28,24},{1,5},{5... | collective-permute-start | bytes 614408 | tf_op jit(solution)/shard_map/ppermute | solution.py:466
  3.3 2.6 %collective-permute-start.4 = (bf16[128,1280]{1,0:T(8,128)(2,1)S(1)}, bf16[128,1280]{1,0:T(8,128)(2,1)S(1)}, u32[]{:S(2)}, u32[]{:S(2)}) collective-permute-start(bf16[128,1280]{1,0:T(8,128)(2,1)S(1)} %get-tuple-element.37.refs_3_.refs_4_), channel_id=1, source_target_pairs={{0,8},{4,20},{8,0},{12,28},{16,24},{20,4},{24,16},{28,12},{1,9},{5... | collective-permute-start | bytes 983048 | tf_op jit(solution)/shard_map/ppermute | solution.py:471
  5.9 0.0 collective-permute-done.given_ref
  5.9 0.0 slice-done
  5.9 0.0 slice-done.1
  5.9 3.0 %attend.1 = (bf16[640,128]{1,0:T(8,128)(2,1)S(1)}, bf16[128,1280]{1,0:T(8,128)(2,1)S(1)}, bf16[160,128]{1,0:T(8,128)(2,1)S(1)}, bf16[160,128]{1,0:T(8,128)(2,1)S...) custom-call(bf16[80,1280]{1,0:T(8,128)(2,1)S(1)} %get-tuple-element.26.kept_ref, ...), custom_call_target="tpu_custom_call" | custom-call | flops 629145600 | bytes 4915200 | tf_op jit(solution)/shard_map/attend/pallas_call | solution.py:301
  8.9 1.6 %collective-permute-start.5 = (bf16[128,1280]{1,0:T(8,128)(2,1)S(1)}, bf16[128,1280]{1,0:T(8,128)(2,1)S(1)}, u32[]{:S(2)}, u32[]{:S(2)}) collective-permute-start(bf16[128,1280]{1,0:T(8,128)(2,1)S(1)} %get-tuple-element.37.refs_3_.refs_4_), channel_id=1, source_target_pairs={{0,16},{4,12},{8,24},{12,4},{16,0},{20,28},{24,8},{28,20},{1,17},{... | collective-permute-start | bytes 983048 | tf_op jit(solution)/shard_map/ppermute | solution.py:471
  10.5 1.4 %collective-permute-start.1 = (bf16[160,128]{1,0:T(8,128)(2,1)S(1)}, bf16[160,128]{1,0:T(8,128)(2,1)S(1)}, u32[]{:S(2)}, u32[]{:S(2)}) collective-permute-start(bf16[160,128]{1,0:T(8,128)(2,1)S(1)} %get-tuple-element.33), channel_id=1, source_target_pairs={{0,8},{4,20},{8,0},{12,28},{16,24},{20,4},{24,16},{28,12},{1,9},{5... | collective-permute-start | bytes 122888 | tf_op jit(solution)/shard_map/ppermute | solution.py:471
  11.9 0.5 %collective-permute-start.2 = (bf16[160,128]{1,0:T(8,128)(2,1)S(1)}, bf16[160,128]{1,0:T(8,128)(2,1)S(1)}, u32[]{:S(2)}, u32[]{:S(2)}) collective-permute-start(bf16[160,128]{1,0:T(8,128)(2,1)S(1)} %get-tuple-element.34), channel_id=1, source_target_pairs={{0,16},{4,12},{8,24},{12,4},{16,0},{20,28},{24,8},{28,20},{1,17},{... | collective-permute-start | bytes 122888 | tf_op jit(solution)/shard_map/ppermute | solution.py:471
  12.4 0.0 collective-permute-done.4.refs_4_.refs_5_
  12.4 1.6 %collective-permute-start.6 = (bf16[128,1280]{1,0:T(8,128)(2,1)S(1)}, bf16[128,1280]{1,0:T(8,128)(2,1)S(1)}, u32[]{:S(2)}, u32[]{:S(2)}) collective-permute-start(bf16[128,1280]{1,0:T(8,128)(2,1)S(1)} %collective-permute-done.4.refs_4_.refs_5_), channel_id=1, source_target_pairs={{0,16},{4,12},{8,24},{12,4},{16,0},{20,28},{24,8},{28,20},{1,17},{... | collective-permute-start | bytes 983048 | tf_op jit(solution)/shard_map/ppermute | solution.py:471
  14.0 0.6 %collective-permute-start.3 = (bf16[160,128]{1,0:T(8,128)(2,1)S(1)}, bf16[160,128]{1,0:T(8,128)(2,1)S(1)}, u32[]{:S(2)}, u32[]{:S(2)}) collective-permute-start(bf16[160,128]{1,0:T(8,128)(2,1)S(1)} %get-tuple-element.35), channel_id=1, source_target_pairs={{0,24},{4,28},{8,16},{12,20},{16,8},{20,12},{24,0},{28,4},{1,25},{... | collective-permute-start | bytes 122888 | tf_op jit(solution)/shard_map/ppermute | solution.py:471
  14.5 0.5 %collective-permute-done.1.refs_1_ = bf16[160,128]{1,0:T(8,128)(2,1)S(1)} collective-permute-done((bf16[160,128]{1,0:T(8,128)(2,1)S(1)}, bf16[160,128]{1,0:T(8,128)(2,1)S(1)}, u32[]{:S(2)}, u32[]{:S(2)}) %collective-permute-start.1) | collective-permute-done | bytes 40992 | tf_op jit(solution)/shard_map/ppermute | solution.py:471
  15.0 1.9 %collective-permute-done.2.refs_2_ = bf16[160,128]{1,0:T(8,128)(2,1)S(1)} collective-permute-done((bf16[160,128]{1,0:T(8,128)(2,1)S(1)}, bf16[160,128]{1,0:T(8,128)(2,1)S(1)}, u32[]{:S(2)}, u32[]{:S(2)}) %collective-permute-start.2) | collective-permute-done | bytes 40992 | tf_op jit(solution)/shard_map/ppermute | solution.py:471
  17.0 0.0 collective-permute-done.5.refs_5_.refs_6_
  17.0 0.4 %near_rows.1.refs_8_ = f32[160,1280]{1,0:T(8,128)S(1)} custom-call(bf16[160,128]{1,0:T(8,128)(2,1)S(1)} %get-tuple-element.32.refs_0_, bf16[160,128]{1,0:T(8,128)(2,1)S(1)} %collective-permute-done.1.refs_1_, bf16[160,128]{1,0:T(8,128)(2,1)S(1)} %collective-permute-done.2.refs_2_, bf16[128,1280]{1,0:T(8,128)(2,1)S(1)} %get-tuple-element.37.refs_3_.refs_4_, ...), custom_call_target="tpu_custom_call" | custom-call | flops 3145728000 | bytes 983040 | tf_op jit(solution)/shard_map/near_rows/pallas_call | solution.py:375
  17.4 0.0 copy-start
  17.4 2.0 %collective-permute-done.3.refs_3_ = bf16[160,128]{1,0:T(8,128)(2,1)S(1)} collective-permute-done((bf16[160,128]{1,0:T(8,128)(2,1)S(1)}, bf16[160,128]{1,0:T(8,128)(2,1)S(1)}, u32[]{:S(2)}, u32[]{:S(2)}) %collective-permute-start.3) | collective-permute-done | bytes 40992 | tf_op jit(solution)/shard_map/ppermute | solution.py:471
  19.4 1.6 %collective-permute-done.6.refs_7_ = bf16[128,1280]{1,0:T(8,128)(2,1)S(1)} collective-permute-done((bf16[128,1280]{1,0:T(8,128)(2,1)S(1)}, bf16[128,1280]{1,0:T(8,128)(2,1)S(1)}, u32[]{:S(2)}, u32[]{:S(2)}) %collective-permute-start.6) | collective-permute-done | bytes 327712 | tf_op jit(solution)/shard_map/ppermute | solution.py:471
  20.9 0.3 far_rows.1
  21.3 0.0 copy-start.1
  21.3 0.3 collective-permute-start.7
  21.6 1.2 %collective-permute-done.7.refs_1_ = bf16[80,1280]{1,0:T(8,128)(2,1)S(1)} collective-permute-done((bf16[80,1280]{1,0:T(8,128)(2,1)S(1)}, bf16[80,1280]{1,0:T(8,128)(2,1)S(1)}, u32[]{:S(2)}, u32[]{:S(2)}) %collective-permute-start.7) | collective-permute-done | bytes 204832 | tf_op jit(solution)/shard_map/ppermute | solution.py:466
  22.8 2.7 %collective-permute-start.12 = (bf16[80,640]{1,0:T(8,128)(2,1)S(1)}, bf16[80,640]{1,0:T(8,128)(2,1)S(1)}, u32[]{:S(2)}, u32[]{:S(2)}) collective-permute-start(bf16[80,640]{1,0:T(8,128)(2,1)S(1)} %get-tuple-element.47.refs_2_), channel_id=1, source_target_pairs={{0,2},{1,3},{2,0},{3,1},{4,6},{5,7},{6,4},{7,5},{8,10},{9,11},{10,... | collective-permute-start | bytes 307208 | tf_op jit(solution)/shard_map/ppermute | solution.py:466
  25.5 1.6 %collective-permute-start.11 = (bf16[80,640]{1,0:T(8,128)(2,1)S(1)}, bf16[80,640]{1,0:T(8,128)(2,1)S(1)}, u32[]{:S(2)}, u32[]{:S(2)}) collective-permute-start(bf16[80,640]{1,0:T(8,128)(2,1)S(1)} %get-tuple-element.41.refs_0_), channel_id=1, source_target_pairs={{0,1},{1,0},{2,3},{3,2},{4,5},{5,4},{6,7},{7,6},{8,9},{9,8},{10,11... | collective-permute-start | bytes 307208 | tf_op jit(solution)/shard_map/ppermute | solution.py:466
  27.1 0.0 copy-done
  27.1 0.5 %project.1 = (bf16[32,1280]{1,0:T(8,128)(2,1)S(1)}, bf16[32,1280]{1,0:T(8,128)(2,1)S(1)}, bf16[32,1280]{1,0:T(8,128)(2,1)S(1)}, bf16[32,1280]{1,0:T(8,128)(2,1)S(1)}) custom-call(bf16[640,128]{1,0:T(8,128)(2,1)S(1)} %get-tuple-element.28.attended_ref, bf16[128,1280]{1,0:T(8,128)(2,1)S(1)} %get-tuple-element.29.ordered_ref, bf16[640,1280]{1,0:T(8,128)(2,1)S(1)} %copy-done), custom_call_target="tpu_custom_call" | custom-call | flops 209715200 | bytes 1638400 | tf_op jit(solution)/shard_map/project/pallas_call | solution.py:331
  27.6 1.4 %collective-permute-start.8 = (bf16[32,1280]{1,0:T(8,128)(2,1)S(1)}, bf16[32,1280]{1,0:T(8,128)(2,1)S(1)}, u32[]{:S(2)}, u32[]{:S(2)}) collective-permute-start(bf16[32,1280]{1,0:T(8,128)(2,1)S(1)} %get-tuple-element.42), channel_id=1, source_target_pairs={{0,8},{4,20},{8,0},{12,28},{16,24},{20,4},{24,16},{28,12},{1,9},{5... | collective-permute-start | bytes 245768 | tf_op jit(solution)/shard_map/ppermute | solution.py:471
  29.0 1.5 %collective-permute-start.9 = (bf16[32,1280]{1,0:T(8,128)(2,1)S(1)}, bf16[32,1280]{1,0:T(8,128)(2,1)S(1)}, u32[]{:S(2)}, u32[]{:S(2)}) collective-permute-start(bf16[32,1280]{1,0:T(8,128)(2,1)S(1)} %get-tuple-element.44), channel_id=1, source_target_pairs={{0,16},{4,12},{8,24},{12,4},{16,0},{20,28},{24,8},{28,20},{1,17},{... | collective-permute-start | bytes 245768 | tf_op jit(solution)/shard_map/ppermute | solution.py:471
  30.5 0.6 %collective-permute-start.10 = (bf16[32,1280]{1,0:T(8,128)(2,1)S(1)}, bf16[32,1280]{1,0:T(8,128)(2,1)S(1)}, u32[]{:S(2)}, u32[]{:S(2)}) collective-permute-start(bf16[32,1280]{1,0:T(8,128)(2,1)S(1)} %get-tuple-element.46), channel_id=1, source_target_pairs={{0,24},{4,28},{8,16},{12,20},{16,8},{20,12},{24,0},{28,4},{1,25},{... | collective-permute-start | bytes 245768 | tf_op jit(solution)/shard_map/ppermute | solution.py:471
  31.1 0.0 collective-permute-done.12.refs_3_
  31.2 0.2 collective-permute-done.11.refs_1_
  31.4 0.1 add_halves.4
  31.4 1.4 %collective-permute-start.13 = (bf16[80,640]{1,0:T(8,128)(2,1)S(1)}, bf16[80,640]{1,0:T(8,128)(2,1)S(1)}, u32[]{:S(2)}, u32[]{:S(2)}) collective-permute-start(bf16[80,640]{1,0:T(8,128)(2,1)S(1)} %get-tuple-element.48.refs_0_), channel_id=1, source_target_pairs={{0,2},{1,3},{2,0},{3,1},{4,6},{5,7},{6,4},{7,5},{8,10},{9,11},{10,... | collective-permute-start | bytes 307208 | tf_op jit(solution)/shard_map/ppermute | solution.py:466
  32.8 2.4 %collective-permute-start.14 = (bf16[80,640]{1,0:T(8,128)(2,1)S(1)}, bf16[80,640]{1,0:T(8,128)(2,1)S(1)}, u32[]{:S(2)}, u32[]{:S(2)}) collective-permute-start(bf16[80,640]{1,0:T(8,128)(2,1)S(1)} %get-tuple-element.49.refs_2_), channel_id=1, source_target_pairs={{0,1},{1,0},{2,3},{3,2},{4,5},{5,4},{6,7},{7,6},{8,9},{9,8},{10,11... | collective-permute-start | bytes 307208 | tf_op jit(solution)/shard_map/ppermute | solution.py:466
  35.2 0.0 collective-permute-done.8.refs_1_
  35.2 0.0 collective-permute-done.9.refs_2_
  35.2 0.6 %collective-permute-done.10.refs_3_ = bf16[32,1280]{1,0:T(8,128)(2,1)S(1)} collective-permute-done((bf16[32,1280]{1,0:T(8,128)(2,1)S(1)}, bf16[32,1280]{1,0:T(8,128)(2,1)S(1)}, u32[]{:S(2)}, u32[]{:S(2)}) %collective-permute-start.10) | collective-permute-done | bytes 81952 | tf_op jit(solution)/shard_map/ppermute | solution.py:471
  35.9 0.0 copy-done.1
  35.9 1.8 %place_rows.1 = bf16[160,5120]{1,0:T(8,128)(2,1)} custom-call(s32[1,160]{1,0:T(1,128)S(1)} %bitcast.4, bf16[32,1280]{1,0:T(8,128)(2,1)S(1)} %get-tuple-element.30.refs_0_, bf16[32,1280]{1,0:T(8,128)(2,1)S(1)} %collective-permute-done.8.refs_1_, bf16[32,1280]{1,0:T(8,128)(2,1)S(1)} %collective-permute-done.9.refs_2_, ...), custom_call_target="tpu_custom_call" | custom-call | flops 20971520000 | bytes 1638400 | tf_op jit(solution)/shard_map/place_rows/pallas_call | solution.py:421
  37.7 1.0 %collective-permute-done.13.refs_1_ = bf16[80,640]{1,0:T(8,128)(2,1)S(1)} collective-permute-done((bf16[80,640]{1,0:T(8,128)(2,1)S(1)}, bf16[80,640]{1,0:T(8,128)(2,1)S(1)}, u32[]{:S(2)}, u32[]{:S(2)}) %collective-permute-start.13) | collective-permute-done | bytes 102432 | tf_op jit(solution)/shard_map/ppermute | solution.py:466
  38.7 0.4 %collective-permute-done.14.refs_3_ = bf16[80,640]{1,0:T(8,128)(2,1)S(1)} collective-permute-done((bf16[80,640]{1,0:T(8,128)(2,1)S(1)}, bf16[80,640]{1,0:T(8,128)(2,1)S(1)}, u32[]{:S(2)}, u32[]{:S(2)}) %collective-permute-start.14) | collective-permute-done | bytes 102432 | tf_op jit(solution)/shard_map/ppermute | solution.py:466
  39.1 0.8 %add_halves.5 = f32[80,1280]{1,0:T(8,128)} custom-call(bf16[80,640]{1,0:T(8,128)(2,1)S(1)} %get-tuple-element.48.refs_0_, bf16[80,640]{1,0:T(8,128)(2,1)S(1)} %collective-permute-done.13.refs_1_, bf16[80,640]{1,0:T(8,128)(2,1)S(1)} %get-tuple-element.49.refs_2_, bf16[80,640]{1,0:T(8,128)(2,1)S(1)} %collective-permute-done.14.refs_3_), custom_call_target="tpu_custom_call" | custom-call | flops 102400 | bytes 819200 | tf_op jit(solution)/shard_map/add_halves/pallas_call | solution.py:449
  (2 shorter events, 0.0 us)
Async XLA Ops:
  0.6 5.3 %slice-start = ((s8[4915200]{0:T(1024)(128)(4,1)}), s8[4194304]{0:T(1024)(128)(4,1)S(1)}, s32[]{:S(2)}) async-start(s8[4915200]{0:T(1024)(128)(4,1)} %bitcast.1), calls=%async_computation | async-start | bytes 8388608
  0.6 5.3 %slice-start.1 = ((s8[4915200]{0:T(1024)(128)(4,1)}), s8[720896]{0:T(1024)(128)(4,1)S(1)}, s32[]{:S(2)}) async-start(s8[4915200]{0:T(1024)(128)(4,1)} %bitcast.1), calls=%async_computation.1 | async-start | bytes 1441792
  2.8 3.1 %collective-permute-start = (bf16[80,1280]{1,0:T(8,128)(2,1)S(1)}, bf16[80,1280]{1,0:T(8,128)(2,1)S(1)}, u32[]{:S(2)}, u32[]{:S(2)}) collective-permute-start(bf16[80,1280]{1,0:T(8,128)(2,1)S(1)} %get-tuple-element.27), channel_id=1, source_target_pairs={{0,4},{4,0},{8,12},{12,8},{16,20},{20,16},{24,28},{28,24},{1,5},{5... | collective-permute-start | bytes 614408 | tf_op jit(solution)/shard_map/ppermute | solution.py:466
  3.3 9.1 %collective-permute-start.4 = (bf16[128,1280]{1,0:T(8,128)(2,1)S(1)}, bf16[128,1280]{1,0:T(8,128)(2,1)S(1)}, u32[]{:S(2)}, u32[]{:S(2)}) collective-permute-start(bf16[128,1280]{1,0:T(8,128)(2,1)S(1)} %get-tuple-element.37.refs_3_.refs_4_), channel_id=1, source_target_pairs={{0,8},{4,20},{8,0},{12,28},{16,24},{20,4},{24,16},{28,12},{1,9},{5... | collective-permute-start | bytes 983048 | tf_op jit(solution)/shard_map/ppermute | solution.py:471
  8.9 8.0 %collective-permute-start.5 = (bf16[128,1280]{1,0:T(8,128)(2,1)S(1)}, bf16[128,1280]{1,0:T(8,128)(2,1)S(1)}, u32[]{:S(2)}, u32[]{:S(2)}) collective-permute-start(bf16[128,1280]{1,0:T(8,128)(2,1)S(1)} %get-tuple-element.37.refs_3_.refs_4_), channel_id=1, source_target_pairs={{0,16},{4,12},{8,24},{12,4},{16,0},{20,28},{24,8},{28,20},{1,17},{... | collective-permute-start | bytes 983048 | tf_op jit(solution)/shard_map/ppermute | solution.py:471
  10.5 4.5 %collective-permute-start.1 = (bf16[160,128]{1,0:T(8,128)(2,1)S(1)}, bf16[160,128]{1,0:T(8,128)(2,1)S(1)}, u32[]{:S(2)}, u32[]{:S(2)}) collective-permute-start(bf16[160,128]{1,0:T(8,128)(2,1)S(1)} %get-tuple-element.33), channel_id=1, source_target_pairs={{0,8},{4,20},{8,0},{12,28},{16,24},{20,4},{24,16},{28,12},{1,9},{5... | collective-permute-start | bytes 122888 | tf_op jit(solution)/shard_map/ppermute | solution.py:471
  11.9 5.0 %collective-permute-start.2 = (bf16[160,128]{1,0:T(8,128)(2,1)S(1)}, bf16[160,128]{1,0:T(8,128)(2,1)S(1)}, u32[]{:S(2)}, u32[]{:S(2)}) collective-permute-start(bf16[160,128]{1,0:T(8,128)(2,1)S(1)} %get-tuple-element.34), channel_id=1, source_target_pairs={{0,16},{4,12},{8,24},{12,4},{16,0},{20,28},{24,8},{28,20},{1,17},{... | collective-permute-start | bytes 122888 | tf_op jit(solution)/shard_map/ppermute | solution.py:471
  12.4 8.5 %collective-permute-start.6 = (bf16[128,1280]{1,0:T(8,128)(2,1)S(1)}, bf16[128,1280]{1,0:T(8,128)(2,1)S(1)}, u32[]{:S(2)}, u32[]{:S(2)}) collective-permute-start(bf16[128,1280]{1,0:T(8,128)(2,1)S(1)} %collective-permute-done.4.refs_4_.refs_5_), channel_id=1, source_target_pairs={{0,16},{4,12},{8,24},{12,4},{16,0},{20,28},{24,8},{28,20},{1,17},{... | collective-permute-start | bytes 983048 | tf_op jit(solution)/shard_map/ppermute | solution.py:471
  14.0 5.4 %collective-permute-start.3 = (bf16[160,128]{1,0:T(8,128)(2,1)S(1)}, bf16[160,128]{1,0:T(8,128)(2,1)S(1)}, u32[]{:S(2)}, u32[]{:S(2)}) collective-permute-start(bf16[160,128]{1,0:T(8,128)(2,1)S(1)} %get-tuple-element.35), channel_id=1, source_target_pairs={{0,24},{4,28},{8,16},{12,20},{16,8},{20,12},{24,0},{28,4},{1,25},{... | collective-permute-start | bytes 122888 | tf_op jit(solution)/shard_map/ppermute | solution.py:471
  17.4 9.7 %copy-start = (bf16[640,1280]{1,0:T(8,128)(2,1)S(1)}, bf16[640,1280]{1,0:T(8,128)(2,1)}, u32[]{:S(2)}) copy-start(bf16[640,1280]{1,0:T(8,128)(2,1)} %w_ref.3) | copy-start | bytes 4915204
  21.3 14.6 %copy-start.1 = (s32[160]{0:T(256)S(1)}, s32[160]{0:T(256)}, u32[]{:S(2)}) copy-start(s32[160]{0:T(256)} %param.11) | copy-start | bytes 1924
  21.3 1.5 %collective-permute-start.7 = (bf16[80,1280]{1,0:T(8,128)(2,1)S(1)}, bf16[80,1280]{1,0:T(8,128)(2,1)S(1)}, u32[]{:S(2)}, u32[]{:S(2)}) collective-permute-start(bf16[80,1280]{1,0:T(8,128)(2,1)S(1)} %get-tuple-element.40), channel_id=1, source_target_pairs={{0,4},{4,0},{8,12},{12,8},{16,20},{20,16},{24,28},{28,24},{1,5},{5... | collective-permute-start | bytes 614408 | tf_op jit(solution)/shard_map/ppermute | solution.py:466
  22.8 8.3 %collective-permute-start.12 = (bf16[80,640]{1,0:T(8,128)(2,1)S(1)}, bf16[80,640]{1,0:T(8,128)(2,1)S(1)}, u32[]{:S(2)}, u32[]{:S(2)}) collective-permute-start(bf16[80,640]{1,0:T(8,128)(2,1)S(1)} %get-tuple-element.47.refs_2_), channel_id=1, source_target_pairs={{0,2},{1,3},{2,0},{3,1},{4,6},{5,7},{6,4},{7,5},{8,10},{9,11},{10,... | collective-permute-start | bytes 307208 | tf_op jit(solution)/shard_map/ppermute | solution.py:466
  25.5 5.9 %collective-permute-start.11 = (bf16[80,640]{1,0:T(8,128)(2,1)S(1)}, bf16[80,640]{1,0:T(8,128)(2,1)S(1)}, u32[]{:S(2)}, u32[]{:S(2)}) collective-permute-start(bf16[80,640]{1,0:T(8,128)(2,1)S(1)} %get-tuple-element.41.refs_0_), channel_id=1, source_target_pairs={{0,1},{1,0},{2,3},{3,2},{4,5},{5,4},{6,7},{7,6},{8,9},{9,8},{10,11... | collective-permute-start | bytes 307208 | tf_op jit(solution)/shard_map/ppermute | solution.py:466
  27.6 7.7 %collective-permute-start.8 = (bf16[32,1280]{1,0:T(8,128)(2,1)S(1)}, bf16[32,1280]{1,0:T(8,128)(2,1)S(1)}, u32[]{:S(2)}, u32[]{:S(2)}) collective-permute-start(bf16[32,1280]{1,0:T(8,128)(2,1)S(1)} %get-tuple-element.42), channel_id=1, source_target_pairs={{0,8},{4,20},{8,0},{12,28},{16,24},{20,4},{24,16},{28,12},{1,9},{5... | collective-permute-start | bytes 245768 | tf_op jit(solution)/shard_map/ppermute | solution.py:471
  29.0 6.2 %collective-permute-start.9 = (bf16[32,1280]{1,0:T(8,128)(2,1)S(1)}, bf16[32,1280]{1,0:T(8,128)(2,1)S(1)}, u32[]{:S(2)}, u32[]{:S(2)}) collective-permute-start(bf16[32,1280]{1,0:T(8,128)(2,1)S(1)} %get-tuple-element.44), channel_id=1, source_target_pairs={{0,16},{4,12},{8,24},{12,4},{16,0},{20,28},{24,8},{28,20},{1,17},{... | collective-permute-start | bytes 245768 | tf_op jit(solution)/shard_map/ppermute | solution.py:471
  30.5 5.3 %collective-permute-start.10 = (bf16[32,1280]{1,0:T(8,128)(2,1)S(1)}, bf16[32,1280]{1,0:T(8,128)(2,1)S(1)}, u32[]{:S(2)}, u32[]{:S(2)}) collective-permute-start(bf16[32,1280]{1,0:T(8,128)(2,1)S(1)} %get-tuple-element.46), channel_id=1, source_target_pairs={{0,24},{4,28},{8,16},{12,20},{16,8},{20,12},{24,0},{28,4},{1,25},{... | collective-permute-start | bytes 245768 | tf_op jit(solution)/shard_map/ppermute | solution.py:471
  31.4 7.3 %collective-permute-start.13 = (bf16[80,640]{1,0:T(8,128)(2,1)S(1)}, bf16[80,640]{1,0:T(8,128)(2,1)S(1)}, u32[]{:S(2)}, u32[]{:S(2)}) collective-permute-start(bf16[80,640]{1,0:T(8,128)(2,1)S(1)} %get-tuple-element.48.refs_0_), channel_id=1, source_target_pairs={{0,2},{1,3},{2,0},{3,1},{4,6},{5,7},{6,4},{7,5},{8,10},{9,11},{10,... | collective-permute-start | bytes 307208 | tf_op jit(solution)/shard_map/ppermute | solution.py:466
  32.8 6.3 %collective-permute-start.14 = (bf16[80,640]{1,0:T(8,128)(2,1)S(1)}, bf16[80,640]{1,0:T(8,128)(2,1)S(1)}, u32[]{:S(2)}, u32[]{:S(2)}) collective-permute-start(bf16[80,640]{1,0:T(8,128)(2,1)S(1)} %get-tuple-element.49.refs_2_), channel_id=1, source_target_pairs={{0,1},{1,0},{2,3},{3,2},{4,5},{5,4},{6,7},{7,6},{8,9},{9,8},{10,11... | collective-permute-start | bytes 307208 | tf_op jit(solution)/shard_map/ppermute | solution.py:466

commit v8 on v7

--- a/solution.py
+++ b/solution.py
@@ -233,13 +233,49 @@
     )
 
 
-def attend_kernel(
-    kept_ref, given_ref, gain_ref, w_ref, *refs
-):
-    attended_ref, ordered_ref = refs[:2]
-    sent_refs = refs[2:-1]
-    sent = refs[-1]
-    rows, width = ordered_ref.shape
+def qkv_kernel(kept_ref, given_ref, gain_ref, w_ref, qkv_ref, ordered_ref):
+    rows = ordered_ref.shape[0]
+    pairs = 1 << PAIR_BITS
+    window_rows = rows // (2 * pairs)
+    core = lax.axis_index("enc") % 2
+    for ref, side in ((kept_ref, core), (given_ref, 1 - core)):
+        for b in range(pairs):
+            ordered_ref[place(2 * b + side, window_rows), :] = ref[
+                b * window_rows : (b + 1) * window_rows, :
+            ]
+    values = ordered_ref[...].astype(jnp.float32)
+    mean_square = jnp.mean(values * values, axis=-1, keepdims=True)
+    normed = (values * lax.rsqrt(mean_square + 1e-06) * gain_ref[...][None, :]).astype(
+        jnp.bfloat16
+    )
+    inner = w_ref.shape[1] // 3
+    for part in range(3):
+        columns = slice(part * inner, (part + 1) * inner)
+        qkv_ref[:, columns] = jnp.dot(
+            normed, w_ref[:, columns], preferred_element_type=jnp.float32
+        ).astype(jnp.bfloat16)
+
+
+def qkv_ordered(kept, given, gain, w_qkv):
+    width = kept.shape[1]
+    rows = 2 * (kept.shape[0] - SUBLANES)
+    return pl.pallas_call(
+        qkv_kernel,
+        out_shape=(
+            jax.ShapeDtypeStruct((rows, w_qkv.shape[1]), jnp.bfloat16),
+            jax.ShapeDtypeStruct((rows, width), jnp.bfloat16),
+        ),
+        in_specs=[VMEM] * 4,
+        out_specs=(VMEM,) * 2,
+        compiler_params=params(24),
+        cost_estimate=cost(2 * rows * w_qkv.size, 2 * w_qkv.size),
+        name="qkv",
+    )(kept, given, in_hbm(gain), in_vmem(w_qkv))
+
+
+def attend_kernel(kept_ref, given_ref, qkv_ref, *refs):
+    attended_ref, sent_refs, sent = refs[0], refs[1:-1], refs[-1]
+    rows = qkv_ref.shape[0]
     pairs = len(sent_refs)
     window_rows = rows // (2 * pairs)
     inner = attended_ref.shape[0]
@@ -251,24 +287,11 @@
     for ref, side in ((kept_ref, core), (given_ref, 1 - core)):
         lengths = ref[rows // 2 :, :rows].astype(jnp.float32)
         for b in range(pairs):
-            window = 2 * b + side
-            ordered_ref[place(window, window_rows), :] = ref[
-                b * window_rows : (b + 1) * window_rows, :
-            ]
-            live = jnp.where(key_window == window, lengths[b : b + 1], live)
+            live = jnp.where(key_window == 2 * b + side, lengths[b : b + 1], live)
     allowed = (key_window == iota((rows, rows), 1) // window_rows) & (
         (key_row % window_rows).astype(jnp.float32) < live
     )
-    values = ordered_ref[...].astype(jnp.float32)
-    mean_square = jnp.mean(values * values, axis=-1, keepdims=True)
-    normed = (values * lax.rsqrt(mean_square + 1e-06) * gain_ref[...][None, :]).astype(jnp.bfloat16)
-    projected = []
-    for part in range(3):
-        columns = w_ref[:, part * inner : (part + 1) * inner]
-        projected.append(jnp.dot(normed, columns, preferred_element_type=jnp.float32))
-    queries = projected[0].astype(jnp.bfloat16)
-    keys_all = projected[1].astype(jnp.bfloat16)
-    values_across = projected[2].T.astype(jnp.bfloat16)
+    values_across = qkv_ref[:, 2 * inner :].astype(jnp.float32).T.astype(jnp.bfloat16)
     scale = 1.0 / math.sqrt(HD)
     for head in range(inner // HD):
         first = head * HD
@@ -276,9 +299,10 @@
         high = -(-(first + HD) // LANES) * LANES
         lane = iota((rows, high - low), 1) + low
         own = (lane >= first) & (lane < first + HD)
-        keys = jnp.where(own, keys_all[:, low:high], jnp.zeros((), jnp.bfloat16))
+        keys = qkv_ref[:, inner + low : inner + high]
+        keys = jnp.where(own, keys, jnp.zeros((), jnp.bfloat16))
         scores = lax.dot_general(
-            keys, queries[:, low:high], ROWS_WITH_ROWS, preferred_element_type=jnp.float32
+            keys, qkv_ref[:, low:high], ROWS_WITH_ROWS, preferred_element_type=jnp.float32
         )
         scores = jnp.where(allowed, scores * scale, -1e30)
         raised = jnp.exp(scores - jnp.max(scores, axis=0, keepdims=True))
@@ -293,27 +317,21 @@
         sent_refs[b][...] = sent[b]
 
 
-def attend_ordered(kept, given, gain, w_qkv, pairs):
-    width = kept.shape[1]
-    rows = 2 * (kept.shape[0] - SUBLANES)
-    inner = w_qkv.shape[1] // 3
+def attend_ordered(kept, given, qkv, pairs):
+    rows = qkv.shape[0]
+    inner = qkv.shape[1] // 3
     heads = inner // pairs
     return pl.pallas_call(
         attend_kernel,
-        out_shape=(
-            jax.ShapeDtypeStruct((inner, rows), jnp.bfloat16),
-            jax.ShapeDtypeStruct((rows, width), jnp.bfloat16),
-        )
+        out_shape=(jax.ShapeDtypeStruct((inner, rows), jnp.bfloat16),)
         + (jax.ShapeDtypeStruct((heads, rows), jnp.bfloat16),) * pairs,
-        in_specs=[VMEM] * 4,
-        out_specs=(VMEM,) * (2 + pairs),
-        scratch_shapes=[
-            pltpu.VMEM((pairs, heads, rows), jnp.bfloat16),
-        ],
+        in_specs=[VMEM] * 3,
+        out_specs=(VMEM,) * (1 + pairs),
+        scratch_shapes=[pltpu.VMEM((pairs, heads, rows), jnp.bfloat16)],
         compiler_params=params(24),
-        cost_estimate=cost(2 * rows * width * 3 * inner, 2 * w_qkv.size),
+        cost_estimate=cost(4 * rows * rows * inner, 6 * rows * inner),
         name="attend",
-    )(kept, given, in_hbm(gain), in_vmem(w_qkv))
+    )(kept, given, qkv)
 
 
 def project_kernel(attended_ref, ordered_ref, w_ref, *encoded_refs):
@@ -479,8 +497,9 @@
 
     held, kept, given = pick_rows(window_owner, window_len, slot_token, pixels, cotangent)
     given = swap(given, "enc", 1)
-    attended, ordered, *sent = attend_ordered(kept, given, gain, w_qkv, pairs)
-    blocks = [held, chip_swap(held, 1), chip_swap(after(held, attended), 2)]
+    qkv, ordered = qkv_ordered(kept, given, gain, w_qkv)
+    attended, *sent = attend_ordered(kept, given, qkv, pairs)
+    blocks = [held, chip_swap(held, 1), chip_swap(after(held, qkv), 2)]
     blocks.append(chip_swap(after(blocks[1], attended), 2))
     columns = [sent[0]] + [chip_swap(sent[b], b) for b in range(1, pairs)]
     encoded = project_ordered(attended, ordered, w_out, pairs)

time: 40.1 us -> 40 us (level)
  waiting for transfers between devices: 9.47 us -> 8.14 us
  starting transfers between devices: 20.6 us -> 21.4 us
    pallas_call x0 -> x1, Pallas kernels: none -> 1.77 us  [qkv_ordered(): pl.pallas_call(qkv_kernel, out_shape=(jax.ShapeDtypeStruct((rows, w_qkv.s...]
    ppermute x9, waiting for transfers between devices: 6.59 us -> 5.06 us  [chip_swap(): lax.ppermute(value, 'enc', [(i, i ^ 2 * turn(relative, i % 2)) for i in r...]
    pallas_call x1, Pallas kernels: 3.04 us -> 1.66 us  [attend_ordered(): pl.pallas_call(attend_kernel, out_shape=(jax.ShapeDtypeStruct((inner, row...]
    ppermute x6, starting transfers between devices: 8.89 us -> 9.31 us  [swap(): return lax.ppermute(value, axis, [(i, i ^ bits) for i in range(size)])]
  transfers between devices with their start and end apart: 15 -> 15, of which waited for: 9 -> 10; matrix products, arithmetic and copies ran while one was open for 0% -> 0% of each run, Pallas kernels for 15% -> 16%
where the time goes in v8:
time: 40 us; the launch traced here: 39.8 us
  starting transfers between devices  21.4 us (54%)
  Pallas kernels  9.52 us (24%)
  waiting for transfers between devices  8.14 us (20%)
  between operations  0.74 us (2%)
    ppermute x9, starting transfers between devices, chip_swap(): lax.ppermute(value, 'enc', [(i, i ^ 2 * turn(relative, i % 2)) for i in r...  12.1 us
    ppermute x6, starting transfers between devices, swap(): return lax.ppermute(value, axis, [(i, i ^ bits) for i in range(size)])  9.31 us
    ppermute x9, waiting for transfers between devices, chip_swap(): lax.ppermute(value, 'enc', [(i, i ^ 2 * turn(relative, i % 2)) for i in r...  5.06 us
    ppermute x6, waiting for transfers between devices, swap(): return lax.ppermute(value, axis, [(i, i ^ bits) for i in range(size)])  3.07 us
    pallas_call x1, Pallas kernels, pick_rows(): pl.pallas_call(pick_kernel, out_shape=(jax.ShapeDtypeStruct((rows, width)...  2.15 us
    pallas_call x1, Pallas kernels, place_rows(): pl.pallas_call(place_kernel, out_shape=jax.ShapeDtypeStruct((tokens, MERG...  1.83 us
    pallas_call x1, Pallas kernels, qkv_ordered(): pl.pallas_call(qkv_kernel, out_shape=(jax.ShapeDtypeStruct((rows, w_qkv.s...  1.77 us
    pallas_call x1, Pallas kernels, attend_ordered(): pl.pallas_call(attend_kernel, out_shape=(jax.ShapeDtypeStruct((inner, row...  1.66 us
  transfers between devices with their start and end apart: 15, of which 10 were waited for; matrix products, arithmetic and copies ran while one was open for 0% of the time, Pallas kernels for 16%

profile of v8, /device:TPU:0, one launch (start us, length us, event | category | flops | bytes accessed | tf_op | source)
XLA Modules:
  0.0 39.8 jit_solution(1986403509672572040)
XLA Ops:
  0.6 0.0 slice-start
  0.6 0.0 slice-start.1
  0.7 2.1 %pick_rows.1 = (bf16[128,1280]{1,0:T(8,128)(2,1)S(1)}, bf16[80,1280]{1,0:T(8,128)(2,1)S(1)}, bf16[80,1280]{1,0:T(8,128)(2,1)S(1)}) custom-call(s32[8]{0:T(128)} %owner_hbm.1, s32[8]{0:T(128)} %len_hbm.1, s32[1,160]{1,0:T(1,128)} %bitcast.3, bf16[128,1280]{1,0:T(8,128)(2,1)} %pixels_hbm.1, bf16[160,5120]{1,0:T(8,128)(2,1)} %cotangent_hbm.1), custom_call_target="tpu_custom_call" | custom-call | flops 20971520000 | bytes 1638400 | tf_op jit(solution)/shard_map/pick_rows/pallas_call | solution.py:210
  2.8 0.5 %collective-permute-start = (bf16[80,1280]{1,0:T(8,128)(2,1)S(1)}, bf16[80,1280]{1,0:T(8,128)(2,1)S(1)}, u32[]{:S(2)}, u32[]{:S(2)}) collective-permute-start(bf16[80,1280]{1,0:T(8,128)(2,1)S(1)} %get-tuple-element.28), channel_id=1, source_target_pairs={{0,4},{4,0},{8,12},{12,8},{16,20},{20,16},{24,28},{28,24},{1,5},{5... | collective-permute-start | bytes 614408 | tf_op jit(solution)/shard_map/ppermute | solution.py:484
  3.3 2.6 %collective-permute-start.4 = (bf16[128,1280]{1,0:T(8,128)(2,1)S(1)}, bf16[128,1280]{1,0:T(8,128)(2,1)S(1)}, u32[]{:S(2)}, u32[]{:S(2)}) collective-permute-start(bf16[128,1280]{1,0:T(8,128)(2,1)S(1)} %get-tuple-element.39.refs_3_.refs_4_), channel_id=1, source_target_pairs={{0,8},{4,20},{8,0},{12,28},{16,24},{20,4},{24,16},{28,12},{1,9},{5... | collective-permute-start | bytes 983048 | tf_op jit(solution)/shard_map/ppermute | solution.py:489
  5.9 0.0 collective-permute-done.given_ref
  5.9 0.0 slice-done
  5.9 0.0 slice-done.1
  5.9 1.8 %qkv.1 = (bf16[128,1920]{1,0:T(8,128)(2,1)S(1)}, bf16[128,1280]{1,0:T(8,128)(2,1)S(1)}) custom-call(bf16[80,1280]{1,0:T(8,128)(2,1)S(1)} %get-tuple-element.27.kept_ref, bf16[80,1280]{1,0:T(8,128)(2,1)S(1)} %collective-permute-done.given_ref, f32[1280]{0:T(1024)} %gain_ref.1, bf16[1280,1920]{1,0:T(8,128)(2,1)S(1)} %bitcast.2), custom_call_target="tpu_custom_call" | custom-call | flops 629145600 | bytes 4915200 | tf_op jit(solution)/shard_map/qkv/pallas_call | solution.py:262
  7.7 1.6 %collective-permute-start.5 = (bf16[128,1280]{1,0:T(8,128)(2,1)S(1)}, bf16[128,1280]{1,0:T(8,128)(2,1)S(1)}, u32[]{:S(2)}, u32[]{:S(2)}) collective-permute-start(bf16[128,1280]{1,0:T(8,128)(2,1)S(1)} %get-tuple-element.39.refs_3_.refs_4_), channel_id=1, source_target_pairs={{0,16},{4,12},{8,24},{12,4},{16,0},{20,28},{24,8},{28,20},{1,17},{... | collective-permute-start | bytes 983048 | tf_op jit(solution)/shard_map/ppermute | solution.py:489
  9.3 1.7 %attend.1 = (bf16[640,128]{1,0:T(8,128)(2,1)S(1)}, bf16[160,128]{1,0:T(8,128)(2,1)S(1)}, bf16[160,128]{1,0:T(8,128)(2,1)S(1)}, bf16[160,128]{1,0:T(8,128)(2,1)S(1)}, bf16[160,128]{1,0:T(8,128)(2,1)S(1)}) custom-call(bf16[80,1280]{1,0:T(8,128)(2,1)S(1)} %get-tuple-element.27.kept_ref, bf16[80,1280]{1,0:T(8,128)(2,1)S(1)} %collective-permute-done.given_ref, ...), custom_call_target="tpu_custom_call" | custom-call | flops 41943040 | bytes 491520 | tf_op jit(solution)/shard_map/attend/pallas_call | solution.py:324
  10.9 1.4 %collective-permute-start.1 = (bf16[160,128]{1,0:T(8,128)(2,1)S(1)}, bf16[160,128]{1,0:T(8,128)(2,1)S(1)}, u32[]{:S(2)}, u32[]{:S(2)}) collective-permute-start(bf16[160,128]{1,0:T(8,128)(2,1)S(1)} %get-tuple-element.35), channel_id=1, source_target_pairs={{0,8},{4,20},{8,0},{12,28},{16,24},{20,4},{24,16},{28,12},{1,9},{5... | collective-permute-start | bytes 122888 | tf_op jit(solution)/shard_map/ppermute | solution.py:489
  12.3 0.5 %collective-permute-start.2 = (bf16[160,128]{1,0:T(8,128)(2,1)S(1)}, bf16[160,128]{1,0:T(8,128)(2,1)S(1)}, u32[]{:S(2)}, u32[]{:S(2)}) collective-permute-start(bf16[160,128]{1,0:T(8,128)(2,1)S(1)} %get-tuple-element.36), channel_id=1, source_target_pairs={{0,16},{4,12},{8,24},{12,4},{16,0},{20,28},{24,8},{28,20},{1,17},{... | collective-permute-start | bytes 122888 | tf_op jit(solution)/shard_map/ppermute | solution.py:489
  12.8 0.0 collective-permute-done.4.refs_4_.refs_5_
  12.9 1.5 %collective-permute-start.6 = (bf16[128,1280]{1,0:T(8,128)(2,1)S(1)}, bf16[128,1280]{1,0:T(8,128)(2,1)S(1)}, u32[]{:S(2)}, u32[]{:S(2)}) collective-permute-start(bf16[128,1280]{1,0:T(8,128)(2,1)S(1)} %collective-permute-done.4.refs_4_.refs_5_), channel_id=1, source_target_pairs={{0,16},{4,12},{8,24},{12,4},{16,0},{20,28},{24,8},{28,20},{1,17},{... | collective-permute-start | bytes 983048 | tf_op jit(solution)/shard_map/ppermute | solution.py:489
  14.4 0.9 %collective-permute-start.3 = (bf16[160,128]{1,0:T(8,128)(2,1)S(1)}, bf16[160,128]{1,0:T(8,128)(2,1)S(1)}, u32[]{:S(2)}, u32[]{:S(2)}) collective-permute-start(bf16[160,128]{1,0:T(8,128)(2,1)S(1)} %get-tuple-element.37), channel_id=1, source_target_pairs={{0,24},{4,28},{8,16},{12,20},{16,8},{20,12},{24,0},{28,4},{1,25},{... | collective-permute-start | bytes 122888 | tf_op jit(solution)/shard_map/ppermute | solution.py:489
  15.3 0.1 collective-permute-done.1.refs_1_
  15.4 0.9 %collective-permute-done.2.refs_2_ = bf16[160,128]{1,0:T(8,128)(2,1)S(1)} collective-permute-done((bf16[160,128]{1,0:T(8,128)(2,1)S(1)}, bf16[160,128]{1,0:T(8,128)(2,1)S(1)}, u32[]{:S(2)}, u32[]{:S(2)}) %collective-permute-start.2) | collective-permute-done | bytes 40992 | tf_op jit(solution)/shard_map/ppermute | solution.py:489
  16.3 0.0 collective-permute-done.5.refs_5_.refs_6_
  16.3 0.4 %near_rows.1.refs_8_ = f32[160,1280]{1,0:T(8,128)S(1)} custom-call(bf16[160,128]{1,0:T(8,128)(2,1)S(1)} %get-tuple-element.34.refs_0_, bf16[160,128]{1,0:T(8,128)(2,1)S(1)} %collective-permute-done.1.refs_1_, bf16[160,128]{1,0:T(8,128)(2,1)S(1)} %collective-permute-done.2.refs_2_, bf16[128,1280]{1,0:T(8,128)(2,1)S(1)} %get-tuple-element.39.refs_3_.refs_4_, ...), custom_call_target="tpu_custom_call" | custom-call | flops 3145728000 | bytes 983040 | tf_op jit(solution)/shard_map/near_rows/pallas_call | solution.py:393
  16.8 0.0 copy-start
  16.8 3.0 %collective-permute-done.3.refs_3_ = bf16[160,128]{1,0:T(8,128)(2,1)S(1)} collective-permute-done((bf16[160,128]{1,0:T(8,128)(2,1)S(1)}, bf16[160,128]{1,0:T(8,128)(2,1)S(1)}, u32[]{:S(2)}, u32[]{:S(2)}) %collective-permute-start.3) | collective-permute-done | bytes 40992 | tf_op jit(solution)/shard_map/ppermute | solution.py:489
  19.8 0.6 %collective-permute-done.6.refs_7_ = bf16[128,1280]{1,0:T(8,128)(2,1)S(1)} collective-permute-done((bf16[128,1280]{1,0:T(8,128)(2,1)S(1)}, bf16[128,1280]{1,0:T(8,128)(2,1)S(1)}, u32[]{:S(2)}, u32[]{:S(2)}) %collective-permute-start.6) | collective-permute-done | bytes 327712 | tf_op jit(solution)/shard_map/ppermute | solution.py:489
  20.4 0.3 far_rows.1
  20.7 0.0 copy-start.1
  20.7 0.7 %collective-permute-start.7 = (bf16[80,1280]{1,0:T(8,128)(2,1)S(1)}, bf16[80,1280]{1,0:T(8,128)(2,1)S(1)}, u32[]{:S(2)}, u32[]{:S(2)}) collective-permute-start(bf16[80,1280]{1,0:T(8,128)(2,1)S(1)} %get-tuple-element.42), channel_id=1, source_target_pairs={{0,4},{4,0},{8,12},{12,8},{16,20},{20,16},{24,28},{28,24},{1,5},{5... | collective-permute-start | bytes 614408 | tf_op jit(solution)/shard_map/ppermute | solution.py:484
  21.5 1.1 %collective-permute-done.7.refs_1_ = bf16[80,1280]{1,0:T(8,128)(2,1)S(1)} collective-permute-done((bf16[80,1280]{1,0:T(8,128)(2,1)S(1)}, bf16[80,1280]{1,0:T(8,128)(2,1)S(1)}, u32[]{:S(2)}, u32[]{:S(2)}) %collective-permute-start.7) | collective-permute-done | bytes 204832 | tf_op jit(solution)/shard_map/ppermute | solution.py:484
  22.6 2.7 %collective-permute-start.12 = (bf16[80,640]{1,0:T(8,128)(2,1)S(1)}, bf16[80,640]{1,0:T(8,128)(2,1)S(1)}, u32[]{:S(2)}, u32[]{:S(2)}) collective-permute-start(bf16[80,640]{1,0:T(8,128)(2,1)S(1)} %get-tuple-element.49.refs_2_), channel_id=1, source_target_pairs={{0,2},{1,3},{2,0},{3,1},{4,6},{5,7},{6,4},{7,5},{8,10},{9,11},{10,... | collective-permute-start | bytes 307208 | tf_op jit(solution)/shard_map/ppermute | solution.py:484
  25.3 1.6 %collective-permute-start.11 = (bf16[80,640]{1,0:T(8,128)(2,1)S(1)}, bf16[80,640]{1,0:T(8,128)(2,1)S(1)}, u32[]{:S(2)}, u32[]{:S(2)}) collective-permute-start(bf16[80,640]{1,0:T(8,128)(2,1)S(1)} %get-tuple-element.43.refs_0_), channel_id=1, source_target_pairs={{0,1},{1,0},{2,3},{3,2},{4,5},{5,4},{6,7},{7,6},{8,9},{9,8},{10,11... | collective-permute-start | bytes 307208 | tf_op jit(solution)/shard_map/ppermute | solution.py:484
  26.8 0.0 copy-done
  26.8 0.5 %project.1 = (bf16[32,1280]{1,0:T(8,128)(2,1)S(1)}, bf16[32,1280]{1,0:T(8,128)(2,1)S(1)}, bf16[32,1280]{1,0:T(8,128)(2,1)S(1)}, bf16[32,1280]{1,0:T(8,128)(2,1)S(1)}) custom-call(bf16[640,128]{1,0:T(8,128)(2,1)S(1)} %get-tuple-element.30.attended_ref, bf16[128,1280]{1,0:T(8,128)(2,1)S(1)} %get-tuple-element.31.ordered_ref, bf16[640,1280]{1,0:T(8,128)(2,1)S(1)} %copy-done), custom_call_target="tpu_custom_call" | custom-call | flops 209715200 | bytes 1638400 | tf_op jit(solution)/shard_map/project/pallas_call | solution.py:349
  27.3 1.6 %collective-permute-start.8 = (bf16[32,1280]{1,0:T(8,128)(2,1)S(1)}, bf16[32,1280]{1,0:T(8,128)(2,1)S(1)}, u32[]{:S(2)}, u32[]{:S(2)}) collective-permute-start(bf16[32,1280]{1,0:T(8,128)(2,1)S(1)} %get-tuple-element.44), channel_id=1, source_target_pairs={{0,8},{4,20},{8,0},{12,28},{16,24},{20,4},{24,16},{28,12},{1,9},{5... | collective-permute-start | bytes 245768 | tf_op jit(solution)/shard_map/ppermute | solution.py:489
  28.9 1.3 %collective-permute-start.9 = (bf16[32,1280]{1,0:T(8,128)(2,1)S(1)}, bf16[32,1280]{1,0:T(8,128)(2,1)S(1)}, u32[]{:S(2)}, u32[]{:S(2)}) collective-permute-start(bf16[32,1280]{1,0:T(8,128)(2,1)S(1)} %get-tuple-element.46), channel_id=1, source_target_pairs={{0,16},{4,12},{8,24},{12,4},{16,0},{20,28},{24,8},{28,20},{1,17},{... | collective-permute-start | bytes 245768 | tf_op jit(solution)/shard_map/ppermute | solution.py:489
  30.2 0.7 %collective-permute-start.10 = (bf16[32,1280]{1,0:T(8,128)(2,1)S(1)}, bf16[32,1280]{1,0:T(8,128)(2,1)S(1)}, u32[]{:S(2)}, u32[]{:S(2)}) collective-permute-start(bf16[32,1280]{1,0:T(8,128)(2,1)S(1)} %get-tuple-element.48), channel_id=1, source_target_pairs={{0,24},{4,28},{8,16},{12,20},{16,8},{20,12},{24,0},{28,4},{1,25},{... | collective-permute-start | bytes 245768 | tf_op jit(solution)/shard_map/ppermute | solution.py:489
  30.9 0.2 collective-permute-done.12.refs_3_
  31.0 0.2 collective-permute-done.11.refs_1_
  31.2 0.1 add_halves.4
  31.3 1.4 %collective-permute-start.13 = (bf16[80,640]{1,0:T(8,128)(2,1)S(1)}, bf16[80,640]{1,0:T(8,128)(2,1)S(1)}, u32[]{:S(2)}, u32[]{:S(2)}) collective-permute-start(bf16[80,640]{1,0:T(8,128)(2,1)S(1)} %get-tuple-element.50.refs_0_), channel_id=1, source_target_pairs={{0,2},{1,3},{2,0},{3,1},{4,6},{5,7},{6,4},{7,5},{8,10},{9,11},{10,... | collective-permute-start | bytes 307208 | tf_op jit(solution)/shard_map/ppermute | solution.py:484
  32.7 2.4 %collective-permute-start.14 = (bf16[80,640]{1,0:T(8,128)(2,1)S(1)}, bf16[80,640]{1,0:T(8,128)(2,1)S(1)}, u32[]{:S(2)}, u32[]{:S(2)}) collective-permute-start(bf16[80,640]{1,0:T(8,128)(2,1)S(1)} %get-tuple-element.51.refs_2_), channel_id=1, source_target_pairs={{0,1},{1,0},{2,3},{3,2},{4,5},{5,4},{6,7},{7,6},{8,9},{9,8},{10,11... | collective-permute-start | bytes 307208 | tf_op jit(solution)/shard_map/ppermute | solution.py:484
  35.1 0.0 collective-permute-done.8.refs_1_
  35.1 0.0 collective-permute-done.9.refs_2_
  35.1 0.4 %collective-permute-done.10.refs_3_ = bf16[32,1280]{1,0:T(8,128)(2,1)S(1)} collective-permute-done((bf16[32,1280]{1,0:T(8,128)(2,1)S(1)}, bf16[32,1280]{1,0:T(8,128)(2,1)S(1)}, u32[]{:S(2)}, u32[]{:S(2)}) %collective-permute-start.10) | collective-permute-done | bytes 81952 | tf_op jit(solution)/shard_map/ppermute | solution.py:489
  35.5 0.0 copy-done.1
  35.5 1.8 %place_rows.1 = bf16[160,5120]{1,0:T(8,128)(2,1)} custom-call(s32[1,160]{1,0:T(1,128)S(1)} %bitcast.4, bf16[32,1280]{1,0:T(8,128)(2,1)S(1)} %get-tuple-element.32.refs_0_, bf16[32,1280]{1,0:T(8,128)(2,1)S(1)} %collective-permute-done.8.refs_1_, bf16[32,1280]{1,0:T(8,128)(2,1)S(1)} %collective-permute-done.9.refs_2_, ...), custom_call_target="tpu_custom_call" | custom-call | flops 20971520000 | bytes 1638400 | tf_op jit(solution)/shard_map/place_rows/pallas_call | solution.py:439
  37.4 1.2 %collective-permute-done.13.refs_1_ = bf16[80,640]{1,0:T(8,128)(2,1)S(1)} collective-permute-done((bf16[80,640]{1,0:T(8,128)(2,1)S(1)}, bf16[80,640]{1,0:T(8,128)(2,1)S(1)}, u32[]{:S(2)}, u32[]{:S(2)}) %collective-permute-start.13) | collective-permute-done | bytes 102432 | tf_op jit(solution)/shard_map/ppermute | solution.py:484
  38.6 0.4 %collective-permute-done.14.refs_3_ = bf16[80,640]{1,0:T(8,128)(2,1)S(1)} collective-permute-done((bf16[80,640]{1,0:T(8,128)(2,1)S(1)}, bf16[80,640]{1,0:T(8,128)(2,1)S(1)}, u32[]{:S(2)}, u32[]{:S(2)}) %collective-permute-start.14) | collective-permute-done | bytes 102432 | tf_op jit(solution)/shard_map/ppermute | solution.py:484
  39.0 0.8 %add_halves.5 = f32[80,1280]{1,0:T(8,128)} custom-call(bf16[80,640]{1,0:T(8,128)(2,1)S(1)} %get-tuple-element.50.refs_0_, bf16[80,640]{1,0:T(8,128)(2,1)S(1)} %collective-permute-done.13.refs_1_, bf16[80,640]{1,0:T(8,128)(2,1)S(1)} %get-tuple-element.51.refs_2_, bf16[80,640]{1,0:T(8,128)(2,1)S(1)} %collective-permute-done.14.refs_3_), custom_call_target="tpu_custom_call" | custom-call | flops 102400 | bytes 819200 | tf_op jit(solution)/shard_map/add_halves/pallas_call | solution.py:467
  (2 shorter events, 0.0 us)
Async XLA Ops:
  0.6 5.3 %slice-start = ((s8[4915200]{0:T(1024)(128)(4,1)}), s8[4194304]{0:T(1024)(128)(4,1)S(1)}, s32[]{:S(2)}) async-start(s8[4915200]{0:T(1024)(128)(4,1)} %bitcast.1), calls=%async_computation | async-start | bytes 8388608
  0.6 5.2 %slice-start.1 = ((s8[4915200]{0:T(1024)(128)(4,1)}), s8[720896]{0:T(1024)(128)(4,1)S(1)}, s32[]{:S(2)}) async-start(s8[4915200]{0:T(1024)(128)(4,1)} %bitcast.1), calls=%async_computation.1 | async-start | bytes 1441792
  2.8 3.1 %collective-permute-start = (bf16[80,1280]{1,0:T(8,128)(2,1)S(1)}, bf16[80,1280]{1,0:T(8,128)(2,1)S(1)}, u32[]{:S(2)}, u32[]{:S(2)}) collective-permute-start(bf16[80,1280]{1,0:T(8,128)(2,1)S(1)} %get-tuple-element.28), channel_id=1, source_target_pairs={{0,4},{4,0},{8,12},{12,8},{16,20},{20,16},{24,28},{28,24},{1,5},{5... | collective-permute-start | bytes 614408 | tf_op jit(solution)/shard_map/ppermute | solution.py:484
  3.3 9.5 %collective-permute-start.4 = (bf16[128,1280]{1,0:T(8,128)(2,1)S(1)}, bf16[128,1280]{1,0:T(8,128)(2,1)S(1)}, u32[]{:S(2)}, u32[]{:S(2)}) collective-permute-start(bf16[128,1280]{1,0:T(8,128)(2,1)S(1)} %get-tuple-element.39.refs_3_.refs_4_), channel_id=1, source_target_pairs={{0,8},{4,20},{8,0},{12,28},{16,24},{20,4},{24,16},{28,12},{1,9},{5... | collective-permute-start | bytes 983048 | tf_op jit(solution)/shard_map/ppermute | solution.py:489
  7.7 8.7 %collective-permute-start.5 = (bf16[128,1280]{1,0:T(8,128)(2,1)S(1)}, bf16[128,1280]{1,0:T(8,128)(2,1)S(1)}, u32[]{:S(2)}, u32[]{:S(2)}) collective-permute-start(bf16[128,1280]{1,0:T(8,128)(2,1)S(1)} %get-tuple-element.39.refs_3_.refs_4_), channel_id=1, source_target_pairs={{0,16},{4,12},{8,24},{12,4},{16,0},{20,28},{24,8},{28,20},{1,17},{... | collective-permute-start | bytes 983048 | tf_op jit(solution)/shard_map/ppermute | solution.py:489
  10.9 4.5 %collective-permute-start.1 = (bf16[160,128]{1,0:T(8,128)(2,1)S(1)}, bf16[160,128]{1,0:T(8,128)(2,1)S(1)}, u32[]{:S(2)}, u32[]{:S(2)}) collective-permute-start(bf16[160,128]{1,0:T(8,128)(2,1)S(1)} %get-tuple-element.35), channel_id=1, source_target_pairs={{0,8},{4,20},{8,0},{12,28},{16,24},{20,4},{24,16},{28,12},{1,9},{5... | collective-permute-start | bytes 122888 | tf_op jit(solution)/shard_map/ppermute | solution.py:489
  12.3 4.0 %collective-permute-start.2 = (bf16[160,128]{1,0:T(8,128)(2,1)S(1)}, bf16[160,128]{1,0:T(8,128)(2,1)S(1)}, u32[]{:S(2)}, u32[]{:S(2)}) collective-permute-start(bf16[160,128]{1,0:T(8,128)(2,1)S(1)} %get-tuple-element.36), channel_id=1, source_target_pairs={{0,16},{4,12},{8,24},{12,4},{16,0},{20,28},{24,8},{28,20},{1,17},{... | collective-permute-start | bytes 122888 | tf_op jit(solution)/shard_map/ppermute | solution.py:489
  12.9 7.5 %collective-permute-start.6 = (bf16[128,1280]{1,0:T(8,128)(2,1)S(1)}, bf16[128,1280]{1,0:T(8,128)(2,1)S(1)}, u32[]{:S(2)}, u32[]{:S(2)}) collective-permute-start(bf16[128,1280]{1,0:T(8,128)(2,1)S(1)} %collective-permute-done.4.refs_4_.refs_5_), channel_id=1, source_target_pairs={{0,16},{4,12},{8,24},{12,4},{16,0},{20,28},{24,8},{28,20},{1,17},{... | collective-permute-start | bytes 983048 | tf_op jit(solution)/shard_map/ppermute | solution.py:489
  14.4 5.4 %collective-permute-start.3 = (bf16[160,128]{1,0:T(8,128)(2,1)S(1)}, bf16[160,128]{1,0:T(8,128)(2,1)S(1)}, u32[]{:S(2)}, u32[]{:S(2)}) collective-permute-start(bf16[160,128]{1,0:T(8,128)(2,1)S(1)} %get-tuple-element.37), channel_id=1, source_target_pairs={{0,24},{4,28},{8,16},{12,20},{16,8},{20,12},{24,0},{28,4},{1,25},{... | collective-permute-start | bytes 122888 | tf_op jit(solution)/shard_map/ppermute | solution.py:489
  16.8 10.1 %copy-start = (bf16[640,1280]{1,0:T(8,128)(2,1)S(1)}, bf16[640,1280]{1,0:T(8,128)(2,1)}, u32[]{:S(2)}) copy-start(bf16[640,1280]{1,0:T(8,128)(2,1)} %w_ref.3) | copy-start | bytes 4915204
  20.7 14.8 %copy-start.1 = (s32[160]{0:T(256)S(1)}, s32[160]{0:T(256)}, u32[]{:S(2)}) copy-start(s32[160]{0:T(256)} %param.11) | copy-start | bytes 1924
  20.7 1.8 %collective-permute-start.7 = (bf16[80,1280]{1,0:T(8,128)(2,1)S(1)}, bf16[80,1280]{1,0:T(8,128)(2,1)S(1)}, u32[]{:S(2)}, u32[]{:S(2)}) collective-permute-start(bf16[80,1280]{1,0:T(8,128)(2,1)S(1)} %get-tuple-element.42), channel_id=1, source_target_pairs={{0,4},{4,0},{8,12},{12,8},{16,20},{20,16},{24,28},{28,24},{1,5},{5... | collective-permute-start | bytes 614408 | tf_op jit(solution)/shard_map/ppermute | solution.py:484
  22.6 8.4 %collective-permute-start.12 = (bf16[80,640]{1,0:T(8,128)(2,1)S(1)}, bf16[80,640]{1,0:T(8,128)(2,1)S(1)}, u32[]{:S(2)}, u32[]{:S(2)}) collective-permute-start(bf16[80,640]{1,0:T(8,128)(2,1)S(1)} %get-tuple-element.49.refs_2_), channel_id=1, source_target_pairs={{0,2},{1,3},{2,0},{3,1},{4,6},{5,7},{6,4},{7,5},{8,10},{9,11},{10,... | collective-permute-start | bytes 307208 | tf_op jit(solution)/shard_map/ppermute | solution.py:484
  25.3 6.0 %collective-permute-start.11 = (bf16[80,640]{1,0:T(8,128)(2,1)S(1)}, bf16[80,640]{1,0:T(8,128)(2,1)S(1)}, u32[]{:S(2)}, u32[]{:S(2)}) collective-permute-start(bf16[80,640]{1,0:T(8,128)(2,1)S(1)} %get-tuple-element.43.refs_0_), channel_id=1, source_target_pairs={{0,1},{1,0},{2,3},{3,2},{4,5},{5,4},{6,7},{7,6},{8,9},{9,8},{10,11... | collective-permute-start | bytes 307208 | tf_op jit(solution)/shard_map/ppermute | solution.py:484
  27.3 7.8 %collective-permute-start.8 = (bf16[32,1280]{1,0:T(8,128)(2,1)S(1)}, bf16[32,1280]{1,0:T(8,128)(2,1)S(1)}, u32[]{:S(2)}, u32[]{:S(2)}) collective-permute-start(bf16[32,1280]{1,0:T(8,128)(2,1)S(1)} %get-tuple-element.44), channel_id=1, source_target_pairs={{0,8},{4,20},{8,0},{12,28},{16,24},{20,4},{24,16},{28,12},{1,9},{5... | collective-permute-start | bytes 245768 | tf_op jit(solution)/shard_map/ppermute | solution.py:489
  28.9 6.2 %collective-permute-start.9 = (bf16[32,1280]{1,0:T(8,128)(2,1)S(1)}, bf16[32,1280]{1,0:T(8,128)(2,1)S(1)}, u32[]{:S(2)}, u32[]{:S(2)}) collective-permute-start(bf16[32,1280]{1,0:T(8,128)(2,1)S(1)} %get-tuple-element.46), channel_id=1, source_target_pairs={{0,16},{4,12},{8,24},{12,4},{16,0},{20,28},{24,8},{28,20},{1,17},{... | collective-permute-start | bytes 245768 | tf_op jit(solution)/shard_map/ppermute | solution.py:489
  30.2 5.3 %collective-permute-start.10 = (bf16[32,1280]{1,0:T(8,128)(2,1)S(1)}, bf16[32,1280]{1,0:T(8,128)(2,1)S(1)}, u32[]{:S(2)}, u32[]{:S(2)}) collective-permute-start(bf16[32,1280]{1,0:T(8,128)(2,1)S(1)} %get-tuple-element.48), channel_id=1, source_target_pairs={{0,24},{4,28},{8,16},{12,20},{16,8},{20,12},{24,0},{28,4},{1,25},{... | collective-permute-start | bytes 245768 | tf_op jit(solution)/shard_map/ppermute | solution.py:489
  31.3 7.3 %collective-permute-start.13 = (bf16[80,640]{1,0:T(8,128)(2,1)S(1)}, bf16[80,640]{1,0:T(8,128)(2,1)S(1)}, u32[]{:S(2)}, u32[]{:S(2)}) collective-permute-start(bf16[80,640]{1,0:T(8,128)(2,1)S(1)} %get-tuple-element.50.refs_0_), channel_id=1, source_target_pairs={{0,2},{1,3},{2,0},{3,1},{4,6},{5,7},{6,4},{7,5},{8,10},{9,11},{10,... | collective-permute-start | bytes 307208 | tf_op jit(solution)/shard_map/ppermute | solution.py:484
  32.7 6.4 %collective-permute-start.14 = (bf16[80,640]{1,0:T(8,128)(2,1)S(1)}, bf16[80,640]{1,0:T(8,128)(2,1)S(1)}, u32[]{:S(2)}, u32[]{:S(2)}) collective-permute-start(bf16[80,640]{1,0:T(8,128)(2,1)S(1)} %get-tuple-element.51.refs_2_), channel_id=1, source_target_pairs={{0,1},{1,0},{2,3},{3,2},{4,5},{5,4},{6,7},{7,6},{8,9},{9,8},{10,11... | collective-permute-start | bytes 307208 | tf_op jit(solution)/shard_map/ppermute | solution.py:484

commit v9 on v8

--- a/solution.py
+++ b/solution.py
@@ -105,6 +105,7 @@
 SUBLANES = 16
 PAIR_BITS = 2
 NEAR = 40
+LATE = 1
 PLACE = 200
 VMEM = pl.BlockSpec(memory_space=pltpu.VMEM)
 HBM = pl.BlockSpec(memory_space=pltpu.HBM)
@@ -370,9 +371,9 @@
 
 
 def near_kernel(pairs, *refs):
-    columns, blocks = refs[: pairs - 1], refs[pairs - 1 : -1]
-    near = range(pairs - 1)
-    refs[-1][...] = products(columns, blocks, [(b, o) for b in near for o in near])
+    early = [b for b in range(pairs) if b != LATE]
+    columns, blocks = dict(zip(early, refs)), refs[pairs - 1 : -1]
+    refs[-1][...] = products(columns, blocks, [(b, o) for b in early for o in range(pairs - 1)])
 
 
 def far_kernel(scale, pairs, *refs):
@@ -380,7 +381,8 @@
     kept_ref, given_ref = refs[2 * pairs + 1 :]
     head = kept_ref.shape[0]
     last = pairs - 1
-    places = [(last, o) for o in range(pairs)] + [(b, last) for b in range(last)]
+    places = [(LATE, o) for o in range(pairs)]
+    places += [(b, last) for b in range(pairs) if b != LATE]
     total = (near_ref[...] + products(columns, blocks, places)) * scale
     first = lax.axis_index("enc") % 2 == 0
     kept_ref[...] = jnp.where(first, total[:head], total[head:])
@@ -504,7 +506,7 @@
     columns = [sent[0]] + [chip_swap(sent[b], b) for b in range(1, pairs)]
     encoded = project_ordered(attended, ordered, w_out, pairs)
     scale = 1.0 / math.sqrt(rows * group * replicas)
-    near = near_rows(columns[:-1], blocks[:-1])
+    near = near_rows([columns[b] for b in range(pairs) if b != LATE], blocks[:-1])
     mine, other = far_rows(columns, blocks, near, scale)
     halves = add_halves([(mine, swap(other, "enc", 1))], jnp.bfloat16, split=True)
     arrived = [encoded[0]]

time: 40 us -> 39.9 us (level)
    ppermute x6, starting transfers between devices: 9.31 us -> 8.63 us  [swap(): return lax.ppermute(value, axis, [(i, i ^ bits) for i in range(size)])]
    ppermute x6, waiting for transfers between devices: 3.07 us -> 3.63 us  [swap(): return lax.ppermute(value, axis, [(i, i ^ bits) for i in range(size)])]
  transfers between devices with their start and end apart: 15 -> 15, of which waited for: 10 -> 7; matrix products, arithmetic and copies ran while one was open for 0% -> 0% of each run, Pallas kernels for 16% -> 16%
where the time goes in v9:
time: 39.9 us; the launch traced here: 39.8 us
  starting transfers between devices  21 us (53%)
  Pallas kernels  9.48 us (24%)
  waiting for transfers between devices  8.53 us (21%)
  between operations  0.76 us (2%)
    ppermute x9, starting transfers between devices, chip_swap(): lax.ppermute(value, 'enc', [(i, i ^ 2 * turn(relative, i % 2)) for i in r...  12.3 us
    ppermute x6, starting transfers between devices, swap(): return lax.ppermute(value, axis, [(i, i ^ bits) for i in range(size)])  8.63 us
    ppermute x9, waiting for transfers between devices, chip_swap(): lax.ppermute(value, 'enc', [(i, i ^ 2 * turn(relative, i % 2)) for i in r...  4.9 us
    ppermute x6, waiting for transfers between devices, swap(): return lax.ppermute(value, axis, [(i, i ^ bits) for i in range(size)])  3.63 us
    pallas_call x1, Pallas kernels, pick_rows(): pl.pallas_call(pick_kernel, out_shape=(jax.ShapeDtypeStruct((rows, width)...  2.14 us
    pallas_call x1, Pallas kernels, place_rows(): pl.pallas_call(place_kernel, out_shape=jax.ShapeDtypeStruct((tokens, MERG...  1.83 us
    pallas_call x1, Pallas kernels, qkv_ordered(): pl.pallas_call(qkv_kernel, out_shape=(jax.ShapeDtypeStruct((rows, w_qkv.s...  1.76 us
    pallas_call x1, Pallas kernels, attend_ordered(): pl.pallas_call(attend_kernel, out_shape=(jax.ShapeDtypeStruct((inner, row...  1.66 us
  transfers between devices with their start and end apart: 15, of which 7 were waited for; matrix products, arithmetic and copies ran while one was open for 0% of the time, Pallas kernels for 16%

profile of v9, /device:TPU:0, one launch (start us, length us, event | category | flops | bytes accessed | tf_op | source)
XLA Modules:
  0.0 39.8 jit_solution(16036423539526171237)
XLA Ops:
  0.6 0.0 slice-start
  0.6 0.0 slice-start.1
  0.7 2.1 %pick_rows.1 = (bf16[128,1280]{1,0:T(8,128)(2,1)S(1)}, bf16[80,1280]{1,0:T(8,128)(2,1)S(1)}, bf16[80,1280]{1,0:T(8,128)(2,1)S(1)}) custom-call(s32[8]{0:T(128)} %owner_hbm.1, s32[8]{0:T(128)} %len_hbm.1, s32[1,160]{1,0:T(1,128)} %bitcast.3, bf16[128,1280]{1,0:T(8,128)(2,1)} %pixels_hbm.1, bf16[160,5120]{1,0:T(8,128)(2,1)} %cotangent_hbm.1), custom_call_target="tpu_custom_call" | custom-call | flops 20971520000 | bytes 1638400 | tf_op jit(solution)/shard_map/pick_rows/pallas_call | solution.py:211
  2.8 0.5 %collective-permute-start = (bf16[80,1280]{1,0:T(8,128)(2,1)S(1)}, bf16[80,1280]{1,0:T(8,128)(2,1)S(1)}, u32[]{:S(2)}, u32[]{:S(2)}) collective-permute-start(bf16[80,1280]{1,0:T(8,128)(2,1)S(1)} %get-tuple-element.28), channel_id=1, source_target_pairs={{0,4},{4,0},{8,12},{12,8},{16,20},{20,16},{24,28},{28,24},{1,5},{5... | collective-permute-start | bytes 614408 | tf_op jit(solution)/shard_map/ppermute | solution.py:486
  3.3 2.6 %collective-permute-start.4 = (bf16[128,1280]{1,0:T(8,128)(2,1)S(1)}, bf16[128,1280]{1,0:T(8,128)(2,1)S(1)}, u32[]{:S(2)}, u32[]{:S(2)}) collective-permute-start(bf16[128,1280]{1,0:T(8,128)(2,1)S(1)} %get-tuple-element.39.refs_3_.refs_4_), channel_id=1, source_target_pairs={{0,8},{4,20},{8,0},{12,28},{16,24},{20,4},{24,16},{28,12},{1,9},{5... | collective-permute-start | bytes 983048 | tf_op jit(solution)/shard_map/ppermute | solution.py:491
  5.9 0.0 collective-permute-done.given_ref
  5.9 0.0 slice-done
  5.9 0.0 slice-done.1
  5.9 1.8 %qkv.1 = (bf16[128,1920]{1,0:T(8,128)(2,1)S(1)}, bf16[128,1280]{1,0:T(8,128)(2,1)S(1)}) custom-call(bf16[80,1280]{1,0:T(8,128)(2,1)S(1)} %get-tuple-element.27.kept_ref, bf16[80,1280]{1,0:T(8,128)(2,1)S(1)} %collective-permute-done.given_ref, f32[1280]{0:T(1024)} %gain_ref.1, bf16[1280,1920]{1,0:T(8,128)(2,1)S(1)} %bitcast.2), custom_call_target="tpu_custom_call" | custom-call | flops 629145600 | bytes 4915200 | tf_op jit(solution)/shard_map/qkv/pallas_call | solution.py:263
  7.7 1.6 %collective-permute-start.5 = (bf16[128,1280]{1,0:T(8,128)(2,1)S(1)}, bf16[128,1280]{1,0:T(8,128)(2,1)S(1)}, u32[]{:S(2)}, u32[]{:S(2)}) collective-permute-start(bf16[128,1280]{1,0:T(8,128)(2,1)S(1)} %get-tuple-element.39.refs_3_.refs_4_), channel_id=1, source_target_pairs={{0,16},{4,12},{8,24},{12,4},{16,0},{20,28},{24,8},{28,20},{1,17},{... | collective-permute-start | bytes 983048 | tf_op jit(solution)/shard_map/ppermute | solution.py:491
  9.3 1.7 %attend.1 = (bf16[640,128]{1,0:T(8,128)(2,1)S(1)}, bf16[160,128]{1,0:T(8,128)(2,1)S(1)}, bf16[160,128]{1,0:T(8,128)(2,1)S(1)}, bf16[160,128]{1,0:T(8,128)(2,1)S(1)}, bf16[160,128]{1,0:T(8,128)(2,1)S(1)}) custom-call(bf16[80,1280]{1,0:T(8,128)(2,1)S(1)} %get-tuple-element.27.kept_ref, bf16[80,1280]{1,0:T(8,128)(2,1)S(1)} %collective-permute-done.given_ref, ...), custom_call_target="tpu_custom_call" | custom-call | flops 41943040 | bytes 491520 | tf_op jit(solution)/shard_map/attend/pallas_call | solution.py:325
  10.9 0.6 %collective-permute-start.2 = (bf16[160,128]{1,0:T(8,128)(2,1)S(1)}, bf16[160,128]{1,0:T(8,128)(2,1)S(1)}, u32[]{:S(2)}, u32[]{:S(2)}) collective-permute-start(bf16[160,128]{1,0:T(8,128)(2,1)S(1)} %get-tuple-element.36), channel_id=1, source_target_pairs={{0,16},{4,12},{8,24},{12,4},{16,0},{20,28},{24,8},{28,20},{1,17},{... | collective-permute-start | bytes 122888 | tf_op jit(solution)/shard_map/ppermute | solution.py:491
  11.5 2.3 %collective-permute-start.3 = (bf16[160,128]{1,0:T(8,128)(2,1)S(1)}, bf16[160,128]{1,0:T(8,128)(2,1)S(1)}, u32[]{:S(2)}, u32[]{:S(2)}) collective-permute-start(bf16[160,128]{1,0:T(8,128)(2,1)S(1)} %get-tuple-element.37), channel_id=1, source_target_pairs={{0,24},{4,28},{8,16},{12,20},{16,8},{20,12},{24,0},{28,4},{1,25},{... | collective-permute-start | bytes 122888 | tf_op jit(solution)/shard_map/ppermute | solution.py:491
  13.8 0.0 collective-permute-done.4.refs_4_.refs_5_
  13.8 0.5 %collective-permute-start.6 = (bf16[128,1280]{1,0:T(8,128)(2,1)S(1)}, bf16[128,1280]{1,0:T(8,128)(2,1)S(1)}, u32[]{:S(2)}, u32[]{:S(2)}) collective-permute-start(bf16[128,1280]{1,0:T(8,128)(2,1)S(1)} %collective-permute-done.4.refs_4_.refs_5_), channel_id=1, source_target_pairs={{0,16},{4,12},{8,24},{12,4},{16,0},{20,28},{24,8},{28,20},{1,17},{... | collective-permute-start | bytes 983048 | tf_op jit(solution)/shard_map/ppermute | solution.py:491
  14.3 1.2 %collective-permute-start.1 = (bf16[160,128]{1,0:T(8,128)(2,1)S(1)}, bf16[160,128]{1,0:T(8,128)(2,1)S(1)}, u32[]{:S(2)}, u32[]{:S(2)}) collective-permute-start(bf16[160,128]{1,0:T(8,128)(2,1)S(1)} %get-tuple-element.35), channel_id=1, source_target_pairs={{0,8},{4,20},{8,0},{12,28},{16,24},{20,4},{24,16},{28,12},{1,9},{5... | collective-permute-start | bytes 122888 | tf_op jit(solution)/shard_map/ppermute | solution.py:491
  15.6 0.0 collective-permute-done.2.refs_1_.refs_2_
  15.6 1.4 %collective-permute-done.3.refs_2_.refs_3_ = bf16[160,128]{1,0:T(8,128)(2,1)S(1)} collective-permute-done((bf16[160,128]{1,0:T(8,128)(2,1)S(1)}, bf16[160,128]{1,0:T(8,128)(2,1)S(1)}, u32[]{:S(2)}, u32[]{:S(2)}) %collective-permute-start.3) | collective-permute-done | bytes 40992 | tf_op jit(solution)/shard_map/ppermute | solution.py:491
  16.9 0.0 collective-permute-done.5.refs_5_.refs_6_
  16.9 0.4 %near_rows.1.refs_8_ = f32[160,1280]{1,0:T(8,128)S(1)} custom-call(bf16[160,128]{1,0:T(8,128)(2,1)S(1)} %get-tuple-element.34.refs_0_, bf16[160,128]{1,0:T(8,128)(2,1)S(1)} %collective-permute-done.2.refs_1_.refs_2_, bf16[160,128]{1,0:T(8,128)(2,1)S(1)} %collective-permute-done.3.refs_2_.refs_3_, bf16[128,1280]{1,0:T(8,128)(2,1)S(1)} %get-tuple-element.39.refs_3_.refs_4_, ...), custom_call_target="tpu_custom_call" | custom-call | flops 3145728000 | bytes 983040 | tf_op jit(solution)/shard_map/near_rows/pallas_call | solution.py:395
  17.3 0.0 copy-start
  17.4 1.5 %collective-permute-done.1.refs_1_ = bf16[160,128]{1,0:T(8,128)(2,1)S(1)} collective-permute-done((bf16[160,128]{1,0:T(8,128)(2,1)S(1)}, bf16[160,128]{1,0:T(8,128)(2,1)S(1)}, u32[]{:S(2)}, u32[]{:S(2)}) %collective-permute-start.1) | collective-permute-done | bytes 40992 | tf_op jit(solution)/shard_map/ppermute | solution.py:491
  18.8 2.1 %collective-permute-done.6.refs_7_ = bf16[128,1280]{1,0:T(8,128)(2,1)S(1)} collective-permute-done((bf16[128,1280]{1,0:T(8,128)(2,1)S(1)}, bf16[128,1280]{1,0:T(8,128)(2,1)S(1)}, u32[]{:S(2)}, u32[]{:S(2)}) %collective-permute-start.6) | collective-permute-done | bytes 327712 | tf_op jit(solution)/shard_map/ppermute | solution.py:491
  20.9 0.3 far_rows.1
  21.2 0.0 copy-start.1
  21.2 0.1 collective-permute-start.7
  21.3 1.4 %collective-permute-done.7.refs_1_ = bf16[80,1280]{1,0:T(8,128)(2,1)S(1)} collective-permute-done((bf16[80,1280]{1,0:T(8,128)(2,1)S(1)}, bf16[80,1280]{1,0:T(8,128)(2,1)S(1)}, u32[]{:S(2)}, u32[]{:S(2)}) %collective-permute-start.7) | collective-permute-done | bytes 204832 | tf_op jit(solution)/shard_map/ppermute | solution.py:486
  22.8 2.7 %collective-permute-start.12 = (bf16[80,640]{1,0:T(8,128)(2,1)S(1)}, bf16[80,640]{1,0:T(8,128)(2,1)S(1)}, u32[]{:S(2)}, u32[]{:S(2)}) collective-permute-start(bf16[80,640]{1,0:T(8,128)(2,1)S(1)} %get-tuple-element.49.refs_2_), channel_id=1, source_target_pairs={{0,2},{1,3},{2,0},{3,1},{4,6},{5,7},{6,4},{7,5},{8,10},{9,11},{10,... | collective-permute-start | bytes 307208 | tf_op jit(solution)/shard_map/ppermute | solution.py:486
  25.4 1.6 %collective-permute-start.11 = (bf16[80,640]{1,0:T(8,128)(2,1)S(1)}, bf16[80,640]{1,0:T(8,128)(2,1)S(1)}, u32[]{:S(2)}, u32[]{:S(2)}) collective-permute-start(bf16[80,640]{1,0:T(8,128)(2,1)S(1)} %get-tuple-element.43.refs_0_), channel_id=1, source_target_pairs={{0,1},{1,0},{2,3},{3,2},{4,5},{5,4},{6,7},{7,6},{8,9},{9,8},{10,11... | collective-permute-start | bytes 307208 | tf_op jit(solution)/shard_map/ppermute | solution.py:486
  27.0 0.0 copy-done
  27.0 0.5 %project.1 = (bf16[32,1280]{1,0:T(8,128)(2,1)S(1)}, bf16[32,1280]{1,0:T(8,128)(2,1)S(1)}, bf16[32,1280]{1,0:T(8,128)(2,1)S(1)}, bf16[32,1280]{1,0:T(8,128)(2,1)S(1)}) custom-call(bf16[640,128]{1,0:T(8,128)(2,1)S(1)} %get-tuple-element.30.attended_ref, bf16[128,1280]{1,0:T(8,128)(2,1)S(1)} %get-tuple-element.31.ordered_ref, bf16[640,1280]{1,0:T(8,128)(2,1)S(1)} %copy-done), custom_call_target="tpu_custom_call" | custom-call | flops 209715200 | bytes 1638400 | tf_op jit(solution)/shard_map/project/pallas_call | solution.py:350
  27.5 1.4 %collective-permute-start.8 = (bf16[32,1280]{1,0:T(8,128)(2,1)S(1)}, bf16[32,1280]{1,0:T(8,128)(2,1)S(1)}, u32[]{:S(2)}, u32[]{:S(2)}) collective-permute-start(bf16[32,1280]{1,0:T(8,128)(2,1)S(1)} %get-tuple-element.44), channel_id=1, source_target_pairs={{0,8},{4,20},{8,0},{12,28},{16,24},{20,4},{24,16},{28,12},{1,9},{5... | collective-permute-start | bytes 245768 | tf_op jit(solution)/shard_map/ppermute | solution.py:491
  28.9 0.7 %collective-permute-start.9 = (bf16[32,1280]{1,0:T(8,128)(2,1)S(1)}, bf16[32,1280]{1,0:T(8,128)(2,1)S(1)}, u32[]{:S(2)}, u32[]{:S(2)}) collective-permute-start(bf16[32,1280]{1,0:T(8,128)(2,1)S(1)} %get-tuple-element.46), channel_id=1, source_target_pairs={{0,16},{4,12},{8,24},{12,4},{16,0},{20,28},{24,8},{28,20},{1,17},{... | collective-permute-start | bytes 245768 | tf_op jit(solution)/shard_map/ppermute | solution.py:491
  29.6 1.4 %collective-permute-start.10 = (bf16[32,1280]{1,0:T(8,128)(2,1)S(1)}, bf16[32,1280]{1,0:T(8,128)(2,1)S(1)}, u32[]{:S(2)}, u32[]{:S(2)}) collective-permute-start(bf16[32,1280]{1,0:T(8,128)(2,1)S(1)} %get-tuple-element.48), channel_id=1, source_target_pairs={{0,24},{4,28},{8,16},{12,20},{16,8},{20,12},{24,0},{28,4},{1,25},{... | collective-permute-start | bytes 245768 | tf_op jit(solution)/shard_map/ppermute | solution.py:491
  31.0 0.0 collective-permute-done.12.refs_3_
  31.1 0.1 collective-permute-done.11.refs_1_
  31.2 0.1 add_halves.4
  31.2 1.4 %collective-permute-start.13 = (bf16[80,640]{1,0:T(8,128)(2,1)S(1)}, bf16[80,640]{1,0:T(8,128)(2,1)S(1)}, u32[]{:S(2)}, u32[]{:S(2)}) collective-permute-start(bf16[80,640]{1,0:T(8,128)(2,1)S(1)} %get-tuple-element.50.refs_0_), channel_id=1, source_target_pairs={{0,2},{1,3},{2,0},{3,1},{4,6},{5,7},{6,4},{7,5},{8,10},{9,11},{10,... | collective-permute-start | bytes 307208 | tf_op jit(solution)/shard_map/ppermute | solution.py:486
  32.6 2.4 %collective-permute-start.14 = (bf16[80,640]{1,0:T(8,128)(2,1)S(1)}, bf16[80,640]{1,0:T(8,128)(2,1)S(1)}, u32[]{:S(2)}, u32[]{:S(2)}) collective-permute-start(bf16[80,640]{1,0:T(8,128)(2,1)S(1)} %get-tuple-element.51.refs_2_), channel_id=1, source_target_pairs={{0,1},{1,0},{2,3},{3,2},{4,5},{5,4},{6,7},{7,6},{8,9},{9,8},{10,11... | collective-permute-start | bytes 307208 | tf_op jit(solution)/shard_map/ppermute | solution.py:486
  35.1 0.0 collective-permute-done.8.refs_1_
  35.1 0.0 collective-permute-done.9.refs_2_
  35.1 0.0 collective-permute-done.10.refs_3_
  35.1 0.0 copy-done.1
  35.1 1.8 %place_rows.1 = bf16[160,5120]{1,0:T(8,128)(2,1)} custom-call(s32[1,160]{1,0:T(1,128)S(1)} %bitcast.4, bf16[32,1280]{1,0:T(8,128)(2,1)S(1)} %get-tuple-element.32.refs_0_, bf16[32,1280]{1,0:T(8,128)(2,1)S(1)} %collective-permute-done.8.refs_1_, bf16[32,1280]{1,0:T(8,128)(2,1)S(1)} %collective-permute-done.9.refs_2_, ...), custom_call_target="tpu_custom_call" | custom-call | flops 20971520000 | bytes 1638400 | tf_op jit(solution)/shard_map/place_rows/pallas_call | solution.py:441
  36.9 1.6 %collective-permute-done.13.refs_1_ = bf16[80,640]{1,0:T(8,128)(2,1)S(1)} collective-permute-done((bf16[80,640]{1,0:T(8,128)(2,1)S(1)}, bf16[80,640]{1,0:T(8,128)(2,1)S(1)}, u32[]{:S(2)}, u32[]{:S(2)}) %collective-permute-start.13) | collective-permute-done | bytes 102432 | tf_op jit(solution)/shard_map/ppermute | solution.py:486
  38.5 0.4 %collective-permute-done.14.refs_3_ = bf16[80,640]{1,0:T(8,128)(2,1)S(1)} collective-permute-done((bf16[80,640]{1,0:T(8,128)(2,1)S(1)}, bf16[80,640]{1,0:T(8,128)(2,1)S(1)}, u32[]{:S(2)}, u32[]{:S(2)}) %collective-permute-start.14) | collective-permute-done | bytes 102432 | tf_op jit(solution)/shard_map/ppermute | solution.py:486
  39.0 0.8 %add_halves.5 = f32[80,1280]{1,0:T(8,128)} custom-call(bf16[80,640]{1,0:T(8,128)(2,1)S(1)} %get-tuple-element.50.refs_0_, bf16[80,640]{1,0:T(8,128)(2,1)S(1)} %collective-permute-done.13.refs_1_, bf16[80,640]{1,0:T(8,128)(2,1)S(1)} %get-tuple-element.51.refs_2_, bf16[80,640]{1,0:T(8,128)(2,1)S(1)} %collective-permute-done.14.refs_3_), custom_call_target="tpu_custom_call" | custom-call | flops 102400 | bytes 819200 | tf_op jit(solution)/shard_map/add_halves/pallas_call | solution.py:469
  (2 shorter events, 0.0 us)
Async XLA Ops:
  0.6 5.3 %slice-start = ((s8[4915200]{0:T(1024)(128)(4,1)}), s8[4194304]{0:T(1024)(128)(4,1)S(1)}, s32[]{:S(2)}) async-start(s8[4915200]{0:T(1024)(128)(4,1)} %bitcast.1), calls=%async_computation | async-start | bytes 8388608
  0.6 5.3 %slice-start.1 = ((s8[4915200]{0:T(1024)(128)(4,1)}), s8[720896]{0:T(1024)(128)(4,1)S(1)}, s32[]{:S(2)}) async-start(s8[4915200]{0:T(1024)(128)(4,1)} %bitcast.1), calls=%async_computation.1 | async-start | bytes 1441792
  2.8 3.1 %collective-permute-start = (bf16[80,1280]{1,0:T(8,128)(2,1)S(1)}, bf16[80,1280]{1,0:T(8,128)(2,1)S(1)}, u32[]{:S(2)}, u32[]{:S(2)}) collective-permute-start(bf16[80,1280]{1,0:T(8,128)(2,1)S(1)} %get-tuple-element.28), channel_id=1, source_target_pairs={{0,4},{4,0},{8,12},{12,8},{16,20},{20,16},{24,28},{28,24},{1,5},{5... | collective-permute-start | bytes 614408 | tf_op jit(solution)/shard_map/ppermute | solution.py:486
  3.3 10.5 %collective-permute-start.4 = (bf16[128,1280]{1,0:T(8,128)(2,1)S(1)}, bf16[128,1280]{1,0:T(8,128)(2,1)S(1)}, u32[]{:S(2)}, u32[]{:S(2)}) collective-permute-start(bf16[128,1280]{1,0:T(8,128)(2,1)S(1)} %get-tuple-element.39.refs_3_.refs_4_), channel_id=1, source_target_pairs={{0,8},{4,20},{8,0},{12,28},{16,24},{20,4},{24,16},{28,12},{1,9},{5... | collective-permute-start | bytes 983048 | tf_op jit(solution)/shard_map/ppermute | solution.py:491
  7.7 9.2 %collective-permute-start.5 = (bf16[128,1280]{1,0:T(8,128)(2,1)S(1)}, bf16[128,1280]{1,0:T(8,128)(2,1)S(1)}, u32[]{:S(2)}, u32[]{:S(2)}) collective-permute-start(bf16[128,1280]{1,0:T(8,128)(2,1)S(1)} %get-tuple-element.39.refs_3_.refs_4_), channel_id=1, source_target_pairs={{0,16},{4,12},{8,24},{12,4},{16,0},{20,28},{24,8},{28,20},{1,17},{... | collective-permute-start | bytes 983048 | tf_op jit(solution)/shard_map/ppermute | solution.py:491
  10.9 4.6 %collective-permute-start.2 = (bf16[160,128]{1,0:T(8,128)(2,1)S(1)}, bf16[160,128]{1,0:T(8,128)(2,1)S(1)}, u32[]{:S(2)}, u32[]{:S(2)}) collective-permute-start(bf16[160,128]{1,0:T(8,128)(2,1)S(1)} %get-tuple-element.36), channel_id=1, source_target_pairs={{0,16},{4,12},{8,24},{12,4},{16,0},{20,28},{24,8},{28,20},{1,17},{... | collective-permute-start | bytes 122888 | tf_op jit(solution)/shard_map/ppermute | solution.py:491
  11.5 5.4 %collective-permute-start.3 = (bf16[160,128]{1,0:T(8,128)(2,1)S(1)}, bf16[160,128]{1,0:T(8,128)(2,1)S(1)}, u32[]{:S(2)}, u32[]{:S(2)}) collective-permute-start(bf16[160,128]{1,0:T(8,128)(2,1)S(1)} %get-tuple-element.37), channel_id=1, source_target_pairs={{0,24},{4,28},{8,16},{12,20},{16,8},{20,12},{24,0},{28,4},{1,25},{... | collective-permute-start | bytes 122888 | tf_op jit(solution)/shard_map/ppermute | solution.py:491
  13.8 7.1 %collective-permute-start.6 = (bf16[128,1280]{1,0:T(8,128)(2,1)S(1)}, bf16[128,1280]{1,0:T(8,128)(2,1)S(1)}, u32[]{:S(2)}, u32[]{:S(2)}) collective-permute-start(bf16[128,1280]{1,0:T(8,128)(2,1)S(1)} %collective-permute-done.4.refs_4_.refs_5_), channel_id=1, source_target_pairs={{0,16},{4,12},{8,24},{12,4},{16,0},{20,28},{24,8},{28,20},{1,17},{... | collective-permute-start | bytes 983048 | tf_op jit(solution)/shard_map/ppermute | solution.py:491
  14.3 4.5 %collective-permute-start.1 = (bf16[160,128]{1,0:T(8,128)(2,1)S(1)}, bf16[160,128]{1,0:T(8,128)(2,1)S(1)}, u32[]{:S(2)}, u32[]{:S(2)}) collective-permute-start(bf16[160,128]{1,0:T(8,128)(2,1)S(1)} %get-tuple-element.35), channel_id=1, source_target_pairs={{0,8},{4,20},{8,0},{12,28},{16,24},{20,4},{24,16},{28,12},{1,9},{5... | collective-permute-start | bytes 122888 | tf_op jit(solution)/shard_map/ppermute | solution.py:491
  17.3 9.7 %copy-start = (bf16[640,1280]{1,0:T(8,128)(2,1)S(1)}, bf16[640,1280]{1,0:T(8,128)(2,1)}, u32[]{:S(2)}) copy-start(bf16[640,1280]{1,0:T(8,128)(2,1)} %w_ref.3) | copy-start | bytes 4915204
  21.2 13.9 %copy-start.1 = (s32[160]{0:T(256)S(1)}, s32[160]{0:T(256)}, u32[]{:S(2)}) copy-start(s32[160]{0:T(256)} %param.11) | copy-start | bytes 1924
  21.2 1.5 %collective-permute-start.7 = (bf16[80,1280]{1,0:T(8,128)(2,1)S(1)}, bf16[80,1280]{1,0:T(8,128)(2,1)S(1)}, u32[]{:S(2)}, u32[]{:S(2)}) collective-permute-start(bf16[80,1280]{1,0:T(8,128)(2,1)S(1)} %get-tuple-element.42), channel_id=1, source_target_pairs={{0,4},{4,0},{8,12},{12,8},{16,20},{20,16},{24,28},{28,24},{1,5},{5... | collective-permute-start | bytes 614408 | tf_op jit(solution)/shard_map/ppermute | solution.py:486
  22.8 8.3 %collective-permute-start.12 = (bf16[80,640]{1,0:T(8,128)(2,1)S(1)}, bf16[80,640]{1,0:T(8,128)(2,1)S(1)}, u32[]{:S(2)}, u32[]{:S(2)}) collective-permute-start(bf16[80,640]{1,0:T(8,128)(2,1)S(1)} %get-tuple-element.49.refs_2_), channel_id=1, source_target_pairs={{0,2},{1,3},{2,0},{3,1},{4,6},{5,7},{6,4},{7,5},{8,10},{9,11},{10,... | collective-permute-start | bytes 307208 | tf_op jit(solution)/shard_map/ppermute | solution.py:486
  25.4 5.7 %collective-permute-start.11 = (bf16[80,640]{1,0:T(8,128)(2,1)S(1)}, bf16[80,640]{1,0:T(8,128)(2,1)S(1)}, u32[]{:S(2)}, u32[]{:S(2)}) collective-permute-start(bf16[80,640]{1,0:T(8,128)(2,1)S(1)} %get-tuple-element.43.refs_0_), channel_id=1, source_target_pairs={{0,1},{1,0},{2,3},{3,2},{4,5},{5,4},{6,7},{7,6},{8,9},{9,8},{10,11... | collective-permute-start | bytes 307208 | tf_op jit(solution)/shard_map/ppermute | solution.py:486
  27.5 7.6 %collective-permute-start.8 = (bf16[32,1280]{1,0:T(8,128)(2,1)S(1)}, bf16[32,1280]{1,0:T(8,128)(2,1)S(1)}, u32[]{:S(2)}, u32[]{:S(2)}) collective-permute-start(bf16[32,1280]{1,0:T(8,128)(2,1)S(1)} %get-tuple-element.44), channel_id=1, source_target_pairs={{0,8},{4,20},{8,0},{12,28},{16,24},{20,4},{24,16},{28,12},{1,9},{5... | collective-permute-start | bytes 245768 | tf_op jit(solution)/shard_map/ppermute | solution.py:491
  28.9 6.1 %collective-permute-start.9 = (bf16[32,1280]{1,0:T(8,128)(2,1)S(1)}, bf16[32,1280]{1,0:T(8,128)(2,1)S(1)}, u32[]{:S(2)}, u32[]{:S(2)}) collective-permute-start(bf16[32,1280]{1,0:T(8,128)(2,1)S(1)} %get-tuple-element.46), channel_id=1, source_target_pairs={{0,16},{4,12},{8,24},{12,4},{16,0},{20,28},{24,8},{28,20},{1,17},{... | collective-permute-start | bytes 245768 | tf_op jit(solution)/shard_map/ppermute | solution.py:491
  29.6 5.4 %collective-permute-start.10 = (bf16[32,1280]{1,0:T(8,128)(2,1)S(1)}, bf16[32,1280]{1,0:T(8,128)(2,1)S(1)}, u32[]{:S(2)}, u32[]{:S(2)}) collective-permute-start(bf16[32,1280]{1,0:T(8,128)(2,1)S(1)} %get-tuple-element.48), channel_id=1, source_target_pairs={{0,24},{4,28},{8,16},{12,20},{16,8},{20,12},{24,0},{28,4},{1,25},{... | collective-permute-start | bytes 245768 | tf_op jit(solution)/shard_map/ppermute | solution.py:491
  31.2 7.3 %collective-permute-start.13 = (bf16[80,640]{1,0:T(8,128)(2,1)S(1)}, bf16[80,640]{1,0:T(8,128)(2,1)S(1)}, u32[]{:S(2)}, u32[]{:S(2)}) collective-permute-start(bf16[80,640]{1,0:T(8,128)(2,1)S(1)} %get-tuple-element.50.refs_0_), channel_id=1, source_target_pairs={{0,2},{1,3},{2,0},{3,1},{4,6},{5,7},{6,4},{7,5},{8,10},{9,11},{10,... | collective-permute-start | bytes 307208 | tf_op jit(solution)/shard_map/ppermute | solution.py:486
  32.6 6.3 %collective-permute-start.14 = (bf16[80,640]{1,0:T(8,128)(2,1)S(1)}, bf16[80,640]{1,0:T(8,128)(2,1)S(1)}, u32[]{:S(2)}, u32[]{:S(2)}) collective-permute-start(bf16[80,640]{1,0:T(8,128)(2,1)S(1)} %get-tuple-element.51.refs_2_), channel_id=1, source_target_pairs={{0,1},{1,0},{2,3},{3,2},{4,5},{5,4},{6,7},{7,6},{8,9},{9,8},{10,11... | collective-permute-start | bytes 307208 | tf_op jit(solution)/shard_map/ppermute | solution.py:486

commit v10 on v8

--- a/solution.py
+++ b/solution.py
@@ -306,7 +306,8 @@
         )
         scores = jnp.where(allowed, scores * scale, -1e30)
         raised = jnp.exp(scores - jnp.max(scores, axis=0, keepdims=True))
-        weight = (raised / jnp.sum(raised, axis=0, keepdims=True)).astype(jnp.bfloat16)
+        share = 1.0 / jnp.sum(raised, axis=0, keepdims=True)
+        weight = (raised * share).astype(jnp.bfloat16)
         mixed = jnp.dot(
             values_across[first : first + HD, :], weight, preferred_element_type=jnp.float32
         ).astype(jnp.bfloat16)

time: 40 us -> 40 us (level)
  no operation moved by 1% of the time
where the time goes in v10:
time: 40 us; the launch traced here: 39.8 us
  starting transfers between devices  21.4 us (54%)
  Pallas kernels  9.51 us (24%)
  waiting for transfers between devices  8.13 us (20%)
  between operations  0.74 us (2%)
    ppermute x9, starting transfers between devices, chip_swap(): lax.ppermute(value, 'enc', [(i, i ^ 2 * turn(relative, i % 2)) for i in r...  12.1 us
    ppermute x6, starting transfers between devices, swap(): return lax.ppermute(value, axis, [(i, i ^ bits) for i in range(size)])  9.32 us
    ppermute x9, waiting for transfers between devices, chip_swap(): lax.ppermute(value, 'enc', [(i, i ^ 2 * turn(relative, i % 2)) for i in r...  5.06 us
    ppermute x6, waiting for transfers between devices, swap(): return lax.ppermute(value, axis, [(i, i ^ bits) for i in range(size)])  3.07 us
    pallas_call x1, Pallas kernels, pick_rows(): pl.pallas_call(pick_kernel, out_shape=(jax.ShapeDtypeStruct((rows, width)...  2.15 us
    pallas_call x1, Pallas kernels, place_rows(): pl.pallas_call(place_kernel, out_shape=jax.ShapeDtypeStruct((tokens, MERG...  1.83 us
    pallas_call x1, Pallas kernels, qkv_ordered(): pl.pallas_call(qkv_kernel, out_shape=(jax.ShapeDtypeStruct((rows, w_qkv.s...  1.76 us
    pallas_call x1, Pallas kernels, attend_ordered(): pl.pallas_call(attend_kernel, out_shape=(jax.ShapeDtypeStruct((inner, row...  1.66 us
  transfers between devices with their start and end apart: 15, of which 10 were waited for; matrix products, arithmetic and copies ran while one was open for 0% of the time, Pallas kernels for 16%

profile of v10, /device:TPU:0, one launch (start us, length us, event | category | flops | bytes accessed | tf_op | source)
XLA Modules:
  0.0 39.8 jit_solution(1986403509672572040)
XLA Ops:
  0.6 0.0 slice-start
  0.6 0.0 slice-start.1
  0.7 2.1 %pick_rows.1 = (bf16[128,1280]{1,0:T(8,128)(2,1)S(1)}, bf16[80,1280]{1,0:T(8,128)(2,1)S(1)}, bf16[80,1280]{1,0:T(8,128)(2,1)S(1)}) custom-call(s32[8]{0:T(128)} %owner_hbm.1, s32[8]{0:T(128)} %len_hbm.1, s32[1,160]{1,0:T(1,128)} %bitcast.3, bf16[128,1280]{1,0:T(8,128)(2,1)} %pixels_hbm.1, bf16[160,5120]{1,0:T(8,128)(2,1)} %cotangent_hbm.1), custom_call_target="tpu_custom_call" | custom-call | flops 20971520000 | bytes 1638400 | tf_op jit(solution)/shard_map/pick_rows/pallas_call | solution.py:210
  2.8 0.5 %collective-permute-start = (bf16[80,1280]{1,0:T(8,128)(2,1)S(1)}, bf16[80,1280]{1,0:T(8,128)(2,1)S(1)}, u32[]{:S(2)}, u32[]{:S(2)}) collective-permute-start(bf16[80,1280]{1,0:T(8,128)(2,1)S(1)} %get-tuple-element.28), channel_id=1, source_target_pairs={{0,4},{4,0},{8,12},{12,8},{16,20},{20,16},{24,28},{28,24},{1,5},{5... | collective-permute-start | bytes 614408 | tf_op jit(solution)/shard_map/ppermute | solution.py:485
  3.3 2.6 %collective-permute-start.4 = (bf16[128,1280]{1,0:T(8,128)(2,1)S(1)}, bf16[128,1280]{1,0:T(8,128)(2,1)S(1)}, u32[]{:S(2)}, u32[]{:S(2)}) collective-permute-start(bf16[128,1280]{1,0:T(8,128)(2,1)S(1)} %get-tuple-element.39.refs_3_.refs_4_), channel_id=1, source_target_pairs={{0,8},{4,20},{8,0},{12,28},{16,24},{20,4},{24,16},{28,12},{1,9},{5... | collective-permute-start | bytes 983048 | tf_op jit(solution)/shard_map/ppermute | solution.py:490
  5.9 0.0 collective-permute-done.given_ref
  5.9 0.0 slice-done
  5.9 0.0 slice-done.1
  5.9 1.8 %qkv.1 = (bf16[128,1920]{1,0:T(8,128)(2,1)S(1)}, bf16[128,1280]{1,0:T(8,128)(2,1)S(1)}) custom-call(bf16[80,1280]{1,0:T(8,128)(2,1)S(1)} %get-tuple-element.27.kept_ref, bf16[80,1280]{1,0:T(8,128)(2,1)S(1)} %collective-permute-done.given_ref, f32[1280]{0:T(1024)} %gain_ref.1, bf16[1280,1920]{1,0:T(8,128)(2,1)S(1)} %bitcast.2), custom_call_target="tpu_custom_call" | custom-call | flops 629145600 | bytes 4915200 | tf_op jit(solution)/shard_map/qkv/pallas_call | solution.py:262
  7.7 1.6 %collective-permute-start.5 = (bf16[128,1280]{1,0:T(8,128)(2,1)S(1)}, bf16[128,1280]{1,0:T(8,128)(2,1)S(1)}, u32[]{:S(2)}, u32[]{:S(2)}) collective-permute-start(bf16[128,1280]{1,0:T(8,128)(2,1)S(1)} %get-tuple-element.39.refs_3_.refs_4_), channel_id=1, source_target_pairs={{0,16},{4,12},{8,24},{12,4},{16,0},{20,28},{24,8},{28,20},{1,17},{... | collective-permute-start | bytes 983048 | tf_op jit(solution)/shard_map/ppermute | solution.py:490
  9.3 1.7 %attend.1 = (bf16[640,128]{1,0:T(8,128)(2,1)S(1)}, bf16[160,128]{1,0:T(8,128)(2,1)S(1)}, bf16[160,128]{1,0:T(8,128)(2,1)S(1)}, bf16[160,128]{1,0:T(8,128)(2,1)S(1)}, bf16[160,128]{1,0:T(8,128)(2,1)S(1)}) custom-call(bf16[80,1280]{1,0:T(8,128)(2,1)S(1)} %get-tuple-element.27.kept_ref, bf16[80,1280]{1,0:T(8,128)(2,1)S(1)} %collective-permute-done.given_ref, ...), custom_call_target="tpu_custom_call" | custom-call | flops 41943040 | bytes 491520 | tf_op jit(solution)/shard_map/attend/pallas_call | solution.py:325
  10.9 1.4 %collective-permute-start.1 = (bf16[160,128]{1,0:T(8,128)(2,1)S(1)}, bf16[160,128]{1,0:T(8,128)(2,1)S(1)}, u32[]{:S(2)}, u32[]{:S(2)}) collective-permute-start(bf16[160,128]{1,0:T(8,128)(2,1)S(1)} %get-tuple-element.35), channel_id=1, source_target_pairs={{0,8},{4,20},{8,0},{12,28},{16,24},{20,4},{24,16},{28,12},{1,9},{5... | collective-permute-start | bytes 122888 | tf_op jit(solution)/shard_map/ppermute | solution.py:490
  12.3 0.5 %collective-permute-start.2 = (bf16[160,128]{1,0:T(8,128)(2,1)S(1)}, bf16[160,128]{1,0:T(8,128)(2,1)S(1)}, u32[]{:S(2)}, u32[]{:S(2)}) collective-permute-start(bf16[160,128]{1,0:T(8,128)(2,1)S(1)} %get-tuple-element.36), channel_id=1, source_target_pairs={{0,16},{4,12},{8,24},{12,4},{16,0},{20,28},{24,8},{28,20},{1,17},{... | collective-permute-start | bytes 122888 | tf_op jit(solution)/shard_map/ppermute | solution.py:490
  12.8 0.0 collective-permute-done.4.refs_4_.refs_5_
  12.9 1.5 %collective-permute-start.6 = (bf16[128,1280]{1,0:T(8,128)(2,1)S(1)}, bf16[128,1280]{1,0:T(8,128)(2,1)S(1)}, u32[]{:S(2)}, u32[]{:S(2)}) collective-permute-start(bf16[128,1280]{1,0:T(8,128)(2,1)S(1)} %collective-permute-done.4.refs_4_.refs_5_), channel_id=1, source_target_pairs={{0,16},{4,12},{8,24},{12,4},{16,0},{20,28},{24,8},{28,20},{1,17},{... | collective-permute-start | bytes 983048 | tf_op jit(solution)/shard_map/ppermute | solution.py:490
  14.4 0.9 %collective-permute-start.3 = (bf16[160,128]{1,0:T(8,128)(2,1)S(1)}, bf16[160,128]{1,0:T(8,128)(2,1)S(1)}, u32[]{:S(2)}, u32[]{:S(2)}) collective-permute-start(bf16[160,128]{1,0:T(8,128)(2,1)S(1)} %get-tuple-element.37), channel_id=1, source_target_pairs={{0,24},{4,28},{8,16},{12,20},{16,8},{20,12},{24,0},{28,4},{1,25},{... | collective-permute-start | bytes 122888 | tf_op jit(solution)/shard_map/ppermute | solution.py:490
  15.3 0.1 collective-permute-done.1.refs_1_
  15.4 0.9 %collective-permute-done.2.refs_2_ = bf16[160,128]{1,0:T(8,128)(2,1)S(1)} collective-permute-done((bf16[160,128]{1,0:T(8,128)(2,1)S(1)}, bf16[160,128]{1,0:T(8,128)(2,1)S(1)}, u32[]{:S(2)}, u32[]{:S(2)}) %collective-permute-start.2) | collective-permute-done | bytes 40992 | tf_op jit(solution)/shard_map/ppermute | solution.py:490
  16.3 0.0 collective-permute-done.5.refs_5_.refs_6_
  16.3 0.4 %near_rows.1.refs_8_ = f32[160,1280]{1,0:T(8,128)S(1)} custom-call(bf16[160,128]{1,0:T(8,128)(2,1)S(1)} %get-tuple-element.34.refs_0_, bf16[160,128]{1,0:T(8,128)(2,1)S(1)} %collective-permute-done.1.refs_1_, bf16[160,128]{1,0:T(8,128)(2,1)S(1)} %collective-permute-done.2.refs_2_, bf16[128,1280]{1,0:T(8,128)(2,1)S(1)} %get-tuple-element.39.refs_3_.refs_4_, ...), custom_call_target="tpu_custom_call" | custom-call | flops 3145728000 | bytes 983040 | tf_op jit(solution)/shard_map/near_rows/pallas_call | solution.py:394
  16.8 0.0 copy-start
  16.8 3.0 %collective-permute-done.3.refs_3_ = bf16[160,128]{1,0:T(8,128)(2,1)S(1)} collective-permute-done((bf16[160,128]{1,0:T(8,128)(2,1)S(1)}, bf16[160,128]{1,0:T(8,128)(2,1)S(1)}, u32[]{:S(2)}, u32[]{:S(2)}) %collective-permute-start.3) | collective-permute-done | bytes 40992 | tf_op jit(solution)/shard_map/ppermute | solution.py:490
  19.8 0.6 %collective-permute-done.6.refs_7_ = bf16[128,1280]{1,0:T(8,128)(2,1)S(1)} collective-permute-done((bf16[128,1280]{1,0:T(8,128)(2,1)S(1)}, bf16[128,1280]{1,0:T(8,128)(2,1)S(1)}, u32[]{:S(2)}, u32[]{:S(2)}) %collective-permute-start.6) | collective-permute-done | bytes 327712 | tf_op jit(solution)/shard_map/ppermute | solution.py:490
  20.4 0.3 far_rows.1
  20.7 0.0 copy-start.1
  20.7 0.7 %collective-permute-start.7 = (bf16[80,1280]{1,0:T(8,128)(2,1)S(1)}, bf16[80,1280]{1,0:T(8,128)(2,1)S(1)}, u32[]{:S(2)}, u32[]{:S(2)}) collective-permute-start(bf16[80,1280]{1,0:T(8,128)(2,1)S(1)} %get-tuple-element.42), channel_id=1, source_target_pairs={{0,4},{4,0},{8,12},{12,8},{16,20},{20,16},{24,28},{28,24},{1,5},{5... | collective-permute-start | bytes 614408 | tf_op jit(solution)/shard_map/ppermute | solution.py:485
  21.5 1.1 %collective-permute-done.7.refs_1_ = bf16[80,1280]{1,0:T(8,128)(2,1)S(1)} collective-permute-done((bf16[80,1280]{1,0:T(8,128)(2,1)S(1)}, bf16[80,1280]{1,0:T(8,128)(2,1)S(1)}, u32[]{:S(2)}, u32[]{:S(2)}) %collective-permute-start.7) | collective-permute-done | bytes 204832 | tf_op jit(solution)/shard_map/ppermute | solution.py:485
  22.6 2.7 %collective-permute-start.12 = (bf16[80,640]{1,0:T(8,128)(2,1)S(1)}, bf16[80,640]{1,0:T(8,128)(2,1)S(1)}, u32[]{:S(2)}, u32[]{:S(2)}) collective-permute-start(bf16[80,640]{1,0:T(8,128)(2,1)S(1)} %get-tuple-element.49.refs_2_), channel_id=1, source_target_pairs={{0,2},{1,3},{2,0},{3,1},{4,6},{5,7},{6,4},{7,5},{8,10},{9,11},{10,... | collective-permute-start | bytes 307208 | tf_op jit(solution)/shard_map/ppermute | solution.py:485
  25.3 1.6 %collective-permute-start.11 = (bf16[80,640]{1,0:T(8,128)(2,1)S(1)}, bf16[80,640]{1,0:T(8,128)(2,1)S(1)}, u32[]{:S(2)}, u32[]{:S(2)}) collective-permute-start(bf16[80,640]{1,0:T(8,128)(2,1)S(1)} %get-tuple-element.43.refs_0_), channel_id=1, source_target_pairs={{0,1},{1,0},{2,3},{3,2},{4,5},{5,4},{6,7},{7,6},{8,9},{9,8},{10,11... | collective-permute-start | bytes 307208 | tf_op jit(solution)/shard_map/ppermute | solution.py:485
  26.8 0.0 copy-done
  26.8 0.5 %project.1 = (bf16[32,1280]{1,0:T(8,128)(2,1)S(1)}, bf16[32,1280]{1,0:T(8,128)(2,1)S(1)}, bf16[32,1280]{1,0:T(8,128)(2,1)S(1)}, bf16[32,1280]{1,0:T(8,128)(2,1)S(1)}) custom-call(bf16[640,128]{1,0:T(8,128)(2,1)S(1)} %get-tuple-element.30.attended_ref, bf16[128,1280]{1,0:T(8,128)(2,1)S(1)} %get-tuple-element.31.ordered_ref, bf16[640,1280]{1,0:T(8,128)(2,1)S(1)} %copy-done), custom_call_target="tpu_custom_call" | custom-call | flops 209715200 | bytes 1638400 | tf_op jit(solution)/shard_map/project/pallas_call | solution.py:350
  27.3 1.6 %collective-permute-start.8 = (bf16[32,1280]{1,0:T(8,128)(2,1)S(1)}, bf16[32,1280]{1,0:T(8,128)(2,1)S(1)}, u32[]{:S(2)}, u32[]{:S(2)}) collective-permute-start(bf16[32,1280]{1,0:T(8,128)(2,1)S(1)} %get-tuple-element.44), channel_id=1, source_target_pairs={{0,8},{4,20},{8,0},{12,28},{16,24},{20,4},{24,16},{28,12},{1,9},{5... | collective-permute-start | bytes 245768 | tf_op jit(solution)/shard_map/ppermute | solution.py:490
  28.9 1.3 %collective-permute-start.9 = (bf16[32,1280]{1,0:T(8,128)(2,1)S(1)}, bf16[32,1280]{1,0:T(8,128)(2,1)S(1)}, u32[]{:S(2)}, u32[]{:S(2)}) collective-permute-start(bf16[32,1280]{1,0:T(8,128)(2,1)S(1)} %get-tuple-element.46), channel_id=1, source_target_pairs={{0,16},{4,12},{8,24},{12,4},{16,0},{20,28},{24,8},{28,20},{1,17},{... | collective-permute-start | bytes 245768 | tf_op jit(solution)/shard_map/ppermute | solution.py:490
  30.2 0.7 %collective-permute-start.10 = (bf16[32,1280]{1,0:T(8,128)(2,1)S(1)}, bf16[32,1280]{1,0:T(8,128)(2,1)S(1)}, u32[]{:S(2)}, u32[]{:S(2)}) collective-permute-start(bf16[32,1280]{1,0:T(8,128)(2,1)S(1)} %get-tuple-element.48), channel_id=1, source_target_pairs={{0,24},{4,28},{8,16},{12,20},{16,8},{20,12},{24,0},{28,4},{1,25},{... | collective-permute-start | bytes 245768 | tf_op jit(solution)/shard_map/ppermute | solution.py:490
  30.9 0.1 collective-permute-done.12.refs_3_
  31.0 0.2 collective-permute-done.11.refs_1_
  31.2 0.1 add_halves.4
  31.3 1.4 %collective-permute-start.13 = (bf16[80,640]{1,0:T(8,128)(2,1)S(1)}, bf16[80,640]{1,0:T(8,128)(2,1)S(1)}, u32[]{:S(2)}, u32[]{:S(2)}) collective-permute-start(bf16[80,640]{1,0:T(8,128)(2,1)S(1)} %get-tuple-element.50.refs_0_), channel_id=1, source_target_pairs={{0,2},{1,3},{2,0},{3,1},{4,6},{5,7},{6,4},{7,5},{8,10},{9,11},{10,... | collective-permute-start | bytes 307208 | tf_op jit(solution)/shard_map/ppermute | solution.py:485
  32.7 2.4 %collective-permute-start.14 = (bf16[80,640]{1,0:T(8,128)(2,1)S(1)}, bf16[80,640]{1,0:T(8,128)(2,1)S(1)}, u32[]{:S(2)}, u32[]{:S(2)}) collective-permute-start(bf16[80,640]{1,0:T(8,128)(2,1)S(1)} %get-tuple-element.51.refs_2_), channel_id=1, source_target_pairs={{0,1},{1,0},{2,3},{3,2},{4,5},{5,4},{6,7},{7,6},{8,9},{9,8},{10,11... | collective-permute-start | bytes 307208 | tf_op jit(solution)/shard_map/ppermute | solution.py:485
  35.1 0.0 collective-permute-done.8.refs_1_
  35.1 0.0 collective-permute-done.9.refs_2_
  35.1 0.4 %collective-permute-done.10.refs_3_ = bf16[32,1280]{1,0:T(8,128)(2,1)S(1)} collective-permute-done((bf16[32,1280]{1,0:T(8,128)(2,1)S(1)}, bf16[32,1280]{1,0:T(8,128)(2,1)S(1)}, u32[]{:S(2)}, u32[]{:S(2)}) %collective-permute-start.10) | collective-permute-done | bytes 81952 | tf_op jit(solution)/shard_map/ppermute | solution.py:490
  35.5 0.0 copy-done.1
  35.5 1.8 %place_rows.1 = bf16[160,5120]{1,0:T(8,128)(2,1)} custom-call(s32[1,160]{1,0:T(1,128)S(1)} %bitcast.4, bf16[32,1280]{1,0:T(8,128)(2,1)S(1)} %get-tuple-element.32.refs_0_, bf16[32,1280]{1,0:T(8,128)(2,1)S(1)} %collective-permute-done.8.refs_1_, bf16[32,1280]{1,0:T(8,128)(2,1)S(1)} %collective-permute-done.9.refs_2_, ...), custom_call_target="tpu_custom_call" | custom-call | flops 20971520000 | bytes 1638400 | tf_op jit(solution)/shard_map/place_rows/pallas_call | solution.py:440
  37.4 1.2 %collective-permute-done.13.refs_1_ = bf16[80,640]{1,0:T(8,128)(2,1)S(1)} collective-permute-done((bf16[80,640]{1,0:T(8,128)(2,1)S(1)}, bf16[80,640]{1,0:T(8,128)(2,1)S(1)}, u32[]{:S(2)}, u32[]{:S(2)}) %collective-permute-start.13) | collective-permute-done | bytes 102432 | tf_op jit(solution)/shard_map/ppermute | solution.py:485
  38.6 0.4 %collective-permute-done.14.refs_3_ = bf16[80,640]{1,0:T(8,128)(2,1)S(1)} collective-permute-done((bf16[80,640]{1,0:T(8,128)(2,1)S(1)}, bf16[80,640]{1,0:T(8,128)(2,1)S(1)}, u32[]{:S(2)}, u32[]{:S(2)}) %collective-permute-start.14) | collective-permute-done | bytes 102432 | tf_op jit(solution)/shard_map/ppermute | solution.py:485
  39.0 0.8 %add_halves.5 = f32[80,1280]{1,0:T(8,128)} custom-call(bf16[80,640]{1,0:T(8,128)(2,1)S(1)} %get-tuple-element.50.refs_0_, bf16[80,640]{1,0:T(8,128)(2,1)S(1)} %collective-permute-done.13.refs_1_, bf16[80,640]{1,0:T(8,128)(2,1)S(1)} %get-tuple-element.51.refs_2_, bf16[80,640]{1,0:T(8,128)(2,1)S(1)} %collective-permute-done.14.refs_3_), custom_call_target="tpu_custom_call" | custom-call | flops 102400 | bytes 819200 | tf_op jit(solution)/shard_map/add_halves/pallas_call | solution.py:468
  (2 shorter events, 0.0 us)
Async XLA Ops:
  0.6 5.3 %slice-start = ((s8[4915200]{0:T(1024)(128)(4,1)}), s8[4194304]{0:T(1024)(128)(4,1)S(1)}, s32[]{:S(2)}) async-start(s8[4915200]{0:T(1024)(128)(4,1)} %bitcast.1), calls=%async_computation | async-start | bytes 8388608
  0.6 5.3 %slice-start.1 = ((s8[4915200]{0:T(1024)(128)(4,1)}), s8[720896]{0:T(1024)(128)(4,1)S(1)}, s32[]{:S(2)}) async-start(s8[4915200]{0:T(1024)(128)(4,1)} %bitcast.1), calls=%async_computation.1 | async-start | bytes 1441792
  2.8 3.1 %collective-permute-start = (bf16[80,1280]{1,0:T(8,128)(2,1)S(1)}, bf16[80,1280]{1,0:T(8,128)(2,1)S(1)}, u32[]{:S(2)}, u32[]{:S(2)}) collective-permute-start(bf16[80,1280]{1,0:T(8,128)(2,1)S(1)} %get-tuple-element.28), channel_id=1, source_target_pairs={{0,4},{4,0},{8,12},{12,8},{16,20},{20,16},{24,28},{28,24},{1,5},{5... | collective-permute-start | bytes 614408 | tf_op jit(solution)/shard_map/ppermute | solution.py:485
  3.3 9.5 %collective-permute-start.4 = (bf16[128,1280]{1,0:T(8,128)(2,1)S(1)}, bf16[128,1280]{1,0:T(8,128)(2,1)S(1)}, u32[]{:S(2)}, u32[]{:S(2)}) collective-permute-start(bf16[128,1280]{1,0:T(8,128)(2,1)S(1)} %get-tuple-element.39.refs_3_.refs_4_), channel_id=1, source_target_pairs={{0,8},{4,20},{8,0},{12,28},{16,24},{20,4},{24,16},{28,12},{1,9},{5... | collective-permute-start | bytes 983048 | tf_op jit(solution)/shard_map/ppermute | solution.py:490
  7.7 8.7 %collective-permute-start.5 = (bf16[128,1280]{1,0:T(8,128)(2,1)S(1)}, bf16[128,1280]{1,0:T(8,128)(2,1)S(1)}, u32[]{:S(2)}, u32[]{:S(2)}) collective-permute-start(bf16[128,1280]{1,0:T(8,128)(2,1)S(1)} %get-tuple-element.39.refs_3_.refs_4_), channel_id=1, source_target_pairs={{0,16},{4,12},{8,24},{12,4},{16,0},{20,28},{24,8},{28,20},{1,17},{... | collective-permute-start | bytes 983048 | tf_op jit(solution)/shard_map/ppermute | solution.py:490
  10.9 4.5 %collective-permute-start.1 = (bf16[160,128]{1,0:T(8,128)(2,1)S(1)}, bf16[160,128]{1,0:T(8,128)(2,1)S(1)}, u32[]{:S(2)}, u32[]{:S(2)}) collective-permute-start(bf16[160,128]{1,0:T(8,128)(2,1)S(1)} %get-tuple-element.35), channel_id=1, source_target_pairs={{0,8},{4,20},{8,0},{12,28},{16,24},{20,4},{24,16},{28,12},{1,9},{5... | collective-permute-start | bytes 122888 | tf_op jit(solution)/shard_map/ppermute | solution.py:490
  12.3 4.0 %collective-permute-start.2 = (bf16[160,128]{1,0:T(8,128)(2,1)S(1)}, bf16[160,128]{1,0:T(8,128)(2,1)S(1)}, u32[]{:S(2)}, u32[]{:S(2)}) collective-permute-start(bf16[160,128]{1,0:T(8,128)(2,1)S(1)} %get-tuple-element.36), channel_id=1, source_target_pairs={{0,16},{4,12},{8,24},{12,4},{16,0},{20,28},{24,8},{28,20},{1,17},{... | collective-permute-start | bytes 122888 | tf_op jit(solution)/shard_map/ppermute | solution.py:490
  12.9 7.5 %collective-permute-start.6 = (bf16[128,1280]{1,0:T(8,128)(2,1)S(1)}, bf16[128,1280]{1,0:T(8,128)(2,1)S(1)}, u32[]{:S(2)}, u32[]{:S(2)}) collective-permute-start(bf16[128,1280]{1,0:T(8,128)(2,1)S(1)} %collective-permute-done.4.refs_4_.refs_5_), channel_id=1, source_target_pairs={{0,16},{4,12},{8,24},{12,4},{16,0},{20,28},{24,8},{28,20},{1,17},{... | collective-permute-start | bytes 983048 | tf_op jit(solution)/shard_map/ppermute | solution.py:490
  14.4 5.4 %collective-permute-start.3 = (bf16[160,128]{1,0:T(8,128)(2,1)S(1)}, bf16[160,128]{1,0:T(8,128)(2,1)S(1)}, u32[]{:S(2)}, u32[]{:S(2)}) collective-permute-start(bf16[160,128]{1,0:T(8,128)(2,1)S(1)} %get-tuple-element.37), channel_id=1, source_target_pairs={{0,24},{4,28},{8,16},{12,20},{16,8},{20,12},{24,0},{28,4},{1,25},{... | collective-permute-start | bytes 122888 | tf_op jit(solution)/shard_map/ppermute | solution.py:490
  16.8 10.1 %copy-start = (bf16[640,1280]{1,0:T(8,128)(2,1)S(1)}, bf16[640,1280]{1,0:T(8,128)(2,1)}, u32[]{:S(2)}) copy-start(bf16[640,1280]{1,0:T(8,128)(2,1)} %w_ref.3) | copy-start | bytes 4915204
  20.7 14.8 %copy-start.1 = (s32[160]{0:T(256)S(1)}, s32[160]{0:T(256)}, u32[]{:S(2)}) copy-start(s32[160]{0:T(256)} %param.11) | copy-start | bytes 1924
  20.7 1.8 %collective-permute-start.7 = (bf16[80,1280]{1,0:T(8,128)(2,1)S(1)}, bf16[80,1280]{1,0:T(8,128)(2,1)S(1)}, u32[]{:S(2)}, u32[]{:S(2)}) collective-permute-start(bf16[80,1280]{1,0:T(8,128)(2,1)S(1)} %get-tuple-element.42), channel_id=1, source_target_pairs={{0,4},{4,0},{8,12},{12,8},{16,20},{20,16},{24,28},{28,24},{1,5},{5... | collective-permute-start | bytes 614408 | tf_op jit(solution)/shard_map/ppermute | solution.py:485
  22.6 8.4 %collective-permute-start.12 = (bf16[80,640]{1,0:T(8,128)(2,1)S(1)}, bf16[80,640]{1,0:T(8,128)(2,1)S(1)}, u32[]{:S(2)}, u32[]{:S(2)}) collective-permute-start(bf16[80,640]{1,0:T(8,128)(2,1)S(1)} %get-tuple-element.49.refs_2_), channel_id=1, source_target_pairs={{0,2},{1,3},{2,0},{3,1},{4,6},{5,7},{6,4},{7,5},{8,10},{9,11},{10,... | collective-permute-start | bytes 307208 | tf_op jit(solution)/shard_map/ppermute | solution.py:485
  25.3 5.9 %collective-permute-start.11 = (bf16[80,640]{1,0:T(8,128)(2,1)S(1)}, bf16[80,640]{1,0:T(8,128)(2,1)S(1)}, u32[]{:S(2)}, u32[]{:S(2)}) collective-permute-start(bf16[80,640]{1,0:T(8,128)(2,1)S(1)} %get-tuple-element.43.refs_0_), channel_id=1, source_target_pairs={{0,1},{1,0},{2,3},{3,2},{4,5},{5,4},{6,7},{7,6},{8,9},{9,8},{10,11... | collective-permute-start | bytes 307208 | tf_op jit(solution)/shard_map/ppermute | solution.py:485
  27.3 7.8 %collective-permute-start.8 = (bf16[32,1280]{1,0:T(8,128)(2,1)S(1)}, bf16[32,1280]{1,0:T(8,128)(2,1)S(1)}, u32[]{:S(2)}, u32[]{:S(2)}) collective-permute-start(bf16[32,1280]{1,0:T(8,128)(2,1)S(1)} %get-tuple-element.44), channel_id=1, source_target_pairs={{0,8},{4,20},{8,0},{12,28},{16,24},{20,4},{24,16},{28,12},{1,9},{5... | collective-permute-start | bytes 245768 | tf_op jit(solution)/shard_map/ppermute | solution.py:490
  28.9 6.2 %collective-permute-start.9 = (bf16[32,1280]{1,0:T(8,128)(2,1)S(1)}, bf16[32,1280]{1,0:T(8,128)(2,1)S(1)}, u32[]{:S(2)}, u32[]{:S(2)}) collective-permute-start(bf16[32,1280]{1,0:T(8,128)(2,1)S(1)} %get-tuple-element.46), channel_id=1, source_target_pairs={{0,16},{4,12},{8,24},{12,4},{16,0},{20,28},{24,8},{28,20},{1,17},{... | collective-permute-start | bytes 245768 | tf_op jit(solution)/shard_map/ppermute | solution.py:490
  30.2 5.3 %collective-permute-start.10 = (bf16[32,1280]{1,0:T(8,128)(2,1)S(1)}, bf16[32,1280]{1,0:T(8,128)(2,1)S(1)}, u32[]{:S(2)}, u32[]{:S(2)}) collective-permute-start(bf16[32,1280]{1,0:T(8,128)(2,1)S(1)} %get-tuple-element.48), channel_id=1, source_target_pairs={{0,24},{4,28},{8,16},{12,20},{16,8},{20,12},{24,0},{28,4},{1,25},{... | collective-permute-start | bytes 245768 | tf_op jit(solution)/shard_map/ppermute | solution.py:490
  31.3 7.3 %collective-permute-start.13 = (bf16[80,640]{1,0:T(8,128)(2,1)S(1)}, bf16[80,640]{1,0:T(8,128)(2,1)S(1)}, u32[]{:S(2)}, u32[]{:S(2)}) collective-permute-start(bf16[80,640]{1,0:T(8,128)(2,1)S(1)} %get-tuple-element.50.refs_0_), channel_id=1, source_target_pairs={{0,2},{1,3},{2,0},{3,1},{4,6},{5,7},{6,4},{7,5},{8,10},{9,11},{10,... | collective-permute-start | bytes 307208 | tf_op jit(solution)/shard_map/ppermute | solution.py:485
  32.7 6.4 %collective-permute-start.14 = (bf16[80,640]{1,0:T(8,128)(2,1)S(1)}, bf16[80,640]{1,0:T(8,128)(2,1)S(1)}, u32[]{:S(2)}, u32[]{:S(2)}) collective-permute-start(bf16[80,640]{1,0:T(8,128)(2,1)S(1)} %get-tuple-element.51.refs_2_), channel_id=1, source_target_pairs={{0,1},{1,0},{2,3},{3,2},{4,5},{5,4},{6,7},{7,6},{8,9},{9,8},{10,11... | collective-permute-start | bytes 307208 | tf_op jit(solution)/shard_map/ppermute | solution.py:485

commit v11 on v9

--- a/solution.py
+++ b/solution.py
@@ -105,7 +105,7 @@
 SUBLANES = 16
 PAIR_BITS = 2
 NEAR = 40
-LATE = 1
+LATE = 2
 PLACE = 200
 VMEM = pl.BlockSpec(memory_space=pltpu.VMEM)
 HBM = pl.BlockSpec(memory_space=pltpu.HBM)

time: 39.9 us -> 40.3 us (1.010)
  waiting for transfers between devices: 8.53 us -> 9.42 us
  starting transfers between devices: 21 us -> 20.4 us
    ppermute x9, waiting for transfers between devices: 4.9 us -> 5.8 us  [chip_swap(): lax.ppermute(value, 'enc', [(i, i ^ 2 * turn(relative, i % 2)) for i in r...]
    ppermute x9, starting transfers between devices: 12.3 us -> 11.8 us  [chip_swap(): lax.ppermute(value, 'enc', [(i, i ^ 2 * turn(relative, i % 2)) for i in r...]
  transfers between devices with their start and end apart: 15 -> 15, of which waited for: 7 -> 7; matrix products, arithmetic and copies ran while one was open for 0% -> 0% of each run, Pallas kernels for 16% -> 15%
where the time goes in v11:
time: 40.3 us; the launch traced here: 40.1 us
  starting transfers between devices  20.4 us (51%)
  Pallas kernels  9.49 us (24%)
  waiting for transfers between devices  9.42 us (23%)
  between operations  0.76 us (2%)
    ppermute x9, starting transfers between devices, chip_swap(): lax.ppermute(value, 'enc', [(i, i ^ 2 * turn(relative, i % 2)) for i in r...  11.8 us
    ppermute x6, starting transfers between devices, swap(): return lax.ppermute(value, axis, [(i, i ^ bits) for i in range(size)])  8.63 us
    ppermute x9, waiting for transfers between devices, chip_swap(): lax.ppermute(value, 'enc', [(i, i ^ 2 * turn(relative, i % 2)) for i in r...  5.8 us
    ppermute x6, waiting for transfers between devices, swap(): return lax.ppermute(value, axis, [(i, i ^ bits) for i in range(size)])  3.63 us
    pallas_call x1, Pallas kernels, pick_rows(): pl.pallas_call(pick_kernel, out_shape=(jax.ShapeDtypeStruct((rows, width)...  2.15 us
    pallas_call x1, Pallas kernels, place_rows(): pl.pallas_call(place_kernel, out_shape=jax.ShapeDtypeStruct((tokens, MERG...  1.83 us
    pallas_call x1, Pallas kernels, qkv_ordered(): pl.pallas_call(qkv_kernel, out_shape=(jax.ShapeDtypeStruct((rows, w_qkv.s...  1.76 us
    pallas_call x1, Pallas kernels, attend_ordered(): pl.pallas_call(attend_kernel, out_shape=(jax.ShapeDtypeStruct((inner, row...  1.66 us
  transfers between devices with their start and end apart: 15, of which 7 were waited for; matrix products, arithmetic and copies ran while one was open for 0% of the time, Pallas kernels for 15%

profile of v11, /device:TPU:0, one launch (start us, length us, event | category | flops | bytes accessed | tf_op | source)
XLA Modules:
  0.0 40.1 jit_solution(9021028694454489578)
XLA Ops:
  0.6 0.0 slice-start
  0.6 0.0 slice-start.1
  0.7 2.1 %pick_rows.1 = (bf16[128,1280]{1,0:T(8,128)(2,1)S(1)}, bf16[80,1280]{1,0:T(8,128)(2,1)S(1)}, bf16[80,1280]{1,0:T(8,128)(2,1)S(1)}) custom-call(s32[8]{0:T(128)} %owner_hbm.1, s32[8]{0:T(128)} %len_hbm.1, s32[1,160]{1,0:T(1,128)} %bitcast.3, bf16[128,1280]{1,0:T(8,128)(2,1)} %pixels_hbm.1, bf16[160,5120]{1,0:T(8,128)(2,1)} %cotangent_hbm.1), custom_call_target="tpu_custom_call" | custom-call | flops 20971520000 | bytes 1638400 | tf_op jit(solution)/shard_map/pick_rows/pallas_call | solution.py:211
  2.8 0.5 %collective-permute-start = (bf16[80,1280]{1,0:T(8,128)(2,1)S(1)}, bf16[80,1280]{1,0:T(8,128)(2,1)S(1)}, u32[]{:S(2)}, u32[]{:S(2)}) collective-permute-start(bf16[80,1280]{1,0:T(8,128)(2,1)S(1)} %get-tuple-element.28), channel_id=1, source_target_pairs={{0,4},{4,0},{8,12},{12,8},{16,20},{20,16},{24,28},{28,24},{1,5},{5... | collective-permute-start | bytes 614408 | tf_op jit(solution)/shard_map/ppermute | solution.py:486
  3.3 2.6 %collective-permute-start.4 = (bf16[128,1280]{1,0:T(8,128)(2,1)S(1)}, bf16[128,1280]{1,0:T(8,128)(2,1)S(1)}, u32[]{:S(2)}, u32[]{:S(2)}) collective-permute-start(bf16[128,1280]{1,0:T(8,128)(2,1)S(1)} %get-tuple-element.39.refs_3_.refs_4_), channel_id=1, source_target_pairs={{0,8},{4,20},{8,0},{12,28},{16,24},{20,4},{24,16},{28,12},{1,9},{5... | collective-permute-start | bytes 983048 | tf_op jit(solution)/shard_map/ppermute | solution.py:491
  5.9 0.0 collective-permute-done.given_ref
  5.9 0.0 slice-done
  5.9 0.0 slice-done.1
  5.9 1.8 %qkv.1 = (bf16[128,1920]{1,0:T(8,128)(2,1)S(1)}, bf16[128,1280]{1,0:T(8,128)(2,1)S(1)}) custom-call(bf16[80,1280]{1,0:T(8,128)(2,1)S(1)} %get-tuple-element.27.kept_ref, bf16[80,1280]{1,0:T(8,128)(2,1)S(1)} %collective-permute-done.given_ref, f32[1280]{0:T(1024)} %gain_ref.1, bf16[1280,1920]{1,0:T(8,128)(2,1)S(1)} %bitcast.2), custom_call_target="tpu_custom_call" | custom-call | flops 629145600 | bytes 4915200 | tf_op jit(solution)/shard_map/qkv/pallas_call | solution.py:263
  7.7 1.6 %collective-permute-start.5 = (bf16[128,1280]{1,0:T(8,128)(2,1)S(1)}, bf16[128,1280]{1,0:T(8,128)(2,1)S(1)}, u32[]{:S(2)}, u32[]{:S(2)}) collective-permute-start(bf16[128,1280]{1,0:T(8,128)(2,1)S(1)} %get-tuple-element.39.refs_3_.refs_4_), channel_id=1, source_target_pairs={{0,16},{4,12},{8,24},{12,4},{16,0},{20,28},{24,8},{28,20},{1,17},{... | collective-permute-start | bytes 983048 | tf_op jit(solution)/shard_map/ppermute | solution.py:491
  9.3 1.7 %attend.1 = (bf16[640,128]{1,0:T(8,128)(2,1)S(1)}, bf16[160,128]{1,0:T(8,128)(2,1)S(1)}, bf16[160,128]{1,0:T(8,128)(2,1)S(1)}, bf16[160,128]{1,0:T(8,128)(2,1)S(1)}, bf16[160,128]{1,0:T(8,128)(2,1)S(1)}) custom-call(bf16[80,1280]{1,0:T(8,128)(2,1)S(1)} %get-tuple-element.27.kept_ref, bf16[80,1280]{1,0:T(8,128)(2,1)S(1)} %collective-permute-done.given_ref, ...), custom_call_target="tpu_custom_call" | custom-call | flops 41943040 | bytes 491520 | tf_op jit(solution)/shard_map/attend/pallas_call | solution.py:325
  10.9 1.4 %collective-permute-start.1 = (bf16[160,128]{1,0:T(8,128)(2,1)S(1)}, bf16[160,128]{1,0:T(8,128)(2,1)S(1)}, u32[]{:S(2)}, u32[]{:S(2)}) collective-permute-start(bf16[160,128]{1,0:T(8,128)(2,1)S(1)} %get-tuple-element.35), channel_id=1, source_target_pairs={{0,8},{4,20},{8,0},{12,28},{16,24},{20,4},{24,16},{28,12},{1,9},{5... | collective-permute-start | bytes 122888 | tf_op jit(solution)/shard_map/ppermute | solution.py:491
  12.3 0.6 %collective-permute-start.3 = (bf16[160,128]{1,0:T(8,128)(2,1)S(1)}, bf16[160,128]{1,0:T(8,128)(2,1)S(1)}, u32[]{:S(2)}, u32[]{:S(2)}) collective-permute-start(bf16[160,128]{1,0:T(8,128)(2,1)S(1)} %get-tuple-element.37), channel_id=1, source_target_pairs={{0,24},{4,28},{8,16},{12,20},{16,8},{20,12},{24,0},{28,4},{1,25},{... | collective-permute-start | bytes 122888 | tf_op jit(solution)/shard_map/ppermute | solution.py:491
  13.0 0.0 collective-permute-done.4.refs_4_.refs_5_
  13.0 1.5 %collective-permute-start.6 = (bf16[128,1280]{1,0:T(8,128)(2,1)S(1)}, bf16[128,1280]{1,0:T(8,128)(2,1)S(1)}, u32[]{:S(2)}, u32[]{:S(2)}) collective-permute-start(bf16[128,1280]{1,0:T(8,128)(2,1)S(1)} %collective-permute-done.4.refs_4_.refs_5_), channel_id=1, source_target_pairs={{0,16},{4,12},{8,24},{12,4},{16,0},{20,28},{24,8},{28,20},{1,17},{... | collective-permute-start | bytes 983048 | tf_op jit(solution)/shard_map/ppermute | solution.py:491
  14.5 0.5 %collective-permute-start.2 = (bf16[160,128]{1,0:T(8,128)(2,1)S(1)}, bf16[160,128]{1,0:T(8,128)(2,1)S(1)}, u32[]{:S(2)}, u32[]{:S(2)}) collective-permute-start(bf16[160,128]{1,0:T(8,128)(2,1)S(1)} %get-tuple-element.36), channel_id=1, source_target_pairs={{0,16},{4,12},{8,24},{12,4},{16,0},{20,28},{24,8},{28,20},{1,17},{... | collective-permute-start | bytes 122888 | tf_op jit(solution)/shard_map/ppermute | solution.py:491
  15.0 0.4 collective-permute-done.1.refs_1_
  15.3 2.4 %collective-permute-done.3.refs_2_.refs_3_ = bf16[160,128]{1,0:T(8,128)(2,1)S(1)} collective-permute-done((bf16[160,128]{1,0:T(8,128)(2,1)S(1)}, bf16[160,128]{1,0:T(8,128)(2,1)S(1)}, u32[]{:S(2)}, u32[]{:S(2)}) %collective-permute-start.3) | collective-permute-done | bytes 40992 | tf_op jit(solution)/shard_map/ppermute | solution.py:491
  17.7 0.0 collective-permute-done.5.refs_5_.refs_6_
  17.7 0.4 %near_rows.1.refs_8_ = f32[160,1280]{1,0:T(8,128)S(1)} custom-call(bf16[160,128]{1,0:T(8,128)(2,1)S(1)} %get-tuple-element.34.refs_0_, bf16[160,128]{1,0:T(8,128)(2,1)S(1)} %collective-permute-done.1.refs_1_, bf16[160,128]{1,0:T(8,128)(2,1)S(1)} %collective-permute-done.3.refs_2_.refs_3_, bf16[128,1280]{1,0:T(8,128)(2,1)S(1)} %get-tuple-element.39.refs_3_.refs_4_, ...), custom_call_target="tpu_custom_call" | custom-call | flops 3145728000 | bytes 983040 | tf_op jit(solution)/shard_map/near_rows/pallas_call | solution.py:395
  18.2 0.0 copy-start
  18.2 3.0 %collective-permute-done.2.refs_2_ = bf16[160,128]{1,0:T(8,128)(2,1)S(1)} collective-permute-done((bf16[160,128]{1,0:T(8,128)(2,1)S(1)}, bf16[160,128]{1,0:T(8,128)(2,1)S(1)}, u32[]{:S(2)}, u32[]{:S(2)}) %collective-permute-start.2) | collective-permute-done | bytes 40992 | tf_op jit(solution)/shard_map/ppermute | solution.py:491
  21.2 0.0 collective-permute-done.6.refs_7_
  21.2 0.3 far_rows.1
  21.5 0.0 copy-start.1
  21.6 0.1 collective-permute-start.7
  21.6 1.4 %collective-permute-done.7.refs_1_ = bf16[80,1280]{1,0:T(8,128)(2,1)S(1)} collective-permute-done((bf16[80,1280]{1,0:T(8,128)(2,1)S(1)}, bf16[80,1280]{1,0:T(8,128)(2,1)S(1)}, u32[]{:S(2)}, u32[]{:S(2)}) %collective-permute-start.7) | collective-permute-done | bytes 204832 | tf_op jit(solution)/shard_map/ppermute | solution.py:486
  23.1 2.7 %collective-permute-start.12 = (bf16[80,640]{1,0:T(8,128)(2,1)S(1)}, bf16[80,640]{1,0:T(8,128)(2,1)S(1)}, u32[]{:S(2)}, u32[]{:S(2)}) collective-permute-start(bf16[80,640]{1,0:T(8,128)(2,1)S(1)} %get-tuple-element.49.refs_2_), channel_id=1, source_target_pairs={{0,2},{1,3},{2,0},{3,1},{4,6},{5,7},{6,4},{7,5},{8,10},{9,11},{10,... | collective-permute-start | bytes 307208 | tf_op jit(solution)/shard_map/ppermute | solution.py:486
  25.8 1.6 %collective-permute-start.11 = (bf16[80,640]{1,0:T(8,128)(2,1)S(1)}, bf16[80,640]{1,0:T(8,128)(2,1)S(1)}, u32[]{:S(2)}, u32[]{:S(2)}) collective-permute-start(bf16[80,640]{1,0:T(8,128)(2,1)S(1)} %get-tuple-element.43.refs_0_), channel_id=1, source_target_pairs={{0,1},{1,0},{2,3},{3,2},{4,5},{5,4},{6,7},{7,6},{8,9},{9,8},{10,11... | collective-permute-start | bytes 307208 | tf_op jit(solution)/shard_map/ppermute | solution.py:486
  27.4 0.0 copy-done
  27.4 0.5 %project.1 = (bf16[32,1280]{1,0:T(8,128)(2,1)S(1)}, bf16[32,1280]{1,0:T(8,128)(2,1)S(1)}, bf16[32,1280]{1,0:T(8,128)(2,1)S(1)}, bf16[32,1280]{1,0:T(8,128)(2,1)S(1)}) custom-call(bf16[640,128]{1,0:T(8,128)(2,1)S(1)} %get-tuple-element.30.attended_ref, bf16[128,1280]{1,0:T(8,128)(2,1)S(1)} %get-tuple-element.31.ordered_ref, bf16[640,1280]{1,0:T(8,128)(2,1)S(1)} %copy-done), custom_call_target="tpu_custom_call" | custom-call | flops 209715200 | bytes 1638400 | tf_op jit(solution)/shard_map/project/pallas_call | solution.py:350
  27.8 1.4 %collective-permute-start.8 = (bf16[32,1280]{1,0:T(8,128)(2,1)S(1)}, bf16[32,1280]{1,0:T(8,128)(2,1)S(1)}, u32[]{:S(2)}, u32[]{:S(2)}) collective-permute-start(bf16[32,1280]{1,0:T(8,128)(2,1)S(1)} %get-tuple-element.44), channel_id=1, source_target_pairs={{0,8},{4,20},{8,0},{12,28},{16,24},{20,4},{24,16},{28,12},{1,9},{5... | collective-permute-start | bytes 245768 | tf_op jit(solution)/shard_map/ppermute | solution.py:491
  29.2 0.8 %collective-permute-start.9 = (bf16[32,1280]{1,0:T(8,128)(2,1)S(1)}, bf16[32,1280]{1,0:T(8,128)(2,1)S(1)}, u32[]{:S(2)}, u32[]{:S(2)}) collective-permute-start(bf16[32,1280]{1,0:T(8,128)(2,1)S(1)} %get-tuple-element.46), channel_id=1, source_target_pairs={{0,16},{4,12},{8,24},{12,4},{16,0},{20,28},{24,8},{28,20},{1,17},{... | collective-permute-start | bytes 245768 | tf_op jit(solution)/shard_map/ppermute | solution.py:491
  30.0 1.4 %collective-permute-start.10 = (bf16[32,1280]{1,0:T(8,128)(2,1)S(1)}, bf16[32,1280]{1,0:T(8,128)(2,1)S(1)}, u32[]{:S(2)}, u32[]{:S(2)}) collective-permute-start(bf16[32,1280]{1,0:T(8,128)(2,1)S(1)} %get-tuple-element.48), channel_id=1, source_target_pairs={{0,24},{4,28},{8,16},{12,20},{16,8},{20,12},{24,0},{28,4},{1,25},{... | collective-permute-start | bytes 245768 | tf_op jit(solution)/shard_map/ppermute | solution.py:491
  31.4 0.0 collective-permute-done.12.refs_3_
  31.4 0.1 collective-permute-done.11.refs_1_
  31.5 0.1 add_halves.4
  31.6 1.4 %collective-permute-start.13 = (bf16[80,640]{1,0:T(8,128)(2,1)S(1)}, bf16[80,640]{1,0:T(8,128)(2,1)S(1)}, u32[]{:S(2)}, u32[]{:S(2)}) collective-permute-start(bf16[80,640]{1,0:T(8,128)(2,1)S(1)} %get-tuple-element.50.refs_0_), channel_id=1, source_target_pairs={{0,2},{1,3},{2,0},{3,1},{4,6},{5,7},{6,4},{7,5},{8,10},{9,11},{10,... | collective-permute-start | bytes 307208 | tf_op jit(solution)/shard_map/ppermute | solution.py:486
  33.0 2.4 %collective-permute-start.14 = (bf16[80,640]{1,0:T(8,128)(2,1)S(1)}, bf16[80,640]{1,0:T(8,128)(2,1)S(1)}, u32[]{:S(2)}, u32[]{:S(2)}) collective-permute-start(bf16[80,640]{1,0:T(8,128)(2,1)S(1)} %get-tuple-element.51.refs_2_), channel_id=1, source_target_pairs={{0,1},{1,0},{2,3},{3,2},{4,5},{5,4},{6,7},{7,6},{8,9},{9,8},{10,11... | collective-permute-start | bytes 307208 | tf_op jit(solution)/shard_map/ppermute | solution.py:486
  35.4 0.0 collective-permute-done.8.refs_1_
  35.4 0.0 collective-permute-done.9.refs_2_
  35.4 0.0 collective-permute-done.10.refs_3_
  35.4 0.0 copy-done.1
  35.4 1.8 %place_rows.1 = bf16[160,5120]{1,0:T(8,128)(2,1)} custom-call(s32[1,160]{1,0:T(1,128)S(1)} %bitcast.4, bf16[32,1280]{1,0:T(8,128)(2,1)S(1)} %get-tuple-element.32.refs_0_, bf16[32,1280]{1,0:T(8,128)(2,1)S(1)} %collective-permute-done.8.refs_1_, bf16[32,1280]{1,0:T(8,128)(2,1)S(1)} %collective-permute-done.9.refs_2_, ...), custom_call_target="tpu_custom_call" | custom-call | flops 20971520000 | bytes 1638400 | tf_op jit(solution)/shard_map/place_rows/pallas_call | solution.py:441
  37.2 1.6 %collective-permute-done.13.refs_1_ = bf16[80,640]{1,0:T(8,128)(2,1)S(1)} collective-permute-done((bf16[80,640]{1,0:T(8,128)(2,1)S(1)}, bf16[80,640]{1,0:T(8,128)(2,1)S(1)}, u32[]{:S(2)}, u32[]{:S(2)}) %collective-permute-start.13) | collective-permute-done | bytes 102432 | tf_op jit(solution)/shard_map/ppermute | solution.py:486
  38.9 0.4 %collective-permute-done.14.refs_3_ = bf16[80,640]{1,0:T(8,128)(2,1)S(1)} collective-permute-done((bf16[80,640]{1,0:T(8,128)(2,1)S(1)}, bf16[80,640]{1,0:T(8,128)(2,1)S(1)}, u32[]{:S(2)}, u32[]{:S(2)}) %collective-permute-start.14) | collective-permute-done | bytes 102432 | tf_op jit(solution)/shard_map/ppermute | solution.py:486
  39.3 0.8 %add_halves.5 = f32[80,1280]{1,0:T(8,128)} custom-call(bf16[80,640]{1,0:T(8,128)(2,1)S(1)} %get-tuple-element.50.refs_0_, bf16[80,640]{1,0:T(8,128)(2,1)S(1)} %collective-permute-done.13.refs_1_, bf16[80,640]{1,0:T(8,128)(2,1)S(1)} %get-tuple-element.51.refs_2_, bf16[80,640]{1,0:T(8,128)(2,1)S(1)} %collective-permute-done.14.refs_3_), custom_call_target="tpu_custom_call" | custom-call | flops 102400 | bytes 819200 | tf_op jit(solution)/shard_map/add_halves/pallas_call | solution.py:469
  (2 shorter events, 0.0 us)
Async XLA Ops:
  0.6 5.3 %slice-start = ((s8[4915200]{0:T(1024)(128)(4,1)}), s8[4194304]{0:T(1024)(128)(4,1)S(1)}, s32[]{:S(2)}) async-start(s8[4915200]{0:T(1024)(128)(4,1)} %bitcast.1), calls=%async_computation | async-start | bytes 8388608
  0.6 5.3 %slice-start.1 = ((s8[4915200]{0:T(1024)(128)(4,1)}), s8[720896]{0:T(1024)(128)(4,1)S(1)}, s32[]{:S(2)}) async-start(s8[4915200]{0:T(1024)(128)(4,1)} %bitcast.1), calls=%async_computation.1 | async-start | bytes 1441792
  2.8 3.1 %collective-permute-start = (bf16[80,1280]{1,0:T(8,128)(2,1)S(1)}, bf16[80,1280]{1,0:T(8,128)(2,1)S(1)}, u32[]{:S(2)}, u32[]{:S(2)}) collective-permute-start(bf16[80,1280]{1,0:T(8,128)(2,1)S(1)} %get-tuple-element.28), channel_id=1, source_target_pairs={{0,4},{4,0},{8,12},{12,8},{16,20},{20,16},{24,28},{28,24},{1,5},{5... | collective-permute-start | bytes 614408 | tf_op jit(solution)/shard_map/ppermute | solution.py:486
  3.3 9.6 %collective-permute-start.4 = (bf16[128,1280]{1,0:T(8,128)(2,1)S(1)}, bf16[128,1280]{1,0:T(8,128)(2,1)S(1)}, u32[]{:S(2)}, u32[]{:S(2)}) collective-permute-start(bf16[128,1280]{1,0:T(8,128)(2,1)S(1)} %get-tuple-element.39.refs_3_.refs_4_), channel_id=1, source_target_pairs={{0,8},{4,20},{8,0},{12,28},{16,24},{20,4},{24,16},{28,12},{1,9},{5... | collective-permute-start | bytes 983048 | tf_op jit(solution)/shard_map/ppermute | solution.py:491
  7.7 10.1 %collective-permute-start.5 = (bf16[128,1280]{1,0:T(8,128)(2,1)S(1)}, bf16[128,1280]{1,0:T(8,128)(2,1)S(1)}, u32[]{:S(2)}, u32[]{:S(2)}) collective-permute-start(bf16[128,1280]{1,0:T(8,128)(2,1)S(1)} %get-tuple-element.39.refs_3_.refs_4_), channel_id=1, source_target_pairs={{0,16},{4,12},{8,24},{12,4},{16,0},{20,28},{24,8},{28,20},{1,17},{... | collective-permute-start | bytes 983048 | tf_op jit(solution)/shard_map/ppermute | solution.py:491
  10.9 4.4 %collective-permute-start.1 = (bf16[160,128]{1,0:T(8,128)(2,1)S(1)}, bf16[160,128]{1,0:T(8,128)(2,1)S(1)}, u32[]{:S(2)}, u32[]{:S(2)}) collective-permute-start(bf16[160,128]{1,0:T(8,128)(2,1)S(1)} %get-tuple-element.35), channel_id=1, source_target_pairs={{0,8},{4,20},{8,0},{12,28},{16,24},{20,4},{24,16},{28,12},{1,9},{5... | collective-permute-start | bytes 122888 | tf_op jit(solution)/shard_map/ppermute | solution.py:491
  12.3 5.4 %collective-permute-start.3 = (bf16[160,128]{1,0:T(8,128)(2,1)S(1)}, bf16[160,128]{1,0:T(8,128)(2,1)S(1)}, u32[]{:S(2)}, u32[]{:S(2)}) collective-permute-start(bf16[160,128]{1,0:T(8,128)(2,1)S(1)} %get-tuple-element.37), channel_id=1, source_target_pairs={{0,24},{4,28},{8,16},{12,20},{16,8},{20,12},{24,0},{28,4},{1,25},{... | collective-permute-start | bytes 122888 | tf_op jit(solution)/shard_map/ppermute | solution.py:491
  13.0 8.2 %collective-permute-start.6 = (bf16[128,1280]{1,0:T(8,128)(2,1)S(1)}, bf16[128,1280]{1,0:T(8,128)(2,1)S(1)}, u32[]{:S(2)}, u32[]{:S(2)}) collective-permute-start(bf16[128,1280]{1,0:T(8,128)(2,1)S(1)} %collective-permute-done.4.refs_4_.refs_5_), channel_id=1, source_target_pairs={{0,16},{4,12},{8,24},{12,4},{16,0},{20,28},{24,8},{28,20},{1,17},{... | collective-permute-start | bytes 983048 | tf_op jit(solution)/shard_map/ppermute | solution.py:491
  14.5 6.7 %collective-permute-start.2 = (bf16[160,128]{1,0:T(8,128)(2,1)S(1)}, bf16[160,128]{1,0:T(8,128)(2,1)S(1)}, u32[]{:S(2)}, u32[]{:S(2)}) collective-permute-start(bf16[160,128]{1,0:T(8,128)(2,1)S(1)} %get-tuple-element.36), channel_id=1, source_target_pairs={{0,16},{4,12},{8,24},{12,4},{16,0},{20,28},{24,8},{28,20},{1,17},{... | collective-permute-start | bytes 122888 | tf_op jit(solution)/shard_map/ppermute | solution.py:491
  18.2 9.2 %copy-start = (bf16[640,1280]{1,0:T(8,128)(2,1)S(1)}, bf16[640,1280]{1,0:T(8,128)(2,1)}, u32[]{:S(2)}) copy-start(bf16[640,1280]{1,0:T(8,128)(2,1)} %w_ref.3) | copy-start | bytes 4915204
  21.5 13.9 %copy-start.1 = (s32[160]{0:T(256)S(1)}, s32[160]{0:T(256)}, u32[]{:S(2)}) copy-start(s32[160]{0:T(256)} %param.11) | copy-start | bytes 1924
  21.6 1.5 %collective-permute-start.7 = (bf16[80,1280]{1,0:T(8,128)(2,1)S(1)}, bf16[80,1280]{1,0:T(8,128)(2,1)S(1)}, u32[]{:S(2)}, u32[]{:S(2)}) collective-permute-start(bf16[80,1280]{1,0:T(8,128)(2,1)S(1)} %get-tuple-element.42), channel_id=1, source_target_pairs={{0,4},{4,0},{8,12},{12,8},{16,20},{20,16},{24,28},{28,24},{1,5},{5... | collective-permute-start | bytes 614408 | tf_op jit(solution)/shard_map/ppermute | solution.py:486
  23.1 8.3 %collective-permute-start.12 = (bf16[80,640]{1,0:T(8,128)(2,1)S(1)}, bf16[80,640]{1,0:T(8,128)(2,1)S(1)}, u32[]{:S(2)}, u32[]{:S(2)}) collective-permute-start(bf16[80,640]{1,0:T(8,128)(2,1)S(1)} %get-tuple-element.49.refs_2_), channel_id=1, source_target_pairs={{0,2},{1,3},{2,0},{3,1},{4,6},{5,7},{6,4},{7,5},{8,10},{9,11},{10,... | collective-permute-start | bytes 307208 | tf_op jit(solution)/shard_map/ppermute | solution.py:486
  25.8 5.7 %collective-permute-start.11 = (bf16[80,640]{1,0:T(8,128)(2,1)S(1)}, bf16[80,640]{1,0:T(8,128)(2,1)S(1)}, u32[]{:S(2)}, u32[]{:S(2)}) collective-permute-start(bf16[80,640]{1,0:T(8,128)(2,1)S(1)} %get-tuple-element.43.refs_0_), channel_id=1, source_target_pairs={{0,1},{1,0},{2,3},{3,2},{4,5},{5,4},{6,7},{7,6},{8,9},{9,8},{10,11... | collective-permute-start | bytes 307208 | tf_op jit(solution)/shard_map/ppermute | solution.py:486
  27.8 7.6 %collective-permute-start.8 = (bf16[32,1280]{1,0:T(8,128)(2,1)S(1)}, bf16[32,1280]{1,0:T(8,128)(2,1)S(1)}, u32[]{:S(2)}, u32[]{:S(2)}) collective-permute-start(bf16[32,1280]{1,0:T(8,128)(2,1)S(1)} %get-tuple-element.44), channel_id=1, source_target_pairs={{0,8},{4,20},{8,0},{12,28},{16,24},{20,4},{24,16},{28,12},{1,9},{5... | collective-permute-start | bytes 245768 | tf_op jit(solution)/shard_map/ppermute | solution.py:491
  29.2 6.2 %collective-permute-start.9 = (bf16[32,1280]{1,0:T(8,128)(2,1)S(1)}, bf16[32,1280]{1,0:T(8,128)(2,1)S(1)}, u32[]{:S(2)}, u32[]{:S(2)}) collective-permute-start(bf16[32,1280]{1,0:T(8,128)(2,1)S(1)} %get-tuple-element.46), channel_id=1, source_target_pairs={{0,16},{4,12},{8,24},{12,4},{16,0},{20,28},{24,8},{28,20},{1,17},{... | collective-permute-start | bytes 245768 | tf_op jit(solution)/shard_map/ppermute | solution.py:491
  30.0 5.4 %collective-permute-start.10 = (bf16[32,1280]{1,0:T(8,128)(2,1)S(1)}, bf16[32,1280]{1,0:T(8,128)(2,1)S(1)}, u32[]{:S(2)}, u32[]{:S(2)}) collective-permute-start(bf16[32,1280]{1,0:T(8,128)(2,1)S(1)} %get-tuple-element.48), channel_id=1, source_target_pairs={{0,24},{4,28},{8,16},{12,20},{16,8},{20,12},{24,0},{28,4},{1,25},{... | collective-permute-start | bytes 245768 | tf_op jit(solution)/shard_map/ppermute | solution.py:491
  31.6 7.3 %collective-permute-start.13 = (bf16[80,640]{1,0:T(8,128)(2,1)S(1)}, bf16[80,640]{1,0:T(8,128)(2,1)S(1)}, u32[]{:S(2)}, u32[]{:S(2)}) collective-permute-start(bf16[80,640]{1,0:T(8,128)(2,1)S(1)} %get-tuple-element.50.refs_0_), channel_id=1, source_target_pairs={{0,2},{1,3},{2,0},{3,1},{4,6},{5,7},{6,4},{7,5},{8,10},{9,11},{10,... | collective-permute-start | bytes 307208 | tf_op jit(solution)/shard_map/ppermute | solution.py:486
  33.0 6.3 %collective-permute-start.14 = (bf16[80,640]{1,0:T(8,128)(2,1)S(1)}, bf16[80,640]{1,0:T(8,128)(2,1)S(1)}, u32[]{:S(2)}, u32[]{:S(2)}) collective-permute-start(bf16[80,640]{1,0:T(8,128)(2,1)S(1)} %get-tuple-element.51.refs_2_), channel_id=1, source_target_pairs={{0,1},{1,0},{2,3},{3,2},{4,5},{5,4},{6,7},{7,6},{8,9},{9,8},{10,11... | collective-permute-start | bytes 307208 | tf_op jit(solution)/shard_map/ppermute | solution.py:486
